TPU v7x, 32 devices: a whole 2x2x4 slice. The times are simulated.
32 devices in a mesh: row: 4 (over y, x), col: 8 (over z, core).
Axes of the slice: x: 2, y: 2, z: 4, core: 2. Of those that a mesh axis runs over, the one named last changes fastest.
Arguments:
- ancestor: float32 [2, 1024, 1024], P(None, 'row', 'col')
- panel: float32 [2, 1024, 512], P(None, 'col'), may hold values from -0.75 to 0.75
- factor_inv: float32 [2, 512, 512], P(None, 'row'), as said below
- pattern: int32 [2, 4], replicated, may hold values from 0 to 3, each once within a row
Outputs:
- column_block: float32 [2, 1024, 512], P(None, ('row', 'col'))
- diagonal_inv: float32 [2, 512], replicated
Inputs may be any that keep to these rules, and one draw needn't show every extreme that they name: `pattern`: each row names each of the 4 tile positions exactly once. `factor_inv`: each block is lower triangular with its diagonal between 0.5 and 2.
All inputs are finite; a program needn't handle non-finite values.
Results may differ from a plain program's by a relative error of at most 0.0001.
Values sent between devices are 32-bit elements; how exact they have to be, the bound alone decides.
No kernel may reach another device: no remote copies, remote signals or barrier semaphores. Data moves between devices by JAX's collectives and lax.ppermute only.
A program may use at most 64 MiB of HBM per device.

v0:
```python
import jax
import jax.numpy as jnp
from jax import lax
from jax.sharding import PartitionSpec as P

B = 256


def scatter_rows(totals, targets, limit, pieces):
    inside = (targets >= 0) & (targets < limit)
    targets = jnp.where(inside, targets, limit)

    def one_group(accum, target, values):
        return accum.at[target].add(values, mode="drop")

    return jax.vmap(one_group)(totals, targets, pieces)


def spread_tiles(moving, pattern, row_first, col_first, row_count, col_count):
    groups = moving.shape[0]
    width_cols = moving.shape[2]
    initial = (
        jnp.zeros((groups, col_count, width_cols), jnp.float32),
        jnp.zeros((groups, row_count, width_cols), jnp.float32),
    )
    pieces = lax.all_gather(moving, "col", axis=1, tiled=True)
    count = pieces.shape[1]
    global_rows = jnp.arange(count, dtype=jnp.int32)
    ancestor_rows = jnp.take(pattern, global_rows // B, axis=1) * B + global_rows % B
    col_totals = scatter_rows(initial[0], ancestor_rows - col_first, col_count, pieces)
    row_totals = scatter_rows(initial[1], ancestor_rows - row_first, row_count, pieces)
    return (col_totals, row_totals)


def per_device(ancestor, panel, factor_inv, pattern):
    highest = lax.Precision.HIGHEST
    row_count = ancestor.shape[1]
    col_count = ancestor.shape[2]
    row_first = lax.axis_index("row") * row_count
    col_first = lax.axis_index("col") * col_count
    full_inverse = lax.all_gather(factor_inv, "row", axis=1, tiled=True)
    moving = jnp.einsum("srw,swv->srv", panel, full_inverse, precision=highest)
    col_part, row_part = spread_tiles(moving, pattern, row_first, col_first, row_count, col_count)
    partial_value = jnp.einsum("sij,sjw->siw", ancestor, col_part, precision=highest)
    summed = lax.psum_scatter(partial_value, "col", scatter_dimension=1, tiled=True)
    column_sq = jnp.sum(full_inverse * full_inverse, axis=1)
    local_terms = jnp.sum(row_part * partial_value, axis=1)
    totals = lax.psum(local_terms, ("row", "col"))
    column_block = -summed
    diagonal_inv = column_sq + totals
    return (column_block, diagonal_inv)


def solution(mesh):
    in_specs = (P(None, "row", "col"), P(None, "col", None), P(None, "row", None), P())
    out_specs = (P(None, ("row", "col"), None), P())
    return jax.shard_map(
        per_device, mesh=mesh, in_specs=in_specs, out_specs=out_specs, check_vma=False
    )
```

profile of v0, /device:TPU:0, one launch (start us, length us, event | category | flops | bytes accessed | tf_op | source)
XLA Modules:
  0.0 178.0 jit_solution(3011049615384248206)
XLA Ops:
  7.2 0.0 copy-start
  7.2 0.0 copy-start.6
  7.2 0.0 copy-start.7
  7.2 0.0 copy-start.4
  7.2 0.0 copy-start.5
  7.2 0.0 copy-start.3
  7.2 0.0 all-gather.3.cloned.1.call-start
  7.3 0.7 all-gather.3.cloned.1.call-update
  8.0 0.0 all-gather.5.cloned.1.call-start
  8.0 39.9 %all-gather.3.cloned.1.call-done = f32[2,512,512]{2,1,0:T(8,128)} async-done(((f32[2,128,512]{2,1,0:T(8,128)}), f32[2,512,512]{2,1,0:T(8,128)}) %all-gather.3.cloned.1.call-update) | async-done | bytes 2097168 | tf_op jit(solution)/shard_map/all_gather | solution.py:41
  48.0 0.0 copy-done
  48.0 3.7 %fusion.16 = f32[2,128,512]{2,1,0:T(8,128)} fusion(f32[2,128,512]{2,1,0:T(8,128)S(1)} %copy-done, f32[2,512,512]{2,1,0:T(8,128)} %all-gather.3.cloned.1.call-done), kind=kOutput, calls=%fused_computation.46 | convolution fusion | flops 805306368 | bytes 3145728 | tf_op jit(solution)/shard_map/srw,swv->srv/dot_general | solution.py:42
  51.7 0.0 all-gather.5.cloned.1.call-update
  51.7 0.0 reduce-scatter.2.cloned.1.call-start
  51.7 0.0 copy-done.3
  51.8 0.1 copy.15
  51.9 2.8 %gather_fusion = s32[1024,2]{1,0:T(8,128)S(1)} fusion(s32[2,4]{0,1:T(4,128)S(1)} %copy.15, s32[1024]{0:T(1024)S(1)} %broadcast_clamp_fusion), kind=kCustom, calls=%fused_computation | custom fusion | bytes 20480 | tf_op jit(solution)/shard_map/jit(_take)/gather | solution.py:29
  54.7 0.0 copy-start.2
  54.7 0.9 compare_select_fusion.1
  55.6 0.2 copy.16
  55.8 0.2 copy.20
  56.0 0.0 copy-done.6
  56.0 0.0 copy-done.7
  56.0 0.1 and_reduce_fusion
  56.1 0.3 copy.26
  56.4 0.3 copy.24
  56.7 0.0 copy-done.4
  56.7 0.0 copy-done.5
  56.7 0.1 multiply_reduce_fusion.2
  56.9 0.2 copy.27
  57.1 0.1 broadcast_select_fusion
  57.2 0.0 copy-start.1
  57.2 0.2 copy.23
  57.4 0.6 copy.32
  58.0 0.2 copy.25
  58.2 0.9 broadcast_select_fusion.1
  59.1 1.2 copy.19
  60.3 38.7 %all-gather.5.cloned.1.call-done = f32[2,1024,512]{2,1,0:T(8,128)} async-done(((f32[2,128,512]{2,1,0:T(8,128)}), f32[2,1024,512]{2,1,0:T(8,128)}) %all-gather.5.cloned.1.call-update) | async-done | bytes 4194320 | tf_op jit(solution)/shard_map/all_gather | solution.py:26
  99.0 13.4 %scatter_custom_fusion = f32[256,512]{1,0:T(8,128)S(1)} fusion(s32[2048]{0:T(1024)S(1)} %bitcast.36, f32[2048,512]{1,0:T(8,128)} %bitcast.37, f32[]{:T(128)} %constant.52.clone.1), kind=kCustom, calls=%fused_computation.13 | custom fusion | flops 1048576 | bytes 524800
  112.4 14.3 %scatter_custom_fusion.1 = f32[512,512]{1,0:T(8,128)} fusion(s32[2048]{0:T(1024)} %bitcast.35, f32[2048,512]{1,0:T(8,128)} %bitcast.38, f32[]{:T(128)} %constant.52.clone.1), kind=kCustom, calls=%fused_computation.11 | custom fusion | flops 1048576 | bytes 1049088
  126.6 0.0 copy-done.2
  126.6 3.2 %multiply_reduce_fusion.1 = (f32[2,512]{1,0:T(2,128)S(1)}, f32[2,256,512]{2,1,0:T(8,128)}) fusion(f32[512,512]{1,0:T(8,128)} %scatter_custom_fusion.1, f32[2,128,512]{2,1,0:T(8,128)S(1)} %bitcast.31, f32[2,256,128]{2,1,0:T(8,128)S(1)} %copy-done.2), kind=kOutput, calls=%fused_computation.7 | convolution fusion | flops 403176448 | bytes 2887680 | tf_op jit(solution)/shard_map/sij,sjw->siw/dot_general | solution.py:44
  129.8 0.0 reduce-scatter.2.cloned.1.call-update
  129.9 0.0 copy-done.1
  129.9 0.2 multiply_reduce_fusion
  130.1 39.2 %psum.7 = f32[2,512]{1,0:T(2,128)S(1)} all-reduce(f32[2,512]{1,0:T(2,128)S(1)} %get-tuple-element.8), channel_id=1, replica_groups=mesh['row'=4,'col'=8] {'row','col'}, use_global_device_ids=true, to_apply=%region_5.6 | all-reduce | flops 1024 | bytes 8192 | tf_op jit(solution)/shard_map/psum | solution.py:48
  169.3 0.6 add.100
  169.9 1.6 neg.3
  (7 shorter events, 0.0 us)
Async XLA Ops:
  7.2 40.8 %copy-start = (f32[2,128,512]{2,1,0:T(8,128)S(1)}, f32[2,128,512]{2,1,0:T(8,128)}, u32[]{:S(2)}) copy-start(f32[2,128,512]{2,1,0:T(8,128)} %param.5) | copy-start | bytes 1572868
  7.2 48.8 %copy-start.6 = (s32[2]{0:T(128)S(1)}, s32[2]{0:T(128)}, u32[]{:S(2)}) copy-start(s32[2]{0:T(128)} %constant.74) | copy-start | bytes 28
  7.2 48.8 %copy-start.7 = (s32[2]{0:T(128)S(1)}, s32[2]{0:T(128)}, u32[]{:S(2)}) copy-start(s32[2]{0:T(128)} %constant.68) | copy-start | bytes 28
  7.2 49.5 %copy-start.4 = (s32[2]{0:T(128)S(1)}, s32[2]{0:T(128)}, u32[]{:S(2)}) copy-start(s32[2]{0:T(128)} %constant.71) | copy-start | bytes 28
  7.2 49.5 %copy-start.5 = (s32[2]{0:T(128)S(1)}, s32[2]{0:T(128)}, u32[]{:S(2)}) copy-start(s32[2]{0:T(128)} %constant.65) | copy-start | bytes 28
  7.2 44.5 %copy-start.3 = (s32[2,4]{1,0:T(2,128)S(1)}, s32[2,4]{1,0:T(2,128)}, u32[]{:S(2)}) copy-start(s32[2,4]{1,0:T(2,128)} %param.7) | copy-start | bytes 100
  7.2 40.7 %all-gather.3.cloned.1.call-start = ((), (), s32[]{:S(2)}) async-start(), calls=%async_computation.1 | async-start | bytes 2621440 | tf_op jit(solution)/shard_map/all_gather | solution.py:41
  8.0 91.0 %all-gather.5.cloned.1.call-start = ((), (), s32[]{:S(2)}) async-start(), calls=%async_computation.2 | async-start | bytes 4718592 | tf_op jit(solution)/shard_map/all_gather | solution.py:26
  51.7 118.2 %reduce-scatter.2.cloned.1.call-start = ((), (), s32[]{:S(2)}) async-start(), calls=%async_computation.3 | async-start | bytes 1179648 | tf_op jit(solution)/shard_map/reduce_scatter | solution.py:45
  54.7 71.9 %copy-start.2 = (f32[2,256,128]{2,1,0:T(8,128)S(1)}, f32[2,256,128]{2,1,0:T(8,128)}, u32[]{:S(2)}) copy-start(f32[2,256,128]{2,1,0:T(8,128)} %param.4) | copy-start | bytes 786436
  57.2 72.7 %copy-start.1 = (f32[2,512,512]{2,1,0:T(8,128)S(1)}, f32[2,512,512]{2,1,0:T(8,128)}, u32[]{:S(2)}) copy-start(f32[2,512,512]{2,1,0:T(8,128)} %all-gather.3.cloned.1.call-done) | copy-start | bytes 6291460
Sparse Core Ops, SparseCore 0:
  9.9 38.0 all-gather.2
  51.8 47.1 all-gather.4
  130.0 31.3 reduce-scatter.1
where the time goes:
time: 178 us
  waiting for transfers between devices  79.3 us (45%)
  blocking collectives  39.2 us (22%)
  other arithmetic  32.1 us (18%)
  between operations  13.9 us (8%)
  matrix products  6.92 us (4%)
  local copies, waits for them, and re-layouts  6.42 us (4%)
    all_gather x1, waiting for transfers between devices, per_device(): full_inverse = lax.all_gather(factor_inv, 'row', axis=1, tiled=True)  39.9 us
    psum x1, blocking collectives, per_device(): totals = lax.psum(local_terms, ('row', 'col'))  39.2 us
    all_gather x1, waiting for transfers between devices, spread_tiles(): pieces = lax.all_gather(moving, 'col', axis=1, tiled=True)  38.7 us
    unnamed x6, other arithmetic  28.8 us
    dot_general x1, matrix products, per_device(): moving = jnp.einsum('srw,swv->srv', panel, full_inverse, precision=highest)  3.7 us
  transfers between devices with their start and end apart: 3, of which 2 were waited for; matrix products, arithmetic and copies ran while one was open for 5% of the time, Pallas kernels for 0%

commit v1 on v0

v1 whole, which is shorter than its diff:
```python
import jax
import jax.numpy as jnp
from jax import lax
from jax.sharding import PartitionSpec as P

B = 256


def pick_rows(pieces, pattern, first):
    count = pieces.shape[0]
    per_tile = count // pattern.shape[1]
    tile, within = first // per_tile, first % per_tile
    picked = []
    for s in range(pattern.shape[0]):
        stored = jnp.argmax(pattern[s] == tile).astype(jnp.int32)
        chunk = stored * per_tile + within
        picked.append(lax.dynamic_index_in_dim(pieces[:, s], chunk, 0, keepdims=False))
    return jnp.stack(picked)


def solution(mesh):
    rows, cols = mesh.shape["row"], mesh.shape["col"]
    highest = lax.Precision.HIGHEST

    def per_device(ancestor, panel, factor_inv, pattern):
        row = lax.axis_index("row")
        col = lax.axis_index("col")
        depth = factor_inv.shape[1]
        mine = lax.dynamic_slice_in_dim(panel, row * depth, depth, axis=2)
        part = jnp.einsum("srw,swv->srv", mine, factor_inv, precision=highest)
        scaled = lax.psum_scatter(part, "row", scatter_dimension=1, tiled=True)
        pieces = lax.all_gather(scaled, "col", axis=0, tiled=False)
        chosen = pick_rows(pieces, pattern, col)
        swap = [(r * cols + c, c * rows + r) for r in range(rows) for c in range(cols)]
        own_rows = lax.ppermute(chosen, ("row", "col"), swap)
        spread = lax.all_gather(chosen, "row", axis=1, tiled=True)
        partial = jnp.einsum("sij,sjw->siw", ancestor, spread, precision=highest)
        product = lax.psum_scatter(partial, "col", scatter_dimension=1, tiled=True)
        squares = jnp.sum(factor_inv * factor_inv, axis=1)
        terms = jnp.sum(own_rows * product, axis=1) + jnp.where(col == 0, squares, 0.0)
        diagonal_inv = lax.psum(terms, ("row", "col"))
        return -product, diagonal_inv

    in_specs = (P(None, "row", "col"), P(None, "col", None), P(None, "row", None), P())
    out_specs = (P(None, ("row", "col"), None), P())
    return jax.shard_map(
        per_device, mesh=mesh, in_specs=in_specs, out_specs=out_specs, check_vma=False
    )
```

time: 178 us -> 154 us (0.87)
  other arithmetic: 32.1 us -> 2.96 us
  blocking collectives: 39.2 us -> 47 us
  local copies, waits for them, and re-layouts: 6.42 us -> 3.17 us
  matrix products: 6.92 us -> 4.41 us
    reduce_scatter x1 -> x2, waiting for transfers between devices: 0.01 us -> 58.9 us  [the longest x1 31.2 us: per_device(): product = lax.psum_scatter(partial, 'col', scatter_dimension=1, tiled=True)]
    all_gather x2 -> x1, waiting for transfers between devices: 78.6 us -> 20.4 us  [per_device(): pieces = lax.all_gather(scaled, 'col', axis=0, tiled=False)]
    unnamed x6 -> x0, other arithmetic: 28.8 us -> none
    all_gather x0 -> x1, blocking collectives: none -> 10.1 us  [per_device(): spread = lax.all_gather(chosen, 'row', axis=1, tiled=True)]
    gather x1 -> x0, local copies, waits for them, and re-layouts: 2.81 us -> none  [spread_tiles(): jnp.take(pattern, global_rows // B, axis=1) * B + global_rows % B]
    dot_general x2, matrix products: 6.92 us -> 4.41 us  [the longest x1 2.41 us: per_device(): part = jnp.einsum('srw,swv->srv', mine, factor_inv, precision=highest)]
    psum x1, blocking collectives: 39.2 us -> 36.9 us  [per_device(): diagonal_inv = lax.psum(terms, ('row', 'col'))]
  transfers between devices with their start and end apart: 3 -> 4, of which waited for: 2 -> 3; matrix products, arithmetic and copies ran while one was open for 5% -> 1% of each run, Pallas kernels for 0% -> 0%
where the time goes in v1:
time: 154 us; the launch traced here: 153 us
  waiting for transfers between devices  79.4 us (52%)
  blocking collectives  47 us (31%)
  between operations  15.2 us (10%)
  matrix products  4.41 us (3%)
  local copies, waits for them, and re-layouts  3.17 us (2%)
  other arithmetic  2.96 us (2%)
    psum x1, blocking collectives, per_device(): diagonal_inv = lax.psum(terms, ('row', 'col'))  36.9 us
    reduce_scatter x1, waiting for transfers between devices, per_device(): product = lax.psum_scatter(partial, 'col', scatter_dimension=1, tiled=True)  31.2 us
    reduce_scatter x1, waiting for transfers between devices, per_device(): scaled = lax.psum_scatter(part, 'row', scatter_dimension=1, tiled=True)  27.7 us
    all_gather x1, waiting for transfers between devices, per_device(): pieces = lax.all_gather(scaled, 'col', axis=0, tiled=False)  20.4 us
    all_gather x1, blocking collectives, per_device(): spread = lax.all_gather(chosen, 'row', axis=1, tiled=True)  10.1 us
  transfers between devices with their start and end apart: 4, of which 3 were waited for; matrix products, arithmetic and copies ran while one was open for 1% of the time, Pallas kernels for 0%

profile of v1, /device:TPU:0, one launch (start us, length us, event | category | flops | bytes accessed | tf_op | source)
XLA Modules:
  0.0 153.0 jit_solution(685957607138778069)
XLA Ops:
  7.2 0.0 copy-start
  7.2 0.0 reduce-scatter.3.cloned.1.call-start
  7.2 1.0 copy-done
  8.2 2.4 %fusion = f32[2,128,512]{2,1,0:T(8,128)} fusion(f32[2,128,512]{2,1,0:T(8,128)} %param.6, f32[2,128,512]{2,1,0:T(8,128)S(1)} %copy-done, s32[]{:T(128)S(6)} %select_n.35), kind=kOutput, calls=%fused_computation.4 | convolution fusion | flops 201326592 | bytes 1179652 | tf_op jit(solution)/shard_map/srw,swv->srv/dot_general | solution.py:30
  10.6 0.0 reduce-scatter.3.cloned.1.call-update
  10.6 0.0 all-gather.3.cloned.1.call-start
  10.7 27.7 %reduce-scatter.3.cloned.1.call-done = f32[2,32,512]{2,1,0:T(8,128)} async-done(((f32[2,128,512]{2,1,0:T(8,128)}), f32[2,32,512]{2,1,0:T(8,128)}) %reduce-scatter.3.cloned.1.call-update) | async-done | bytes 131088 | tf_op jit(solution)/shard_map/reduce_scatter | solution.py:31
  38.4 0.0 all-gather.3.cloned.1.call-update
  38.4 0.0 reduce-scatter.5.cloned.1.call-start
  38.4 0.0 copy-start.3
  38.5 0.7 copy-done.3
  39.1 0.7 bitcast_reduce_fusion
  40.4 0.7 bitcast_reduce_fusion.1
  41.8 20.4 %all-gather.3.cloned.1.call-done = f32[16,32,512]{2,1,0:T(8,128)} async-done(((f32[2,32,512]{2,1,0:T(8,128)}), f32[16,32,512]{2,1,0:T(8,128)}) %all-gather.3.cloned.1.call-update) | async-done | bytes 1048592 | tf_op jit(solution)/shard_map/all_gather | solution.py:32
  62.2 1.3 fusion.3
  63.5 0.0 copy-start.2
  63.6 10.1 %all_gather.11 = f32[2,128,512]{2,1,0:T(8,128)S(1)} all-gather(f32[2,32,512]{2,1,0:T(8,128)S(1)} %pad_maximum_fusion), channel_id=1, replica_groups=mesh['row'=4,'col'=8] {'row'}, dimensions={1}, use_global_device_ids=true | all-gather | bytes 655360 | tf_op jit(solution)/shard_map/all_gather | solution.py:36
  73.6 0.0 copy-done.2
  73.7 2.0 %convolution_bitcast_fusion = f32[2,256,512]{2,1,0:T(8,128)} fusion(f32[2,128,512]{2,1,0:T(8,128)S(1)} %all_gather.11, f32[2,256,128]{2,1,0:T(8,128)S(1)} %copy-done.2), kind=kOutput, calls=%fused_computation | convolution fusion | flops 402653184 | bytes 1835008 | tf_op jit(solution)/shard_map/sij,sjw->siw/dot_general | solution.py:37
  75.7 0.0 copy-start.1
  75.7 0.0 reduce-scatter.5.cloned.1.call-update
  75.7 0.8 collective-permute-start
  76.5 0.2 copy-done.1
  76.7 0.1 multiply_reduce_fusion
  76.8 0.0 collective-permute-done
  76.8 31.2 %reduce-scatter.5.cloned.1.call-done = f32[2,32,512]{2,1,0:T(8,128)} async-done(((f32[2,256,512]{2,1,0:T(8,128)}), f32[2,32,512]{2,1,0:T(8,128)}) %reduce-scatter.5.cloned.1.call-update) | async-done | bytes 131088 | tf_op jit(solution)/shard_map/reduce_scatter | solution.py:38
  108.0 1.6 %multiply_reduce_fusion.1 = (f32[2,512]{1,0:T(2,128)S(1)}, f32[2,32,512]{2,1,0:T(8,128)}) fusion(f32[2,32,512]{2,1,0:T(8,128)S(1)} %collective-permute-done, f32[2,32,512]{2,1,0:T(8,128)} %reduce-scatter.5.cloned.1.call-done), kind=kLoop, calls=%fused_computation.3 | loop fusion | flops 97280 | bytes 397312 | tf_op jit(solution)/shard_map/reduce_sum | solution.py:40
  109.6 36.9 %psum.7 = f32[2,512]{1,0:T(2,128)} all-reduce(f32[2,512]{1,0:T(2,128)S(1)} %select_add_fusion), channel_id=1, replica_groups=mesh['row'=4,'col'=8] {'row','col'}, use_global_device_ids=true, to_apply=%region_6.7 | all-reduce | flops 1024 | bytes 8192 | tf_op jit(solution)/shard_map/psum | solution.py:41
  (3 shorter events, 0.0 us)
Async XLA Ops:
  7.2 1.0 copy-start
  7.2 31.2 %reduce-scatter.3.cloned.1.call-start = ((), (), s32[]{:S(2)}) async-start(), calls=%async_computation.2 | async-start | bytes 655360 | tf_op jit(solution)/shard_map/reduce_scatter | solution.py:31
  10.6 51.6 %all-gather.3.cloned.1.call-start = ((), (), s32[]{:S(2)}) async-start(), calls=%async_computation.4 | async-start | bytes 1179648 | tf_op jit(solution)/shard_map/all_gather | solution.py:32
  38.4 69.6 %reduce-scatter.5.cloned.1.call-start = ((), (), s32[]{:S(2)}) async-start(), calls=%async_computation.3 | async-start | bytes 1179648 | tf_op jit(solution)/shard_map/reduce_scatter | solution.py:38
  38.4 0.7 copy-start.3
  63.5 10.1 %copy-start.2 = (f32[2,256,128]{2,1,0:T(8,128)S(1)}, f32[2,256,128]{2,1,0:T(8,128)}, u32[]{:S(2)}) copy-start(f32[2,256,128]{2,1,0:T(8,128)} %param.4) | copy-start | bytes 786436
  75.7 1.0 copy-start.1
  75.7 1.1 collective-permute-start
Sparse Core Ops, SparseCore 0:
  10.8 27.4 reduce-scatter.2
  40.0 22.1 all-gather.2
  75.8 32.1 reduce-scatter.4

commit v2 on v1

v2 whole, which is shorter than its diff:
```python
import jax
import jax.numpy as jnp
from jax import lax
from jax.sharding import PartitionSpec as P

B = 256


def solution(mesh):
    rows, cols = mesh.shape["row"], mesh.shape["col"]
    highest = lax.Precision.HIGHEST

    def per_device(ancestor, panel, factor_inv, pattern):
        row = lax.axis_index("row")
        col = lax.axis_index("col")
        groups, chunk, width = panel.shape
        quarter = chunk // rows
        part = width // cols
        out_rows = ancestor.shape[1] // cols

        mine = lax.dynamic_slice_in_dim(panel, row * quarter, quarter, axis=1)
        pieces = lax.all_gather(mine, "col", axis=0)
        wide = lax.all_gather(ancestor, "col", axis=0)
        columns = lax.dynamic_slice_in_dim(factor_inv, col * part, part, axis=2)
        columns = lax.all_gather(columns, "row", axis=1, tiled=True)

        scaled = jnp.einsum("csqw,swk->cqsk", pieces, columns, precision=highest)
        scaled = scaled.reshape(cols, quarter, groups * part)
        scaled = lax.all_gather(scaled, "row", axis=1, tiled=True)
        scaled = scaled.reshape(pattern.shape[1], B, groups, part)
        order = jnp.argsort(pattern, axis=1)
        products, terms = [], []
        for s in range(groups):
            spread = jnp.take(scaled[:, :, s], order[s], axis=0).reshape(-1, part)
            product = jnp.einsum(
                "cij,cjk->ik", wide[:, s], spread.reshape(cols, chunk, part), precision=highest
            )
            own = lax.dynamic_slice_in_dim(spread, row * product.shape[0], product.shape[0], axis=0)
            squares = jnp.where(row == 0, jnp.sum(columns[s] * columns[s], axis=0), 0.0)
            terms.append(jnp.sum(own * product, axis=0) + squares)
            products.append(product)
        product = jnp.concatenate(products, axis=1).reshape(cols, out_rows, groups * part)
        term = jnp.concatenate(terms)
        tail = jnp.broadcast_to(term, (cols, 8, groups * part))
        moved = lax.all_to_all(jnp.concatenate([product, tail], axis=1), "col", 0, 0)
        moved = moved.reshape(cols, out_rows + 8, groups, part)
        moved = moved.transpose(2, 1, 0, 3).reshape(groups, out_rows + 8, width)
        local = moved[:, out_rows]
        total = local
        for shift in range(1, rows):
            total = total + lax.ppermute(
                local, "row", [(r, (r + shift) % rows) for r in range(rows)]
            )
        return -moved[:, :out_rows], total

    in_specs = (P(None, "row", "col"), P(None, "col", None), P(None, "row", None), P())
    out_specs = (P(None, ("row", "col"), None), P())
    return jax.shard_map(
        per_device, mesh=mesh, in_specs=in_specs, out_specs=out_specs, check_vma=False
    )
```

time: 154 us -> 95.7 us (0.62)
  waiting for transfers between devices: 79.4 us -> 26.7 us
  blocking collectives: 47 us -> 31.7 us
  local copies, waits for them, and re-layouts: 3.17 us -> 9.1 us
  starting transfers between devices: 0.92 us -> 4.51 us
  matrix products: 4.41 us -> 7.05 us
    reduce_scatter x2 -> x0, waiting for transfers between devices: 58.9 us -> none  [the longest x1 31.2 us: per_device(): product = lax.psum_scatter(partial, 'col', scatter_dimension=1, tiled=True)]
    psum x1 -> x0, blocking collectives: 36.9 us -> none  [per_device(): diagonal_inv = lax.psum(terms, ('row', 'col'))]
    all_gather x1 -> x2, blocking collectives: 10.1 us -> 21.5 us  [the longest x1 11.5 us: per_device(): columns = lax.all_gather(columns, 'row', axis=1, tiled=True)]
    all_to_all x0 -> x1, blocking collectives: none -> 10.2 us  [per_device(): lax.all_to_all(jnp.concatenate([product, tail], axis=1), 'col', 0, 0)]
    all_gather x1 -> x2, waiting for transfers between devices: 20.4 us -> 24.6 us  [the longest x1 13.5 us: per_device(): wide = lax.all_gather(ancestor, 'col', axis=0)]
    ppermute x1 -> x3, starting transfers between devices: 0.8 us -> 4.43 us  [per_device(): lax.ppermute(local, 'row', [(r, (r + shift) % rows) for r in range(rows)])]
    dot_general x2 -> x3, matrix products: 4.41 us -> 7.05 us  [the longest x2 4.84 us: per_device(): jnp.einsum('cij,cjk->ik', wide[:, s], spread.reshape(cols, chunk, part),...]
    dynamic_slice x1 -> x2, local copies, waits for them, and re-layouts: 0.02 us -> 1.66 us  [the longest x1 1 us: per_device(): columns = lax.dynamic_slice_in_dim(factor_inv, col * part, part, axis=2)]
  transfers between devices with their start and end apart: 4 -> 5, of which waited for: 3 -> 3; matrix products, arithmetic and copies ran while one was open for 1% -> 11% of each run, Pallas kernels for 0% -> 0%
where the time goes in v2:
time: 95.7 us; the launch traced here: 95.3 us
  blocking collectives  31.7 us (33%)
  waiting for transfers between devices  26.7 us (28%)
  between operations  14.3 us (15%)
  local copies, waits for them, and re-layouts  9.1 us (10%)
  matrix products  7.05 us (7%)
  starting transfers between devices  4.51 us (5%)
  other arithmetic  1.9 us (2%)
    all_gather x1, waiting for transfers between devices, per_device(): wide = lax.all_gather(ancestor, 'col', axis=0)  13.5 us
    all_gather x1, blocking collectives, per_device(): columns = lax.all_gather(columns, 'row', axis=1, tiled=True)  11.5 us
    all_gather x1, waiting for transfers between devices, per_device(): pieces = lax.all_gather(mine, 'col', axis=0)  11.1 us
    all_to_all x1, blocking collectives, per_device(): lax.all_to_all(jnp.concatenate([product, tail], axis=1), 'col', 0, 0)  10.2 us
    all_gather x1, blocking collectives, per_device(): scaled = lax.all_gather(scaled, 'row', axis=1, tiled=True)  10 us
    dot_general x2, matrix products, per_device(): jnp.einsum('cij,cjk->ik', wide[:, s], spread.reshape(cols, chunk, part),...  4.84 us
    ppermute x3, starting transfers between devices, per_device(): lax.ppermute(local, 'row', [(r, (r + shift) % rows) for r in range(rows)])  4.43 us
    unnamed x7, local copies, waits for them, and re-layouts  3.15 us
  transfers between devices with their start and end apart: 5, of which 3 were waited for; matrix products, arithmetic and copies ran while one was open for 11% of the time, Pallas kernels for 0%

profile of v2, /device:TPU:0, one launch (start us, length us, event | category | flops | bytes accessed | tf_op | source)
XLA Modules:
  0.0 95.3 jit_solution(2005877197929893396)
XLA Ops:
  7.2 0.0 all-gather.5.cloned.1.call-start
  7.2 1.0 %copy-done = f32[2,128,512]{2,1,0:T(8,128)S(1)} copy-done((f32[2,128,512]{2,1,0:T(8,128)S(1)}, f32[2,128,512]{2,1,0:T(8,128)}, u32[]{:S(2)}) %copy-start) | copy-done | bytes 524312
  8.2 0.7 constant_dynamic-slice_fusion
  8.9 0.0 all-gather.5.cloned.1.call-update
  8.9 0.0 all-gather.7.cloned.1.call-start
  8.9 0.7 all-gather.7.cloned.1.call-update
  9.7 1.0 %constant_dynamic-slice_fusion.1 = f32[2,128,64]{2,1,0:T(8,128)S(1)} fusion(f32[2,128,512]{2,1,0:T(8,128)} %param.8, s32[]{:T(128)S(6)} %select_n.29), kind=kLoop, calls=%fused_computation.33 | loop fusion | bytes 131076 | tf_op jit(solution)/shard_map/dynamic_slice | solution.py:24
  10.7 0.1 copy.66
  10.8 0.8 copy.45
  11.5 0.6 sort.17
  12.2 11.5 %all_gather.18 = f32[2,512,64]{1,2,0:T(8,128)S(1)} all-gather(f32[2,128,64]{1,2,0:T(8,128)S(1)} %copy.66), channel_id=1, replica_groups=mesh['row'=4,'col'=8] {'row'}, dimensions={1}, use_global_device_ids=true | all-gather | bytes 327680 | tf_op jit(solution)/shard_map/all_gather | solution.py:25
  23.6 0.2 slice_reduce_fusion.1
  23.9 0.1 fusion.5
  24.0 11.1 %all-gather.5.cloned.1.call-done = f32[16,32,512]{2,1,0:T(8,128)} async-done(((f32[2,32,512]{2,1,0:T(8,128)}), f32[16,32,512]{2,1,0:T(8,128)}) %all-gather.5.cloned.1.call-update) | async-done | bytes 1048592 | tf_op jit(solution)/shard_map/all_gather | solution.py:22
  35.1 2.2 %convolution_bitcast_fusion = f32[8,32,2,64]{3,1,0,2:T(8,128)S(1)} fusion(f32[8,2,32,512]{3,2,1,0:T(8,128)} %bitcast.58, f32[2,512,64]{1,2,0:T(8,128)S(1)} %all_gather.18), kind=kOutput, calls=%fused_computation.2 | convolution fusion | flops 201326592 | bytes 1441792 | tf_op jit(solution)/shard_map/csqw,swk->cqsk/dot_general | solution.py:27
  37.3 0.2 copy.48
  37.5 0.2 reshape.32
  37.7 10.0 %all_gather.21 = f32[8,128,128]{2,1,0:T(8,128)S(1)} all-gather(f32[8,32,128]{2,1,0:T(8,128)S(1)} %reshape.32), channel_id=1, replica_groups=mesh['row'=4,'col'=8] {'row'}, dimensions={1}, use_global_device_ids=true | all-gather | bytes 655360 | tf_op jit(solution)/shard_map/all_gather | solution.py:29
  47.7 0.6 reshape.66
  48.3 0.8 fusion.8
  49.1 0.3 copy.67
  49.5 0.6 gather_fusion
  50.0 0.1 broadcast_select_fusion.1
  50.1 0.2 copy.51
  50.3 0.1 reshape_reshape.6
  50.4 0.1 fusion.9
  50.5 0.3 copy.69
  50.9 0.6 gather_fusion.1
  51.4 0.1 broadcast_select_fusion
  51.5 0.2 copy.55
  51.7 0.1 reshape_reshape.7
  51.8 0.1 fusion.10
  51.9 13.5 %all-gather.7.cloned.1.call-done = f32[16,256,128]{2,1,0:T(8,128)} async-done(((f32[2,256,128]{2,1,0:T(8,128)}), f32[16,256,128]{2,1,0:T(8,128)}) %all-gather.7.cloned.1.call-update) | async-done | bytes 2097168 | tf_op jit(solution)/shard_map/all_gather | solution.py:23
  65.4 2.4 %multiply_reduce_fusion.1 = (f32[64]{0:T(128)S(1)}, f32[256,64]{0,1:T(8,128)S(1)}) fusion(f32[1024,64]{0,1:T(8,128)S(1)} %bitcast.60, s32[]{:T(128)S(6)} %select_n.31, f32[8,2,256,128]{3,2,1,0:T(8,128)} %bitcast.55, f32[8,128,64]{1,0,2:T(8,128)S(1)} %reshape_reshape.6), kind=kOutput, calls=%fused_computation.21 | convolution fusion | flops 201359296 | bytes 1442052 | tf_op jit(solution)/shard_map/cij,cjk->ik/dot_general | solution.py:35
  67.8 2.4 %multiply_reduce_fusion = (f32[64]{0:T(128)S(1)}, f32[256,64]{0,1:T(8,128)S(1)}) fusion(f32[1024,64]{0,1:T(8,128)S(1)} %bitcast.61, s32[]{:T(128)S(6)} %select_n.31, f32[8,2,256,128]{3,2,1,0:T(8,128)} %bitcast.56, f32[8,128,64]{1,0,2:T(8,128)S(1)} %reshape_reshape.7), kind=kOutput, calls=%fused_computation.20 | convolution fusion | flops 201359296 | bytes 1442052 | tf_op jit(solution)/shard_map/cij,cjk->ik/dot_general | solution.py:35
  70.3 0.1 copy.58
  70.4 0.1 pad_maximum_fusion.2
  70.5 10.2 %all_to_all.5 = f32[8,40,128]{2,1,0:T(8,128)S(1)} all-to-all(f32[8,40,128]{2,1,0:T(8,128)S(1)} %pad_maximum_fusion), channel_id=1, replica_groups=mesh['row'=4,'col'=8] {'col'}, dimensions={0} | all-to-all | bytes 327680 | tf_op jit(solution)/shard_map/all_to_all | solution.py:45
  80.7 0.2 reshape.37
  81.0 0.1 copy.61
  81.1 0.2 reshape.38
  81.3 1.5 %collective-permute-start = (f32[2,512]{1,0:T(2,128)S(1)}, f32[2,512]{1,0:T(2,128)S(1)}, u32[]{:S(2)}, u32[]{:S(2)}) collective-permute-start(f32[2,512]{1,0:T(2,128)S(1)} %slice_bitcast_fusion.4), channel_id=1, source_target_pairs={{0,8},{8,16},{16,24},{24,0},{1,9},{9,17},{17,25},{25,1},{2,10},{10... | collective-permute-start | bytes 12296 | tf_op jit(solution)/shard_map/ppermute | solution.py:51
  82.8 1.5 %collective-permute-start.1 = (f32[2,512]{1,0:T(2,128)S(1)}, f32[2,512]{1,0:T(2,128)S(1)}, u32[]{:S(2)}, u32[]{:S(2)}) collective-permute-start(f32[2,512]{1,0:T(2,128)S(1)} %slice_bitcast_fusion.4), channel_id=1, source_target_pairs={{0,16},{8,24},{16,0},{24,8},{1,17},{9,25},{17,1},{25,9},{2,18},{10... | collective-permute-start | bytes 12296 | tf_op jit(solution)/shard_map/ppermute | solution.py:51
  84.2 1.5 %collective-permute-start.2 = (f32[2,512]{1,0:T(2,128)S(1)}, f32[2,512]{1,0:T(2,128)S(1)}, u32[]{:S(2)}, u32[]{:S(2)}) collective-permute-start(f32[2,512]{1,0:T(2,128)S(1)} %slice_bitcast_fusion.4), channel_id=1, source_target_pairs={{0,24},{8,0},{16,8},{24,16},{1,25},{9,1},{17,9},{25,17},{2,26},{10... | collective-permute-start | bytes 12296 | tf_op jit(solution)/shard_map/ppermute | solution.py:51
  85.7 0.1 slice_negate_fusion
  85.7 0.7 copy.62
  86.4 1.4 %collective-permute-done.2 = f32[2,512]{1,0:T(2,128)S(1)} collective-permute-done((f32[2,512]{1,0:T(2,128)S(1)}, f32[2,512]{1,0:T(2,128)S(1)}, u32[]{:S(2)}, u32[]{:S(2)}) %collective-permute-start.2) | collective-permute-done | bytes 4128 | tf_op jit(solution)/shard_map/ppermute | solution.py:51
  87.8 0.6 add_add_fusion
  (16 shorter events, 0.1 us)
Async XLA Ops:
  7.2 1.0 %copy-start = (f32[2,128,512]{2,1,0:T(8,128)S(1)}, f32[2,128,512]{2,1,0:T(8,128)}, u32[]{:S(2)}) copy-start(f32[2,128,512]{2,1,0:T(8,128)} %param.7) | copy-start | bytes 1572868
  7.2 27.9 %all-gather.5.cloned.1.call-start = ((), (), s32[]{:S(2)}) async-start(), calls=%async_computation.1 | async-start | bytes 1179648 | tf_op jit(solution)/shard_map/all_gather | solution.py:22
  8.9 56.5 %all-gather.7.cloned.1.call-start = ((), (), s32[]{:S(2)}) async-start(), calls=%async_computation.2 | async-start | bytes 2359296 | tf_op jit(solution)/shard_map/all_gather | solution.py:23
  81.3 5.2 %collective-permute-start = (f32[2,512]{1,0:T(2,128)S(1)}, f32[2,512]{1,0:T(2,128)S(1)}, u32[]{:S(2)}, u32[]{:S(2)}) collective-permute-start(f32[2,512]{1,0:T(2,128)S(1)} %slice_bitcast_fusion.4), channel_id=1, source_target_pairs={{0,8},{8,16},{16,24},{24,0},{1,9},{9,17},{17,25},{25,1},{2,10},{10... | collective-permute-start | bytes 12296 | tf_op jit(solution)/shard_map/ppermute | solution.py:51
  82.8 3.7 %collective-permute-start.1 = (f32[2,512]{1,0:T(2,128)S(1)}, f32[2,512]{1,0:T(2,128)S(1)}, u32[]{:S(2)}, u32[]{:S(2)}) collective-permute-start(f32[2,512]{1,0:T(2,128)S(1)} %slice_bitcast_fusion.4), channel_id=1, source_target_pairs={{0,16},{8,24},{16,0},{24,8},{1,17},{9,25},{17,1},{25,9},{2,18},{10... | collective-permute-start | bytes 12296 | tf_op jit(solution)/shard_map/ppermute | solution.py:51
  84.2 3.6 %collective-permute-start.2 = (f32[2,512]{1,0:T(2,128)S(1)}, f32[2,512]{1,0:T(2,128)S(1)}, u32[]{:S(2)}, u32[]{:S(2)}) collective-permute-start(f32[2,512]{1,0:T(2,128)S(1)} %slice_bitcast_fusion.4), channel_id=1, source_target_pairs={{0,24},{8,0},{16,8},{24,16},{1,25},{9,1},{17,9},{25,17},{2,26},{10... | collective-permute-start | bytes 12296 | tf_op jit(solution)/shard_map/ppermute | solution.py:51
Sparse Core Ops, SparseCore 0:
  10.2 24.8 all-gather.4
  36.7 28.7 all-gather.6

commit v3 on v1

v3 whole, which is shorter than its diff:
```python
import jax
import jax.numpy as jnp
from jax import lax
from jax.sharding import Mesh, PartitionSpec as P

B = 256


def solution(mesh):
    rows, cols = mesh.shape["row"], mesh.shape["col"]
    cores, deep = 2, cols // 2
    fine = Mesh(mesh.devices.reshape(rows, deep, cores), ("row", "z", "core"))
    highest = lax.Precision.HIGHEST

    def shifted(array, axis, size, shift):
        return lax.ppermute(array, axis, [(i, (i + shift) % size) for i in range(size)])

    def per_device(ancestor, panel, factor_inv, pattern):
        row = lax.axis_index("row")
        z = lax.axis_index("z")
        core = lax.axis_index("core")
        groups, chunk, width = panel.shape
        depth = factor_inv.shape[1]
        part = width // deep
        quarter = B // rows
        out_rows = ancestor.shape[1] // cols

        def of(array, s):
            return lax.dynamic_index_in_dim(array, s, 0, keepdims=False)

        def both(mine, other, axis):
            first = jnp.where(core == 0, mine, other)
            second = jnp.where(core == 0, other, mine)
            return jnp.concatenate([first, second], axis=axis)

        panel = lax.dynamic_slice_in_dim(panel, row * depth, depth, axis=2)
        panel_other = shifted(of(panel, 1 - core), "core", cores, 1)
        ancestor_other = shifted(of(ancestor, 1 - core), "core", cores, 1)
        wide = both(of(ancestor, core), ancestor_other, 1)
        wide = lax.all_gather(wide, "z", axis=0)
        tile = both(of(panel, core), panel_other, 0)
        factor = of(factor_inv, core)

        partial = jnp.dot(tile, factor, precision=highest)

        def rows_of(r):
            return lax.dynamic_slice_in_dim(partial, r * quarter, quarter, axis=0)

        scaled = rows_of(row)
        for shift in range(1, rows):
            scaled = scaled + shifted(rows_of((row + shift) % rows), "row", rows, shift)

        def columns_of(array, c):
            return lax.dynamic_slice_in_dim(array, c * part, part, axis=1)

        slots = [columns_of(scaled, z)]
        for shift in range(1, deep):
            slots.append(shifted(columns_of(scaled, (z + shift) % deep), "z", deep, shift))
        slots = lax.all_gather(jnp.stack(slots), "row", axis=1)

        place = of(pattern, core)
        stored = jnp.arange(deep, dtype=jnp.int32)
        stored = jnp.sum(jnp.where(place[:, None] == stored[None, :], stored[:, None], 0), axis=0)
        spread = jnp.take(slots, (z - stored) % deep, axis=0, mode="clip")
        spread = spread.reshape(deep, B, part)
        product = jnp.einsum("tij,tjk->ik", wide, spread, precision=highest)

        own = lax.dynamic_slice_in_dim(
            spread.reshape(deep * B, part), row * product.shape[0], product.shape[0], axis=0
        )
        term = jnp.sum(own * product, axis=0) + jnp.sum(columns_of(factor, z) ** 2, axis=0)

        tail = jnp.broadcast_to(term, (cols, 8, part))
        sent = jnp.concatenate([product.reshape(cols, out_rows, part), tail], axis=1)
        moved = lax.all_to_all(sent, ("z", "core"), 0, 0)
        moved = moved.reshape(deep, groups, out_rows + 8, part)
        moved = moved.transpose(1, 2, 0, 3).reshape(groups, out_rows + 8, width)
        local = moved[:, out_rows]
        total = local
        for shift in range(1, rows):
            total = total + shifted(local, "row", rows, shift)
        return -moved[:, :out_rows], total

    col = ("z", "core")
    in_specs = (P(None, "row", col), P(None, col, None), P(None, "row", None), P())
    out_specs = (P(None, ("row", "z", "core"), None), P())
    return jax.shard_map(
        per_device, mesh=fine, in_specs=in_specs, out_specs=out_specs, check_vma=False
    )
```

time: 154 us -> 72.2 us (0.47)
  waiting for transfers between devices: 79.4 us -> 12.9 us
  blocking collectives: 47 us -> 21.5 us
  starting transfers between devices: 0.92 us -> 14.2 us
  matrix products: 4.41 us -> 2.81 us
    reduce_scatter x2 -> x0, waiting for transfers between devices: 58.9 us -> none  [the longest x1 31.2 us: per_device(): product = lax.psum_scatter(partial, 'col', scatter_dimension=1, tiled=True)]
    psum x1 -> x0, blocking collectives: 36.9 us -> none  [per_device(): diagonal_inv = lax.psum(terms, ('row', 'col'))]
    all_gather x1, waiting for transfers between devices: 20.4 us -> 0.57 us  [per_device(): wide = lax.all_gather(wide, 'z', axis=0)]
    ppermute x1 -> x11, starting transfers between devices: 0.8 us -> 14.2 us  [shifted(): lax.ppermute(array, axis, [(i, (i + shift) % size) for i in range(size)])]
    ppermute x1 -> x11, waiting for transfers between devices: 0.01 us -> 12.3 us  [shifted(): lax.ppermute(array, axis, [(i, (i + shift) % size) for i in range(size)])]
    all_to_all x0 -> x1, blocking collectives: none -> 11.2 us  [per_device(): moved = lax.all_to_all(sent, ('z', 'core'), 0, 0)]
    squeeze x0 -> x3, local copies, waits for them, and re-layouts: none -> 1.96 us  [the longest x2 1.96 us: of(): return lax.dynamic_index_in_dim(array, s, 0, keepdims=False)]
    dot_general x2, matrix products: 4.41 us -> 2.81 us  [the longest x1 2.23 us: per_device(): product = jnp.einsum('tij,tjk->ik', wide, spread, precision=highest)]
  transfers between devices with their start and end apart: 4 -> 12, of which waited for: 3 -> 10; matrix products, arithmetic and copies ran while one was open for 1% -> 7% of each run, Pallas kernels for 0% -> 0%
where the time goes in v3:
time: 72.2 us; the launch traced here: 71.9 us
  blocking collectives  21.5 us (30%)
  between operations  14.3 us (20%)
  starting transfers between devices  14.2 us (20%)
  waiting for transfers between devices  12.9 us (18%)
  local copies, waits for them, and re-layouts  3.52 us (5%)
  matrix products  2.81 us (4%)
  other arithmetic  2.68 us (4%)
    ppermute x11, starting transfers between devices, shifted(): lax.ppermute(array, axis, [(i, (i + shift) % size) for i in range(size)])  14.2 us
    ppermute x11, waiting for transfers between devices, shifted(): lax.ppermute(array, axis, [(i, (i + shift) % size) for i in range(size)])  12.3 us
    all_to_all x1, blocking collectives, per_device(): moved = lax.all_to_all(sent, ('z', 'core'), 0, 0)  11.2 us
    all_gather x1, blocking collectives, per_device(): slots = lax.all_gather(jnp.stack(slots), 'row', axis=1)  10.3 us
    dot_general x1, matrix products, per_device(): product = jnp.einsum('tij,tjk->ik', wide, spread, precision=highest)  2.23 us
    squeeze x2, local copies, waits for them, and re-layouts, of(): return lax.dynamic_index_in_dim(array, s, 0, keepdims=False)  1.96 us
  transfers between devices with their start and end apart: 12, of which 10 were waited for; matrix products, arithmetic and copies ran while one was open for 7% of the time, Pallas kernels for 0%

profile of v3, /device:TPU:0, one launch (start us, length us, event | category | flops | bytes accessed | tf_op | source)
XLA Modules:
  0.0 71.9 jit_solution(15947391315652522643)
XLA Ops:
  7.2 0.0 copy-start
  7.2 0.0 all-gather.4.cloned.1.call-start
  7.2 0.0 copy-start.1
  7.2 1.0 %dynamic-slice_bitcast_fusion = f32[256,128]{1,0:T(8,128)S(1)} fusion(f32[2,256,128]{2,1,0:T(8,128)} %param.4, s32[]{:T(128)S(6)} %select_n.123), kind=kLoop, calls=%fused_computation.17 | loop fusion | bytes 262148 | tf_op jit(solution)/shard_map/jit(dynamic_index_in_dim)/squeeze | solution.py:29
  8.2 0.5 collective-permute-start
  8.7 1.0 %dynamic-slice_bitcast_fusion.1 = f32[128,128]{1,0:T(8,128)S(1)} fusion(f32[2,128,512]{2,1,0:T(8,128)} %param.5, s32[]{:T(128)S(6)} %select_n.130, s32[]{:T(128)S(6)} %select_n.129), kind=kLoop, calls=%fused_computation.21 | loop fusion | bytes 131080 | tf_op jit(solution)/shard_map/jit(dynamic_index_in_dim)/squeeze | solution.py:29
  9.7 0.1 collective-permute-start.1
  9.9 0.0 collective-permute-done
  9.9 0.0 copy-done.1
  9.9 0.0 copy-start.2
  10.0 0.7 %pad_maximum_fusion = f32[256,256]{1,0:T(8,128)} fusion(f32[256,128]{1,0:T(8,128)S(1)} %get-tuple-element.12, f32[256,128]{1,0:T(8,128)S(1)} %get-tuple-element.11), kind=kLoop, calls=%fused_computation.1 | loop fusion | flops 65536 | bytes 524288 | tf_op jit(solution)/shard_map/concatenate | solution.py:34
  10.7 0.0 all-gather.4.cloned.1.call-update
  10.7 0.0 copy-done
  10.7 0.1 select_reduce_fusion
  10.8 0.2 collective-permute-done.1
  11.0 1.0 %bitcast_select_fusion.3 = (f32[128,128]{1,0:T(8,128)S(1)}, f32[128,128]{1,0:T(8,128)S(1)}) fusion(f32[128,128]{1,0:T(8,128)S(1)} %collective-permute-done.1, f32[2,128,512]{2,1,0:T(8,128)} %param.5, s32[]{:T(128)S(6)} %select_n.127, s32[]{:T(128)S(6)} %select_n.129, pred[]{:T(512)S(6)} %eq.30), kind=kLoop, calls=%fused_computation.19 | loop fusion | flops 32768 | bytes 262153 | tf_op jit(solution)/shard_map/jit(_where)/select_n | solution.py:32
  12.0 0.0 copy-done.2
  12.0 0.6 fusion
  12.7 2.7 %collective-permute-start.2 = (f32[64,512]{1,0:T(8,128)S(1)}, f32[64,512]{1,0:T(8,128)S(1)}, u32[]{:S(2)}, u32[]{:S(2)}) collective-permute-start(f32[64,512]{1,0:T(8,128)S(1)} %get-tuple-element.8), channel_id=1, source_target_pairs={{0,8},{8,16},{16,24},{24,0},{1,9},{9,17},{17,25},{25,1},{2,10},{10... | collective-permute-start | bytes 393224 | tf_op jit(solution)/shard_map/ppermute | solution.py:16
  15.4 1.4 %collective-permute-start.3 = (f32[64,512]{1,0:T(8,128)S(1)}, f32[64,512]{1,0:T(8,128)S(1)}, u32[]{:S(2)}, u32[]{:S(2)}) collective-permute-start(f32[64,512]{1,0:T(8,128)S(1)} %get-tuple-element.10), channel_id=1, source_target_pairs={{0,16},{8,24},{16,0},{24,8},{1,17},{9,25},{17,1},{25,9},{2,18},{10... | collective-permute-start | bytes 393224 | tf_op jit(solution)/shard_map/ppermute | solution.py:16
  16.8 1.6 %collective-permute-start.4 = (f32[64,512]{1,0:T(8,128)S(1)}, f32[64,512]{1,0:T(8,128)S(1)}, u32[]{:S(2)}, u32[]{:S(2)}) collective-permute-start(f32[64,512]{1,0:T(8,128)S(1)} %get-tuple-element.9), channel_id=1, source_target_pairs={{0,24},{8,0},{16,8},{24,16},{1,25},{9,1},{17,9},{25,17},{2,26},{10... | collective-permute-start | bytes 393224 | tf_op jit(solution)/shard_map/ppermute | solution.py:16
  18.4 2.2 %collective-permute-done.2 = f32[64,512]{1,0:T(8,128)S(1)} collective-permute-done((f32[64,512]{1,0:T(8,128)S(1)}, f32[64,512]{1,0:T(8,128)S(1)}, u32[]{:S(2)}, u32[]{:S(2)}) %collective-permute-start.2) | collective-permute-done | bytes 131104 | tf_op jit(solution)/shard_map/ppermute | solution.py:16
  20.5 2.5 %collective-permute-done.3 = f32[64,512]{1,0:T(8,128)S(1)} collective-permute-done((f32[64,512]{1,0:T(8,128)S(1)}, f32[64,512]{1,0:T(8,128)S(1)}, u32[]{:S(2)}, u32[]{:S(2)}) %collective-permute-start.3) | collective-permute-done | bytes 131104 | tf_op jit(solution)/shard_map/ppermute | solution.py:16
  23.0 0.4 collective-permute-done.4
  23.5 1.6 %collective-permute-start.5 = (f32[64,128]{1,0:T(8,128)S(1)}, f32[64,128]{1,0:T(8,128)S(1)}, u32[]{:S(2)}, u32[]{:S(2)}) collective-permute-start(f32[64,128]{1,0:T(8,128)S(1)} %get-tuple-element.16), channel_id=1, source_target_pairs={{0,2},{2,4},{4,6},{6,0},{1,3},{3,5},{5,7},{7,1},{8,10},{10,12},{12... | collective-permute-start | bytes 98312 | tf_op jit(solution)/shard_map/ppermute | solution.py:16
  25.1 2.6 %collective-permute-start.6 = (f32[64,128]{1,0:T(8,128)S(1)}, f32[64,128]{1,0:T(8,128)S(1)}, u32[]{:S(2)}, u32[]{:S(2)}) collective-permute-start(f32[64,128]{1,0:T(8,128)S(1)} %get-tuple-element.15), channel_id=1, source_target_pairs={{0,4},{2,6},{4,0},{6,2},{1,5},{3,7},{5,1},{7,3},{8,12},{10,14},{12... | collective-permute-start | bytes 98312 | tf_op jit(solution)/shard_map/ppermute | solution.py:16
  27.7 1.3 %collective-permute-start.7 = (f32[64,128]{1,0:T(8,128)S(1)}, f32[64,128]{1,0:T(8,128)S(1)}, u32[]{:S(2)}, u32[]{:S(2)}) collective-permute-start(f32[64,128]{1,0:T(8,128)S(1)} %get-tuple-element.14), channel_id=1, source_target_pairs={{0,6},{2,0},{4,2},{6,4},{1,7},{3,1},{5,3},{7,5},{8,14},{10,8},{12,... | collective-permute-start | bytes 98312 | tf_op jit(solution)/shard_map/ppermute | solution.py:16
  29.1 0.1 multiply_reduce_fusion
  29.2 1.1 %collective-permute-done.5 = f32[64,128]{1,0:T(8,128)S(1)} collective-permute-done((f32[64,128]{1,0:T(8,128)S(1)}, f32[64,128]{1,0:T(8,128)S(1)}, u32[]{:S(2)}, u32[]{:S(2)}) %collective-permute-start.5) | collective-permute-done | bytes 32800 | tf_op jit(solution)/shard_map/ppermute | solution.py:16
  30.3 2.3 %collective-permute-done.6 = f32[64,128]{1,0:T(8,128)S(1)} collective-permute-done((f32[64,128]{1,0:T(8,128)S(1)}, f32[64,128]{1,0:T(8,128)S(1)}, u32[]{:S(2)}, u32[]{:S(2)}) %collective-permute-start.6) | collective-permute-done | bytes 32800 | tf_op jit(solution)/shard_map/ppermute | solution.py:16
  32.6 0.7 collective-permute-done.7
  33.3 10.3 %all-gather.1 = f32[4,256,128]{2,1,0:T(8,128)S(1)} all-gather(f32[4,64,128]{2,1,0:T(8,128)S(1)} %pad_maximum_fusion.2), channel_id=3, replica_groups=mesh['row'=4,'z'=4,'core'=2] {'row'}, dimensions={1}, use_global_device_ids=true | all-gather | bytes 655360 | tf_op jit(solution)/shard_map/all_gather | solution.py:59
  43.6 0.6 gather_fusion
  44.2 0.6 all-gather.4.cloned.1.call-done
  44.7 2.2 %fusion.6 = (f32[128]{0:T(128)S(1)}, f32[256,128,1]{1,0,2:T(8,128)S(1)}) fusion(f32[1024,128]{1,0:T(8,128)S(1)} %bitcast.46, s32[]{:T(128)S(6)} %select_n.149, f32[4,256,256]{2,1,0:T(8,128)} %bitcast.49, f32[4,256,128]{2,1,0:T(8,128)S(1)} %bitcast.47), kind=kOutput, calls=%fused_computation.13 | convolution fusion | flops 402718592 | bytes 1835524 | tf_op jit(solution)/shard_map/tij,tjk->ik/dot_general | solution.py:66
  47.0 11.2 %all_to_all.5 = f32[8,40,128]{2,1,0:T(8,128)S(1)} all-to-all(f32[8,40,128]{2,1,0:T(8,128)S(1)} %pad_maximum_fusion.1), channel_id=1, replica_groups=mesh['row'=4,'z'=4,'core'=2] {'z','core'}, dimensions={0} | all-to-all | bytes 327680 | tf_op jit(solution)/shard_map/all_to_all | solution.py:75
  58.2 0.1 copy.11
  58.3 0.1 reshape.65
  58.4 1.5 %collective-permute-start.10 = (f32[2,512]{1,0:T(2,128)S(1)}, f32[2,512]{1,0:T(2,128)S(1)}, u32[]{:S(2)}, u32[]{:S(2)}) collective-permute-start(f32[2,512]{1,0:T(2,128)S(1)} %slice_bitcast_fusion), channel_id=1, source_target_pairs={{0,24},{8,0},{16,8},{24,16},{1,25},{9,1},{17,9},{25,17},{2,26},{10... | collective-permute-start | bytes 12296 | tf_op jit(solution)/shard_map/ppermute | solution.py:16
  60.0 0.6 collective-permute-start.8
  60.5 0.2 collective-permute-start.9
  60.7 0.1 slice_negate_fusion
  60.8 0.7 copy.9
  61.5 0.6 collective-permute-done.10
  62.1 2.4 %collective-permute-done.8 = f32[2,512]{1,0:T(2,128)S(1)} collective-permute-done((f32[2,512]{1,0:T(2,128)S(1)}, f32[2,512]{1,0:T(2,128)S(1)}, u32[]{:S(2)}, u32[]{:S(2)}) %collective-permute-start.8) | collective-permute-done | bytes 4128 | tf_op jit(solution)/shard_map/ppermute | solution.py:16
  64.5 0.0 collective-permute-done.9
  64.5 0.6 add_add_fusion.1
  (12 shorter events, 0.2 us)
Async XLA Ops:
  7.2 3.6 %copy-start = (s32[2,4]{1,0:T(2,128)S(1)}, s32[2,4]{1,0:T(2,128)}, u32[]{:S(2)}) copy-start(s32[2,4]{1,0:T(2,128)} %param.7) | copy-start | bytes 100
  7.2 37.5 %all-gather.4.cloned.1.call-start = ((), (), s32[]{:S(2)}) async-start(), calls=%async_computation.1 | async-start | bytes 1310720 | tf_op jit(solution)/shard_map/all_gather | solution.py:40
  7.2 2.7 %copy-start.1 = (f32[2,256,128]{2,1,0:T(8,128)S(1)}, f32[2,256,128]{2,1,0:T(8,128)}, u32[]{:S(2)}) copy-start(f32[2,256,128]{2,1,0:T(8,128)} %param.4) | copy-start | bytes 786436
  8.2 1.7 %collective-permute-start = (f32[256,128]{1,0:T(8,128)S(1)}, f32[256,128]{1,0:T(8,128)S(1)}, u32[]{:S(2)}, u32[]{:S(2)}) collective-permute-start(f32[256,128]{1,0:T(8,128)S(1)} %dynamic-slice_bitcast_fusion), channel_id=1, source_target_pairs={{0,1},{1,0},{2,3},{3,2},{4,5},{5,4},{6,7},{7,6},{8,9},{9,8},{10,11... | collective-permute-start | bytes 393224 | tf_op jit(solution)/shard_map/ppermute | solution.py:16
  9.7 1.3 %collective-permute-start.1 = (f32[128,128]{1,0:T(8,128)S(1)}, f32[128,128]{1,0:T(8,128)S(1)}, u32[]{:S(2)}, u32[]{:S(2)}) collective-permute-start(f32[128,128]{1,0:T(8,128)S(1)} %dynamic-slice_bitcast_fusion.1), channel_id=1, source_target_pairs={{0,1},{1,0},{2,3},{3,2},{4,5},{5,4},{6,7},{7,6},{8,9},{9,8},{10,11... | collective-permute-start | bytes 196616 | tf_op jit(solution)/shard_map/ppermute | solution.py:16
  9.9 2.1 %copy-start.2 = (f32[2,128,512]{2,1,0:T(8,128)S(1)}, f32[2,128,512]{2,1,0:T(8,128)}, u32[]{:S(2)}) copy-start(f32[2,128,512]{2,1,0:T(8,128)} %param.6) | copy-start | bytes 1572868
  12.7 7.8 %collective-permute-start.2 = (f32[64,512]{1,0:T(8,128)S(1)}, f32[64,512]{1,0:T(8,128)S(1)}, u32[]{:S(2)}, u32[]{:S(2)}) collective-permute-start(f32[64,512]{1,0:T(8,128)S(1)} %get-tuple-element.8), channel_id=1, source_target_pairs={{0,8},{8,16},{16,24},{24,0},{1,9},{9,17},{17,25},{25,1},{2,10},{10... | collective-permute-start | bytes 393224 | tf_op jit(solution)/shard_map/ppermute | solution.py:16
  15.4 7.6 %collective-permute-start.3 = (f32[64,512]{1,0:T(8,128)S(1)}, f32[64,512]{1,0:T(8,128)S(1)}, u32[]{:S(2)}, u32[]{:S(2)}) collective-permute-start(f32[64,512]{1,0:T(8,128)S(1)} %get-tuple-element.10), channel_id=1, source_target_pairs={{0,16},{8,24},{16,0},{24,8},{1,17},{9,25},{17,1},{25,9},{2,18},{10... | collective-permute-start | bytes 393224 | tf_op jit(solution)/shard_map/ppermute | solution.py:16
  16.8 6.7 %collective-permute-start.4 = (f32[64,512]{1,0:T(8,128)S(1)}, f32[64,512]{1,0:T(8,128)S(1)}, u32[]{:S(2)}, u32[]{:S(2)}) collective-permute-start(f32[64,512]{1,0:T(8,128)S(1)} %get-tuple-element.9), channel_id=1, source_target_pairs={{0,24},{8,0},{16,8},{24,16},{1,25},{9,1},{17,9},{25,17},{2,26},{10... | collective-permute-start | bytes 393224 | tf_op jit(solution)/shard_map/ppermute | solution.py:16
  23.5 6.7 %collective-permute-start.5 = (f32[64,128]{1,0:T(8,128)S(1)}, f32[64,128]{1,0:T(8,128)S(1)}, u32[]{:S(2)}, u32[]{:S(2)}) collective-permute-start(f32[64,128]{1,0:T(8,128)S(1)} %get-tuple-element.16), channel_id=1, source_target_pairs={{0,2},{2,4},{4,6},{6,0},{1,3},{3,5},{5,7},{7,1},{8,10},{10,12},{12... | collective-permute-start | bytes 98312 | tf_op jit(solution)/shard_map/ppermute | solution.py:16
  25.1 7.4 %collective-permute-start.6 = (f32[64,128]{1,0:T(8,128)S(1)}, f32[64,128]{1,0:T(8,128)S(1)}, u32[]{:S(2)}, u32[]{:S(2)}) collective-permute-start(f32[64,128]{1,0:T(8,128)S(1)} %get-tuple-element.15), channel_id=1, source_target_pairs={{0,4},{2,6},{4,0},{6,2},{1,5},{3,7},{5,1},{7,3},{8,12},{10,14},{12... | collective-permute-start | bytes 98312 | tf_op jit(solution)/shard_map/ppermute | solution.py:16
  27.7 5.5 %collective-permute-start.7 = (f32[64,128]{1,0:T(8,128)S(1)}, f32[64,128]{1,0:T(8,128)S(1)}, u32[]{:S(2)}, u32[]{:S(2)}) collective-permute-start(f32[64,128]{1,0:T(8,128)S(1)} %get-tuple-element.14), channel_id=1, source_target_pairs={{0,6},{2,0},{4,2},{6,4},{1,7},{3,1},{5,3},{7,5},{8,14},{10,8},{12,... | collective-permute-start | bytes 98312 | tf_op jit(solution)/shard_map/ppermute | solution.py:16
  58.4 3.7 %collective-permute-start.10 = (f32[2,512]{1,0:T(2,128)S(1)}, f32[2,512]{1,0:T(2,128)S(1)}, u32[]{:S(2)}, u32[]{:S(2)}) collective-permute-start(f32[2,512]{1,0:T(2,128)S(1)} %slice_bitcast_fusion), channel_id=1, source_target_pairs={{0,24},{8,0},{16,8},{24,16},{1,25},{9,1},{17,9},{25,17},{2,26},{10... | collective-permute-start | bytes 12296 | tf_op jit(solution)/shard_map/ppermute | solution.py:16
  60.0 4.5 %collective-permute-start.8 = (f32[2,512]{1,0:T(2,128)S(1)}, f32[2,512]{1,0:T(2,128)S(1)}, u32[]{:S(2)}, u32[]{:S(2)}) collective-permute-start(f32[2,512]{1,0:T(2,128)S(1)} %slice_bitcast_fusion), channel_id=1, source_target_pairs={{0,8},{8,16},{16,24},{24,0},{1,9},{9,17},{17,25},{25,1},{2,10},{10... | collective-permute-start | bytes 12296 | tf_op jit(solution)/shard_map/ppermute | solution.py:16
  60.5 3.9 %collective-permute-start.9 = (f32[2,512]{1,0:T(2,128)S(1)}, f32[2,512]{1,0:T(2,128)S(1)}, u32[]{:S(2)}, u32[]{:S(2)}) collective-permute-start(f32[2,512]{1,0:T(2,128)S(1)} %slice_bitcast_fusion), channel_id=1, source_target_pairs={{0,16},{8,24},{16,0},{24,8},{1,17},{9,25},{17,1},{25,9},{2,18},{10... | collective-permute-start | bytes 12296 | tf_op jit(solution)/shard_map/ppermute | solution.py:16
Sparse Core Ops, SparseCore 0:
  10.8 33.8 all-gather.3

commit v4 on v3

--- a/solution.py
+++ b/solution.py
@@ -15,11 +15,14 @@
     def shifted(array, axis, size, shift):
         return lax.ppermute(array, axis, [(i, (i + shift) % size) for i in range(size)])
 
+    def gathered(array, axis, size):
+        return [array] + [shifted(array, axis, size, d) for d in range(1, size)]
+
     def per_device(ancestor, panel, factor_inv, pattern):
         row = lax.axis_index("row")
         z = lax.axis_index("z")
         core = lax.axis_index("core")
-        groups, chunk, width = panel.shape
+        _, chunk, width = panel.shape
         depth = factor_inv.shape[1]
         part = width // deep
         quarter = B // rows
@@ -37,7 +40,7 @@
         panel_other = shifted(of(panel, 1 - core), "core", cores, 1)
         ancestor_other = shifted(of(ancestor, 1 - core), "core", cores, 1)
         wide = both(of(ancestor, core), ancestor_other, 1)
-        wide = lax.all_gather(wide, "z", axis=0)
+        wide = jnp.stack(gathered(wide, "z", deep))
         tile = both(of(panel, core), panel_other, 0)
         factor = of(factor_inv, core)
 
@@ -56,25 +59,39 @@
         slots = [columns_of(scaled, z)]
         for shift in range(1, deep):
             slots.append(shifted(columns_of(scaled, (z + shift) % deep), "z", deep, shift))
-        slots = lax.all_gather(jnp.stack(slots), "row", axis=1)
+        slots = jnp.stack(gathered(jnp.stack(slots), "row", rows))
 
         place = of(pattern, core)
         stored = jnp.arange(deep, dtype=jnp.int32)
         stored = jnp.sum(jnp.where(place[:, None] == stored[None, :], stored[:, None], 0), axis=0)
-        spread = jnp.take(slots, (z - stored) % deep, axis=0, mode="clip")
-        spread = spread.reshape(deep, B, part)
+        tiles = (z - jnp.arange(deep, dtype=jnp.int32)) % deep
+        quarters = (row - jnp.arange(rows, dtype=jnp.int32)) % rows
+        from_z = (z - jnp.take(stored, tiles, mode="clip")) % deep
+        spread = slots[quarters[None, :], from_z[:, None]].reshape(deep, B, part)
         product = jnp.einsum("tij,tjk->ik", wide, spread, precision=highest)
 
-        own = lax.dynamic_slice_in_dim(
-            spread.reshape(deep * B, part), row * product.shape[0], product.shape[0], axis=0
-        )
+        held = product.shape[0] // B
+        own = jnp.concatenate([of(spread, (z - (row * held + t)) % deep) for t in range(held)])
         term = jnp.sum(own * product, axis=0) + jnp.sum(columns_of(factor, z) ** 2, axis=0)
 
-        tail = jnp.broadcast_to(term, (cols, 8, part))
-        sent = jnp.concatenate([product.reshape(cols, out_rows, part), tail], axis=1)
-        moved = lax.all_to_all(sent, ("z", "core"), 0, 0)
-        moved = moved.reshape(deep, groups, out_rows + 8, part)
-        moved = moved.transpose(1, 2, 0, 3).reshape(groups, out_rows + 8, width)
+        tail = jnp.broadcast_to(term, (cores, 8, part))
+
+        def rows_for(c):
+            block = lax.dynamic_slice_in_dim(product, c * cores * out_rows, cores * out_rows)
+            block = block.reshape(cores, out_rows, part)
+            return jnp.concatenate([block, tail], axis=1)
+
+        moved = [rows_for(z)]
+        for shift in range(1, deep):
+            moved.append(shifted(rows_for((z + shift) % deep), "z", deep, shift))
+        order = (z - jnp.arange(deep, dtype=jnp.int32)) % deep
+        moved = jnp.take(jnp.stack(moved), order, axis=0, mode="clip")
+        moved = moved.transpose(1, 2, 0, 3).reshape(cores, out_rows + 8, width)
+        other = shifted(of(moved, 1 - core), "core", cores, 1)
+        mine = of(moved, core)
+        first = jnp.where(core == 0, mine, other)
+        second = jnp.where(core == 0, other, mine)
+        moved = jnp.stack([first, second])
         local = moved[:, out_rows]
         total = local
         for shift in range(1, rows):

time: 72.2 us -> 66.1 us (0.916)
  blocking collectives: 21.5 us -> 0 us
  starting transfers between devices: 14.2 us -> 33.4 us
  between operations: 14.3 us -> 0.96 us
  waiting for transfers between devices: 12.9 us -> 22.9 us
  local copies, waits for them, and re-layouts: 3.52 us -> 4.81 us
  matrix products: 2.81 us -> 1.6 us
    ppermute x11 -> x21, starting transfers between devices: 14.2 us -> 33.4 us  [shifted(): lax.ppermute(array, axis, [(i, (i + shift) % size) for i in range(size)])]
    all_to_all x1 -> x0, blocking collectives: 11.2 us -> none  [per_device(): moved = lax.all_to_all(sent, ('z', 'core'), 0, 0)]
    ppermute x11 -> x21, waiting for transfers between devices: 12.3 us -> 22.9 us  [shifted(): lax.ppermute(array, axis, [(i, (i + shift) % size) for i in range(size)])]
    all_gather x1 -> x0, blocking collectives: 10.3 us -> none  [per_device(): slots = lax.all_gather(jnp.stack(slots), 'row', axis=1)]
    gather x1 -> x3, local copies, waits for them, and re-layouts: 0.58 us -> 1.8 us  [the longest x1 0.64 us: per_device(): from_z = (z - jnp.take(stored, tiles, mode='clip')) % deep]
    dot_general x1, matrix products: 2.23 us -> 1.01 us  [per_device(): product = jnp.einsum('tij,tjk->ik', wide, spread, precision=highest)]
    squeeze x2 -> x3, local copies, waits for them, and re-layouts: 1.96 us -> 1.97 us  [of(): return lax.dynamic_index_in_dim(array, s, 0, keepdims=False)]
  transfers between devices with their start and end apart: 12 -> 21, of which waited for: 10 -> 14; matrix products, arithmetic and copies ran while one was open for 7% -> 8% of each run, Pallas kernels for 0% -> 0%
where the time goes in v4:
time: 66.1 us; the launch traced here: 66 us
  starting transfers between devices  33.4 us (51%)
  waiting for transfers between devices  22.9 us (35%)
  local copies, waits for them, and re-layouts  4.81 us (7%)
  other arithmetic  2.25 us (3%)
  matrix products  1.6 us (2%)
  between operations  0.96 us (1%)
    ppermute x21, starting transfers between devices, shifted(): lax.ppermute(array, axis, [(i, (i + shift) % size) for i in range(size)])  33.4 us
    ppermute x21, waiting for transfers between devices, shifted(): lax.ppermute(array, axis, [(i, (i + shift) % size) for i in range(size)])  22.9 us
    squeeze x3, local copies, waits for them, and re-layouts, of(): return lax.dynamic_index_in_dim(array, s, 0, keepdims=False)  1.97 us
  transfers between devices with their start and end apart: 21, of which 14 were waited for; matrix products, arithmetic and copies ran while one was open for 8% of the time, Pallas kernels for 0%

profile of v4, /device:TPU:0, one launch (start us, length us, event | category | flops | bytes accessed | tf_op | source)
XLA Modules:
  0.0 66.0 jit_solution(1337727142951860983)
XLA Ops:
  0.7 1.0 %dynamic-slice_bitcast_fusion.2 = f32[128,128]{1,0:T(8,128)S(1)} fusion(f32[2,128,512]{2,1,0:T(8,128)} %param.5, s32[]{:T(128)S(6)} %select_n.201, s32[]{:T(128)S(6)} %select_n.200), kind=kLoop, calls=%fused_computation.43 | loop fusion | bytes 131080 | tf_op jit(solution)/shard_map/jit(dynamic_index_in_dim)/squeeze | solution.py:32
  1.7 0.5 collective-permute-start.4
  2.2 0.9 %dynamic-slice_bitcast_fusion = f32[256,128]{1,0:T(8,128)S(1)} fusion(f32[2,256,128]{2,1,0:T(8,128)} %param.4, s32[]{:T(128)S(6)} %select_n.194), kind=kLoop, calls=%fused_computation.31 | loop fusion | bytes 262148 | tf_op jit(solution)/shard_map/jit(dynamic_index_in_dim)/squeeze | solution.py:32
  3.1 0.1 collective-permute-start
  3.3 1.0 %bitcast_select_fusion.5 = (f32[128,128]{1,0:T(8,128)S(1)}, f32[128,128]{1,0:T(8,128)S(1)}) fusion(f32[128,128]{1,0:T(8,128)S(1)} %collective-permute-done.4, f32[2,128,512]{2,1,0:T(8,128)} %param.5, s32[]{:T(128)S(6)} %select_n.198, s32[]{:T(128)S(6)} %select_n.200, pred[]{:T(512)S(6)} %eq.39), kind=kLoop, calls=%fused_computation.41 | loop fusion | flops 32768 | bytes 262153 | tf_op jit(solution)/shard_map/jit(_where)/select_n | solution.py:35
  4.3 0.6 fusion.7
  5.0 2.9 %collective-permute-start.5 = (f32[64,512]{1,0:T(8,128)S(1)}, f32[64,512]{1,0:T(8,128)S(1)}, u32[]{:S(2)}, u32[]{:S(2)}) collective-permute-start(f32[64,512]{1,0:T(8,128)S(1)} %get-tuple-element.12), channel_id=1, source_target_pairs={{0,8},{8,16},{16,24},{24,0},{1,9},{9,17},{17,25},{25,1},{2,10},{10... | collective-permute-start | bytes 393224 | tf_op jit(solution)/shard_map/ppermute | solution.py:16
  7.9 1.4 %collective-permute-start.6 = (f32[64,512]{1,0:T(8,128)S(1)}, f32[64,512]{1,0:T(8,128)S(1)}, u32[]{:S(2)}, u32[]{:S(2)}) collective-permute-start(f32[64,512]{1,0:T(8,128)S(1)} %get-tuple-element.14), channel_id=1, source_target_pairs={{0,16},{8,24},{16,0},{24,8},{1,17},{9,25},{17,1},{25,9},{2,18},{10... | collective-permute-start | bytes 393224 | tf_op jit(solution)/shard_map/ppermute | solution.py:16
  9.3 1.6 %collective-permute-start.7 = (f32[64,512]{1,0:T(8,128)S(1)}, f32[64,512]{1,0:T(8,128)S(1)}, u32[]{:S(2)}, u32[]{:S(2)}) collective-permute-start(f32[64,512]{1,0:T(8,128)S(1)} %get-tuple-element.13), channel_id=1, source_target_pairs={{0,24},{8,0},{16,8},{24,16},{1,25},{9,1},{17,9},{25,17},{2,26},{10... | collective-permute-start | bytes 393224 | tf_op jit(solution)/shard_map/ppermute | solution.py:16
  10.9 0.1 select_reduce_fusion
  11.0 0.6 gather_fusion
  11.6 1.4 %collective-permute-done.5 = f32[64,512]{1,0:T(8,128)S(1)} collective-permute-done((f32[64,512]{1,0:T(8,128)S(1)}, f32[64,512]{1,0:T(8,128)S(1)}, u32[]{:S(2)}, u32[]{:S(2)}) %collective-permute-start.5) | collective-permute-done | bytes 131104 | tf_op jit(solution)/shard_map/ppermute | solution.py:16
  13.1 2.3 %collective-permute-done.6 = f32[64,512]{1,0:T(8,128)S(1)} collective-permute-done((f32[64,512]{1,0:T(8,128)S(1)}, f32[64,512]{1,0:T(8,128)S(1)}, u32[]{:S(2)}, u32[]{:S(2)}) %collective-permute-start.6) | collective-permute-done | bytes 131104 | tf_op jit(solution)/shard_map/ppermute | solution.py:16
  15.3 0.4 collective-permute-done.7
  15.8 1.6 %collective-permute-start.8 = (f32[64,128]{1,0:T(8,128)S(1)}, f32[64,128]{1,0:T(8,128)S(1)}, u32[]{:S(2)}, u32[]{:S(2)}) collective-permute-start(f32[64,128]{1,0:T(8,128)S(1)} %get-tuple-element.30), channel_id=1, source_target_pairs={{0,2},{2,4},{4,6},{6,0},{1,3},{3,5},{5,7},{7,1},{8,10},{10,12},{12... | collective-permute-start | bytes 98312 | tf_op jit(solution)/shard_map/ppermute | solution.py:16
  17.5 2.6 %collective-permute-start.9 = (f32[64,128]{1,0:T(8,128)S(1)}, f32[64,128]{1,0:T(8,128)S(1)}, u32[]{:S(2)}, u32[]{:S(2)}) collective-permute-start(f32[64,128]{1,0:T(8,128)S(1)} %get-tuple-element.29), channel_id=1, source_target_pairs={{0,4},{2,6},{4,0},{6,2},{1,5},{3,7},{5,1},{7,3},{8,12},{10,14},{12... | collective-permute-start | bytes 98312 | tf_op jit(solution)/shard_map/ppermute | solution.py:16
  20.1 1.3 %collective-permute-start.10 = (f32[64,128]{1,0:T(8,128)S(1)}, f32[64,128]{1,0:T(8,128)S(1)}, u32[]{:S(2)}, u32[]{:S(2)}) collective-permute-start(f32[64,128]{1,0:T(8,128)S(1)} %get-tuple-element.28), channel_id=1, source_target_pairs={{0,6},{2,0},{4,2},{6,4},{1,7},{3,1},{5,3},{7,5},{8,14},{10,8},{12,... | collective-permute-start | bytes 98312 | tf_op jit(solution)/shard_map/ppermute | solution.py:16
  21.5 0.1 collective-permute-done.8
  21.6 1.1 %collective-permute-done.9 = f32[64,128]{1,0:T(8,128)S(1)} collective-permute-done((f32[64,128]{1,0:T(8,128)S(1)}, f32[64,128]{1,0:T(8,128)S(1)}, u32[]{:S(2)}, u32[]{:S(2)}) %collective-permute-start.9) | collective-permute-done | bytes 32800 | tf_op jit(solution)/shard_map/ppermute | solution.py:16
  22.7 1.3 %collective-permute-done.10 = f32[64,128]{1,0:T(8,128)S(1)} collective-permute-done((f32[64,128]{1,0:T(8,128)S(1)}, f32[64,128]{1,0:T(8,128)S(1)}, u32[]{:S(2)}, u32[]{:S(2)}) %collective-permute-start.10) | collective-permute-done | bytes 32800 | tf_op jit(solution)/shard_map/ppermute | solution.py:16
  24.0 1.8 %collective-permute-start.11 = (f32[4,64,128]{2,1,0:T(8,128)S(1)}, f32[4,64,128]{2,1,0:T(8,128)S(1)}, u32[]{:S(2)}, u32[]{:S(2)}) collective-permute-start(f32[4,64,128]{2,1,0:T(8,128)S(1)} %get-tuple-element.26), channel_id=1, source_target_pairs={{0,8},{8,16},{16,24},{24,0},{1,9},{9,17},{17,25},{25,1},{2,10},{10... | collective-permute-start | bytes 393224 | tf_op jit(solution)/shard_map/ppermute | solution.py:16
  25.8 0.3 collective-permute-start.1
  26.1 3.5 %collective-permute-start.2 = (f32[256,256]{1,0:T(8,128)S(1)}, f32[256,256]{1,0:T(8,128)S(1)}, u32[]{:S(2)}, u32[]{:S(2)}) collective-permute-start(f32[256,256]{1,0:T(8,128)S(1)} %get-tuple-element.18), channel_id=1, source_target_pairs={{0,4},{2,6},{4,0},{6,2},{1,5},{3,7},{5,1},{7,3},{8,12},{10,14},{12... | collective-permute-start | bytes 786440 | tf_op jit(solution)/shard_map/ppermute | solution.py:16
  29.6 0.1 collective-permute-start.3
  29.7 0.5 collective-permute-start.12
  30.2 2.3 %collective-permute-start.13 = (f32[4,64,128]{2,1,0:T(8,128)S(1)}, f32[4,64,128]{2,1,0:T(8,128)S(1)}, u32[]{:S(2)}, u32[]{:S(2)}) collective-permute-start(f32[4,64,128]{2,1,0:T(8,128)S(1)} %get-tuple-element.26), channel_id=1, source_target_pairs={{0,24},{8,0},{16,8},{24,16},{1,25},{9,1},{17,9},{25,17},{2,26},{10... | collective-permute-start | bytes 393224 | tf_op jit(solution)/shard_map/ppermute | solution.py:16
  32.6 0.1 reshape.111
  32.7 0.1 multiply_reduce_fusion
  32.8 1.9 %collective-permute-done.12 = f32[4,64,128]{2,1,0:T(8,128)S(1)} collective-permute-done((f32[4,64,128]{2,1,0:T(8,128)S(1)}, f32[4,64,128]{2,1,0:T(8,128)S(1)}, u32[]{:S(2)}, u32[]{:S(2)}) %collective-permute-start.12) | collective-permute-done | bytes 131104 | tf_op jit(solution)/shard_map/ppermute | solution.py:16
  34.7 0.5 collective-permute-done.13
  35.2 0.6 gather_fusion.1
  35.9 1.1 %collective-permute-done.1 = f32[256,256]{1,0:T(8,128)S(1)} collective-permute-done((f32[256,256]{1,0:T(8,128)S(1)}, f32[256,256]{1,0:T(8,128)S(1)}, u32[]{:S(2)}, u32[]{:S(2)}) %collective-permute-start.1) | collective-permute-done | bytes 262176 | tf_op jit(solution)/shard_map/ppermute | solution.py:16
  37.0 7.6 %collective-permute-done.2 = f32[256,256]{1,0:T(8,128)S(1)} collective-permute-done((f32[256,256]{1,0:T(8,128)S(1)}, f32[256,256]{1,0:T(8,128)S(1)}, u32[]{:S(2)}, u32[]{:S(2)}) %collective-permute-start.2) | collective-permute-done | bytes 262176 | tf_op jit(solution)/shard_map/ppermute | solution.py:16
  44.6 1.0 %fusion.15 = (f32[128]{0:T(128)S(1)}, f32[256,128]{1,0:T(8,128)S(1)}) fusion(f32[4,256,128]{2,1,0:T(8,128)S(1)} %bitcast.68, s32[]{:T(128)S(6)} %select_n.226, f32[1,256,256]{2,1,0:T(8,128)S(1)} %bitcast.84, f32[1,256,256]{2,1,0:T(8,128)S(1)} %bitcast.83, f32[1,256,256]{2,1,0:T(8,128)S(1)} %bitcast.82, f32[1,256,256]{2,1,0:T(8,128)S(1)} %get-tuple-element.17), kind=kOutput, calls=%fused_computation.27 | convolution fusion | flops 403505024 | bytes 1835524 | tf_op jit(solution)/shard_map/tij,tjk->ik/dot_general | solution.py:71
  45.7 6.1 %collective-permute-start.14 = (f32[2,40,128]{2,1,0:T(8,128)S(1)}, f32[2,40,128]{2,1,0:T(8,128)S(1)}, u32[]{:S(2)}, u32[]{:S(2)}) collective-permute-start(f32[2,40,128]{2,1,0:T(8,128)S(1)} %get-tuple-element.32), channel_id=1, source_target_pairs={{0,2},{2,4},{4,6},{6,0},{1,3},{3,5},{5,7},{7,1},{8,10},{10,12},{12... | collective-permute-start | bytes 122888 | tf_op jit(solution)/shard_map/ppermute | solution.py:16
  51.9 2.4 %collective-permute-start.16 = (f32[2,40,128]{2,1,0:T(8,128)S(1)}, f32[2,40,128]{2,1,0:T(8,128)S(1)}, u32[]{:S(2)}, u32[]{:S(2)}) collective-permute-start(f32[2,40,128]{2,1,0:T(8,128)S(1)} %get-tuple-element.34), channel_id=1, source_target_pairs={{0,6},{2,0},{4,2},{6,4},{1,7},{3,1},{5,3},{7,5},{8,14},{10,8},{12,... | collective-permute-start | bytes 122888 | tf_op jit(solution)/shard_map/ppermute | solution.py:16
  54.3 2.5 %collective-permute-done.15 = f32[2,40,128]{2,1,0:T(8,128)S(1)} collective-permute-done((f32[2,40,128]{2,1,0:T(8,128)S(1)}, f32[2,40,128]{2,1,0:T(8,128)S(1)}, u32[]{:S(2)}, u32[]{:S(2)}) %collective-permute-start.15) | collective-permute-done | bytes 40992 | tf_op jit(solution)/shard_map/ppermute | solution.py:16
  56.8 0.6 gather_fusion.2
  57.4 1.3 %collective-permute-done.17 = f32[40,512]{1,0:T(8,128)S(1)} collective-permute-done((f32[40,512]{1,0:T(8,128)S(1)}, f32[40,512]{1,0:T(8,128)S(1)}, u32[]{:S(2)}, u32[]{:S(2)}) %collective-permute-start.17) | collective-permute-done | bytes 81952 | tf_op jit(solution)/shard_map/ppermute | solution.py:16
  58.7 0.1 copy.14
  58.9 2.4 %collective-permute-start.18 = (f32[2,512]{1,0:T(2,128)S(1)}, f32[2,512]{1,0:T(2,128)S(1)}, u32[]{:S(2)}, u32[]{:S(2)}) collective-permute-start(f32[2,512]{1,0:T(2,128)S(1)} %fusion.19), channel_id=1, source_target_pairs={{0,8},{8,16},{16,24},{24,0},{1,9},{9,17},{17,25},{25,1},{2,10},{10... | collective-permute-start | bytes 12296 | tf_op jit(solution)/shard_map/ppermute | solution.py:16
  61.3 0.4 collective-permute-start.19
  61.8 1.4 %collective-permute-start.20 = (f32[2,512]{1,0:T(2,128)S(1)}, f32[2,512]{1,0:T(2,128)S(1)}, u32[]{:S(2)}, u32[]{:S(2)}) collective-permute-start(f32[2,512]{1,0:T(2,128)S(1)} %fusion.19), channel_id=1, source_target_pairs={{0,24},{8,0},{16,8},{24,16},{1,25},{9,1},{17,9},{25,17},{2,26},{10... | collective-permute-start | bytes 12296 | tf_op jit(solution)/shard_map/ppermute | solution.py:16
  63.1 0.1 fusion.11
  63.3 0.7 %copy.15 = f32[2,32,512]{2,1,0:T(8,128)} copy(f32[2,32,512]{2,0,1:T(2,128)S(1)} %fusion.11) | data formatting | bytes 262144
  63.9 1.0 %collective-permute-done.19 = f32[2,512]{1,0:T(2,128)S(1)} collective-permute-done((f32[2,512]{1,0:T(2,128)S(1)}, f32[2,512]{1,0:T(2,128)S(1)}, u32[]{:S(2)}, u32[]{:S(2)}) %collective-permute-start.19) | collective-permute-done | bytes 4128 | tf_op jit(solution)/shard_map/ppermute | solution.py:16
  64.9 0.4 collective-permute-done.20
  65.4 0.6 add_add_fusion.1
  (37 shorter events, 0.7 us)
Async XLA Ops:
  0.6 10.3 %copy-start = (s32[2,4]{1,0:T(2,128)S(1)}, s32[2,4]{1,0:T(2,128)}, u32[]{:S(2)}) copy-start(s32[2,4]{1,0:T(2,128)} %param.7) | copy-start | bytes 100
  0.6 3.7 %copy-start.2 = (f32[2,128,512]{2,1,0:T(8,128)S(1)}, f32[2,128,512]{2,1,0:T(8,128)}, u32[]{:S(2)}) copy-start(f32[2,128,512]{2,1,0:T(8,128)} %param.6) | copy-start | bytes 1572868
  1.7 1.6 %collective-permute-start.4 = (f32[128,128]{1,0:T(8,128)S(1)}, f32[128,128]{1,0:T(8,128)S(1)}, u32[]{:S(2)}, u32[]{:S(2)}) collective-permute-start(f32[128,128]{1,0:T(8,128)S(1)} %dynamic-slice_bitcast_fusion.2), channel_id=1, source_target_pairs={{0,1},{1,0},{2,3},{3,2},{4,5},{5,4},{6,7},{7,6},{8,9},{9,8},{10,11... | collective-permute-start | bytes 196616 | tf_op jit(solution)/shard_map/ppermute | solution.py:16
  3.1 22.6 %collective-permute-start = (f32[256,128]{1,0:T(8,128)S(1)}, f32[256,128]{1,0:T(8,128)S(1)}, u32[]{:S(2)}, u32[]{:S(2)}) collective-permute-start(f32[256,128]{1,0:T(8,128)S(1)} %dynamic-slice_bitcast_fusion), channel_id=1, source_target_pairs={{0,1},{1,0},{2,3},{3,2},{4,5},{5,4},{6,7},{7,6},{8,9},{9,8},{10,11... | collective-permute-start | bytes 393224 | tf_op jit(solution)/shard_map/ppermute | solution.py:16
  5.0 8.1 %collective-permute-start.5 = (f32[64,512]{1,0:T(8,128)S(1)}, f32[64,512]{1,0:T(8,128)S(1)}, u32[]{:S(2)}, u32[]{:S(2)}) collective-permute-start(f32[64,512]{1,0:T(8,128)S(1)} %get-tuple-element.12), channel_id=1, source_target_pairs={{0,8},{8,16},{16,24},{24,0},{1,9},{9,17},{17,25},{25,1},{2,10},{10... | collective-permute-start | bytes 393224 | tf_op jit(solution)/shard_map/ppermute | solution.py:16
  7.9 7.4 %collective-permute-start.6 = (f32[64,512]{1,0:T(8,128)S(1)}, f32[64,512]{1,0:T(8,128)S(1)}, u32[]{:S(2)}, u32[]{:S(2)}) collective-permute-start(f32[64,512]{1,0:T(8,128)S(1)} %get-tuple-element.14), channel_id=1, source_target_pairs={{0,16},{8,24},{16,0},{24,8},{1,17},{9,25},{17,1},{25,9},{2,18},{10... | collective-permute-start | bytes 393224 | tf_op jit(solution)/shard_map/ppermute | solution.py:16
  9.3 6.4 %collective-permute-start.7 = (f32[64,512]{1,0:T(8,128)S(1)}, f32[64,512]{1,0:T(8,128)S(1)}, u32[]{:S(2)}, u32[]{:S(2)}) collective-permute-start(f32[64,512]{1,0:T(8,128)S(1)} %get-tuple-element.13), channel_id=1, source_target_pairs={{0,24},{8,0},{16,8},{24,16},{1,25},{9,1},{17,9},{25,17},{2,26},{10... | collective-permute-start | bytes 393224 | tf_op jit(solution)/shard_map/ppermute | solution.py:16
  15.8 9.9 %copy-start.1 = (f32[2,256,128]{2,1,0:T(8,128)S(1)}, f32[2,256,128]{2,1,0:T(8,128)}, u32[]{:S(2)}) copy-start(f32[2,256,128]{2,1,0:T(8,128)} %param.4) | copy-start | bytes 786436
  15.8 5.8 %collective-permute-start.8 = (f32[64,128]{1,0:T(8,128)S(1)}, f32[64,128]{1,0:T(8,128)S(1)}, u32[]{:S(2)}, u32[]{:S(2)}) collective-permute-start(f32[64,128]{1,0:T(8,128)S(1)} %get-tuple-element.30), channel_id=1, source_target_pairs={{0,2},{2,4},{4,6},{6,0},{1,3},{3,5},{5,7},{7,1},{8,10},{10,12},{12... | collective-permute-start | bytes 98312 | tf_op jit(solution)/shard_map/ppermute | solution.py:16
  17.5 5.2 %collective-permute-start.9 = (f32[64,128]{1,0:T(8,128)S(1)}, f32[64,128]{1,0:T(8,128)S(1)}, u32[]{:S(2)}, u32[]{:S(2)}) collective-permute-start(f32[64,128]{1,0:T(8,128)S(1)} %get-tuple-element.29), channel_id=1, source_target_pairs={{0,4},{2,6},{4,0},{6,2},{1,5},{3,7},{5,1},{7,3},{8,12},{10,14},{12... | collective-permute-start | bytes 98312 | tf_op jit(solution)/shard_map/ppermute | solution.py:16
  20.1 3.9 %collective-permute-start.10 = (f32[64,128]{1,0:T(8,128)S(1)}, f32[64,128]{1,0:T(8,128)S(1)}, u32[]{:S(2)}, u32[]{:S(2)}) collective-permute-start(f32[64,128]{1,0:T(8,128)S(1)} %get-tuple-element.28), channel_id=1, source_target_pairs={{0,6},{2,0},{4,2},{6,4},{1,7},{3,1},{5,3},{7,5},{8,14},{10,8},{12,... | collective-permute-start | bytes 98312 | tf_op jit(solution)/shard_map/ppermute | solution.py:16
  24.0 6.2 %collective-permute-start.11 = (f32[4,64,128]{2,1,0:T(8,128)S(1)}, f32[4,64,128]{2,1,0:T(8,128)S(1)}, u32[]{:S(2)}, u32[]{:S(2)}) collective-permute-start(f32[4,64,128]{2,1,0:T(8,128)S(1)} %get-tuple-element.26), channel_id=1, source_target_pairs={{0,8},{8,16},{16,24},{24,0},{1,9},{9,17},{17,25},{25,1},{2,10},{10... | collective-permute-start | bytes 393224 | tf_op jit(solution)/shard_map/ppermute | solution.py:16
  25.8 11.2 %collective-permute-start.1 = (f32[256,256]{1,0:T(8,128)S(1)}, f32[256,256]{1,0:T(8,128)S(1)}, u32[]{:S(2)}, u32[]{:S(2)}) collective-permute-start(f32[256,256]{1,0:T(8,128)S(1)} %get-tuple-element.18), channel_id=1, source_target_pairs={{0,2},{2,4},{4,6},{6,0},{1,3},{3,5},{5,7},{7,1},{8,10},{10,12},{12... | collective-permute-start | bytes 786440 | tf_op jit(solution)/shard_map/ppermute | solution.py:16
  26.1 18.5 %collective-permute-start.2 = (f32[256,256]{1,0:T(8,128)S(1)}, f32[256,256]{1,0:T(8,128)S(1)}, u32[]{:S(2)}, u32[]{:S(2)}) collective-permute-start(f32[256,256]{1,0:T(8,128)S(1)} %get-tuple-element.18), channel_id=1, source_target_pairs={{0,4},{2,6},{4,0},{6,2},{1,5},{3,7},{5,1},{7,3},{8,12},{10,14},{12... | collective-permute-start | bytes 786440 | tf_op jit(solution)/shard_map/ppermute | solution.py:16
  29.6 15.0 %collective-permute-start.3 = (f32[256,256]{1,0:T(8,128)S(1)}, f32[256,256]{1,0:T(8,128)S(1)}, u32[]{:S(2)}, u32[]{:S(2)}) collective-permute-start(f32[256,256]{1,0:T(8,128)S(1)} %get-tuple-element.18), channel_id=1, source_target_pairs={{0,6},{2,0},{4,2},{6,4},{1,7},{3,1},{5,3},{7,5},{8,14},{10,8},{12,... | collective-permute-start | bytes 786440 | tf_op jit(solution)/shard_map/ppermute | solution.py:16
  29.7 5.0 %collective-permute-start.12 = (f32[4,64,128]{2,1,0:T(8,128)S(1)}, f32[4,64,128]{2,1,0:T(8,128)S(1)}, u32[]{:S(2)}, u32[]{:S(2)}) collective-permute-start(f32[4,64,128]{2,1,0:T(8,128)S(1)} %get-tuple-element.26), channel_id=1, source_target_pairs={{0,16},{8,24},{16,0},{24,8},{1,17},{9,25},{17,1},{25,9},{2,18},{10... | collective-permute-start | bytes 393224 | tf_op jit(solution)/shard_map/ppermute | solution.py:16
  30.2 5.0 %collective-permute-start.13 = (f32[4,64,128]{2,1,0:T(8,128)S(1)}, f32[4,64,128]{2,1,0:T(8,128)S(1)}, u32[]{:S(2)}, u32[]{:S(2)}) collective-permute-start(f32[4,64,128]{2,1,0:T(8,128)S(1)} %get-tuple-element.26), channel_id=1, source_target_pairs={{0,24},{8,0},{16,8},{24,16},{1,25},{9,1},{17,9},{25,17},{2,26},{10... | collective-permute-start | bytes 393224 | tf_op jit(solution)/shard_map/ppermute | solution.py:16
  45.7 8.6 %collective-permute-start.14 = (f32[2,40,128]{2,1,0:T(8,128)S(1)}, f32[2,40,128]{2,1,0:T(8,128)S(1)}, u32[]{:S(2)}, u32[]{:S(2)}) collective-permute-start(f32[2,40,128]{2,1,0:T(8,128)S(1)} %get-tuple-element.32), channel_id=1, source_target_pairs={{0,2},{2,4},{4,6},{6,0},{1,3},{3,5},{5,7},{7,1},{8,10},{10,12},{12... | collective-permute-start | bytes 122888 | tf_op jit(solution)/shard_map/ppermute | solution.py:16
  51.8 4.9 %collective-permute-start.15 = (f32[2,40,128]{2,1,0:T(8,128)S(1)}, f32[2,40,128]{2,1,0:T(8,128)S(1)}, u32[]{:S(2)}, u32[]{:S(2)}) collective-permute-start(f32[2,40,128]{2,1,0:T(8,128)S(1)} %get-tuple-element.33), channel_id=1, source_target_pairs={{0,4},{2,6},{4,0},{6,2},{1,5},{3,7},{5,1},{7,3},{8,12},{10,14},{12... | collective-permute-start | bytes 122888 | tf_op jit(solution)/shard_map/ppermute | solution.py:16
  51.9 4.9 %collective-permute-start.16 = (f32[2,40,128]{2,1,0:T(8,128)S(1)}, f32[2,40,128]{2,1,0:T(8,128)S(1)}, u32[]{:S(2)}, u32[]{:S(2)}) collective-permute-start(f32[2,40,128]{2,1,0:T(8,128)S(1)} %get-tuple-element.34), channel_id=1, source_target_pairs={{0,6},{2,0},{4,2},{6,4},{1,7},{3,1},{5,3},{7,5},{8,14},{10,8},{12,... | collective-permute-start | bytes 122888 | tf_op jit(solution)/shard_map/ppermute | solution.py:16
  57.4 1.3 %collective-permute-start.17 = (f32[40,512]{1,0:T(8,128)S(1)}, f32[40,512]{1,0:T(8,128)S(1)}, u32[]{:S(2)}, u32[]{:S(2)}) collective-permute-start(f32[40,512]{1,0:T(8,128)S(1)} %dynamic-slice_bitcast_fusion.1), channel_id=1, source_target_pairs={{0,1},{1,0},{2,3},{3,2},{4,5},{5,4},{6,7},{7,6},{8,9},{9,8},{10,11... | collective-permute-start | bytes 245768 | tf_op jit(solution)/shard_map/ppermute | solution.py:16
  58.9 5.0 %collective-permute-start.18 = (f32[2,512]{1,0:T(2,128)S(1)}, f32[2,512]{1,0:T(2,128)S(1)}, u32[]{:S(2)}, u32[]{:S(2)}) collective-permute-start(f32[2,512]{1,0:T(2,128)S(1)} %fusion.19), channel_id=1, source_target_pairs={{0,8},{8,16},{16,24},{24,0},{1,9},{9,17},{17,25},{25,1},{2,10},{10... | collective-permute-start | bytes 12296 | tf_op jit(solution)/shard_map/ppermute | solution.py:16
  61.3 3.6 %collective-permute-start.19 = (f32[2,512]{1,0:T(2,128)S(1)}, f32[2,512]{1,0:T(2,128)S(1)}, u32[]{:S(2)}, u32[]{:S(2)}) collective-permute-start(f32[2,512]{1,0:T(2,128)S(1)} %fusion.19), channel_id=1, source_target_pairs={{0,16},{8,24},{16,0},{24,8},{1,17},{9,25},{17,1},{25,9},{2,18},{10... | collective-permute-start | bytes 12296 | tf_op jit(solution)/shard_map/ppermute | solution.py:16
  61.8 3.6 %collective-permute-start.20 = (f32[2,512]{1,0:T(2,128)S(1)}, f32[2,512]{1,0:T(2,128)S(1)}, u32[]{:S(2)}, u32[]{:S(2)}) collective-permute-start(f32[2,512]{1,0:T(2,128)S(1)} %fusion.19), channel_id=1, source_target_pairs={{0,24},{8,0},{16,8},{24,16},{1,25},{9,1},{17,9},{25,17},{2,26},{10... | collective-permute-start | bytes 12296 | tf_op jit(solution)/shard_map/ppermute | solution.py:16

commit v5 on v4

--- a/solution.py
+++ b/solution.py
@@ -25,41 +25,48 @@
         _, chunk, width = panel.shape
         depth = factor_inv.shape[1]
         part = width // deep
-        quarter = B // rows
+        piece = chunk // rows
+        quarter = cores * piece
         out_rows = ancestor.shape[1] // cols
 
         def of(array, s):
             return lax.dynamic_index_in_dim(array, s, 0, keepdims=False)
 
-        def both(mine, other, axis):
-            first = jnp.where(core == 0, mine, other)
-            second = jnp.where(core == 0, other, mine)
-            return jnp.concatenate([first, second], axis=axis)
+        def swapped(array):
+            other = shifted(of(array, 1 - core), "core", cores, 1)
+            mine = of(array, core)
+            return jnp.stack([jnp.where(core == 0, mine, other), jnp.where(core == 0, other, mine)])
 
-        panel = lax.dynamic_slice_in_dim(panel, row * depth, depth, axis=2)
-        panel_other = shifted(of(panel, 1 - core), "core", cores, 1)
-        ancestor_other = shifted(of(ancestor, 1 - core), "core", cores, 1)
-        wide = both(of(ancestor, core), ancestor_other, 1)
-        wide = jnp.stack(gathered(wide, "z", deep))
-        tile = both(of(panel, core), panel_other, 0)
-        factor = of(factor_inv, core)
+        def after(array, far, shift):
+            if shift < deep:
+                array, got = lax.optimization_barrier((array, far[shift - 1]))
+                far = far[: shift - 1] + [got] + far[shift:]
+            return array, far
 
-        partial = jnp.dot(tile, factor, precision=highest)
+        far = [shifted(ancestor, "z", deep, d) for d in range(1, deep)]
+
+        mine = lax.dynamic_slice_in_dim(panel, row * depth, depth, axis=2)
+        partial = jnp.einsum("srw,swv->srv", mine, factor_inv, precision=highest)
 
         def rows_of(r):
-            return lax.dynamic_slice_in_dim(partial, r * quarter, quarter, axis=0)
+            return lax.dynamic_slice_in_dim(partial, r * piece, piece, axis=1)
 
         scaled = rows_of(row)
         for shift in range(1, rows):
             scaled = scaled + shifted(rows_of((row + shift) % rows), "row", rows, shift)
+        scaled, far = after(scaled, far, 2)
+        scaled = swapped(scaled)
 
         def columns_of(array, c):
             return lax.dynamic_slice_in_dim(array, c * part, part, axis=1)
 
+        scaled = scaled.reshape(quarter, width)
         slots = [columns_of(scaled, z)]
         for shift in range(1, deep):
             slots.append(shifted(columns_of(scaled, (z + shift) % deep), "z", deep, shift))
-        slots = jnp.stack(gathered(jnp.stack(slots), "row", rows))
+        slots, far = after(jnp.stack(slots), far, 1)
+        slots = jnp.stack(gathered(slots, "row", rows))
+        slots = slots.reshape(rows, deep, cores, piece, part)
 
         place = of(pattern, core)
         stored = jnp.arange(deep, dtype=jnp.int32)
@@ -67,12 +74,15 @@
         tiles = (z - jnp.arange(deep, dtype=jnp.int32)) % deep
         quarters = (row - jnp.arange(rows, dtype=jnp.int32)) % rows
         from_z = (z - jnp.take(stored, tiles, mode="clip")) % deep
-        spread = slots[quarters[None, :], from_z[:, None]].reshape(deep, B, part)
-        product = jnp.einsum("tij,tjk->ik", wide, spread, precision=highest)
+        spread = slots[quarters[None, :], from_z[:, None]]
+        spread = spread.transpose(0, 2, 1, 3, 4).reshape(deep, cores, chunk, part)
+        wide = jnp.stack([swapped(a) for a in [ancestor] + far])
+        product = jnp.einsum("tcij,tcjk->ik", wide, spread, precision=highest)
+        spread = spread.reshape(deep, B, part)
 
         held = product.shape[0] // B
         own = jnp.concatenate([of(spread, (z - (row * held + t)) % deep) for t in range(held)])
-        term = jnp.sum(own * product, axis=0) + jnp.sum(columns_of(factor, z) ** 2, axis=0)
+        term = jnp.sum(own * product, axis=0) + jnp.sum(columns_of(of(factor_inv, core), z) ** 2, axis=0)
 
         tail = jnp.broadcast_to(term, (cores, 8, part))
 

time: 66.1 us -> 63.1 us (0.955)
  waiting for transfers between devices: 22.9 us -> 20 us
  local copies, waits for them, and re-layouts: 4.81 us -> 3.65 us
  matrix products: 1.6 us -> 2.63 us
    ppermute x21 -> x24, waiting for transfers between devices: 22.9 us -> 20 us  [shifted(): lax.ppermute(array, axis, [(i, (i + shift) % size) for i in range(size)])]
    squeeze x3 -> x6, local copies, waits for them, and re-layouts: 1.97 us -> 0.07 us  [of(): return lax.dynamic_index_in_dim(array, s, 0, keepdims=False)]
    dot_general x2, matrix products: 1.6 us -> 2.63 us  [the longest x1 1.62 us: per_device(): partial = jnp.einsum('srw,swv->srv', mine, factor_inv, precision=highest)]
    select_n x2 -> x0, other arithmetic: 1.02 us -> none  [both(): first = jnp.where(core == 0, mine, other)]
    reduce_sum x1, other arithmetic: 0.1 us -> 1 us  [per_device(): jnp.sum(columns_of(of(factor_inv, core), z) ** 2, axis=0)]
    unnamed x7, local copies, waits for them, and re-layouts: 0.7 us -> 1.37 us
    ppermute x21 -> x24, starting transfers between devices: 33.4 us -> 33.3 us  [shifted(): lax.ppermute(array, axis, [(i, (i + shift) % size) for i in range(size)])]
  transfers between devices with their start and end apart: 21 -> 24, of which waited for: 14 -> 13; matrix products, arithmetic and copies ran while one was open for 8% -> 9% of each run, Pallas kernels for 0% -> 0%
where the time goes in v5:
time: 63.1 us; the launch traced here: 62.9 us
  starting transfers between devices  33.3 us (53%)
  waiting for transfers between devices  20 us (32%)
  local copies, waits for them, and re-layouts  3.65 us (6%)
  matrix products  2.63 us (4%)
  other arithmetic  2.3 us (4%)
  between operations  0.97 us (2%)
    ppermute x24, starting transfers between devices, shifted(): lax.ppermute(array, axis, [(i, (i + shift) % size) for i in range(size)])  33.3 us
    ppermute x24, waiting for transfers between devices, shifted(): lax.ppermute(array, axis, [(i, (i + shift) % size) for i in range(size)])  20 us
    dot_general x1, matrix products, per_device(): partial = jnp.einsum('srw,swv->srv', mine, factor_inv, precision=highest)  1.62 us
    unnamed x7, local copies, waits for them, and re-layouts  1.37 us
  transfers between devices with their start and end apart: 24, of which 13 were waited for; matrix products, arithmetic and copies ran while one was open for 9% of the time, Pallas kernels for 0%

profile of v5, /device:TPU:0, one launch (start us, length us, event | category | flops | bytes accessed | tf_op | source)
XLA Modules:
  0.0 62.9 jit_solution(8200807125642247139)
XLA Ops:
  0.6 4.1 %collective-permute-start.4 = (f32[2,256,128]{2,1,0:T(8,128)}, f32[2,256,128]{2,1,0:T(8,128)S(1)}, u32[]{:S(2)}, u32[]{:S(2)}) collective-permute-start(f32[2,256,128]{2,1,0:T(8,128)} %param.4), channel_id=1, source_target_pairs={{0,4},{2,6},{4,0},{6,2},{1,5},{3,7},{5,1},{7,3},{8,12},{10,14},{12... | collective-permute-start | bytes 786440 | tf_op jit(solution)/shard_map/ppermute | solution.py:16
  4.7 1.3 %collective-permute-start.12 = (f32[2,256,128]{2,1,0:T(8,128)}, f32[2,256,128]{2,1,0:T(8,128)S(1)}, u32[]{:S(2)}, u32[]{:S(2)}) collective-permute-start(f32[2,256,128]{2,1,0:T(8,128)} %param.4), channel_id=1, source_target_pairs={{0,6},{2,0},{4,2},{6,4},{1,7},{3,1},{5,3},{7,5},{8,14},{10,8},{12,... | collective-permute-start | bytes 786440 | tf_op jit(solution)/shard_map/ppermute | solution.py:16
  6.1 1.6 %fusion.18 = f32[2,128,512]{2,1,0:T(8,128)S(1)} fusion(f32[2,128,512]{2,1,0:T(8,128)} %param.6, f32[2,128,512]{2,1,0:T(8,128)S(1)} %copy-done, s32[]{:T(128)S(6)} %select_n.224), kind=kOutput, calls=%fused_computation.46 | convolution fusion | flops 201326592 | bytes 1179652 | tf_op jit(solution)/shard_map/srw,swv->srv/dot_general | solution.py:49
  7.8 1.5 %collective-permute-start.1 = (f32[2,32,512]{2,1,0:T(8,128)S(1)}, f32[2,32,512]{2,1,0:T(8,128)S(1)}, u32[]{:S(2)}, u32[]{:S(2)}) collective-permute-start(f32[2,32,512]{2,1,0:T(8,128)S(1)} %get-tuple-element.18), channel_id=1, source_target_pairs={{0,8},{8,16},{16,24},{24,0},{1,9},{9,17},{17,25},{25,1},{2,10},{10... | collective-permute-start | bytes 393224 | tf_op jit(solution)/shard_map/ppermute | solution.py:16
  9.3 1.4 %collective-permute-start.3 = (f32[2,32,512]{2,1,0:T(8,128)S(1)}, f32[2,32,512]{2,1,0:T(8,128)S(1)}, u32[]{:S(2)}, u32[]{:S(2)}) collective-permute-start(f32[2,32,512]{2,1,0:T(8,128)S(1)} %get-tuple-element.19), channel_id=1, source_target_pairs={{0,24},{8,0},{16,8},{24,16},{1,25},{9,1},{17,9},{25,17},{2,26},{10... | collective-permute-start | bytes 393224 | tf_op jit(solution)/shard_map/ppermute | solution.py:16
  10.7 1.5 %collective-permute-start.2 = (f32[2,32,512]{2,1,0:T(8,128)S(1)}, f32[2,32,512]{2,1,0:T(8,128)S(1)}, u32[]{:S(2)}, u32[]{:S(2)}) collective-permute-start(f32[2,32,512]{2,1,0:T(8,128)S(1)} %get-tuple-element.20), channel_id=1, source_target_pairs={{0,16},{8,24},{16,0},{24,8},{1,17},{9,25},{17,1},{25,9},{2,18},{10... | collective-permute-start | bytes 393224 | tf_op jit(solution)/shard_map/ppermute | solution.py:16
  12.3 0.7 %copy-done.2 = s32[2,4]{1,0:T(2,128)S(1)} copy-done((s32[2,4]{1,0:T(2,128)S(1)}, s32[2,4]{1,0:T(2,128)}, u32[]{:S(2)}) %copy-start.2) | copy-done | bytes 56
  12.9 0.1 select_reduce_fusion
  13.1 0.6 %gather_fusion = s32[4]{0:T(128)S(1)} fusion(s32[4]{0:T(128)S(1)} %select_reduce_fusion, s32[1024]{0:T(1024)S(1)} %pad_clamp_fusion), kind=kCustom, calls=%fused_computation | custom fusion | bytes 48 | tf_op jit(solution)/shard_map/jit(_take)/gather | solution.py:76
  13.7 0.1 broadcast_or_fusion
  13.8 0.1 reshape.124
  13.9 1.0 %multiply_reduce_fusion = f32[128]{0:T(128)S(1)} fusion(f32[2,128,512]{2,1,0:T(8,128)} %param.6, s32[]{:T(128)S(6)} %select_n.256, s32[]{:T(128)S(6)} %select_n.257), kind=kLoop, calls=%fused_computation.61 | loop fusion | flops 32640 | bytes 66056 | tf_op jit(solution)/shard_map/reduce_sum | solution.py:85
  14.9 0.7 %collective-permute-start.9 = (f32[2,256,128]{2,1,0:T(8,128)S(1)}, f32[2,256,128]{2,1,0:T(8,128)S(1)}, u32[]{:S(2)}, u32[]{:S(2)}) collective-permute-start(f32[2,256,128]{2,1,0:T(8,128)S(1)} %copy-done.1), channel_id=1, source_target_pairs={{0,2},{2,4},{4,6},{6,0},{1,3},{3,5},{5,7},{7,1},{8,10},{10,12},{12... | collective-permute-start | bytes 786440 | tf_op jit(solution)/shard_map/ppermute | solution.py:16
  15.7 0.6 collective-permute-done.3
  16.3 1.3 %collective-permute-done = f32[256,128]{1,0:T(8,128)S(1)} collective-permute-done((f32[256,128]{1,0:T(8,128)S(1)}, f32[256,128]{1,0:T(8,128)S(1)}, u32[]{:S(2)}, u32[]{:S(2)}) %collective-permute-start) | collective-permute-done | bytes 131104 | tf_op jit(solution)/shard_map/ppermute | solution.py:16
  17.6 0.1 collective-permute-done.4
  17.8 0.1 collective-permute-start.5
  17.9 0.4 collective-permute-start.13
  18.4 0.7 %collective-permute-done.5 = f32[32,512]{1,0:T(8,128)S(1)} collective-permute-done((f32[32,512]{1,0:T(8,128)S(1)}, f32[32,512]{1,0:T(8,128)S(1)}, u32[]{:S(2)}, u32[]{:S(2)}) %collective-permute-start.5) | collective-permute-done | bytes 65568 | tf_op jit(solution)/shard_map/ppermute | solution.py:16
  19.1 8.5 %collective-permute-start.8 = (f32[64,128]{1,0:T(8,128)S(1)}, f32[64,128]{1,0:T(8,128)S(1)}, u32[]{:S(2)}, u32[]{:S(2)}) collective-permute-start(f32[64,128]{1,0:T(8,128)S(1)} %get-tuple-element.38), channel_id=1, source_target_pairs={{0,6},{2,0},{4,2},{6,4},{1,7},{3,1},{5,3},{7,5},{8,14},{10,8},{12,... | collective-permute-start | bytes 98312 | tf_op jit(solution)/shard_map/ppermute | solution.py:16
  27.6 2.9 %collective-permute-start.7 = (f32[64,128]{1,0:T(8,128)S(1)}, f32[64,128]{1,0:T(8,128)S(1)}, u32[]{:S(2)}, u32[]{:S(2)}) collective-permute-start(f32[64,128]{1,0:T(8,128)S(1)} %get-tuple-element.39), channel_id=1, source_target_pairs={{0,4},{2,6},{4,0},{6,2},{1,5},{3,7},{5,1},{7,3},{8,12},{10,14},{12... | collective-permute-start | bytes 98312 | tf_op jit(solution)/shard_map/ppermute | solution.py:16
  30.4 0.6 collective-permute-done.8
  31.0 2.6 %collective-permute-done.7 = f32[64,128]{1,0:T(8,128)S(1)} collective-permute-done((f32[64,128]{1,0:T(8,128)S(1)}, f32[64,128]{1,0:T(8,128)S(1)}, u32[]{:S(2)}, u32[]{:S(2)}) %collective-permute-start.7) | collective-permute-done | bytes 32800 | tf_op jit(solution)/shard_map/ppermute | solution.py:16
  33.6 2.6 %collective-permute-done.6 = f32[64,128]{1,0:T(8,128)S(1)} collective-permute-done((f32[64,128]{1,0:T(8,128)S(1)}, f32[64,128]{1,0:T(8,128)S(1)}, u32[]{:S(2)}, u32[]{:S(2)}) %collective-permute-start.6) | collective-permute-done | bytes 32800 | tf_op jit(solution)/shard_map/ppermute | solution.py:16
  36.2 2.5 %collective-permute-start.16 = (f32[4,64,128]{2,1,0:T(8,128)S(1)}, f32[4,64,128]{2,1,0:T(8,128)S(1)}, u32[]{:S(2)}, u32[]{:S(2)}) collective-permute-start(f32[4,64,128]{2,1,0:T(8,128)S(1)} %pad_maximum_fusion.3), channel_id=1, source_target_pairs={{0,24},{8,0},{16,8},{24,16},{1,25},{9,1},{17,9},{25,17},{2,26},{10... | collective-permute-start | bytes 393224 | tf_op jit(solution)/shard_map/ppermute | solution.py:16
  38.7 0.5 collective-permute-start.15
  39.2 0.6 collective-permute-start.14
  39.8 0.1 collective-permute-start.10
  40.0 1.8 %collective-permute-done.16 = f32[4,64,128]{2,1,0:T(8,128)S(1)} collective-permute-done((f32[4,64,128]{2,1,0:T(8,128)S(1)}, f32[4,64,128]{2,1,0:T(8,128)S(1)}, u32[]{:S(2)}, u32[]{:S(2)}) %collective-permute-start.16) | collective-permute-done | bytes 131104 | tf_op jit(solution)/shard_map/ppermute | solution.py:16
  41.9 4.0 %collective-permute-done.15 = f32[4,64,128]{2,1,0:T(8,128)S(1)} collective-permute-done((f32[4,64,128]{2,1,0:T(8,128)S(1)}, f32[4,64,128]{2,1,0:T(8,128)S(1)}, u32[]{:S(2)}, u32[]{:S(2)}) %collective-permute-start.15) | collective-permute-done | bytes 131104 | tf_op jit(solution)/shard_map/ppermute | solution.py:16
  45.9 0.6 gather_fusion.1
  46.7 1.0 %fusion.9 = (f32[128]{0:T(128)S(1)}, f32[256,128]{1,0:T(8,128)S(1)}) fusion(f32[4,256,128]{2,1,0:T(8,128)S(1)} %bitcast.138, s32[]{:T(128)S(6)} %select_n.255, f32[4,2,128,128]{3,2,0,1:T(8,128)S(1)} %bitcast.139, f32[1,2,256,128]{3,2,0,1:T(8,128)S(1)} %get-tuple-element.52, f32[1,2,256,128]{3,2,0,1:T(8,128)S(1)} %get-tuple-element.51, ...), kind=kOutput, calls=%fused_computation.25 | convolution fusion | flops 403505024 | bytes 1835524 | tf_op jit(solution)/shard_map/tcij,tcjk->ik/dot_general | solution.py:80
  47.7 0.1 collective-permute-start.17
  47.8 0.4 collective-permute-start.18
  48.2 3.4 %collective-permute-start.19 = (f32[2,40,128]{2,1,0:T(8,128)S(1)}, f32[2,40,128]{2,1,0:T(8,128)S(1)}, u32[]{:S(2)}, u32[]{:S(2)}) collective-permute-start(f32[2,40,128]{2,1,0:T(8,128)S(1)} %get-tuple-element.44), channel_id=1, source_target_pairs={{0,6},{2,0},{4,2},{6,4},{1,7},{3,1},{5,3},{7,5},{8,14},{10,8},{12,... | collective-permute-start | bytes 122888 | tf_op jit(solution)/shard_map/ppermute | solution.py:16
  51.6 2.0 %collective-permute-done.17 = f32[2,40,128]{2,1,0:T(8,128)S(1)} collective-permute-done((f32[2,40,128]{2,1,0:T(8,128)S(1)}, f32[2,40,128]{2,1,0:T(8,128)S(1)}, u32[]{:S(2)}, u32[]{:S(2)}) %collective-permute-start.17) | collective-permute-done | bytes 40992 | tf_op jit(solution)/shard_map/ppermute | solution.py:16
  53.6 0.6 collective-permute-done.19
  54.2 0.6 gather_fusion.2
  54.8 0.1 collective-permute-start.20
  54.9 1.3 %collective-permute-done.20 = f32[40,512]{1,0:T(8,128)S(1)} collective-permute-done((f32[40,512]{1,0:T(8,128)S(1)}, f32[40,512]{1,0:T(8,128)S(1)}, u32[]{:S(2)}, u32[]{:S(2)}) %collective-permute-start.20) | collective-permute-done | bytes 81952 | tf_op jit(solution)/shard_map/ppermute | solution.py:16
  56.2 0.1 copy.33
  56.3 0.2 collective-permute-start.23
  56.5 1.2 %collective-permute-start.22 = (f32[2,512]{1,0:T(2,128)S(1)}, f32[2,512]{1,0:T(2,128)S(1)}, u32[]{:S(2)}, u32[]{:S(2)}) collective-permute-start(f32[2,512]{1,0:T(2,128)S(1)} %fusion.25), channel_id=1, source_target_pairs={{0,16},{8,24},{16,0},{24,8},{1,17},{9,25},{17,1},{25,9},{2,18},{10... | collective-permute-start | bytes 12296 | tf_op jit(solution)/shard_map/ppermute | solution.py:16
  57.8 1.7 %collective-permute-start.21 = (f32[2,512]{1,0:T(2,128)S(1)}, f32[2,512]{1,0:T(2,128)S(1)}, u32[]{:S(2)}, u32[]{:S(2)}) collective-permute-start(f32[2,512]{1,0:T(2,128)S(1)} %fusion.25), channel_id=1, source_target_pairs={{0,8},{8,16},{16,24},{24,0},{1,9},{9,17},{17,25},{25,1},{2,10},{10... | collective-permute-start | bytes 12296 | tf_op jit(solution)/shard_map/ppermute | solution.py:16
  59.4 0.1 fusion.8
  59.6 0.7 %copy.34 = f32[2,32,512]{2,1,0:T(8,128)} copy(f32[2,32,512]{2,0,1:T(2,128)S(1)} %fusion.8) | data formatting | bytes 262144
  60.3 2.0 %collective-permute-done.21 = f32[2,512]{1,0:T(2,128)S(1)} collective-permute-done((f32[2,512]{1,0:T(2,128)S(1)}, f32[2,512]{1,0:T(2,128)S(1)}, u32[]{:S(2)}, u32[]{:S(2)}) %collective-permute-start.21) | collective-permute-done | bytes 4128 | tf_op jit(solution)/shard_map/ppermute | solution.py:16
  62.3 0.6 add_add_fusion.1
  (53 shorter events, 0.8 us)
Async XLA Ops:
  0.6 5.5 %copy-start = (f32[2,128,512]{2,1,0:T(8,128)S(1)}, f32[2,128,512]{2,1,0:T(8,128)}, u32[]{:S(2)}) copy-start(f32[2,128,512]{2,1,0:T(8,128)} %param.5) | copy-start | bytes 1572868
  0.6 17.1 %collective-permute-start.4 = (f32[2,256,128]{2,1,0:T(8,128)}, f32[2,256,128]{2,1,0:T(8,128)S(1)}, u32[]{:S(2)}, u32[]{:S(2)}) collective-permute-start(f32[2,256,128]{2,1,0:T(8,128)} %param.4), channel_id=1, source_target_pairs={{0,4},{2,6},{4,0},{6,2},{1,5},{3,7},{5,1},{7,3},{8,12},{10,14},{12... | collective-permute-start | bytes 786440 | tf_op jit(solution)/shard_map/ppermute | solution.py:16
  4.7 13.1 %collective-permute-start.12 = (f32[2,256,128]{2,1,0:T(8,128)}, f32[2,256,128]{2,1,0:T(8,128)S(1)}, u32[]{:S(2)}, u32[]{:S(2)}) collective-permute-start(f32[2,256,128]{2,1,0:T(8,128)} %param.4), channel_id=1, source_target_pairs={{0,6},{2,0},{4,2},{6,4},{1,7},{3,1},{5,3},{7,5},{8,14},{10,8},{12,... | collective-permute-start | bytes 786440 | tf_op jit(solution)/shard_map/ppermute | solution.py:16
  7.8 7.2 %collective-permute-start.1 = (f32[2,32,512]{2,1,0:T(8,128)S(1)}, f32[2,32,512]{2,1,0:T(8,128)S(1)}, u32[]{:S(2)}, u32[]{:S(2)}) collective-permute-start(f32[2,32,512]{2,1,0:T(8,128)S(1)} %get-tuple-element.18), channel_id=1, source_target_pairs={{0,8},{8,16},{16,24},{24,0},{1,9},{9,17},{17,25},{25,1},{2,10},{10... | collective-permute-start | bytes 393224 | tf_op jit(solution)/shard_map/ppermute | solution.py:16
  9.3 7.0 %collective-permute-start.3 = (f32[2,32,512]{2,1,0:T(8,128)S(1)}, f32[2,32,512]{2,1,0:T(8,128)S(1)}, u32[]{:S(2)}, u32[]{:S(2)}) collective-permute-start(f32[2,32,512]{2,1,0:T(8,128)S(1)} %get-tuple-element.19), channel_id=1, source_target_pairs={{0,24},{8,0},{16,8},{24,16},{1,25},{9,1},{17,9},{25,17},{2,26},{10... | collective-permute-start | bytes 393224 | tf_op jit(solution)/shard_map/ppermute | solution.py:16
  10.7 5.5 %collective-permute-start.2 = (f32[2,32,512]{2,1,0:T(8,128)S(1)}, f32[2,32,512]{2,1,0:T(8,128)S(1)}, u32[]{:S(2)}, u32[]{:S(2)}) collective-permute-start(f32[2,32,512]{2,1,0:T(8,128)S(1)} %get-tuple-element.20), channel_id=1, source_target_pairs={{0,16},{8,24},{16,0},{24,8},{1,17},{9,25},{17,1},{25,9},{2,18},{10... | collective-permute-start | bytes 393224 | tf_op jit(solution)/shard_map/ppermute | solution.py:16
  12.3 0.7 %copy-start.2 = (s32[2,4]{1,0:T(2,128)S(1)}, s32[2,4]{1,0:T(2,128)}, u32[]{:S(2)}) copy-start(s32[2,4]{1,0:T(2,128)} %param.7) | copy-start | bytes 100
  13.7 1.2 %copy-start.1 = (f32[2,256,128]{2,1,0:T(8,128)S(1)}, f32[2,256,128]{2,1,0:T(8,128)}, u32[]{:S(2)}) copy-start(f32[2,256,128]{2,1,0:T(8,128)} %param.4) | copy-start | bytes 786436
  14.9 21.2 %collective-permute-start.9 = (f32[2,256,128]{2,1,0:T(8,128)S(1)}, f32[2,256,128]{2,1,0:T(8,128)S(1)}, u32[]{:S(2)}, u32[]{:S(2)}) collective-permute-start(f32[2,256,128]{2,1,0:T(8,128)S(1)} %copy-done.1), channel_id=1, source_target_pairs={{0,2},{2,4},{4,6},{6,0},{1,3},{3,5},{5,7},{7,1},{8,10},{10,12},{12... | collective-permute-start | bytes 786440 | tf_op jit(solution)/shard_map/ppermute | solution.py:16
  16.3 1.3 %collective-permute-start = (f32[256,128]{1,0:T(8,128)S(1)}, f32[256,128]{1,0:T(8,128)S(1)}, u32[]{:S(2)}, u32[]{:S(2)}) collective-permute-start(f32[256,128]{1,0:T(8,128)S(1)} %dynamic-slice_bitcast_fusion.3), channel_id=1, source_target_pairs={{0,1},{1,0},{2,3},{3,2},{4,5},{5,4},{6,7},{7,6},{8,9},{9,8},{10,11... | collective-permute-start | bytes 393224 | tf_op jit(solution)/shard_map/ppermute | solution.py:16
  17.8 1.3 %collective-permute-start.5 = (f32[32,512]{1,0:T(8,128)S(1)}, f32[32,512]{1,0:T(8,128)S(1)}, u32[]{:S(2)}, u32[]{:S(2)}) collective-permute-start(f32[32,512]{1,0:T(8,128)S(1)} %dynamic-slice_bitcast_fusion.5), channel_id=1, source_target_pairs={{0,1},{1,0},{2,3},{3,2},{4,5},{5,4},{6,7},{7,6},{8,9},{9,8},{10,11... | collective-permute-start | bytes 196616 | tf_op jit(solution)/shard_map/ppermute | solution.py:16
  17.9 21.9 %collective-permute-start.13 = (f32[256,128]{1,0:T(8,128)S(1)}, f32[256,128]{1,0:T(8,128)S(1)}, u32[]{:S(2)}, u32[]{:S(2)}) collective-permute-start(f32[256,128]{1,0:T(8,128)S(1)} %dynamic-slice_bitcast_fusion), channel_id=1, source_target_pairs={{0,1},{1,0},{2,3},{3,2},{4,5},{5,4},{6,7},{7,6},{8,9},{9,8},{10,11... | collective-permute-start | bytes 393224 | tf_op jit(solution)/shard_map/ppermute | solution.py:16
  19.1 11.9 %collective-permute-start.8 = (f32[64,128]{1,0:T(8,128)S(1)}, f32[64,128]{1,0:T(8,128)S(1)}, u32[]{:S(2)}, u32[]{:S(2)}) collective-permute-start(f32[64,128]{1,0:T(8,128)S(1)} %get-tuple-element.38), channel_id=1, source_target_pairs={{0,6},{2,0},{4,2},{6,4},{1,7},{3,1},{5,3},{7,5},{8,14},{10,8},{12,... | collective-permute-start | bytes 98312 | tf_op jit(solution)/shard_map/ppermute | solution.py:16
  27.6 6.0 %collective-permute-start.7 = (f32[64,128]{1,0:T(8,128)S(1)}, f32[64,128]{1,0:T(8,128)S(1)}, u32[]{:S(2)}, u32[]{:S(2)}) collective-permute-start(f32[64,128]{1,0:T(8,128)S(1)} %get-tuple-element.39), channel_id=1, source_target_pairs={{0,4},{2,6},{4,0},{6,2},{1,5},{3,7},{5,1},{7,3},{8,12},{10,14},{12... | collective-permute-start | bytes 98312 | tf_op jit(solution)/shard_map/ppermute | solution.py:16
  30.4 5.7 %collective-permute-start.6 = (f32[64,128]{1,0:T(8,128)S(1)}, f32[64,128]{1,0:T(8,128)S(1)}, u32[]{:S(2)}, u32[]{:S(2)}) collective-permute-start(f32[64,128]{1,0:T(8,128)S(1)} %get-tuple-element.40), channel_id=1, source_target_pairs={{0,2},{2,4},{4,6},{6,0},{1,3},{3,5},{5,7},{7,1},{8,10},{10,12},{12... | collective-permute-start | bytes 98312 | tf_op jit(solution)/shard_map/ppermute | solution.py:16
  31.0 8.9 %collective-permute-start.11 = (f32[256,128]{1,0:T(8,128)S(1)}, f32[256,128]{1,0:T(8,128)S(1)}, u32[]{:S(2)}, u32[]{:S(2)}) collective-permute-start(f32[256,128]{1,0:T(8,128)S(1)} %dynamic-slice_bitcast_fusion.1), channel_id=1, source_target_pairs={{0,1},{1,0},{2,3},{3,2},{4,5},{5,4},{6,7},{7,6},{8,9},{9,8},{10,11... | collective-permute-start | bytes 393224 | tf_op jit(solution)/shard_map/ppermute | solution.py:16
  36.2 5.7 %collective-permute-start.16 = (f32[4,64,128]{2,1,0:T(8,128)S(1)}, f32[4,64,128]{2,1,0:T(8,128)S(1)}, u32[]{:S(2)}, u32[]{:S(2)}) collective-permute-start(f32[4,64,128]{2,1,0:T(8,128)S(1)} %pad_maximum_fusion.3), channel_id=1, source_target_pairs={{0,24},{8,0},{16,8},{24,16},{1,25},{9,1},{17,9},{25,17},{2,26},{10... | collective-permute-start | bytes 393224 | tf_op jit(solution)/shard_map/ppermute | solution.py:16
  38.7 7.1 %collective-permute-start.15 = (f32[4,64,128]{2,1,0:T(8,128)S(1)}, f32[4,64,128]{2,1,0:T(8,128)S(1)}, u32[]{:S(2)}, u32[]{:S(2)}) collective-permute-start(f32[4,64,128]{2,1,0:T(8,128)S(1)} %pad_maximum_fusion.3), channel_id=1, source_target_pairs={{0,16},{8,24},{16,0},{24,8},{1,17},{9,25},{17,1},{25,9},{2,18},{10... | collective-permute-start | bytes 393224 | tf_op jit(solution)/shard_map/ppermute | solution.py:16
  39.2 6.6 %collective-permute-start.14 = (f32[4,64,128]{2,1,0:T(8,128)S(1)}, f32[4,64,128]{2,1,0:T(8,128)S(1)}, u32[]{:S(2)}, u32[]{:S(2)}) collective-permute-start(f32[4,64,128]{2,1,0:T(8,128)S(1)} %pad_maximum_fusion.3), channel_id=1, source_target_pairs={{0,8},{8,16},{16,24},{24,0},{1,9},{9,17},{17,25},{25,1},{2,10},{10... | collective-permute-start | bytes 393224 | tf_op jit(solution)/shard_map/ppermute | solution.py:16
  39.8 6.7 %collective-permute-start.10 = (f32[256,128]{1,0:T(8,128)S(1)}, f32[256,128]{1,0:T(8,128)S(1)}, u32[]{:S(2)}, u32[]{:S(2)}) collective-permute-start(f32[256,128]{1,0:T(8,128)S(1)} %dynamic-slice_bitcast_fusion.2), channel_id=1, source_target_pairs={{0,1},{1,0},{2,3},{3,2},{4,5},{5,4},{6,7},{7,6},{8,9},{9,8},{10,11... | collective-permute-start | bytes 393224 | tf_op jit(solution)/shard_map/ppermute | solution.py:16
  47.7 5.9 %collective-permute-start.17 = (f32[2,40,128]{2,1,0:T(8,128)S(1)}, f32[2,40,128]{2,1,0:T(8,128)S(1)}, u32[]{:S(2)}, u32[]{:S(2)}) collective-permute-start(f32[2,40,128]{2,1,0:T(8,128)S(1)} %get-tuple-element.42), channel_id=1, source_target_pairs={{0,2},{2,4},{4,6},{6,0},{1,3},{3,5},{5,7},{7,1},{8,10},{10,12},{12... | collective-permute-start | bytes 122888 | tf_op jit(solution)/shard_map/ppermute | solution.py:16
  47.8 5.8 %collective-permute-start.18 = (f32[2,40,128]{2,1,0:T(8,128)S(1)}, f32[2,40,128]{2,1,0:T(8,128)S(1)}, u32[]{:S(2)}, u32[]{:S(2)}) collective-permute-start(f32[2,40,128]{2,1,0:T(8,128)S(1)} %get-tuple-element.43), channel_id=1, source_target_pairs={{0,4},{2,6},{4,0},{6,2},{1,5},{3,7},{5,1},{7,3},{8,12},{10,14},{12... | collective-permute-start | bytes 122888 | tf_op jit(solution)/shard_map/ppermute | solution.py:16
  48.2 6.0 %collective-permute-start.19 = (f32[2,40,128]{2,1,0:T(8,128)S(1)}, f32[2,40,128]{2,1,0:T(8,128)S(1)}, u32[]{:S(2)}, u32[]{:S(2)}) collective-permute-start(f32[2,40,128]{2,1,0:T(8,128)S(1)} %get-tuple-element.44), channel_id=1, source_target_pairs={{0,6},{2,0},{4,2},{6,4},{1,7},{3,1},{5,3},{7,5},{8,14},{10,8},{12,... | collective-permute-start | bytes 122888 | tf_op jit(solution)/shard_map/ppermute | solution.py:16
  54.8 1.3 %collective-permute-start.20 = (f32[40,512]{1,0:T(8,128)S(1)}, f32[40,512]{1,0:T(8,128)S(1)}, u32[]{:S(2)}, u32[]{:S(2)}) collective-permute-start(f32[40,512]{1,0:T(8,128)S(1)} %dynamic-slice_bitcast_fusion.4), channel_id=1, source_target_pairs={{0,1},{1,0},{2,3},{3,2},{4,5},{5,4},{6,7},{7,6},{8,9},{9,8},{10,11... | collective-permute-start | bytes 245768 | tf_op jit(solution)/shard_map/ppermute | solution.py:16
  56.3 3.9 %collective-permute-start.23 = (f32[2,512]{1,0:T(2,128)S(1)}, f32[2,512]{1,0:T(2,128)S(1)}, u32[]{:S(2)}, u32[]{:S(2)}) collective-permute-start(f32[2,512]{1,0:T(2,128)S(1)} %fusion.25), channel_id=1, source_target_pairs={{0,24},{8,0},{16,8},{24,16},{1,25},{9,1},{17,9},{25,17},{2,26},{10... | collective-permute-start | bytes 12296 | tf_op jit(solution)/shard_map/ppermute | solution.py:16
  56.5 3.7 %collective-permute-start.22 = (f32[2,512]{1,0:T(2,128)S(1)}, f32[2,512]{1,0:T(2,128)S(1)}, u32[]{:S(2)}, u32[]{:S(2)}) collective-permute-start(f32[2,512]{1,0:T(2,128)S(1)} %fusion.25), channel_id=1, source_target_pairs={{0,16},{8,24},{16,0},{24,8},{1,17},{9,25},{17,1},{25,9},{2,18},{10... | collective-permute-start | bytes 12296 | tf_op jit(solution)/shard_map/ppermute | solution.py:16
  57.8 4.5 %collective-permute-start.21 = (f32[2,512]{1,0:T(2,128)S(1)}, f32[2,512]{1,0:T(2,128)S(1)}, u32[]{:S(2)}, u32[]{:S(2)}) collective-permute-start(f32[2,512]{1,0:T(2,128)S(1)} %fusion.25), channel_id=1, source_target_pairs={{0,8},{8,16},{16,24},{24,0},{1,9},{9,17},{17,25},{25,1},{2,10},{10... | collective-permute-start | bytes 12296 | tf_op jit(solution)/shard_map/ppermute | solution.py:16

commit v6 on v5

--- a/solution.py
+++ b/solution.py
@@ -37,13 +37,9 @@
             mine = of(array, core)
             return jnp.stack([jnp.where(core == 0, mine, other), jnp.where(core == 0, other, mine)])
 
-        def after(array, far, shift):
-            if shift < deep:
-                array, got = lax.optimization_barrier((array, far[shift - 1]))
-                far = far[: shift - 1] + [got] + far[shift:]
-            return array, far
-
-        far = [shifted(ancestor, "z", deep, d) for d in range(1, deep)]
+        early = [d for d in range(1, deep) if deep < 4 * d < 3 * deep]
+        late = [d for d in range(1, deep) if d not in early]
+        far = {d: shifted(ancestor, "z", deep, d) for d in early}
 
         mine = lax.dynamic_slice_in_dim(panel, row * depth, depth, axis=2)
         partial = jnp.einsum("srw,swv->srv", mine, factor_inv, precision=highest)
@@ -54,8 +50,7 @@
         scaled = rows_of(row)
         for shift in range(1, rows):
             scaled = scaled + shifted(rows_of((row + shift) % rows), "row", rows, shift)
-        scaled, far = after(scaled, far, 2)
-        scaled = swapped(scaled)
+        scaled, far = lax.optimization_barrier((swapped(scaled), far))
 
         def columns_of(array, c):
             return lax.dynamic_slice_in_dim(array, c * part, part, axis=1)
@@ -64,7 +59,8 @@
         slots = [columns_of(scaled, z)]
         for shift in range(1, deep):
             slots.append(shifted(columns_of(scaled, (z + shift) % deep), "z", deep, shift))
-        slots, far = after(jnp.stack(slots), far, 1)
+        slots, held_back = lax.optimization_barrier((jnp.stack(slots), ancestor))
+        far |= {d: shifted(held_back, "z", deep, d) for d in late}
         slots = jnp.stack(gathered(slots, "row", rows))
         slots = slots.reshape(rows, deep, cores, piece, part)
 
@@ -76,7 +72,7 @@
         from_z = (z - jnp.take(stored, tiles, mode="clip")) % deep
         spread = slots[quarters[None, :], from_z[:, None]]
         spread = spread.transpose(0, 2, 1, 3, 4).reshape(deep, cores, chunk, part)
-        wide = jnp.stack([swapped(a) for a in [ancestor] + far])
+        wide = jnp.stack([swapped(a) for a in [held_back] + [far[d] for d in range(1, deep)]])
         product = jnp.einsum("tcij,tcjk->ik", wide, spread, precision=highest)
         spread = spread.reshape(deep, B, part)
 

time: 63.1 us -> 63.3 us (level)
  waiting for transfers between devices: 20 us -> 26.9 us
  starting transfers between devices: 33.3 us -> 26.7 us
    ppermute x24, waiting for transfers between devices: 20 us -> 26.9 us  [shifted(): lax.ppermute(array, axis, [(i, (i + shift) % size) for i in range(size)])]
    ppermute x24, starting transfers between devices: 33.3 us -> 26.7 us  [shifted(): lax.ppermute(array, axis, [(i, (i + shift) % size) for i in range(size)])]
  transfers between devices with their start and end apart: 24 -> 24, of which waited for: 13 -> 16; matrix products, arithmetic and copies ran while one was open for 9% -> 8% of each run, Pallas kernels for 0% -> 0%
where the time goes in v6:
time: 63.3 us; the launch traced here: 63.1 us
  waiting for transfers between devices  26.9 us (42%)
  starting transfers between devices  26.7 us (42%)
  local copies, waits for them, and re-layouts  3.63 us (6%)
  matrix products  2.63 us (4%)
  other arithmetic  2.29 us (4%)
  between operations  1 us (2%)
    ppermute x24, waiting for transfers between devices, shifted(): lax.ppermute(array, axis, [(i, (i + shift) % size) for i in range(size)])  26.9 us
    ppermute x24, starting transfers between devices, shifted(): lax.ppermute(array, axis, [(i, (i + shift) % size) for i in range(size)])  26.7 us
    dot_general x1, matrix products, per_device(): partial = jnp.einsum('srw,swv->srv', mine, factor_inv, precision=highest)  1.61 us
    unnamed x7, local copies, waits for them, and re-layouts  1.37 us
  transfers between devices with their start and end apart: 24, of which 16 were waited for; matrix products, arithmetic and copies ran while one was open for 8% of the time, Pallas kernels for 0%

profile of v6, /device:TPU:0, one launch (start us, length us, event | category | flops | bytes accessed | tf_op | source)
XLA Modules:
  0.0 63.1 jit_solution(1640086838305011600)
XLA Ops:
  0.6 4.1 %collective-permute-start.4 = (f32[2,256,128]{2,1,0:T(8,128)}, f32[2,256,128]{2,1,0:T(8,128)S(1)}, u32[]{:S(2)}, u32[]{:S(2)}) collective-permute-start(f32[2,256,128]{2,1,0:T(8,128)} %param.4), channel_id=1, source_target_pairs={{0,4},{2,6},{4,0},{6,2},{1,5},{3,7},{5,1},{7,3},{8,12},{10,14},{12... | collective-permute-start | bytes 786440 | tf_op jit(solution)/shard_map/ppermute | solution.py:16
  4.7 1.6 %fusion.18 = f32[2,128,512]{2,1,0:T(8,128)S(1)} fusion(f32[2,128,512]{2,1,0:T(8,128)} %param.6, f32[2,128,512]{2,1,0:T(8,128)S(1)} %copy-done, s32[]{:T(128)S(6)} %select_n.220), kind=kOutput, calls=%fused_computation.47 | convolution fusion | flops 201326592 | bytes 1179652 | tf_op jit(solution)/shard_map/srw,swv->srv/dot_general | solution.py:45
  6.4 1.6 %collective-permute-start = (f32[2,32,512]{2,1,0:T(8,128)S(1)}, f32[2,32,512]{2,1,0:T(8,128)S(1)}, u32[]{:S(2)}, u32[]{:S(2)}) collective-permute-start(f32[2,32,512]{2,1,0:T(8,128)S(1)} %get-tuple-element.18), channel_id=1, source_target_pairs={{0,8},{8,16},{16,24},{24,0},{1,9},{9,17},{17,25},{25,1},{2,10},{10... | collective-permute-start | bytes 393224 | tf_op jit(solution)/shard_map/ppermute | solution.py:16
  8.0 1.4 %collective-permute-start.2 = (f32[2,32,512]{2,1,0:T(8,128)S(1)}, f32[2,32,512]{2,1,0:T(8,128)S(1)}, u32[]{:S(2)}, u32[]{:S(2)}) collective-permute-start(f32[2,32,512]{2,1,0:T(8,128)S(1)} %get-tuple-element.19), channel_id=1, source_target_pairs={{0,24},{8,0},{16,8},{24,16},{1,25},{9,1},{17,9},{25,17},{2,26},{10... | collective-permute-start | bytes 393224 | tf_op jit(solution)/shard_map/ppermute | solution.py:16
  9.4 1.5 %collective-permute-start.1 = (f32[2,32,512]{2,1,0:T(8,128)S(1)}, f32[2,32,512]{2,1,0:T(8,128)S(1)}, u32[]{:S(2)}, u32[]{:S(2)}) collective-permute-start(f32[2,32,512]{2,1,0:T(8,128)S(1)} %get-tuple-element.20), channel_id=1, source_target_pairs={{0,16},{8,24},{16,0},{24,8},{1,17},{9,25},{17,1},{25,9},{2,18},{10... | collective-permute-start | bytes 393224 | tf_op jit(solution)/shard_map/ppermute | solution.py:16
  10.9 0.7 %copy-done.2 = s32[2,4]{1,0:T(2,128)S(1)} copy-done((s32[2,4]{1,0:T(2,128)S(1)}, s32[2,4]{1,0:T(2,128)}, u32[]{:S(2)}) %copy-start.2) | copy-done | bytes 56
  11.6 0.1 select_reduce_fusion
  11.7 0.6 %gather_fusion = s32[4]{0:T(128)S(1)} fusion(s32[4]{0:T(128)S(1)} %select_reduce_fusion, s32[1024]{0:T(1024)S(1)} %pad_clamp_fusion), kind=kCustom, calls=%fused_computation | custom fusion | bytes 48 | tf_op jit(solution)/shard_map/jit(_take)/gather | solution.py:72
  12.4 1.5 %collective-permute-done = f32[2,32,512]{2,1,0:T(8,128)S(1)} collective-permute-done((f32[2,32,512]{2,1,0:T(8,128)S(1)}, f32[2,32,512]{2,1,0:T(8,128)S(1)}, u32[]{:S(2)}, u32[]{:S(2)}) %collective-permute-start) | collective-permute-done | bytes 131104 | tf_op jit(solution)/shard_map/ppermute | solution.py:16
  13.8 1.4 %collective-permute-done.2 = f32[2,32,512]{2,1,0:T(8,128)S(1)} collective-permute-done((f32[2,32,512]{2,1,0:T(8,128)S(1)}, f32[2,32,512]{2,1,0:T(8,128)S(1)}, u32[]{:S(2)}, u32[]{:S(2)}) %collective-permute-start.2) | collective-permute-done | bytes 131104 | tf_op jit(solution)/shard_map/ppermute | solution.py:16
  15.3 0.1 collective-permute-start.3
  15.3 0.1 broadcast_or_fusion
  15.4 0.1 reshape.124
  15.5 1.0 %multiply_reduce_fusion = f32[128]{0:T(128)S(1)} fusion(f32[2,128,512]{2,1,0:T(8,128)} %param.6, s32[]{:T(128)S(6)} %select_n.256, s32[]{:T(128)S(6)} %select_n.257), kind=kLoop, calls=%fused_computation.61 | loop fusion | flops 32640 | bytes 66056 | tf_op jit(solution)/shard_map/reduce_sum | solution.py:81
  16.6 0.3 collective-permute-done.4
  16.9 3.6 %collective-permute-start.7 = (f32[64,128]{1,0:T(8,128)S(1)}, f32[64,128]{1,0:T(8,128)S(1)}, u32[]{:S(2)}, u32[]{:S(2)}) collective-permute-start(f32[64,128]{1,0:T(8,128)S(1)} %get-tuple-element.38), channel_id=1, source_target_pairs={{0,6},{2,0},{4,2},{6,4},{1,7},{3,1},{5,3},{7,5},{8,14},{10,8},{12,... | collective-permute-start | bytes 98312 | tf_op jit(solution)/shard_map/ppermute | solution.py:16
  20.5 0.6 %collective-permute-start.5 = (f32[64,128]{1,0:T(8,128)S(1)}, f32[64,128]{1,0:T(8,128)S(1)}, u32[]{:S(2)}, u32[]{:S(2)}) collective-permute-start(f32[64,128]{1,0:T(8,128)S(1)} %get-tuple-element.40), channel_id=1, source_target_pairs={{0,2},{2,4},{4,6},{6,0},{1,3},{3,5},{5,7},{7,1},{8,10},{10,12},{12... | collective-permute-start | bytes 98312 | tf_op jit(solution)/shard_map/ppermute | solution.py:16
  21.2 0.9 %collective-permute-done.7 = f32[64,128]{1,0:T(8,128)S(1)} collective-permute-done((f32[64,128]{1,0:T(8,128)S(1)}, f32[64,128]{1,0:T(8,128)S(1)}, u32[]{:S(2)}, u32[]{:S(2)}) %collective-permute-start.7) | collective-permute-done | bytes 32800 | tf_op jit(solution)/shard_map/ppermute | solution.py:16
  22.1 3.2 %collective-permute-done.6 = f32[64,128]{1,0:T(8,128)S(1)} collective-permute-done((f32[64,128]{1,0:T(8,128)S(1)}, f32[64,128]{1,0:T(8,128)S(1)}, u32[]{:S(2)}, u32[]{:S(2)}) %collective-permute-start.6) | collective-permute-done | bytes 32800 | tf_op jit(solution)/shard_map/ppermute | solution.py:16
  25.3 0.9 %collective-permute-done.5 = f32[64,128]{1,0:T(8,128)S(1)} collective-permute-done((f32[64,128]{1,0:T(8,128)S(1)}, f32[64,128]{1,0:T(8,128)S(1)}, u32[]{:S(2)}, u32[]{:S(2)}) %collective-permute-start.5) | collective-permute-done | bytes 32800 | tf_op jit(solution)/shard_map/ppermute | solution.py:16
  26.2 2.5 %collective-permute-start.16 = (f32[4,64,128]{2,1,0:T(8,128)S(1)}, f32[4,64,128]{2,1,0:T(8,128)S(1)}, u32[]{:S(2)}, u32[]{:S(2)}) collective-permute-start(f32[4,64,128]{2,1,0:T(8,128)S(1)} %pad_maximum_fusion.3), channel_id=1, source_target_pairs={{0,24},{8,0},{16,8},{24,16},{1,25},{9,1},{17,9},{25,17},{2,26},{10... | collective-permute-start | bytes 393224 | tf_op jit(solution)/shard_map/ppermute | solution.py:16
  28.7 0.5 collective-permute-start.15
  29.2 0.6 collective-permute-start.14
  29.8 0.6 collective-permute-start.12
  30.4 0.1 collective-permute-start.8
  30.5 1.3 %collective-permute-done.8 = f32[256,128]{1,0:T(8,128)S(1)} collective-permute-done((f32[256,128]{1,0:T(8,128)S(1)}, f32[256,128]{1,0:T(8,128)S(1)}, u32[]{:S(2)}, u32[]{:S(2)}) %collective-permute-start.8) | collective-permute-done | bytes 131104 | tf_op jit(solution)/shard_map/ppermute | solution.py:16
  31.8 1.5 %collective-permute-start.9 = (f32[2,256,128]{2,1,0:T(8,128)S(1)}, f32[2,256,128]{2,1,0:T(8,128)S(1)}, u32[]{:S(2)}, u32[]{:S(2)}) collective-permute-start(f32[2,256,128]{2,1,0:T(8,128)S(1)} %copy-done.1), channel_id=1, source_target_pairs={{0,2},{2,4},{4,6},{6,0},{1,3},{3,5},{5,7},{7,1},{8,10},{10,12},{12... | collective-permute-start | bytes 786440 | tf_op jit(solution)/shard_map/ppermute | solution.py:16
  33.3 2.9 %collective-permute-done.12 = f32[2,256,128]{2,1,0:T(8,128)S(1)} collective-permute-done((f32[2,256,128]{2,1,0:T(8,128)S(1)}, f32[2,256,128]{2,1,0:T(8,128)S(1)}, u32[]{:S(2)}, u32[]{:S(2)}) %collective-permute-start.12) | collective-permute-done | bytes 262176 | tf_op jit(solution)/shard_map/ppermute | solution.py:16
  36.2 0.1 collective-permute-start.13
  36.4 0.6 gather_fusion.1
  37.1 5.3 %collective-permute-done.9 = f32[2,256,128]{2,1,0:T(8,128)S(1)} collective-permute-done((f32[2,256,128]{2,1,0:T(8,128)S(1)}, f32[2,256,128]{2,1,0:T(8,128)S(1)}, u32[]{:S(2)}, u32[]{:S(2)}) %collective-permute-start.9) | collective-permute-done | bytes 262176 | tf_op jit(solution)/shard_map/ppermute | solution.py:16
  42.6 1.2 %collective-permute-done.10 = f32[256,128]{1,0:T(8,128)S(1)} collective-permute-done((f32[256,128]{1,0:T(8,128)S(1)}, f32[256,128]{1,0:T(8,128)S(1)}, u32[]{:S(2)}, u32[]{:S(2)}) %collective-permute-start.10) | collective-permute-done | bytes 131104 | tf_op jit(solution)/shard_map/ppermute | solution.py:16
  43.9 1.0 %fusion.9 = (f32[128]{0:T(128)S(1)}, f32[256,128]{1,0:T(8,128)S(1)}) fusion(f32[4,256,128]{2,1,0:T(8,128)S(1)} %bitcast.138, s32[]{:T(128)S(6)} %select_n.255, f32[4,2,128,128]{3,2,0,1:T(8,128)S(1)} %bitcast.139, f32[1,2,256,128]{3,2,0,1:T(8,128)S(1)} %get-tuple-element.52, f32[1,2,256,128]{3,2,0,1:T(8,128)S(1)} %get-tuple-element.51, ...), kind=kOutput, calls=%fused_computation.25 | convolution fusion | flops 403505024 | bytes 1835524 | tf_op jit(solution)/shard_map/tcij,tcjk->ik/dot_general | solution.py:76
  45.0 2.4 %collective-permute-start.18 = (f32[2,40,128]{2,1,0:T(8,128)S(1)}, f32[2,40,128]{2,1,0:T(8,128)S(1)}, u32[]{:S(2)}, u32[]{:S(2)}) collective-permute-start(f32[2,40,128]{2,1,0:T(8,128)S(1)} %get-tuple-element.43), channel_id=1, source_target_pairs={{0,4},{2,6},{4,0},{6,2},{1,5},{3,7},{5,1},{7,3},{8,12},{10,14},{12... | collective-permute-start | bytes 122888 | tf_op jit(solution)/shard_map/ppermute | solution.py:16
  47.4 1.5 %collective-permute-start.19 = (f32[2,40,128]{2,1,0:T(8,128)S(1)}, f32[2,40,128]{2,1,0:T(8,128)S(1)}, u32[]{:S(2)}, u32[]{:S(2)}) collective-permute-start(f32[2,40,128]{2,1,0:T(8,128)S(1)} %get-tuple-element.44), channel_id=1, source_target_pairs={{0,6},{2,0},{4,2},{6,4},{1,7},{3,1},{5,3},{7,5},{8,14},{10,8},{12,... | collective-permute-start | bytes 122888 | tf_op jit(solution)/shard_map/ppermute | solution.py:16
  48.8 2.4 %collective-permute-done.17 = f32[2,40,128]{2,1,0:T(8,128)S(1)} collective-permute-done((f32[2,40,128]{2,1,0:T(8,128)S(1)}, f32[2,40,128]{2,1,0:T(8,128)S(1)}, u32[]{:S(2)}, u32[]{:S(2)}) %collective-permute-start.17) | collective-permute-done | bytes 40992 | tf_op jit(solution)/shard_map/ppermute | solution.py:16
  51.2 0.7 %collective-permute-done.18 = f32[2,40,128]{2,1,0:T(8,128)S(1)} collective-permute-done((f32[2,40,128]{2,1,0:T(8,128)S(1)}, f32[2,40,128]{2,1,0:T(8,128)S(1)}, u32[]{:S(2)}, u32[]{:S(2)}) %collective-permute-start.18) | collective-permute-done | bytes 40992 | tf_op jit(solution)/shard_map/ppermute | solution.py:16
  52.0 0.6 gather_fusion.2
  52.6 0.1 collective-permute-start.20
  52.6 1.3 %collective-permute-done.20 = f32[40,512]{1,0:T(8,128)S(1)} collective-permute-done((f32[40,512]{1,0:T(8,128)S(1)}, f32[40,512]{1,0:T(8,128)S(1)}, u32[]{:S(2)}, u32[]{:S(2)}) %collective-permute-start.20) | collective-permute-done | bytes 81952 | tf_op jit(solution)/shard_map/ppermute | solution.py:16
  54.0 0.1 copy.33
  54.1 2.4 %collective-permute-start.23 = (f32[2,512]{1,0:T(2,128)S(1)}, f32[2,512]{1,0:T(2,128)S(1)}, u32[]{:S(2)}, u32[]{:S(2)}) collective-permute-start(f32[2,512]{1,0:T(2,128)S(1)} %fusion.25), channel_id=1, source_target_pairs={{0,24},{8,0},{16,8},{24,16},{1,25},{9,1},{17,9},{25,17},{2,26},{10... | collective-permute-start | bytes 12296 | tf_op jit(solution)/shard_map/ppermute | solution.py:16
  56.5 1.5 %collective-permute-start.22 = (f32[2,512]{1,0:T(2,128)S(1)}, f32[2,512]{1,0:T(2,128)S(1)}, u32[]{:S(2)}, u32[]{:S(2)}) collective-permute-start(f32[2,512]{1,0:T(2,128)S(1)} %fusion.25), channel_id=1, source_target_pairs={{0,16},{8,24},{16,0},{24,8},{1,17},{9,25},{17,1},{25,9},{2,18},{10... | collective-permute-start | bytes 12296 | tf_op jit(solution)/shard_map/ppermute | solution.py:16
  58.0 0.1 fusion.8
  58.2 0.7 %copy.34 = f32[2,32,512]{2,1,0:T(8,128)} copy(f32[2,32,512]{2,0,1:T(2,128)S(1)} %fusion.8) | data formatting | bytes 262144
  58.8 1.3 %collective-permute-done.22 = f32[2,512]{1,0:T(2,128)S(1)} collective-permute-done((f32[2,512]{1,0:T(2,128)S(1)}, f32[2,512]{1,0:T(2,128)S(1)}, u32[]{:S(2)}, u32[]{:S(2)}) %collective-permute-start.22) | collective-permute-done | bytes 4128 | tf_op jit(solution)/shard_map/ppermute | solution.py:16
  60.1 2.4 %collective-permute-done.21 = f32[2,512]{1,0:T(2,128)S(1)} collective-permute-done((f32[2,512]{1,0:T(2,128)S(1)}, f32[2,512]{1,0:T(2,128)S(1)}, u32[]{:S(2)}, u32[]{:S(2)}) %collective-permute-start.21) | collective-permute-done | bytes 4128 | tf_op jit(solution)/shard_map/ppermute | solution.py:16
  62.5 0.6 add_add_fusion.1
  (53 shorter events, 1.0 us)
Async XLA Ops:
  0.6 4.1 %copy-start = (f32[2,128,512]{2,1,0:T(8,128)S(1)}, f32[2,128,512]{2,1,0:T(8,128)}, u32[]{:S(2)}) copy-start(f32[2,128,512]{2,1,0:T(8,128)} %param.5) | copy-start | bytes 1572868
  0.6 16.2 %collective-permute-start.4 = (f32[2,256,128]{2,1,0:T(8,128)}, f32[2,256,128]{2,1,0:T(8,128)S(1)}, u32[]{:S(2)}, u32[]{:S(2)}) collective-permute-start(f32[2,256,128]{2,1,0:T(8,128)} %param.4), channel_id=1, source_target_pairs={{0,4},{2,6},{4,0},{6,2},{1,5},{3,7},{5,1},{7,3},{8,12},{10,14},{12... | collective-permute-start | bytes 786440 | tf_op jit(solution)/shard_map/ppermute | solution.py:16
  6.4 7.4 %collective-permute-start = (f32[2,32,512]{2,1,0:T(8,128)S(1)}, f32[2,32,512]{2,1,0:T(8,128)S(1)}, u32[]{:S(2)}, u32[]{:S(2)}) collective-permute-start(f32[2,32,512]{2,1,0:T(8,128)S(1)} %get-tuple-element.18), channel_id=1, source_target_pairs={{0,8},{8,16},{16,24},{24,0},{1,9},{9,17},{17,25},{25,1},{2,10},{10... | collective-permute-start | bytes 393224 | tf_op jit(solution)/shard_map/ppermute | solution.py:16
  8.0 7.2 %collective-permute-start.2 = (f32[2,32,512]{2,1,0:T(8,128)S(1)}, f32[2,32,512]{2,1,0:T(8,128)S(1)}, u32[]{:S(2)}, u32[]{:S(2)}) collective-permute-start(f32[2,32,512]{2,1,0:T(8,128)S(1)} %get-tuple-element.19), channel_id=1, source_target_pairs={{0,24},{8,0},{16,8},{24,16},{1,25},{9,1},{17,9},{25,17},{2,26},{10... | collective-permute-start | bytes 393224 | tf_op jit(solution)/shard_map/ppermute | solution.py:16
  9.4 5.8 %collective-permute-start.1 = (f32[2,32,512]{2,1,0:T(8,128)S(1)}, f32[2,32,512]{2,1,0:T(8,128)S(1)}, u32[]{:S(2)}, u32[]{:S(2)}) collective-permute-start(f32[2,32,512]{2,1,0:T(8,128)S(1)} %get-tuple-element.20), channel_id=1, source_target_pairs={{0,16},{8,24},{16,0},{24,8},{1,17},{9,25},{17,1},{25,9},{2,18},{10... | collective-permute-start | bytes 393224 | tf_op jit(solution)/shard_map/ppermute | solution.py:16
  10.9 0.7 %copy-start.2 = (s32[2,4]{1,0:T(2,128)S(1)}, s32[2,4]{1,0:T(2,128)}, u32[]{:S(2)}) copy-start(s32[2,4]{1,0:T(2,128)} %param.7) | copy-start | bytes 100
  15.3 1.3 %collective-permute-start.3 = (f32[32,512]{1,0:T(8,128)S(1)}, f32[32,512]{1,0:T(8,128)S(1)}, u32[]{:S(2)}, u32[]{:S(2)}) collective-permute-start(f32[32,512]{1,0:T(8,128)S(1)} %dynamic-slice_bitcast_fusion.5), channel_id=1, source_target_pairs={{0,1},{1,0},{2,3},{3,2},{4,5},{5,4},{6,7},{7,6},{8,9},{9,8},{10,11... | collective-permute-start | bytes 196616 | tf_op jit(solution)/shard_map/ppermute | solution.py:16
  16.9 5.2 %collective-permute-start.7 = (f32[64,128]{1,0:T(8,128)S(1)}, f32[64,128]{1,0:T(8,128)S(1)}, u32[]{:S(2)}, u32[]{:S(2)}) collective-permute-start(f32[64,128]{1,0:T(8,128)S(1)} %get-tuple-element.38), channel_id=1, source_target_pairs={{0,6},{2,0},{4,2},{6,4},{1,7},{3,1},{5,3},{7,5},{8,14},{10,8},{12,... | collective-permute-start | bytes 98312 | tf_op jit(solution)/shard_map/ppermute | solution.py:16
  20.5 4.8 %collective-permute-start.6 = (f32[64,128]{1,0:T(8,128)S(1)}, f32[64,128]{1,0:T(8,128)S(1)}, u32[]{:S(2)}, u32[]{:S(2)}) collective-permute-start(f32[64,128]{1,0:T(8,128)S(1)} %get-tuple-element.39), channel_id=1, source_target_pairs={{0,4},{2,6},{4,0},{6,2},{1,5},{3,7},{5,1},{7,3},{8,12},{10,14},{12... | collective-permute-start | bytes 98312 | tf_op jit(solution)/shard_map/ppermute | solution.py:16
  20.5 9.3 %copy-start.1 = (f32[2,256,128]{2,1,0:T(8,128)S(1)}, f32[2,256,128]{2,1,0:T(8,128)}, u32[]{:S(2)}) copy-start(f32[2,256,128]{2,1,0:T(8,128)} %param.4) | copy-start | bytes 786436
  20.5 5.7 %collective-permute-start.5 = (f32[64,128]{1,0:T(8,128)S(1)}, f32[64,128]{1,0:T(8,128)S(1)}, u32[]{:S(2)}, u32[]{:S(2)}) collective-permute-start(f32[64,128]{1,0:T(8,128)S(1)} %get-tuple-element.40), channel_id=1, source_target_pairs={{0,2},{2,4},{4,6},{6,0},{1,3},{3,5},{5,7},{7,1},{8,10},{10,12},{12... | collective-permute-start | bytes 98312 | tf_op jit(solution)/shard_map/ppermute | solution.py:16
  21.2 9.3 %collective-permute-start.11 = (f32[256,128]{1,0:T(8,128)S(1)}, f32[256,128]{1,0:T(8,128)S(1)}, u32[]{:S(2)}, u32[]{:S(2)}) collective-permute-start(f32[256,128]{1,0:T(8,128)S(1)} %dynamic-slice_bitcast_fusion.1), channel_id=1, source_target_pairs={{0,1},{1,0},{2,3},{3,2},{4,5},{5,4},{6,7},{7,6},{8,9},{9,8},{10,11... | collective-permute-start | bytes 393224 | tf_op jit(solution)/shard_map/ppermute | solution.py:16
  26.2 10.1 %collective-permute-start.16 = (f32[4,64,128]{2,1,0:T(8,128)S(1)}, f32[4,64,128]{2,1,0:T(8,128)S(1)}, u32[]{:S(2)}, u32[]{:S(2)}) collective-permute-start(f32[4,64,128]{2,1,0:T(8,128)S(1)} %pad_maximum_fusion.3), channel_id=1, source_target_pairs={{0,24},{8,0},{16,8},{24,16},{1,25},{9,1},{17,9},{25,17},{2,26},{10... | collective-permute-start | bytes 393224 | tf_op jit(solution)/shard_map/ppermute | solution.py:16
  28.7 7.6 %collective-permute-start.15 = (f32[4,64,128]{2,1,0:T(8,128)S(1)}, f32[4,64,128]{2,1,0:T(8,128)S(1)}, u32[]{:S(2)}, u32[]{:S(2)}) collective-permute-start(f32[4,64,128]{2,1,0:T(8,128)S(1)} %pad_maximum_fusion.3), channel_id=1, source_target_pairs={{0,16},{8,24},{16,0},{24,8},{1,17},{9,25},{17,1},{25,9},{2,18},{10... | collective-permute-start | bytes 393224 | tf_op jit(solution)/shard_map/ppermute | solution.py:16
  29.2 7.1 %collective-permute-start.14 = (f32[4,64,128]{2,1,0:T(8,128)S(1)}, f32[4,64,128]{2,1,0:T(8,128)S(1)}, u32[]{:S(2)}, u32[]{:S(2)}) collective-permute-start(f32[4,64,128]{2,1,0:T(8,128)S(1)} %pad_maximum_fusion.3), channel_id=1, source_target_pairs={{0,8},{8,16},{16,24},{24,0},{1,9},{9,17},{17,25},{25,1},{2,10},{10... | collective-permute-start | bytes 393224 | tf_op jit(solution)/shard_map/ppermute | solution.py:16
  29.8 6.4 %collective-permute-start.12 = (f32[2,256,128]{2,1,0:T(8,128)S(1)}, f32[2,256,128]{2,1,0:T(8,128)S(1)}, u32[]{:S(2)}, u32[]{:S(2)}) collective-permute-start(f32[2,256,128]{2,1,0:T(8,128)S(1)} %copy-done.1), channel_id=1, source_target_pairs={{0,6},{2,0},{4,2},{6,4},{1,7},{3,1},{5,3},{7,5},{8,14},{10,8},{12,... | collective-permute-start | bytes 786440 | tf_op jit(solution)/shard_map/ppermute | solution.py:16
  30.4 1.4 %collective-permute-start.8 = (f32[256,128]{1,0:T(8,128)S(1)}, f32[256,128]{1,0:T(8,128)S(1)}, u32[]{:S(2)}, u32[]{:S(2)}) collective-permute-start(f32[256,128]{1,0:T(8,128)S(1)} %dynamic-slice_bitcast_fusion.3), channel_id=1, source_target_pairs={{0,1},{1,0},{2,3},{3,2},{4,5},{5,4},{6,7},{7,6},{8,9},{9,8},{10,11... | collective-permute-start | bytes 393224 | tf_op jit(solution)/shard_map/ppermute | solution.py:16
  31.8 10.5 %collective-permute-start.9 = (f32[2,256,128]{2,1,0:T(8,128)S(1)}, f32[2,256,128]{2,1,0:T(8,128)S(1)}, u32[]{:S(2)}, u32[]{:S(2)}) collective-permute-start(f32[2,256,128]{2,1,0:T(8,128)S(1)} %copy-done.1), channel_id=1, source_target_pairs={{0,2},{2,4},{4,6},{6,0},{1,3},{3,5},{5,7},{7,1},{8,10},{10,12},{12... | collective-permute-start | bytes 786440 | tf_op jit(solution)/shard_map/ppermute | solution.py:16
  36.2 6.3 %collective-permute-start.13 = (f32[256,128]{1,0:T(8,128)S(1)}, f32[256,128]{1,0:T(8,128)S(1)}, u32[]{:S(2)}, u32[]{:S(2)}) collective-permute-start(f32[256,128]{1,0:T(8,128)S(1)} %dynamic-slice_bitcast_fusion), channel_id=1, source_target_pairs={{0,1},{1,0},{2,3},{3,2},{4,5},{5,4},{6,7},{7,6},{8,9},{9,8},{10,11... | collective-permute-start | bytes 393224 | tf_op jit(solution)/shard_map/ppermute | solution.py:16
  42.4 1.4 %collective-permute-start.10 = (f32[256,128]{1,0:T(8,128)S(1)}, f32[256,128]{1,0:T(8,128)S(1)}, u32[]{:S(2)}, u32[]{:S(2)}) collective-permute-start(f32[256,128]{1,0:T(8,128)S(1)} %dynamic-slice_bitcast_fusion.2), channel_id=1, source_target_pairs={{0,1},{1,0},{2,3},{3,2},{4,5},{5,4},{6,7},{7,6},{8,9},{9,8},{10,11... | collective-permute-start | bytes 393224 | tf_op jit(solution)/shard_map/ppermute | solution.py:16
  45.0 6.3 %collective-permute-start.17 = (f32[2,40,128]{2,1,0:T(8,128)S(1)}, f32[2,40,128]{2,1,0:T(8,128)S(1)}, u32[]{:S(2)}, u32[]{:S(2)}) collective-permute-start(f32[2,40,128]{2,1,0:T(8,128)S(1)} %get-tuple-element.42), channel_id=1, source_target_pairs={{0,2},{2,4},{4,6},{6,0},{1,3},{3,5},{5,7},{7,1},{8,10},{10,12},{12... | collective-permute-start | bytes 122888 | tf_op jit(solution)/shard_map/ppermute | solution.py:16
  45.0 6.9 %collective-permute-start.18 = (f32[2,40,128]{2,1,0:T(8,128)S(1)}, f32[2,40,128]{2,1,0:T(8,128)S(1)}, u32[]{:S(2)}, u32[]{:S(2)}) collective-permute-start(f32[2,40,128]{2,1,0:T(8,128)S(1)} %get-tuple-element.43), channel_id=1, source_target_pairs={{0,4},{2,6},{4,0},{6,2},{1,5},{3,7},{5,1},{7,3},{8,12},{10,14},{12... | collective-permute-start | bytes 122888 | tf_op jit(solution)/shard_map/ppermute | solution.py:16
  47.4 4.6 %collective-permute-start.19 = (f32[2,40,128]{2,1,0:T(8,128)S(1)}, f32[2,40,128]{2,1,0:T(8,128)S(1)}, u32[]{:S(2)}, u32[]{:S(2)}) collective-permute-start(f32[2,40,128]{2,1,0:T(8,128)S(1)} %get-tuple-element.44), channel_id=1, source_target_pairs={{0,6},{2,0},{4,2},{6,4},{1,7},{3,1},{5,3},{7,5},{8,14},{10,8},{12,... | collective-permute-start | bytes 122888 | tf_op jit(solution)/shard_map/ppermute | solution.py:16
  52.6 1.3 %collective-permute-start.20 = (f32[40,512]{1,0:T(8,128)S(1)}, f32[40,512]{1,0:T(8,128)S(1)}, u32[]{:S(2)}, u32[]{:S(2)}) collective-permute-start(f32[40,512]{1,0:T(8,128)S(1)} %dynamic-slice_bitcast_fusion.4), channel_id=1, source_target_pairs={{0,1},{1,0},{2,3},{3,2},{4,5},{5,4},{6,7},{7,6},{8,9},{9,8},{10,11... | collective-permute-start | bytes 245768 | tf_op jit(solution)/shard_map/ppermute | solution.py:16
  54.1 4.7 %collective-permute-start.23 = (f32[2,512]{1,0:T(2,128)S(1)}, f32[2,512]{1,0:T(2,128)S(1)}, u32[]{:S(2)}, u32[]{:S(2)}) collective-permute-start(f32[2,512]{1,0:T(2,128)S(1)} %fusion.25), channel_id=1, source_target_pairs={{0,24},{8,0},{16,8},{24,16},{1,25},{9,1},{17,9},{25,17},{2,26},{10... | collective-permute-start | bytes 12296 | tf_op jit(solution)/shard_map/ppermute | solution.py:16
  56.5 3.6 %collective-permute-start.22 = (f32[2,512]{1,0:T(2,128)S(1)}, f32[2,512]{1,0:T(2,128)S(1)}, u32[]{:S(2)}, u32[]{:S(2)}) collective-permute-start(f32[2,512]{1,0:T(2,128)S(1)} %fusion.25), channel_id=1, source_target_pairs={{0,16},{8,24},{16,0},{24,8},{1,17},{9,25},{17,1},{25,9},{2,18},{10... | collective-permute-start | bytes 12296 | tf_op jit(solution)/shard_map/ppermute | solution.py:16
  58.0 4.5 %collective-permute-start.21 = (f32[2,512]{1,0:T(2,128)S(1)}, f32[2,512]{1,0:T(2,128)S(1)}, u32[]{:S(2)}, u32[]{:S(2)}) collective-permute-start(f32[2,512]{1,0:T(2,128)S(1)} %fusion.25), channel_id=1, source_target_pairs={{0,8},{8,16},{16,24},{24,0},{1,9},{9,17},{17,25},{25,1},{2,10},{10... | collective-permute-start | bytes 12296 | tf_op jit(solution)/shard_map/ppermute | solution.py:16

commit v7 on v6

v7 whole, which is shorter than its diff:
```python
import jax
import jax.numpy as jnp
from jax import lax
from jax.sharding import Mesh, PartitionSpec as P

B = 256


def solution(mesh):
    rows, cols = mesh.shape["row"], mesh.shape["col"]
    cores, deep = 2, cols // 2
    fine = Mesh(mesh.devices.reshape(rows, deep, cores), ("row", "z", "core"))
    highest = lax.Precision.HIGHEST

    def shifted(array, axis, size, shift):
        return lax.ppermute(array, axis, [(i, (i + shift) % size) for i in range(size)])

    def gathered(array, axis, size):
        return [array] + [shifted(array, axis, size, d) for d in range(1, size)]

    def per_device(ancestor, panel, factor_inv, pattern):
        row = lax.axis_index("row")
        z = lax.axis_index("z")
        core = lax.axis_index("core")
        groups, chunk, width = panel.shape
        depth = factor_inv.shape[1]
        part = width // deep
        piece = chunk // rows
        out_rows = ancestor.shape[1] // cols
        tiles = ancestor.shape[1] // B

        def picked(slots, place, at):
            value = slots[0]
            for d in range(1, len(slots)):
                value = jnp.where((place - at) % len(slots) == d, slots[d], value)
            return value

        early = [d for d in range(1, deep) if deep < 4 * d < 3 * deep]
        late = [d for d in range(1, deep) if d not in early]
        far = {d: shifted(ancestor, "z", deep, d) for d in early}

        mine = lax.dynamic_slice_in_dim(panel, row * depth, depth, axis=2)
        partial = jnp.einsum("srw,swv->srv", mine, factor_inv, precision=highest)

        def rows_of(r):
            return lax.dynamic_slice_in_dim(partial, r * piece, piece, axis=1)

        scaled = rows_of(row)
        for shift in range(1, rows):
            scaled = scaled + shifted(rows_of((row + shift) % rows), "row", rows, shift)
        scaled, far = lax.optimization_barrier((scaled, far))

        def columns_of(array, c):
            return lax.dynamic_slice_in_dim(array, c * part, part, axis=2)

        slots = [columns_of(scaled, z)]
        for shift in range(1, deep):
            slots.append(shifted(columns_of(scaled, (z + shift) % deep), "z", deep, shift))
        if deep > 1:
            slots[1], held_back = lax.optimization_barrier((slots[1], ancestor))
            far |= {d: shifted(held_back, "z", deep, d) for d in late}
            slots, far[1] = lax.optimization_barrier((slots, far[1]))
        scaled = jnp.stack(gathered(jnp.stack(slots), "row", rows))

        count = jnp.arange(deep, dtype=jnp.int32)
        stored = jnp.sum(
            jnp.where(pattern[:, :, None] == count, count[:, None], 0), axis=1, dtype=jnp.int32
        )
        from_z = (z - jnp.take(stored, (z - count) % deep, axis=1, mode="clip")) % deep
        from_row = (row - jnp.arange(rows, dtype=jnp.int32)) % rows
        group = jnp.arange(groups, dtype=jnp.int32)
        spread = scaled[from_row, from_z[:, :, None], group[:, None, None]]
        spread = spread.reshape(groups, deep, chunk, part)
        wide = jnp.stack([ancestor] + [far[d] for d in range(1, deep)])
        product = jnp.einsum("dsij,sdjk->sik", wide, spread, precision=highest)
        product = product + shifted(product, "core", cores, 1)

        own = [
            lax.dynamic_index_in_dim(spread, (z - (row * tiles + t)) % deep, 1, keepdims=False)
            for t in range(tiles)
        ]
        own = jnp.stack(own, axis=1)
        other = shifted(own, "core", cores, 1)
        halves = [jnp.where(core == 0, own, other), jnp.where(core == 0, other, own)]
        own = jnp.stack(halves, axis=2).reshape(groups, -1, part)
        squares = jnp.sum(columns_of(factor_inv, z) ** 2, axis=1)
        term = jnp.sum(own * product, axis=1) + squares
        tail = jnp.broadcast_to(term[:, None], (groups, 8, part))

        def rows_for(c):
            block = lax.dynamic_slice_in_dim(product, (c * cores + core) * out_rows, out_rows, axis=1)
            return jnp.concatenate([block, tail], axis=1)

        moved = [rows_for(z)]
        for shift in range(1, deep):
            moved.append(shifted(rows_for((z + shift) % deep), "z", deep, shift))
        moved = jnp.concatenate([picked(moved, z, c) for c in range(deep)], axis=2)
        local = moved[:, out_rows]
        total = local
        for shift in range(1, rows):
            total = total + shifted(local, "row", rows, shift)
        return -moved[:, :out_rows], total

    col = ("z", "core")
    in_specs = (P(None, "row", col), P(None, col, None), P(None, "row", None), P())
    out_specs = (P(None, ("row", "z", "core"), None), P())
    return jax.shard_map(
        per_device, mesh=fine, in_specs=in_specs, out_specs=out_specs, check_vma=False
    )
```

time: 63.3 us -> 66.4 us (1.049)
  waiting for transfers between devices: 26.9 us -> 32.7 us
  starting transfers between devices: 26.7 us -> 24.4 us
  local copies, waits for them, and re-layouts: 3.63 us -> 2.66 us
    ppermute x24 -> x20, waiting for transfers between devices: 26.9 us -> 32.7 us  [shifted(): lax.ppermute(array, axis, [(i, (i + shift) % size) for i in range(size)])]
    ppermute x24 -> x20, starting transfers between devices: 26.7 us -> 24.4 us  [shifted(): lax.ppermute(array, axis, [(i, (i + shift) % size) for i in range(size)])]
    gather x3 -> x2, local copies, waits for them, and re-layouts: 1.8 us -> 1.27 us  [the longest x1 0.71 us: per_device(): spread = scaled[from_row, from_z[:, :, None], group[:, None, None]]]
  transfers between devices with their start and end apart: 24 -> 20, of which waited for: 16 -> 15; matrix products, arithmetic and copies ran while one was open for 8% -> 7% of each run, Pallas kernels for 0% -> 0%
where the time goes in v7:
time: 66.4 us; the launch traced here: 66.1 us
  waiting for transfers between devices  32.7 us (49%)
  starting transfers between devices  24.4 us (37%)
  other arithmetic  2.71 us (4%)
  matrix products  2.68 us (4%)
  local copies, waits for them, and re-layouts  2.66 us (4%)
  between operations  0.94 us (1%)
    ppermute x20, waiting for transfers between devices, shifted(): lax.ppermute(array, axis, [(i, (i + shift) % size) for i in range(size)])  32.7 us
    ppermute x20, starting transfers between devices, shifted(): lax.ppermute(array, axis, [(i, (i + shift) % size) for i in range(size)])  24.4 us
    dot_general x1, matrix products, per_device(): partial = jnp.einsum('srw,swv->srv', mine, factor_inv, precision=highest)  1.62 us
  transfers between devices with their start and end apart: 20, of which 15 were waited for; matrix products, arithmetic and copies ran while one was open for 7% of the time, Pallas kernels for 0%

profile of v7, /device:TPU:0, one launch (start us, length us, event | category | flops | bytes accessed | tf_op | source)
XLA Modules:
  0.0 66.1 jit_solution(12448334641986646935)
XLA Ops:
  0.7 1.0 %copy-done = f32[2,128,512]{2,1,0:T(8,128)S(1)} copy-done((f32[2,128,512]{2,1,0:T(8,128)S(1)}, f32[2,128,512]{2,1,0:T(8,128)}, u32[]{:S(2)}) %copy-start) | copy-done | bytes 524312
  1.7 1.6 %fusion.8 = f32[2,128,512]{2,1,0:T(8,128)S(1)} fusion(f32[2,128,512]{2,1,0:T(8,128)} %param.6, f32[2,128,512]{2,1,0:T(8,128)S(1)} %copy-done, s32[]{:T(128)S(6)} %select_n.244), kind=kOutput, calls=%fused_computation.21 | convolution fusion | flops 201326592 | bytes 1179652 | tf_op jit(solution)/shard_map/srw,swv->srv/dot_general | solution.py:43
  3.4 3.0 %collective-permute-start = (f32[2,32,512]{2,1,0:T(8,128)S(1)}, f32[2,32,512]{2,1,0:T(8,128)S(1)}, u32[]{:S(2)}, u32[]{:S(2)}) collective-permute-start(f32[2,32,512]{2,1,0:T(8,128)S(1)} %get-tuple-element.22), channel_id=1, source_target_pairs={{0,8},{8,16},{16,24},{24,0},{1,9},{9,17},{17,25},{25,1},{2,10},{10... | collective-permute-start | bytes 393224 | tf_op jit(solution)/shard_map/ppermute | solution.py:16
  6.4 1.5 %collective-permute-start.1 = (f32[2,32,512]{2,1,0:T(8,128)S(1)}, f32[2,32,512]{2,1,0:T(8,128)S(1)}, u32[]{:S(2)}, u32[]{:S(2)}) collective-permute-start(f32[2,32,512]{2,1,0:T(8,128)S(1)} %get-tuple-element.24), channel_id=1, source_target_pairs={{0,16},{8,24},{16,0},{24,8},{1,17},{9,25},{17,1},{25,9},{2,18},{10... | collective-permute-start | bytes 393224 | tf_op jit(solution)/shard_map/ppermute | solution.py:16
  7.9 1.4 %collective-permute-start.2 = (f32[2,32,512]{2,1,0:T(8,128)S(1)}, f32[2,32,512]{2,1,0:T(8,128)S(1)}, u32[]{:S(2)}, u32[]{:S(2)}) collective-permute-start(f32[2,32,512]{2,1,0:T(8,128)S(1)} %get-tuple-element.23), channel_id=1, source_target_pairs={{0,24},{8,0},{16,8},{24,16},{1,25},{9,1},{17,9},{25,17},{2,26},{10... | collective-permute-start | bytes 393224 | tf_op jit(solution)/shard_map/ppermute | solution.py:16
  9.3 2.6 %collective-permute-start.3 = (f32[2,256,128]{2,1,0:T(8,128)S(1)}, f32[2,256,128]{2,1,0:T(8,128)S(1)}, u32[]{:S(2)}, u32[]{:S(2)}) collective-permute-start(f32[2,256,128]{2,1,0:T(8,128)S(1)} %copy-done.2), channel_id=1, source_target_pairs={{0,4},{2,6},{4,0},{6,2},{1,5},{3,7},{5,1},{7,3},{8,12},{10,14},{12... | collective-permute-start | bytes 786440 | tf_op jit(solution)/shard_map/ppermute | solution.py:16
  11.9 0.1 select_reduce_fusion
  12.1 1.5 %collective-permute-done.1 = f32[2,32,512]{2,1,0:T(8,128)S(1)} collective-permute-done((f32[2,32,512]{2,1,0:T(8,128)S(1)}, f32[2,32,512]{2,1,0:T(8,128)S(1)}, u32[]{:S(2)}, u32[]{:S(2)}) %collective-permute-start.1) | collective-permute-done | bytes 131104 | tf_op jit(solution)/shard_map/ppermute | solution.py:16
  13.6 0.2 collective-permute-done.2
  13.9 9.1 %collective-permute-done.3 = f32[2,256,128]{2,1,0:T(8,128)S(1)} collective-permute-done((f32[2,256,128]{2,1,0:T(8,128)S(1)}, f32[2,256,128]{2,1,0:T(8,128)S(1)}, u32[]{:S(2)}, u32[]{:S(2)}) %collective-permute-start.3) | collective-permute-done | bytes 262176 | tf_op jit(solution)/shard_map/ppermute | solution.py:16
  23.1 0.7 %collective-permute-start.4 = (f32[2,32,128]{2,1,0:T(8,128)S(1)}, f32[2,32,128]{2,1,0:T(8,128)S(1)}, u32[]{:S(2)}, u32[]{:S(2)}) collective-permute-start(f32[2,32,128]{2,1,0:T(8,128)S(1)} %get-tuple-element.36), channel_id=1, source_target_pairs={{0,2},{2,4},{4,6},{6,0},{1,3},{3,5},{5,7},{7,1},{8,10},{10,12},{12... | collective-permute-start | bytes 98312 | tf_op jit(solution)/shard_map/ppermute | solution.py:16
  23.8 0.1 copy.12
  23.9 0.6 gather_fusion
  24.4 4.4 %collective-permute-done.4 = f32[2,32,128]{2,1,0:T(8,128)S(1)} collective-permute-done((f32[2,32,128]{2,1,0:T(8,128)S(1)}, f32[2,32,128]{2,1,0:T(8,128)S(1)}, u32[]{:S(2)}, u32[]{:S(2)}) %collective-permute-start.4) | collective-permute-done | bytes 32800 | tf_op jit(solution)/shard_map/ppermute | solution.py:16
  28.8 2.3 %collective-permute-start.5 = (f32[2,32,128]{2,1,0:T(8,128)S(1)}, f32[2,32,128]{2,1,0:T(8,128)S(1)}, u32[]{:S(2)}, u32[]{:S(2)}) collective-permute-start(f32[2,32,128]{2,1,0:T(8,128)S(1)} %get-tuple-element.35), channel_id=1, source_target_pairs={{0,4},{2,6},{4,0},{6,2},{1,5},{3,7},{5,1},{7,3},{8,12},{10,14},{12... | collective-permute-start | bytes 98312 | tf_op jit(solution)/shard_map/ppermute | solution.py:16
  31.1 1.6 %collective-permute-start.6 = (f32[2,32,128]{2,1,0:T(8,128)S(1)}, f32[2,32,128]{2,1,0:T(8,128)S(1)}, u32[]{:S(2)}, u32[]{:S(2)}) collective-permute-start(f32[2,32,128]{2,1,0:T(8,128)S(1)} %get-tuple-element.34), channel_id=1, source_target_pairs={{0,6},{2,0},{4,2},{6,4},{1,7},{3,1},{5,3},{7,5},{8,14},{10,8},{12,... | collective-permute-start | bytes 98312 | tf_op jit(solution)/shard_map/ppermute | solution.py:16
  32.8 0.1 copy.13
  32.9 0.5 collective-permute-start.8
  33.4 4.1 %collective-permute-done.5 = f32[2,32,128]{2,1,0:T(8,128)S(1)} collective-permute-done((f32[2,32,128]{2,1,0:T(8,128)S(1)}, f32[2,32,128]{2,1,0:T(8,128)S(1)}, u32[]{:S(2)}, u32[]{:S(2)}) %collective-permute-start.5) | collective-permute-done | bytes 32800 | tf_op jit(solution)/shard_map/ppermute | solution.py:16
  37.5 0.2 collective-permute-done.6
  37.7 2.2 %collective-permute-done.7 = f32[2,256,128]{2,1,0:T(8,128)S(1)} collective-permute-done((f32[2,256,128]{2,1,0:T(8,128)S(1)}, f32[2,256,128]{2,1,0:T(8,128)S(1)}, u32[]{:S(2)}, u32[]{:S(2)}) %collective-permute-start.7) | collective-permute-done | bytes 262176 | tf_op jit(solution)/shard_map/ppermute | solution.py:16
  39.9 0.5 collective-permute-start.10
  40.5 1.6 %collective-permute-start.11 = (f32[4,2,32,128]{3,2,1,0:T(8,128)S(1)}, f32[4,2,32,128]{3,2,1,0:T(8,128)S(1)}, u32[]{:S(2)}, u32[]{:S(2)}) collective-permute-start(f32[4,2,32,128]{3,2,1,0:T(8,128)S(1)} %get-tuple-element.33), channel_id=1, source_target_pairs={{0,24},{8,0},{16,8},{24,16},{1,25},{9,1},{17,9},{25,17},{2,26},{10... | collective-permute-start | bytes 393224 | tf_op jit(solution)/shard_map/ppermute | solution.py:16
  42.1 0.4 collective-permute-start.9
  42.5 0.1 shift-left_or_fusion
  42.6 0.1 reshape.92
  42.6 0.9 %multiply_reduce_fusion.1 = f32[2,128]{1,0:T(2,128)S(1)} fusion(f32[2,128,512]{2,1,0:T(8,128)} %param.6, s32[]{:T(128)S(6)} %select_n.252), kind=kLoop, calls=%fused_computation.18 | loop fusion | flops 65280 | bytes 132100 | tf_op jit(solution)/shard_map/reduce_sum | solution.py:86
  43.6 1.7 %collective-permute-done.10 = f32[4,2,32,128]{3,2,1,0:T(8,128)S(1)} collective-permute-done((f32[4,2,32,128]{3,2,1,0:T(8,128)S(1)}, f32[4,2,32,128]{3,2,1,0:T(8,128)S(1)}, u32[]{:S(2)}, u32[]{:S(2)}) %collective-permute-start.10) | collective-permute-done | bytes 131104 | tf_op jit(solution)/shard_map/ppermute | solution.py:16
  45.3 0.1 collective-permute-done.11
  45.4 2.5 %collective-permute-done.9 = f32[4,2,32,128]{3,2,1,0:T(8,128)S(1)} collective-permute-done((f32[4,2,32,128]{3,2,1,0:T(8,128)S(1)}, f32[4,2,32,128]{3,2,1,0:T(8,128)S(1)}, u32[]{:S(2)}, u32[]{:S(2)}) %collective-permute-start.9) | collective-permute-done | bytes 131104 | tf_op jit(solution)/shard_map/ppermute | solution.py:16
  48.0 0.7 %gather_fusion.1 = f32[32,32,128]{2,1,0:T(8,128)S(1)} fusion(f32[4,4,2,32,128]{4,3,2,1,0:T(8,128)S(1)} %pad_maximum_fusion, s32[32]{0:T(128)S(1)} %reshape.92), kind=kCustom, calls=%fused_computation.1 | custom fusion | bytes 1048960 | tf_op jit(solution)/shard_map/gather | solution.py:72
  48.7 0.1 collective-permute-start.13
  48.8 1.1 %convolution_bitcast_fusion = f32[2,256,128]{2,1,0:T(8,128)S(1)} fusion(f32[2,4,128,128]{3,2,1,0:T(8,128)S(1)} %bitcast.49, f32[1,2,256,128]{3,2,0,1:T(8,128)S(1)} %bitcast.66, f32[1,2,256,128]{3,2,0,1:T(8,128)S(1)} %bitcast.64, f32[1,2,256,128]{3,2,0,1:T(8,128)S(1)} %bitcast.65, f32[1,2,256,128]{3,2,0,1:T(8,128)S(1)} %bitcast.63), kind=kOutput, calls=%fused_computation.2 | convolution fusion | flops 403439616 | bytes 1835008 | tf_op jit(solution)/shard_map/dsij,sdjk->sik/dot_general | solution.py:75
  49.9 0.6 collective-permute-start.12
  50.5 1.1 %collective-permute-done.12 = f32[2,256,128]{2,1,0:T(8,128)S(1)} collective-permute-done((f32[2,256,128]{2,1,0:T(8,128)S(1)}, f32[2,256,128]{2,1,0:T(8,128)S(1)}, u32[]{:S(2)}, u32[]{:S(2)}) %collective-permute-start.12) | collective-permute-done | bytes 262176 | tf_op jit(solution)/shard_map/ppermute | solution.py:16
  51.6 0.1 multiply_reduce_fusion
  51.7 1.4 %collective-permute-start.14 = (f32[2,40,128]{2,1,0:T(8,128)S(1)}, f32[2,40,128]{2,1,0:T(8,128)S(1)}, u32[]{:S(2)}, u32[]{:S(2)}) collective-permute-start(f32[2,40,128]{2,1,0:T(8,128)S(1)} %get-tuple-element.40), channel_id=1, source_target_pairs={{0,6},{2,0},{4,2},{6,4},{1,7},{3,1},{5,3},{7,5},{8,14},{10,8},{12,... | collective-permute-start | bytes 122888 | tf_op jit(solution)/shard_map/ppermute | solution.py:16
  53.2 1.4 %collective-permute-start.15 = (f32[2,40,128]{2,1,0:T(8,128)S(1)}, f32[2,40,128]{2,1,0:T(8,128)S(1)}, u32[]{:S(2)}, u32[]{:S(2)}) collective-permute-start(f32[2,40,128]{2,1,0:T(8,128)S(1)} %get-tuple-element.39), channel_id=1, source_target_pairs={{0,4},{2,6},{4,0},{6,2},{1,5},{3,7},{5,1},{7,3},{8,12},{10,14},{12... | collective-permute-start | bytes 122888 | tf_op jit(solution)/shard_map/ppermute | solution.py:16
  54.5 1.3 %collective-permute-start.16 = (f32[2,40,128]{2,1,0:T(8,128)S(1)}, f32[2,40,128]{2,1,0:T(8,128)S(1)}, u32[]{:S(2)}, u32[]{:S(2)}) collective-permute-start(f32[2,40,128]{2,1,0:T(8,128)S(1)} %get-tuple-element.38), channel_id=1, source_target_pairs={{0,2},{2,4},{4,6},{6,0},{1,3},{3,5},{5,7},{7,1},{8,10},{10,12},{12... | collective-permute-start | bytes 122888 | tf_op jit(solution)/shard_map/ppermute | solution.py:16
  55.8 2.7 %collective-permute-done.15 = f32[2,40,128]{2,1,0:T(8,128)S(1)} collective-permute-done((f32[2,40,128]{2,1,0:T(8,128)S(1)}, f32[2,40,128]{2,1,0:T(8,128)S(1)}, u32[]{:S(2)}, u32[]{:S(2)}) %collective-permute-start.15) | collective-permute-done | bytes 40992 | tf_op jit(solution)/shard_map/ppermute | solution.py:16
  58.5 1.8 %collective-permute-done.16 = f32[2,40,128]{2,1,0:T(8,128)S(1)} collective-permute-done((f32[2,40,128]{2,1,0:T(8,128)S(1)}, f32[2,40,128]{2,1,0:T(8,128)S(1)}, u32[]{:S(2)}, u32[]{:S(2)}) %collective-permute-start.16) | collective-permute-done | bytes 40992 | tf_op jit(solution)/shard_map/ppermute | solution.py:16
  60.4 0.6 collective-permute-start.17
  61.0 0.6 collective-permute-start.18
  61.6 2.3 %collective-permute-start.19 = (f32[2,512]{1,0:T(2,128)S(1)}, f32[2,512]{1,0:T(2,128)S(1)}, u32[]{:S(2)}, u32[]{:S(2)}) collective-permute-start(f32[2,512]{1,0:T(2,128)S(1)} %bitcast.62), channel_id=1, source_target_pairs={{0,24},{8,0},{16,8},{24,16},{1,25},{9,1},{17,9},{25,17},{2,26},{10... | collective-permute-start | bytes 12296 | tf_op jit(solution)/shard_map/ppermute | solution.py:16
  63.9 0.7 %slice_negate_fusion = f32[2,32,512]{2,1,0:T(8,128)} fusion(f32[2,40,512]{2,1,0:T(8,128)S(1)} %pad_maximum_fusion.2), kind=kLoop, calls=%fused_computation.14 | loop fusion | flops 32768 | bytes 262144 | tf_op jit(solution)/shard_map/neg | solution.py:102
  64.6 0.4 collective-permute-done.17
  65.0 0.6 collective-permute-done.19
  65.5 0.6 add_add_fusion.1
  (34 shorter events, 0.4 us)
Async XLA Ops:
  0.6 1.0 %copy-start = (f32[2,128,512]{2,1,0:T(8,128)S(1)}, f32[2,128,512]{2,1,0:T(8,128)}, u32[]{:S(2)}) copy-start(f32[2,128,512]{2,1,0:T(8,128)} %param.5) | copy-start | bytes 1572868
  3.3 6.0 %copy-start.2 = (f32[2,256,128]{2,1,0:T(8,128)S(1)}, f32[2,256,128]{2,1,0:T(8,128)}, u32[]{:S(2)}) copy-start(f32[2,256,128]{2,1,0:T(8,128)} %param.4) | copy-start | bytes 786436
  3.4 8.7 %collective-permute-start = (f32[2,32,512]{2,1,0:T(8,128)S(1)}, f32[2,32,512]{2,1,0:T(8,128)S(1)}, u32[]{:S(2)}, u32[]{:S(2)}) collective-permute-start(f32[2,32,512]{2,1,0:T(8,128)S(1)} %get-tuple-element.22), channel_id=1, source_target_pairs={{0,8},{8,16},{16,24},{24,0},{1,9},{9,17},{17,25},{25,1},{2,10},{10... | collective-permute-start | bytes 393224 | tf_op jit(solution)/shard_map/ppermute | solution.py:16
  6.4 5.5 %copy-start.1 = (s32[2,4]{1,0:T(2,128)S(1)}, s32[2,4]{1,0:T(2,128)}, u32[]{:S(2)}) copy-start(s32[2,4]{1,0:T(2,128)} %param.7) | copy-start | bytes 100
  6.4 7.3 %collective-permute-start.1 = (f32[2,32,512]{2,1,0:T(8,128)S(1)}, f32[2,32,512]{2,1,0:T(8,128)S(1)}, u32[]{:S(2)}, u32[]{:S(2)}) collective-permute-start(f32[2,32,512]{2,1,0:T(8,128)S(1)} %get-tuple-element.24), channel_id=1, source_target_pairs={{0,16},{8,24},{16,0},{24,8},{1,17},{9,25},{17,1},{25,9},{2,18},{10... | collective-permute-start | bytes 393224 | tf_op jit(solution)/shard_map/ppermute | solution.py:16
  7.9 6.0 %collective-permute-start.2 = (f32[2,32,512]{2,1,0:T(8,128)S(1)}, f32[2,32,512]{2,1,0:T(8,128)S(1)}, u32[]{:S(2)}, u32[]{:S(2)}) collective-permute-start(f32[2,32,512]{2,1,0:T(8,128)S(1)} %get-tuple-element.23), channel_id=1, source_target_pairs={{0,24},{8,0},{16,8},{24,16},{1,25},{9,1},{17,9},{25,17},{2,26},{10... | collective-permute-start | bytes 393224 | tf_op jit(solution)/shard_map/ppermute | solution.py:16
  9.3 13.7 %collective-permute-start.3 = (f32[2,256,128]{2,1,0:T(8,128)S(1)}, f32[2,256,128]{2,1,0:T(8,128)S(1)}, u32[]{:S(2)}, u32[]{:S(2)}) collective-permute-start(f32[2,256,128]{2,1,0:T(8,128)S(1)} %copy-done.2), channel_id=1, source_target_pairs={{0,4},{2,6},{4,0},{6,2},{1,5},{3,7},{5,1},{7,3},{8,12},{10,14},{12... | collective-permute-start | bytes 786440 | tf_op jit(solution)/shard_map/ppermute | solution.py:16
  23.1 5.8 %collective-permute-start.4 = (f32[2,32,128]{2,1,0:T(8,128)S(1)}, f32[2,32,128]{2,1,0:T(8,128)S(1)}, u32[]{:S(2)}, u32[]{:S(2)}) collective-permute-start(f32[2,32,128]{2,1,0:T(8,128)S(1)} %get-tuple-element.36), channel_id=1, source_target_pairs={{0,2},{2,4},{4,6},{6,0},{1,3},{3,5},{5,7},{7,1},{8,10},{10,12},{12... | collective-permute-start | bytes 98312 | tf_op jit(solution)/shard_map/ppermute | solution.py:16
  28.8 11.1 %collective-permute-start.7 = (f32[2,256,128]{2,1,0:T(8,128)S(1)}, f32[2,256,128]{2,1,0:T(8,128)S(1)}, u32[]{:S(2)}, u32[]{:S(2)}) collective-permute-start(f32[2,256,128]{2,1,0:T(8,128)S(1)} %copy-done.2), channel_id=1, source_target_pairs={{0,2},{2,4},{4,6},{6,0},{1,3},{3,5},{5,7},{7,1},{8,10},{10,12},{12... | collective-permute-start | bytes 786440 | tf_op jit(solution)/shard_map/ppermute | solution.py:16
  28.8 8.6 %collective-permute-start.5 = (f32[2,32,128]{2,1,0:T(8,128)S(1)}, f32[2,32,128]{2,1,0:T(8,128)S(1)}, u32[]{:S(2)}, u32[]{:S(2)}) collective-permute-start(f32[2,32,128]{2,1,0:T(8,128)S(1)} %get-tuple-element.35), channel_id=1, source_target_pairs={{0,4},{2,6},{4,0},{6,2},{1,5},{3,7},{5,1},{7,3},{8,12},{10,14},{12... | collective-permute-start | bytes 98312 | tf_op jit(solution)/shard_map/ppermute | solution.py:16
  31.1 6.5 %collective-permute-start.6 = (f32[2,32,128]{2,1,0:T(8,128)S(1)}, f32[2,32,128]{2,1,0:T(8,128)S(1)}, u32[]{:S(2)}, u32[]{:S(2)}) collective-permute-start(f32[2,32,128]{2,1,0:T(8,128)S(1)} %get-tuple-element.34), channel_id=1, source_target_pairs={{0,6},{2,0},{4,2},{6,4},{1,7},{3,1},{5,3},{7,5},{8,14},{10,8},{12,... | collective-permute-start | bytes 98312 | tf_op jit(solution)/shard_map/ppermute | solution.py:16
  32.9 15.9 %collective-permute-start.8 = (f32[2,256,128]{2,1,0:T(8,128)S(1)}, f32[2,256,128]{2,1,0:T(8,128)S(1)}, u32[]{:S(2)}, u32[]{:S(2)}) collective-permute-start(f32[2,256,128]{2,1,0:T(8,128)S(1)} %copy-done.2), channel_id=1, source_target_pairs={{0,6},{2,0},{4,2},{6,4},{1,7},{3,1},{5,3},{7,5},{8,14},{10,8},{12,... | collective-permute-start | bytes 786440 | tf_op jit(solution)/shard_map/ppermute | solution.py:16
  39.9 5.4 %collective-permute-start.10 = (f32[4,2,32,128]{3,2,1,0:T(8,128)S(1)}, f32[4,2,32,128]{3,2,1,0:T(8,128)S(1)}, u32[]{:S(2)}, u32[]{:S(2)}) collective-permute-start(f32[4,2,32,128]{3,2,1,0:T(8,128)S(1)} %get-tuple-element.33), channel_id=1, source_target_pairs={{0,16},{8,24},{16,0},{24,8},{1,17},{9,25},{17,1},{25,9},{2,18},{10... | collective-permute-start | bytes 393224 | tf_op jit(solution)/shard_map/ppermute | solution.py:16
  40.5 5.0 %collective-permute-start.11 = (f32[4,2,32,128]{3,2,1,0:T(8,128)S(1)}, f32[4,2,32,128]{3,2,1,0:T(8,128)S(1)}, u32[]{:S(2)}, u32[]{:S(2)}) collective-permute-start(f32[4,2,32,128]{3,2,1,0:T(8,128)S(1)} %get-tuple-element.33), channel_id=1, source_target_pairs={{0,24},{8,0},{16,8},{24,16},{1,25},{9,1},{17,9},{25,17},{2,26},{10... | collective-permute-start | bytes 393224 | tf_op jit(solution)/shard_map/ppermute | solution.py:16
  42.1 5.9 %collective-permute-start.9 = (f32[4,2,32,128]{3,2,1,0:T(8,128)S(1)}, f32[4,2,32,128]{3,2,1,0:T(8,128)S(1)}, u32[]{:S(2)}, u32[]{:S(2)}) collective-permute-start(f32[4,2,32,128]{3,2,1,0:T(8,128)S(1)} %get-tuple-element.33), channel_id=1, source_target_pairs={{0,8},{8,16},{16,24},{24,0},{1,9},{9,17},{17,25},{25,1},{2,10},{10... | collective-permute-start | bytes 393224 | tf_op jit(solution)/shard_map/ppermute | solution.py:16
  48.7 1.7 %collective-permute-start.13 = (f32[2,1,128,128]{3,2,0,1:T(8,128)S(1)}, f32[2,1,128,128]{3,2,0,1:T(8,128)S(1)}, u32[]{:S(2)}, u32[]{:S(2)}) collective-permute-start(f32[2,1,128,128]{3,2,0,1:T(8,128)S(1)} %dynamic-slice_bitcast_fusion), channel_id=1, source_target_pairs={{0,1},{1,0},{2,3},{3,2},{4,5},{5,4},{6,7},{7,6},{8,9},{9,8},{10,11... | collective-permute-start | bytes 393224 | tf_op jit(solution)/shard_map/ppermute | solution.py:16
  49.9 1.7 %collective-permute-start.12 = (f32[2,256,128]{2,1,0:T(8,128)S(1)}, f32[2,256,128]{2,1,0:T(8,128)S(1)}, u32[]{:S(2)}, u32[]{:S(2)}) collective-permute-start(f32[2,256,128]{2,1,0:T(8,128)S(1)} %convolution_bitcast_fusion), channel_id=1, source_target_pairs={{0,1},{1,0},{2,3},{3,2},{4,5},{5,4},{6,7},{7,6},{8,9},{9,8},{10,11... | collective-permute-start | bytes 786440 | tf_op jit(solution)/shard_map/ppermute | solution.py:16
  51.7 4.1 %collective-permute-start.14 = (f32[2,40,128]{2,1,0:T(8,128)S(1)}, f32[2,40,128]{2,1,0:T(8,128)S(1)}, u32[]{:S(2)}, u32[]{:S(2)}) collective-permute-start(f32[2,40,128]{2,1,0:T(8,128)S(1)} %get-tuple-element.40), channel_id=1, source_target_pairs={{0,6},{2,0},{4,2},{6,4},{1,7},{3,1},{5,3},{7,5},{8,14},{10,8},{12,... | collective-permute-start | bytes 122888 | tf_op jit(solution)/shard_map/ppermute | solution.py:16
  53.2 5.4 %collective-permute-start.15 = (f32[2,40,128]{2,1,0:T(8,128)S(1)}, f32[2,40,128]{2,1,0:T(8,128)S(1)}, u32[]{:S(2)}, u32[]{:S(2)}) collective-permute-start(f32[2,40,128]{2,1,0:T(8,128)S(1)} %get-tuple-element.39), channel_id=1, source_target_pairs={{0,4},{2,6},{4,0},{6,2},{1,5},{3,7},{5,1},{7,3},{8,12},{10,14},{12... | collective-permute-start | bytes 122888 | tf_op jit(solution)/shard_map/ppermute | solution.py:16
  54.5 5.8 %collective-permute-start.16 = (f32[2,40,128]{2,1,0:T(8,128)S(1)}, f32[2,40,128]{2,1,0:T(8,128)S(1)}, u32[]{:S(2)}, u32[]{:S(2)}) collective-permute-start(f32[2,40,128]{2,1,0:T(8,128)S(1)} %get-tuple-element.38), channel_id=1, source_target_pairs={{0,2},{2,4},{4,6},{6,0},{1,3},{3,5},{5,7},{7,1},{8,10},{10,12},{12... | collective-permute-start | bytes 122888 | tf_op jit(solution)/shard_map/ppermute | solution.py:16
  60.4 4.6 %collective-permute-start.17 = (f32[2,512]{1,0:T(2,128)S(1)}, f32[2,512]{1,0:T(2,128)S(1)}, u32[]{:S(2)}, u32[]{:S(2)}) collective-permute-start(f32[2,512]{1,0:T(2,128)S(1)} %bitcast.60), channel_id=1, source_target_pairs={{0,8},{8,16},{16,24},{24,0},{1,9},{9,17},{17,25},{25,1},{2,10},{10... | collective-permute-start | bytes 12296 | tf_op jit(solution)/shard_map/ppermute | solution.py:16
  61.0 4.0 %collective-permute-start.18 = (f32[2,512]{1,0:T(2,128)S(1)}, f32[2,512]{1,0:T(2,128)S(1)}, u32[]{:S(2)}, u32[]{:S(2)}) collective-permute-start(f32[2,512]{1,0:T(2,128)S(1)} %bitcast.61), channel_id=1, source_target_pairs={{0,16},{8,24},{16,0},{24,8},{1,17},{9,25},{17,1},{25,9},{2,18},{10... | collective-permute-start | bytes 12296 | tf_op jit(solution)/shard_map/ppermute | solution.py:16
  61.6 4.0 %collective-permute-start.19 = (f32[2,512]{1,0:T(2,128)S(1)}, f32[2,512]{1,0:T(2,128)S(1)}, u32[]{:S(2)}, u32[]{:S(2)}) collective-permute-start(f32[2,512]{1,0:T(2,128)S(1)} %bitcast.62), channel_id=1, source_target_pairs={{0,24},{8,0},{16,8},{24,16},{1,25},{9,1},{17,9},{25,17},{2,26},{10... | collective-permute-start | bytes 12296 | tf_op jit(solution)/shard_map/ppermute | solution.py:16

commit v8 on v7

--- a/solution.py
+++ b/solution.py
@@ -35,9 +35,18 @@
                 value = jnp.where((place - at) % len(slots) == d, slots[d], value)
             return value
 
-        early = [d for d in range(1, deep) if deep < 4 * d < 3 * deep]
-        late = [d for d in range(1, deep) if d not in early]
-        far = {d: shifted(ancestor, "z", deep, d) for d in early}
+        def passed(piece, step):
+            pairs = [(i, i + step) for i in range(deep) if 0 <= i + step < deep]
+            return lax.ppermute(piece, "z", pairs)
+
+        before, after = [ancestor], [ancestor]
+
+        def pass_on():
+            if len(before) < deep:
+                before.append(passed(before[-1], 1))
+                after.append(passed(after[-1], -1))
+
+        pass_on()
 
         mine = lax.dynamic_slice_in_dim(panel, row * depth, depth, axis=2)
         partial = jnp.einsum("srw,swv->srv", mine, factor_inv, precision=highest)
@@ -48,7 +57,8 @@
         scaled = rows_of(row)
         for shift in range(1, rows):
             scaled = scaled + shifted(rows_of((row + shift) % rows), "row", rows, shift)
-        scaled, far = lax.optimization_barrier((scaled, far))
+        scaled, before[-1], after[-1] = lax.optimization_barrier((scaled, before[-1], after[-1]))
+        pass_on()
 
         def columns_of(array, c):
             return lax.dynamic_slice_in_dim(array, c * part, part, axis=2)
@@ -56,10 +66,9 @@
         slots = [columns_of(scaled, z)]
         for shift in range(1, deep):
             slots.append(shifted(columns_of(scaled, (z + shift) % deep), "z", deep, shift))
-        if deep > 1:
-            slots[1], held_back = lax.optimization_barrier((slots[1], ancestor))
-            far |= {d: shifted(held_back, "z", deep, d) for d in late}
-            slots, far[1] = lax.optimization_barrier((slots, far[1]))
+        slots, before[-1], after[-1] = lax.optimization_barrier((slots, before[-1], after[-1]))
+        while len(before) < deep:
+            pass_on()
         scaled = jnp.stack(gathered(jnp.stack(slots), "row", rows))
 
         count = jnp.arange(deep, dtype=jnp.int32)
@@ -71,7 +80,8 @@
         group = jnp.arange(groups, dtype=jnp.int32)
         spread = scaled[from_row, from_z[:, :, None], group[:, None, None]]
         spread = spread.reshape(groups, deep, chunk, part)
-        wide = jnp.stack([ancestor] + [far[d] for d in range(1, deep)])
+        far = [jnp.where(z >= d, before[d], after[deep - d]) for d in range(1, deep)]
+        wide = jnp.stack([ancestor] + far)
         product = jnp.einsum("dsij,sdjk->sik", wide, spread, precision=highest)
         product = product + shifted(product, "core", cores, 1)
 

time: 66.4 us -> 67.4 us (1.015)
  starting transfers between devices: 24.4 us -> 38 us
  waiting for transfers between devices: 32.7 us -> 20.1 us
    ppermute x20 -> x17, waiting for transfers between devices: 32.7 us -> 14.1 us  [shifted(): lax.ppermute(array, axis, [(i, (i + shift) % size) for i in range(size)])]
    ppermute x0 -> x6, starting transfers between devices: none -> 16.1 us  [passed(): return lax.ppermute(piece, 'z', pairs)]
    ppermute x0 -> x6, waiting for transfers between devices: none -> 5.99 us  [passed(): return lax.ppermute(piece, 'z', pairs)]
    ppermute x20 -> x17, starting transfers between devices: 24.4 us -> 21.8 us  [shifted(): lax.ppermute(array, axis, [(i, (i + shift) % size) for i in range(size)])]
  transfers between devices with their start and end apart: 20 -> 23, of which waited for: 15 -> 12; matrix products, arithmetic and copies ran while one was open for 7% -> 10% of each run, Pallas kernels for 0% -> 0%
where the time goes in v8:
time: 67.4 us; the launch traced here: 67.1 us
  starting transfers between devices  38 us (56%)
  waiting for transfers between devices  20.1 us (30%)
  other arithmetic  2.81 us (4%)
  matrix products  2.69 us (4%)
  local copies, waits for them, and re-layouts  2.36 us (4%)
  between operations  1.09 us (2%)
    ppermute x17, starting transfers between devices, shifted(): lax.ppermute(array, axis, [(i, (i + shift) % size) for i in range(size)])  21.8 us
    ppermute x6, starting transfers between devices, passed(): return lax.ppermute(piece, 'z', pairs)  16.1 us
    ppermute x17, waiting for transfers between devices, shifted(): lax.ppermute(array, axis, [(i, (i + shift) % size) for i in range(size)])  14.1 us
    ppermute x6, waiting for transfers between devices, passed(): return lax.ppermute(piece, 'z', pairs)  5.99 us
    dot_general x1, matrix products, per_device(): partial = jnp.einsum('srw,swv->srv', mine, factor_inv, precision=highest)  1.62 us
  transfers between devices with their start and end apart: 23, of which 12 were waited for; matrix products, arithmetic and copies ran while one was open for 10% of the time, Pallas kernels for 0%

profile of v8, /device:TPU:0, one launch (start us, length us, event | category | flops | bytes accessed | tf_op | source)
XLA Modules:
  0.0 67.1 jit_solution(17177402803505748285)
XLA Ops:
  0.6 5.1 %collective-permute-start.3 = (f32[2,256,128]{2,1,0:T(8,128)}, f32[2,256,128]{2,1,0:T(8,128)S(1)}, u32[]{:S(2)}, u32[]{:S(2)}) collective-permute-start(f32[2,256,128]{2,1,0:T(8,128)} %param.4), channel_id=1, source_target_pairs={{0,2},{2,4},{4,6},{1,3},{3,5},{5,7},{8,10},{10,12},{12,14},{9,11},... | collective-permute-start | bytes 786440 | tf_op jit(solution)/shard_map/ppermute | solution.py:40
  5.7 1.3 %collective-permute-start.4 = (f32[2,256,128]{2,1,0:T(8,128)}, f32[2,256,128]{2,1,0:T(8,128)S(1)}, u32[]{:S(2)}, u32[]{:S(2)}) collective-permute-start(f32[2,256,128]{2,1,0:T(8,128)} %param.4), channel_id=1, source_target_pairs={{2,0},{4,2},{6,4},{3,1},{5,3},{7,5},{10,8},{12,10},{14,12},{11,9},... | collective-permute-start | bytes 786440 | tf_op jit(solution)/shard_map/ppermute | solution.py:40
  7.1 1.6 %fusion.8 = f32[2,128,512]{2,1,0:T(8,128)S(1)} fusion(f32[2,128,512]{2,1,0:T(8,128)} %param.6, f32[2,128,512]{2,1,0:T(8,128)S(1)} %copy-done, s32[]{:T(128)S(6)} %select_n.265), kind=kOutput, calls=%fused_computation.24 | convolution fusion | flops 201326592 | bytes 1179652 | tf_op jit(solution)/shard_map/srw,swv->srv/dot_general | solution.py:52
  8.8 1.5 %collective-permute-start = (f32[2,32,512]{2,1,0:T(8,128)S(1)}, f32[2,32,512]{2,1,0:T(8,128)S(1)}, u32[]{:S(2)}, u32[]{:S(2)}) collective-permute-start(f32[2,32,512]{2,1,0:T(8,128)S(1)} %get-tuple-element.22), channel_id=1, source_target_pairs={{0,8},{8,16},{16,24},{24,0},{1,9},{9,17},{17,25},{25,1},{2,10},{10... | collective-permute-start | bytes 393224 | tf_op jit(solution)/shard_map/ppermute | solution.py:16
  10.3 1.5 %collective-permute-start.1 = (f32[2,32,512]{2,1,0:T(8,128)S(1)}, f32[2,32,512]{2,1,0:T(8,128)S(1)}, u32[]{:S(2)}, u32[]{:S(2)}) collective-permute-start(f32[2,32,512]{2,1,0:T(8,128)S(1)} %get-tuple-element.24), channel_id=1, source_target_pairs={{0,16},{8,24},{16,0},{24,8},{1,17},{9,25},{17,1},{25,9},{2,18},{10... | collective-permute-start | bytes 393224 | tf_op jit(solution)/shard_map/ppermute | solution.py:16
  11.8 1.4 %collective-permute-start.2 = (f32[2,32,512]{2,1,0:T(8,128)S(1)}, f32[2,32,512]{2,1,0:T(8,128)S(1)}, u32[]{:S(2)}, u32[]{:S(2)}) collective-permute-start(f32[2,32,512]{2,1,0:T(8,128)S(1)} %get-tuple-element.23), channel_id=1, source_target_pairs={{0,24},{8,0},{16,8},{24,16},{1,25},{9,1},{17,9},{25,17},{2,26},{10... | collective-permute-start | bytes 393224 | tf_op jit(solution)/shard_map/ppermute | solution.py:16
  13.3 0.7 copy-done.1
  13.9 0.1 select_reduce_fusion
  14.0 0.1 copy.16
  14.1 0.6 gather_fusion
  14.8 0.1 copy.17
  14.9 1.1 %collective-permute-done = f32[2,32,512]{2,1,0:T(8,128)S(1)} collective-permute-done((f32[2,32,512]{2,1,0:T(8,128)S(1)}, f32[2,32,512]{2,1,0:T(8,128)S(1)}, u32[]{:S(2)}, u32[]{:S(2)}) %collective-permute-start) | collective-permute-done | bytes 131104 | tf_op jit(solution)/shard_map/ppermute | solution.py:16
  16.0 1.5 %collective-permute-done.1 = f32[2,32,512]{2,1,0:T(8,128)S(1)} collective-permute-done((f32[2,32,512]{2,1,0:T(8,128)S(1)}, f32[2,32,512]{2,1,0:T(8,128)S(1)}, u32[]{:S(2)}, u32[]{:S(2)}) %collective-permute-start.1) | collective-permute-done | bytes 131104 | tf_op jit(solution)/shard_map/ppermute | solution.py:16
  17.5 0.1 collective-permute-done.2
  17.6 4.4 %collective-permute-start.8 = (f32[2,256,128]{2,1,0:T(8,128)S(1)}, f32[2,256,128]{2,1,0:T(8,128)S(1)}, u32[]{:S(2)}, u32[]{:S(2)}) collective-permute-start(f32[2,256,128]{2,1,0:T(8,128)S(1)} %collective-permute-done.3), channel_id=1, source_target_pairs={{0,2},{2,4},{4,6},{1,3},{3,5},{5,7},{8,10},{10,12},{12,14},{9,11},... | collective-permute-start | bytes 786440 | tf_op jit(solution)/shard_map/ppermute | solution.py:40
  22.0 1.3 %collective-permute-start.9 = (f32[2,256,128]{2,1,0:T(8,128)S(1)}, f32[2,256,128]{2,1,0:T(8,128)S(1)}, u32[]{:S(2)}, u32[]{:S(2)}) collective-permute-start(f32[2,256,128]{2,1,0:T(8,128)S(1)} %collective-permute-done.4), channel_id=1, source_target_pairs={{2,0},{4,2},{6,4},{3,1},{5,3},{7,5},{10,8},{12,10},{14,12},{11,9},... | collective-permute-start | bytes 786440 | tf_op jit(solution)/shard_map/ppermute | solution.py:40
  23.3 2.7 %collective-permute-start.5 = (f32[2,32,128]{2,1,0:T(8,128)S(1)}, f32[2,32,128]{2,1,0:T(8,128)S(1)}, u32[]{:S(2)}, u32[]{:S(2)}) collective-permute-start(f32[2,32,128]{2,1,0:T(8,128)S(1)} %get-tuple-element.36), channel_id=1, source_target_pairs={{0,2},{2,4},{4,6},{6,0},{1,3},{3,5},{5,7},{7,1},{8,10},{10,12},{12... | collective-permute-start | bytes 98312 | tf_op jit(solution)/shard_map/ppermute | solution.py:16
  26.0 2.6 %collective-permute-start.6 = (f32[2,32,128]{2,1,0:T(8,128)S(1)}, f32[2,32,128]{2,1,0:T(8,128)S(1)}, u32[]{:S(2)}, u32[]{:S(2)}) collective-permute-start(f32[2,32,128]{2,1,0:T(8,128)S(1)} %get-tuple-element.35), channel_id=1, source_target_pairs={{0,4},{2,6},{4,0},{6,2},{1,5},{3,7},{5,1},{7,3},{8,12},{10,14},{12... | collective-permute-start | bytes 98312 | tf_op jit(solution)/shard_map/ppermute | solution.py:16
  28.6 1.3 %collective-permute-start.7 = (f32[2,32,128]{2,1,0:T(8,128)S(1)}, f32[2,32,128]{2,1,0:T(8,128)S(1)}, u32[]{:S(2)}, u32[]{:S(2)}) collective-permute-start(f32[2,32,128]{2,1,0:T(8,128)S(1)} %get-tuple-element.34), channel_id=1, source_target_pairs={{0,6},{2,0},{4,2},{6,4},{1,7},{3,1},{5,3},{7,5},{8,14},{10,8},{12,... | collective-permute-start | bytes 98312 | tf_op jit(solution)/shard_map/ppermute | solution.py:16
  29.9 0.1 shift-left_or_fusion
  30.0 0.1 reshape.92
  30.1 0.9 %multiply_reduce_fusion.1 = f32[2,128]{1,0:T(2,128)S(1)} fusion(f32[2,128,512]{2,1,0:T(8,128)} %param.6, s32[]{:T(128)S(6)} %select_n.273), kind=kLoop, calls=%fused_computation.21 | loop fusion | flops 65280 | bytes 132100 | tf_op jit(solution)/shard_map/reduce_sum | solution.py:96
  31.0 3.5 %collective-permute-done.5 = f32[2,32,128]{2,1,0:T(8,128)S(1)} collective-permute-done((f32[2,32,128]{2,1,0:T(8,128)S(1)}, f32[2,32,128]{2,1,0:T(8,128)S(1)}, u32[]{:S(2)}, u32[]{:S(2)}) %collective-permute-start.5) | collective-permute-done | bytes 32800 | tf_op jit(solution)/shard_map/ppermute | solution.py:16
  34.6 0.2 collective-permute-start.12
  34.8 1.5 %collective-permute-start.13 = (f32[4,2,32,128]{3,2,1,0:T(8,128)S(1)}, f32[4,2,32,128]{3,2,1,0:T(8,128)S(1)}, u32[]{:S(2)}, u32[]{:S(2)}) collective-permute-start(f32[4,2,32,128]{3,2,1,0:T(8,128)S(1)} %get-tuple-element.33), channel_id=1, source_target_pairs={{0,16},{8,24},{16,0},{24,8},{1,17},{9,25},{17,1},{25,9},{2,18},{10... | collective-permute-start | bytes 393224 | tf_op jit(solution)/shard_map/ppermute | solution.py:16
  36.3 2.8 %collective-permute-start.14 = (f32[4,2,32,128]{3,2,1,0:T(8,128)S(1)}, f32[4,2,32,128]{3,2,1,0:T(8,128)S(1)}, u32[]{:S(2)}, u32[]{:S(2)}) collective-permute-start(f32[4,2,32,128]{3,2,1,0:T(8,128)S(1)} %get-tuple-element.33), channel_id=1, source_target_pairs={{0,24},{8,0},{16,8},{24,16},{1,25},{9,1},{17,9},{25,17},{2,26},{10... | collective-permute-start | bytes 393224 | tf_op jit(solution)/shard_map/ppermute | solution.py:16
  39.1 2.8 %collective-permute-start.11 = (f32[2,256,128]{2,1,0:T(8,128)S(1)}, f32[2,256,128]{2,1,0:T(8,128)S(1)}, u32[]{:S(2)}, u32[]{:S(2)}) collective-permute-start(f32[2,256,128]{2,1,0:T(8,128)S(1)} %collective-permute-done.8), channel_id=1, source_target_pairs={{0,2},{2,4},{4,6},{1,3},{3,5},{5,7},{8,10},{10,12},{12,14},{9,11},... | collective-permute-start | bytes 786440 | tf_op jit(solution)/shard_map/ppermute | solution.py:40
  41.9 1.3 %collective-permute-start.10 = (f32[2,256,128]{2,1,0:T(8,128)S(1)}, f32[2,256,128]{2,1,0:T(8,128)S(1)}, u32[]{:S(2)}, u32[]{:S(2)}) collective-permute-start(f32[2,256,128]{2,1,0:T(8,128)S(1)} %collective-permute-done.9), channel_id=1, source_target_pairs={{2,0},{4,2},{6,4},{3,1},{5,3},{7,5},{10,8},{12,10},{14,12},{11,9},... | collective-permute-start | bytes 786440 | tf_op jit(solution)/shard_map/ppermute | solution.py:40
  43.4 0.7 %gather_fusion.1 = f32[32,32,128]{2,1,0:T(8,128)S(1)} fusion(f32[4,4,2,32,128]{4,3,2,1,0:T(8,128)S(1)} %pad_maximum_fusion, s32[32]{0:T(128)S(1)} %reshape.92), kind=kCustom, calls=%fused_computation.1 | custom fusion | bytes 1048960 | tf_op jit(solution)/shard_map/gather | solution.py:81
  44.1 0.1 collective-permute-start.16
  44.2 1.6 %collective-permute-done.11 = f32[2,256,128]{2,1,0:T(8,128)S(1)} collective-permute-done((f32[2,256,128]{2,1,0:T(8,128)S(1)}, f32[2,256,128]{2,1,0:T(8,128)S(1)}, u32[]{:S(2)}, u32[]{:S(2)}) %collective-permute-start.11) | collective-permute-done | bytes 262176 | tf_op jit(solution)/shard_map/ppermute | solution.py:40
  45.8 4.4 %collective-permute-done.10 = f32[2,256,128]{2,1,0:T(8,128)S(1)} collective-permute-done((f32[2,256,128]{2,1,0:T(8,128)S(1)}, f32[2,256,128]{2,1,0:T(8,128)S(1)}, u32[]{:S(2)}, u32[]{:S(2)}) %collective-permute-start.10) | collective-permute-done | bytes 262176 | tf_op jit(solution)/shard_map/ppermute | solution.py:40
  50.2 1.1 %convolution_bitcast_fusion = f32[2,256,128]{2,1,0:T(8,128)S(1)} fusion(f32[2,4,128,128]{3,2,1,0:T(8,128)S(1)} %bitcast.56, f32[1,2,256,128]{3,2,0,1:T(8,128)S(1)} %select_bitcast_fusion, f32[1,2,256,128]{3,2,0,1:T(8,128)S(1)} %select_bitcast_fusion.1, f32[1,2,256,128]{3,2,0,1:T(8,128)S(1)} %select_bitcast_fusion.2, f32[1,2,256,128]{3,2,0,1:T(8,128)S(1)} %bitcast.70), kind=kOutput, calls=%fused_computation.2 | convolution fusion | flops 403439616 | bytes 1835008 | tf_op jit(solution)/shard_map/dsij,sdjk->sik/dot_general | solution.py:85
  51.3 0.1 collective-permute-start.15
  51.5 1.4 %collective-permute-done.15 = f32[2,256,128]{2,1,0:T(8,128)S(1)} collective-permute-done((f32[2,256,128]{2,1,0:T(8,128)S(1)}, f32[2,256,128]{2,1,0:T(8,128)S(1)}, u32[]{:S(2)}, u32[]{:S(2)}) %collective-permute-start.15) | collective-permute-done | bytes 262176 | tf_op jit(solution)/shard_map/ppermute | solution.py:16
  52.9 0.1 multiply_reduce_fusion
  53.1 0.1 collective-permute-start.17
  53.1 2.3 %collective-permute-start.18 = (f32[2,40,128]{2,1,0:T(8,128)S(1)}, f32[2,40,128]{2,1,0:T(8,128)S(1)}, u32[]{:S(2)}, u32[]{:S(2)}) collective-permute-start(f32[2,40,128]{2,1,0:T(8,128)S(1)} %get-tuple-element.39), channel_id=1, source_target_pairs={{0,4},{2,6},{4,0},{6,2},{1,5},{3,7},{5,1},{7,3},{8,12},{10,14},{12... | collective-permute-start | bytes 122888 | tf_op jit(solution)/shard_map/ppermute | solution.py:16
  55.5 0.3 collective-permute-start.19
  55.7 1.9 %collective-permute-done.17 = f32[2,40,128]{2,1,0:T(8,128)S(1)} collective-permute-done((f32[2,40,128]{2,1,0:T(8,128)S(1)}, f32[2,40,128]{2,1,0:T(8,128)S(1)}, u32[]{:S(2)}, u32[]{:S(2)}) %collective-permute-start.17) | collective-permute-done | bytes 40992 | tf_op jit(solution)/shard_map/ppermute | solution.py:16
  57.6 1.0 %collective-permute-done.18 = f32[2,40,128]{2,1,0:T(8,128)S(1)} collective-permute-done((f32[2,40,128]{2,1,0:T(8,128)S(1)}, f32[2,40,128]{2,1,0:T(8,128)S(1)}, u32[]{:S(2)}, u32[]{:S(2)}) %collective-permute-start.18) | collective-permute-done | bytes 40992 | tf_op jit(solution)/shard_map/ppermute | solution.py:16
  58.6 2.7 %collective-permute-done.19 = f32[2,40,128]{2,1,0:T(8,128)S(1)} collective-permute-done((f32[2,40,128]{2,1,0:T(8,128)S(1)}, f32[2,40,128]{2,1,0:T(8,128)S(1)}, u32[]{:S(2)}, u32[]{:S(2)}) %collective-permute-start.19) | collective-permute-done | bytes 40992 | tf_op jit(solution)/shard_map/ppermute | solution.py:16
  61.4 0.6 collective-permute-start.21
  62.0 2.8 %collective-permute-start.22 = (f32[2,512]{1,0:T(2,128)S(1)}, f32[2,512]{1,0:T(2,128)S(1)}, u32[]{:S(2)}, u32[]{:S(2)}) collective-permute-start(f32[2,512]{1,0:T(2,128)S(1)} %bitcast.69), channel_id=1, source_target_pairs={{0,24},{8,0},{16,8},{24,16},{1,25},{9,1},{17,9},{25,17},{2,26},{10... | collective-permute-start | bytes 12296 | tf_op jit(solution)/shard_map/ppermute | solution.py:16
  64.8 0.7 slice_negate_fusion
  65.5 0.4 collective-permute-done.20
  65.9 0.6 collective-permute-done.22
  66.5 0.6 add_add_fusion.1
  (43 shorter events, 0.6 us)
Async XLA Ops:
  0.6 6.5 %copy-start = (f32[2,128,512]{2,1,0:T(8,128)S(1)}, f32[2,128,512]{2,1,0:T(8,128)}, u32[]{:S(2)}) copy-start(f32[2,128,512]{2,1,0:T(8,128)} %param.5) | copy-start | bytes 1572868
  0.6 17.0 %collective-permute-start.3 = (f32[2,256,128]{2,1,0:T(8,128)}, f32[2,256,128]{2,1,0:T(8,128)S(1)}, u32[]{:S(2)}, u32[]{:S(2)}) collective-permute-start(f32[2,256,128]{2,1,0:T(8,128)} %param.4), channel_id=1, source_target_pairs={{0,2},{2,4},{4,6},{1,3},{3,5},{5,7},{8,10},{10,12},{12,14},{9,11},... | collective-permute-start | bytes 786440 | tf_op jit(solution)/shard_map/ppermute | solution.py:40
  5.7 11.9 %collective-permute-start.4 = (f32[2,256,128]{2,1,0:T(8,128)}, f32[2,256,128]{2,1,0:T(8,128)S(1)}, u32[]{:S(2)}, u32[]{:S(2)}) collective-permute-start(f32[2,256,128]{2,1,0:T(8,128)} %param.4), channel_id=1, source_target_pairs={{2,0},{4,2},{6,4},{3,1},{5,3},{7,5},{10,8},{12,10},{14,12},{11,9},... | collective-permute-start | bytes 786440 | tf_op jit(solution)/shard_map/ppermute | solution.py:40
  8.8 7.2 %collective-permute-start = (f32[2,32,512]{2,1,0:T(8,128)S(1)}, f32[2,32,512]{2,1,0:T(8,128)S(1)}, u32[]{:S(2)}, u32[]{:S(2)}) collective-permute-start(f32[2,32,512]{2,1,0:T(8,128)S(1)} %get-tuple-element.22), channel_id=1, source_target_pairs={{0,8},{8,16},{16,24},{24,0},{1,9},{9,17},{17,25},{25,1},{2,10},{10... | collective-permute-start | bytes 393224 | tf_op jit(solution)/shard_map/ppermute | solution.py:16
  10.3 7.2 %collective-permute-start.1 = (f32[2,32,512]{2,1,0:T(8,128)S(1)}, f32[2,32,512]{2,1,0:T(8,128)S(1)}, u32[]{:S(2)}, u32[]{:S(2)}) collective-permute-start(f32[2,32,512]{2,1,0:T(8,128)S(1)} %get-tuple-element.24), channel_id=1, source_target_pairs={{0,16},{8,24},{16,0},{24,8},{1,17},{9,25},{17,1},{25,9},{2,18},{10... | collective-permute-start | bytes 393224 | tf_op jit(solution)/shard_map/ppermute | solution.py:16
  11.8 5.7 %collective-permute-start.2 = (f32[2,32,512]{2,1,0:T(8,128)S(1)}, f32[2,32,512]{2,1,0:T(8,128)S(1)}, u32[]{:S(2)}, u32[]{:S(2)}) collective-permute-start(f32[2,32,512]{2,1,0:T(8,128)S(1)} %get-tuple-element.23), channel_id=1, source_target_pairs={{0,24},{8,0},{16,8},{24,16},{1,25},{9,1},{17,9},{25,17},{2,26},{10... | collective-permute-start | bytes 393224 | tf_op jit(solution)/shard_map/ppermute | solution.py:16
  13.3 0.7 %copy-start.1 = (s32[2,4]{1,0:T(2,128)S(1)}, s32[2,4]{1,0:T(2,128)}, u32[]{:S(2)}) copy-start(s32[2,4]{1,0:T(2,128)} %param.7) | copy-start | bytes 100
  17.6 17.0 %collective-permute-start.8 = (f32[2,256,128]{2,1,0:T(8,128)S(1)}, f32[2,256,128]{2,1,0:T(8,128)S(1)}, u32[]{:S(2)}, u32[]{:S(2)}) collective-permute-start(f32[2,256,128]{2,1,0:T(8,128)S(1)} %collective-permute-done.3), channel_id=1, source_target_pairs={{0,2},{2,4},{4,6},{1,3},{3,5},{5,7},{8,10},{10,12},{12,14},{9,11},... | collective-permute-start | bytes 786440 | tf_op jit(solution)/shard_map/ppermute | solution.py:40
  22.0 12.6 %collective-permute-start.9 = (f32[2,256,128]{2,1,0:T(8,128)S(1)}, f32[2,256,128]{2,1,0:T(8,128)S(1)}, u32[]{:S(2)}, u32[]{:S(2)}) collective-permute-start(f32[2,256,128]{2,1,0:T(8,128)S(1)} %collective-permute-done.4), channel_id=1, source_target_pairs={{2,0},{4,2},{6,4},{3,1},{5,3},{7,5},{10,8},{12,10},{14,12},{11,9},... | collective-permute-start | bytes 786440 | tf_op jit(solution)/shard_map/ppermute | solution.py:40
  23.3 11.3 %collective-permute-start.5 = (f32[2,32,128]{2,1,0:T(8,128)S(1)}, f32[2,32,128]{2,1,0:T(8,128)S(1)}, u32[]{:S(2)}, u32[]{:S(2)}) collective-permute-start(f32[2,32,128]{2,1,0:T(8,128)S(1)} %get-tuple-element.36), channel_id=1, source_target_pairs={{0,2},{2,4},{4,6},{6,0},{1,3},{3,5},{5,7},{7,1},{8,10},{10,12},{12... | collective-permute-start | bytes 98312 | tf_op jit(solution)/shard_map/ppermute | solution.py:16
  26.0 8.6 %collective-permute-start.6 = (f32[2,32,128]{2,1,0:T(8,128)S(1)}, f32[2,32,128]{2,1,0:T(8,128)S(1)}, u32[]{:S(2)}, u32[]{:S(2)}) collective-permute-start(f32[2,32,128]{2,1,0:T(8,128)S(1)} %get-tuple-element.35), channel_id=1, source_target_pairs={{0,4},{2,6},{4,0},{6,2},{1,5},{3,7},{5,1},{7,3},{8,12},{10,14},{12... | collective-permute-start | bytes 98312 | tf_op jit(solution)/shard_map/ppermute | solution.py:16
  28.6 6.0 %collective-permute-start.7 = (f32[2,32,128]{2,1,0:T(8,128)S(1)}, f32[2,32,128]{2,1,0:T(8,128)S(1)}, u32[]{:S(2)}, u32[]{:S(2)}) collective-permute-start(f32[2,32,128]{2,1,0:T(8,128)S(1)} %get-tuple-element.34), channel_id=1, source_target_pairs={{0,6},{2,0},{4,2},{6,4},{1,7},{3,1},{5,3},{7,5},{8,14},{10,8},{12,... | collective-permute-start | bytes 98312 | tf_op jit(solution)/shard_map/ppermute | solution.py:16
  34.6 8.6 %collective-permute-start.12 = (f32[4,2,32,128]{3,2,1,0:T(8,128)S(1)}, f32[4,2,32,128]{3,2,1,0:T(8,128)S(1)}, u32[]{:S(2)}, u32[]{:S(2)}) collective-permute-start(f32[4,2,32,128]{3,2,1,0:T(8,128)S(1)} %get-tuple-element.33), channel_id=1, source_target_pairs={{0,8},{8,16},{16,24},{24,0},{1,9},{9,17},{17,25},{25,1},{2,10},{10... | collective-permute-start | bytes 393224 | tf_op jit(solution)/shard_map/ppermute | solution.py:16
  34.8 8.5 %collective-permute-start.13 = (f32[4,2,32,128]{3,2,1,0:T(8,128)S(1)}, f32[4,2,32,128]{3,2,1,0:T(8,128)S(1)}, u32[]{:S(2)}, u32[]{:S(2)}) collective-permute-start(f32[4,2,32,128]{3,2,1,0:T(8,128)S(1)} %get-tuple-element.33), channel_id=1, source_target_pairs={{0,16},{8,24},{16,0},{24,8},{1,17},{9,25},{17,1},{25,9},{2,18},{10... | collective-permute-start | bytes 393224 | tf_op jit(solution)/shard_map/ppermute | solution.py:16
  36.3 7.0 %collective-permute-start.14 = (f32[4,2,32,128]{3,2,1,0:T(8,128)S(1)}, f32[4,2,32,128]{3,2,1,0:T(8,128)S(1)}, u32[]{:S(2)}, u32[]{:S(2)}) collective-permute-start(f32[4,2,32,128]{3,2,1,0:T(8,128)S(1)} %get-tuple-element.33), channel_id=1, source_target_pairs={{0,24},{8,0},{16,8},{24,16},{1,25},{9,1},{17,9},{25,17},{2,26},{10... | collective-permute-start | bytes 393224 | tf_op jit(solution)/shard_map/ppermute | solution.py:16
  39.1 6.7 %collective-permute-start.11 = (f32[2,256,128]{2,1,0:T(8,128)S(1)}, f32[2,256,128]{2,1,0:T(8,128)S(1)}, u32[]{:S(2)}, u32[]{:S(2)}) collective-permute-start(f32[2,256,128]{2,1,0:T(8,128)S(1)} %collective-permute-done.8), channel_id=1, source_target_pairs={{0,2},{2,4},{4,6},{1,3},{3,5},{5,7},{8,10},{10,12},{12,14},{9,11},... | collective-permute-start | bytes 786440 | tf_op jit(solution)/shard_map/ppermute | solution.py:40
  41.9 8.3 %collective-permute-start.10 = (f32[2,256,128]{2,1,0:T(8,128)S(1)}, f32[2,256,128]{2,1,0:T(8,128)S(1)}, u32[]{:S(2)}, u32[]{:S(2)}) collective-permute-start(f32[2,256,128]{2,1,0:T(8,128)S(1)} %collective-permute-done.9), channel_id=1, source_target_pairs={{2,0},{4,2},{6,4},{3,1},{5,3},{7,5},{10,8},{12,10},{14,12},{11,9},... | collective-permute-start | bytes 786440 | tf_op jit(solution)/shard_map/ppermute | solution.py:40
  44.1 7.3 %collective-permute-start.16 = (f32[2,1,128,128]{3,2,0,1:T(8,128)S(1)}, f32[2,1,128,128]{3,2,0,1:T(8,128)S(1)}, u32[]{:S(2)}, u32[]{:S(2)}) collective-permute-start(f32[2,1,128,128]{3,2,0,1:T(8,128)S(1)} %dynamic-slice_bitcast_fusion), channel_id=1, source_target_pairs={{0,1},{1,0},{2,3},{3,2},{4,5},{5,4},{6,7},{7,6},{8,9},{9,8},{10,11... | collective-permute-start | bytes 393224 | tf_op jit(solution)/shard_map/ppermute | solution.py:16
  45.8 4.4 %copy-start.2 = (f32[2,256,128]{2,1,0:T(8,128)S(1)}, f32[2,256,128]{2,1,0:T(8,128)}, u32[]{:S(2)}) copy-start(f32[2,256,128]{2,1,0:T(8,128)} %param.4) | copy-start | bytes 786436
  51.3 1.6 %collective-permute-start.15 = (f32[2,256,128]{2,1,0:T(8,128)S(1)}, f32[2,256,128]{2,1,0:T(8,128)S(1)}, u32[]{:S(2)}, u32[]{:S(2)}) collective-permute-start(f32[2,256,128]{2,1,0:T(8,128)S(1)} %convolution_bitcast_fusion), channel_id=1, source_target_pairs={{0,1},{1,0},{2,3},{3,2},{4,5},{5,4},{6,7},{7,6},{8,9},{9,8},{10,11... | collective-permute-start | bytes 786440 | tf_op jit(solution)/shard_map/ppermute | solution.py:16
  53.1 4.5 %collective-permute-start.17 = (f32[2,40,128]{2,1,0:T(8,128)S(1)}, f32[2,40,128]{2,1,0:T(8,128)S(1)}, u32[]{:S(2)}, u32[]{:S(2)}) collective-permute-start(f32[2,40,128]{2,1,0:T(8,128)S(1)} %get-tuple-element.40), channel_id=1, source_target_pairs={{0,6},{2,0},{4,2},{6,4},{1,7},{3,1},{5,3},{7,5},{8,14},{10,8},{12,... | collective-permute-start | bytes 122888 | tf_op jit(solution)/shard_map/ppermute | solution.py:16
  53.1 5.4 %collective-permute-start.18 = (f32[2,40,128]{2,1,0:T(8,128)S(1)}, f32[2,40,128]{2,1,0:T(8,128)S(1)}, u32[]{:S(2)}, u32[]{:S(2)}) collective-permute-start(f32[2,40,128]{2,1,0:T(8,128)S(1)} %get-tuple-element.39), channel_id=1, source_target_pairs={{0,4},{2,6},{4,0},{6,2},{1,5},{3,7},{5,1},{7,3},{8,12},{10,14},{12... | collective-permute-start | bytes 122888 | tf_op jit(solution)/shard_map/ppermute | solution.py:16
  55.5 5.8 %collective-permute-start.19 = (f32[2,40,128]{2,1,0:T(8,128)S(1)}, f32[2,40,128]{2,1,0:T(8,128)S(1)}, u32[]{:S(2)}, u32[]{:S(2)}) collective-permute-start(f32[2,40,128]{2,1,0:T(8,128)S(1)} %get-tuple-element.38), channel_id=1, source_target_pairs={{0,2},{2,4},{4,6},{6,0},{1,3},{3,5},{5,7},{7,1},{8,10},{10,12},{12... | collective-permute-start | bytes 122888 | tf_op jit(solution)/shard_map/ppermute | solution.py:16
  61.3 4.6 %collective-permute-start.20 = (f32[2,512]{1,0:T(2,128)S(1)}, f32[2,512]{1,0:T(2,128)S(1)}, u32[]{:S(2)}, u32[]{:S(2)}) collective-permute-start(f32[2,512]{1,0:T(2,128)S(1)} %bitcast.67), channel_id=1, source_target_pairs={{0,8},{8,16},{16,24},{24,0},{1,9},{9,17},{17,25},{25,1},{2,10},{10... | collective-permute-start | bytes 12296 | tf_op jit(solution)/shard_map/ppermute | solution.py:16
  61.4 4.5 %collective-permute-start.21 = (f32[2,512]{1,0:T(2,128)S(1)}, f32[2,512]{1,0:T(2,128)S(1)}, u32[]{:S(2)}, u32[]{:S(2)}) collective-permute-start(f32[2,512]{1,0:T(2,128)S(1)} %bitcast.68), channel_id=1, source_target_pairs={{0,16},{8,24},{16,0},{24,8},{1,17},{9,25},{17,1},{25,9},{2,18},{10... | collective-permute-start | bytes 12296 | tf_op jit(solution)/shard_map/ppermute | solution.py:16
  62.0 4.5 %collective-permute-start.22 = (f32[2,512]{1,0:T(2,128)S(1)}, f32[2,512]{1,0:T(2,128)S(1)}, u32[]{:S(2)}, u32[]{:S(2)}) collective-permute-start(f32[2,512]{1,0:T(2,128)S(1)} %bitcast.69), channel_id=1, source_target_pairs={{0,24},{8,0},{16,8},{24,16},{1,25},{9,1},{17,9},{25,17},{2,26},{10... | collective-permute-start | bytes 12296 | tf_op jit(solution)/shard_map/ppermute | solution.py:16

commit v9 on v7

--- a/solution.py
+++ b/solution.py
@@ -1,9 +1,35 @@
+import functools
+
 import jax
 import jax.numpy as jnp
 from jax import lax
+from jax.experimental import pallas as pl
+from jax.experimental.pallas import tpu as pltpu
 from jax.sharding import Mesh, PartitionSpec as P
 
 B = 256
+
+
+def multiply_tiles(deep, rows, place, *refs):
+    far, slots, (out_ref, spread) = refs[:deep], refs[deep : deep + rows], refs[deep + rows :]
+    groups, height, chunk = far[0].shape
+    piece = slots[0].shape[2]
+    for s in range(groups):
+        for d in range(deep):
+            slot = place[s * deep + d]
+            for e in range(rows):
+                first = pl.multiple_of(place[groups * deep + e] * piece, piece)
+                spread[s, d, pl.ds(first, piece)] = slots[e][slot, s]
+    tiles = (out_ref.shape[1] - height) // chunk
+    for s in range(groups):
+        wide = jnp.concatenate([piece_ref[s] for piece_ref in far], axis=1)
+        tall = spread[s].reshape(deep * chunk, spread.shape[3])
+        out_ref[s, :height] = jnp.dot(
+            wide, tall, precision=lax.Precision.HIGHEST, preferred_element_type=jnp.float32
+        )
+        for t in range(tiles):
+            own = spread[s, place[groups * deep + rows + t]]
+            out_ref[s, height + t * chunk : height + (t + 1) * chunk] = own
 
 
 def solution(mesh):
@@ -45,10 +71,9 @@
         def rows_of(r):
             return lax.dynamic_slice_in_dim(partial, r * piece, piece, axis=1)
 
-        scaled = rows_of(row)
-        for shift in range(1, rows):
-            scaled = scaled + shifted(rows_of((row + shift) % rows), "row", rows, shift)
-        scaled, far = lax.optimization_barrier((scaled, far))
+        sums = [shifted(rows_of((row + d) % rows), "row", rows, d) for d in range(1, rows)]
+        sums[0], far = lax.optimization_barrier((sums[0], far))
+        scaled = sum(sums, rows_of(row))
 
         def columns_of(array, c):
             return lax.dynamic_slice_in_dim(array, c * part, part, axis=2)
@@ -59,30 +84,35 @@
         if deep > 1:
             slots[1], held_back = lax.optimization_barrier((slots[1], ancestor))
             far |= {d: shifted(held_back, "z", deep, d) for d in late}
-            slots, far[1] = lax.optimization_barrier((slots, far[1]))
-        scaled = jnp.stack(gathered(jnp.stack(slots), "row", rows))
+        slots = gathered(jnp.stack(slots), "row", rows)
 
         count = jnp.arange(deep, dtype=jnp.int32)
+        at = (z - count) % deep
         stored = jnp.sum(
-            jnp.where(pattern[:, :, None] == count, count[:, None], 0), axis=1, dtype=jnp.int32
+            jnp.where(pattern[:, :, None] == at, count[:, None], 0), axis=1, dtype=jnp.int32
         )
-        from_z = (z - jnp.take(stored, (z - count) % deep, axis=1, mode="clip")) % deep
-        from_row = (row - jnp.arange(rows, dtype=jnp.int32)) % rows
-        group = jnp.arange(groups, dtype=jnp.int32)
-        spread = scaled[from_row, from_z[:, :, None], group[:, None, None]]
-        spread = spread.reshape(groups, deep, chunk, part)
-        wide = jnp.stack([ancestor] + [far[d] for d in range(1, deep)])
-        product = jnp.einsum("dsij,sdjk->sik", wide, spread, precision=highest)
-        product = product + shifted(product, "core", cores, 1)
+        from_z = ((z - stored) % deep).reshape(-1)
+        quarter = (row - jnp.arange(rows, dtype=jnp.int32)) % rows
+        own_tile = (z - row * tiles - jnp.arange(tiles, dtype=jnp.int32)) % deep
+        place = jnp.concatenate([from_z, quarter, own_tile])
+        height = ancestor.shape[1]
+        whole = pl.BlockSpec(memory_space=pltpu.VMEM)
+        product = pl.pallas_call(
+            functools.partial(multiply_tiles, deep, rows),
+            out_shape=jax.ShapeDtypeStruct((groups, height + tiles * chunk, part), jnp.float32),
+            in_specs=[pl.BlockSpec(memory_space=pltpu.SMEM)] + [whole] * (deep + rows),
+            out_specs=whole,
+            scratch_shapes=[pltpu.VMEM((groups, deep, chunk, part), jnp.float32)],
+            compiler_params=pltpu.CompilerParams(vmem_limit_bytes=32 * 1024 * 1024),
+        )(place, ancestor, *[far[d] for d in range(1, deep)], *slots)
+        other = shifted(product, "core", cores, 1)
 
-        own = [
-            lax.dynamic_index_in_dim(spread, (z - (row * tiles + t)) % deep, 1, keepdims=False)
-            for t in range(tiles)
+        own, own_other = [
+            array[:, height:].reshape(groups, tiles, chunk, part) for array in (product, other)
         ]
-        own = jnp.stack(own, axis=1)
-        other = shifted(own, "core", cores, 1)
-        halves = [jnp.where(core == 0, own, other), jnp.where(core == 0, other, own)]
-        own = jnp.stack(halves, axis=2).reshape(groups, -1, part)
+        product = product[:, :height] + other[:, :height]
+        halves = [jnp.where(core == 0, own, own_other), jnp.where(core == 0, own_other, own)]
+        own = jnp.stack(halves, axis=2).reshape(groups, height, part)
         squares = jnp.sum(columns_of(factor_inv, z) ** 2, axis=1)
         term = jnp.sum(own * product, axis=1) + squares
         tail = jnp.broadcast_to(term[:, None], (groups, 8, part))

time: 66.4 us -> 58.8 us (0.89)
  waiting for transfers between devices: 32.7 us -> 21.7 us
  starting transfers between devices: 24.4 us -> 28.3 us
  Pallas kernels: 0 us -> 1.61 us
  matrix products: 2.68 us -> 1.62 us
  local copies, waits for them, and re-layouts: 2.66 us -> 1.87 us
    ppermute x20 -> x19, waiting for transfers between devices: 32.7 us -> 21.7 us  [shifted(): lax.ppermute(array, axis, [(i, (i + shift) % size) for i in range(size)])]
    ppermute x20 -> x19, starting transfers between devices: 24.4 us -> 28.3 us  [shifted(): lax.ppermute(array, axis, [(i, (i + shift) % size) for i in range(size)])]
    pallas_call x0 -> x1, Pallas kernels: none -> 1.61 us  [per_device(): pl.pallas_call(functools.partial(multiply_tiles, deep, rows), out_shape=j...]
    gather x2 -> x0, local copies, waits for them, and re-layouts: 1.27 us -> none  [the longest x1 0.71 us: per_device(): spread = scaled[from_row, from_z[:, :, None], group[:, None, None]]]
    dot_general x1 -> x0, matrix products: 1.06 us -> none  [per_device(): product = jnp.einsum('dsij,sdjk->sik', wide, spread, precision=highest)]
    unnamed x7, local copies, waits for them, and re-layouts: 1.01 us -> 1.67 us
  transfers between devices with their start and end apart: 20 -> 19, of which waited for: 15 -> 11; matrix products, arithmetic and copies ran while one was open for 7% -> 3% of each run, Pallas kernels for 0% -> 0%
where the time goes in v9:
time: 58.8 us; the launch traced here: 58.6 us
  starting transfers between devices  28.3 us (48%)
  waiting for transfers between devices  21.7 us (37%)
  other arithmetic  2.64 us (4%)
  local copies, waits for them, and re-layouts  1.87 us (3%)
  matrix products  1.62 us (3%)
  Pallas kernels  1.61 us (3%)
  between operations  0.92 us (2%)
    ppermute x19, starting transfers between devices, shifted(): lax.ppermute(array, axis, [(i, (i + shift) % size) for i in range(size)])  28.3 us
    ppermute x19, waiting for transfers between devices, shifted(): lax.ppermute(array, axis, [(i, (i + shift) % size) for i in range(size)])  21.7 us
    unnamed x7, local copies, waits for them, and re-layouts  1.67 us
    dot_general x1, matrix products, per_device(): partial = jnp.einsum('srw,swv->srv', mine, factor_inv, precision=highest)  1.62 us
    pallas_call x1, Pallas kernels, per_device(): pl.pallas_call(functools.partial(multiply_tiles, deep, rows), out_shape=j...  1.61 us
  transfers between devices with their start and end apart: 19, of which 11 were waited for; matrix products, arithmetic and copies ran while one was open for 3% of the time, Pallas kernels for 0%

profile of v9, /device:TPU:0, one launch (start us, length us, event | category | flops | bytes accessed | tf_op | source)
XLA Modules:
  0.0 58.6 jit_solution(16613821164815316210)
XLA Ops:
  0.6 0.0 copy-start
  0.7 1.0 %copy-done = f32[2,128,512]{2,1,0:T(8,128)S(1)} copy-done((f32[2,128,512]{2,1,0:T(8,128)S(1)}, f32[2,128,512]{2,1,0:T(8,128)}, u32[]{:S(2)}) %copy-start) | copy-done | bytes 524312
  1.7 1.6 %fusion = f32[2,128,512]{2,1,0:T(8,128)S(1)} fusion(f32[2,128,512]{2,1,0:T(8,128)} %param.6, f32[2,128,512]{2,1,0:T(8,128)S(1)} %copy-done, s32[]{:T(128)S(6)} %select_n.231), kind=kOutput, calls=%fused_computation.10 | convolution fusion | flops 201326592 | bytes 1179652 | tf_op jit(solution)/shard_map/srw,swv->srv/dot_general | solution.py:69
  3.3 0.0 copy-start.1
  3.4 3.0 %collective-permute-start = (f32[2,32,512]{2,1,0:T(8,128)S(1)}, f32[2,32,512]{2,1,0:T(8,128)S(1)}, u32[]{:S(2)}, u32[]{:S(2)}) collective-permute-start(f32[2,32,512]{2,1,0:T(8,128)S(1)} %get-tuple-element.14), channel_id=1, source_target_pairs={{0,8},{8,16},{16,24},{24,0},{1,9},{9,17},{17,25},{25,1},{2,10},{10... | collective-permute-start | bytes 393224 | tf_op jit(solution)/shard_map/ppermute | solution.py:42
  6.4 2.6 %collective-permute-start.1 = (f32[2,256,128]{2,1,0:T(8,128)S(1)}, f32[2,256,128]{2,1,0:T(8,128)S(1)}, u32[]{:S(2)}, u32[]{:S(2)}) collective-permute-start(f32[2,256,128]{2,1,0:T(8,128)S(1)} %copy-done.1), channel_id=1, source_target_pairs={{0,4},{2,6},{4,0},{6,2},{1,5},{3,7},{5,1},{7,3},{8,12},{10,14},{12... | collective-permute-start | bytes 786440 | tf_op jit(solution)/shard_map/ppermute | solution.py:42
  8.9 1.5 %collective-permute-start.2 = (f32[2,32,512]{2,1,0:T(8,128)S(1)}, f32[2,32,512]{2,1,0:T(8,128)S(1)}, u32[]{:S(2)}, u32[]{:S(2)}) collective-permute-start(f32[2,32,512]{2,1,0:T(8,128)S(1)} %get-tuple-element.16), channel_id=1, source_target_pairs={{0,16},{8,24},{16,0},{24,8},{1,17},{9,25},{17,1},{25,9},{2,18},{10... | collective-permute-start | bytes 393224 | tf_op jit(solution)/shard_map/ppermute | solution.py:42
  10.5 1.4 %collective-permute-start.3 = (f32[2,32,512]{2,1,0:T(8,128)S(1)}, f32[2,32,512]{2,1,0:T(8,128)S(1)}, u32[]{:S(2)}, u32[]{:S(2)}) collective-permute-start(f32[2,32,512]{2,1,0:T(8,128)S(1)} %get-tuple-element.15), channel_id=1, source_target_pairs={{0,24},{8,0},{16,8},{24,16},{1,25},{9,1},{17,9},{25,17},{2,26},{10... | collective-permute-start | bytes 393224 | tf_op jit(solution)/shard_map/ppermute | solution.py:42
  11.9 0.7 %copy-done.2 = s32[2,4]{1,0:T(2,128)S(1)} copy-done((s32[2,4]{1,0:T(2,128)S(1)}, s32[2,4]{1,0:T(2,128)}, u32[]{:S(2)}) %copy-start.2) | copy-done | bytes 56
  12.6 0.1 select_reduce_fusion
  12.7 0.1 sub.51
  12.8 0.0 collective-permute-done
  12.8 7.8 %collective-permute-done.1.refs_2_ = f32[2,256,128]{2,1,0:T(8,128)S(1)} collective-permute-done((f32[2,256,128]{2,1,0:T(8,128)S(1)}, f32[2,256,128]{2,1,0:T(8,128)S(1)}, u32[]{:S(2)}, u32[]{:S(2)}) %collective-permute-start.1) | collective-permute-done | bytes 262176 | tf_op jit(solution)/shard_map/ppermute | solution.py:42
  20.6 0.0 collective-permute-done.2
  20.6 0.0 collective-permute-done.3
  20.7 0.7 %collective-permute-start.4 = (f32[2,32,128]{2,1,0:T(8,128)S(1)}, f32[2,32,128]{2,1,0:T(8,128)S(1)}, u32[]{:S(2)}, u32[]{:S(2)}) collective-permute-start(f32[2,32,128]{2,1,0:T(8,128)S(1)} %get-tuple-element.27), channel_id=1, source_target_pairs={{0,2},{2,4},{4,6},{6,0},{1,3},{3,5},{5,7},{7,1},{8,10},{10,12},{12... | collective-permute-start | bytes 98312 | tf_op jit(solution)/shard_map/ppermute | solution.py:42
  21.4 3.4 %collective-permute-start.7 = (f32[2,32,128]{2,1,0:T(8,128)S(1)}, f32[2,32,128]{2,1,0:T(8,128)S(1)}, u32[]{:S(2)}, u32[]{:S(2)}) collective-permute-start(f32[2,32,128]{2,1,0:T(8,128)S(1)} %get-tuple-element.26), channel_id=1, source_target_pairs={{0,4},{2,6},{4,0},{6,2},{1,5},{3,7},{5,1},{7,3},{8,12},{10,14},{12... | collective-permute-start | bytes 98312 | tf_op jit(solution)/shard_map/ppermute | solution.py:42
  24.8 1.7 %collective-permute-done.4 = f32[2,32,128]{2,1,0:T(8,128)S(1)} collective-permute-done((f32[2,32,128]{2,1,0:T(8,128)S(1)}, f32[2,32,128]{2,1,0:T(8,128)S(1)}, u32[]{:S(2)}, u32[]{:S(2)}) %collective-permute-start.4) | collective-permute-done | bytes 32800 | tf_op jit(solution)/shard_map/ppermute | solution.py:42
  26.5 0.4 collective-permute-start.5
  26.9 3.4 %collective-permute-start.6 = (f32[2,256,128]{2,1,0:T(8,128)S(1)}, f32[2,256,128]{2,1,0:T(8,128)S(1)}, u32[]{:S(2)}, u32[]{:S(2)}) collective-permute-start(f32[2,256,128]{2,1,0:T(8,128)S(1)} %copy-done.1), channel_id=1, source_target_pairs={{0,6},{2,0},{4,2},{6,4},{1,7},{3,1},{5,3},{7,5},{8,14},{10,8},{12,... | collective-permute-start | bytes 786440 | tf_op jit(solution)/shard_map/ppermute | solution.py:42
  30.3 0.0 collective-permute-done.7
  30.3 0.0 collective-permute-done.8
  30.3 1.6 %collective-permute-start.10 = (f32[4,2,32,128]{3,2,1,0:T(8,128)S(1)}, f32[4,2,32,128]{3,2,1,0:T(8,128)S(1)}, u32[]{:S(2)}, u32[]{:S(2)}) collective-permute-start(f32[4,2,32,128]{3,2,1,0:T(8,128)S(1)} %pad_maximum_fusion.2.refs_4_), channel_id=1, source_target_pairs={{0,16},{8,24},{16,0},{24,8},{1,17},{9,25},{17,1},{25,9},{2,18},{10... | collective-permute-start | bytes 393224 | tf_op jit(solution)/shard_map/ppermute | solution.py:42
  31.9 1.4 %collective-permute-start.11 = (f32[4,2,32,128]{3,2,1,0:T(8,128)S(1)}, f32[4,2,32,128]{3,2,1,0:T(8,128)S(1)}, u32[]{:S(2)}, u32[]{:S(2)}) collective-permute-start(f32[4,2,32,128]{3,2,1,0:T(8,128)S(1)} %pad_maximum_fusion.2.refs_4_), channel_id=1, source_target_pairs={{0,24},{8,0},{16,8},{24,16},{1,25},{9,1},{17,9},{25,17},{2,26},{10... | collective-permute-start | bytes 393224 | tf_op jit(solution)/shard_map/ppermute | solution.py:42
  33.4 0.6 %collective-permute-start.9 = (f32[4,2,32,128]{3,2,1,0:T(8,128)S(1)}, f32[4,2,32,128]{3,2,1,0:T(8,128)S(1)}, u32[]{:S(2)}, u32[]{:S(2)}) collective-permute-start(f32[4,2,32,128]{3,2,1,0:T(8,128)S(1)} %pad_maximum_fusion.2.refs_4_), channel_id=1, source_target_pairs={{0,8},{8,16},{16,24},{24,0},{1,9},{9,17},{17,25},{25,1},{2,10},{10... | collective-permute-start | bytes 393224 | tf_op jit(solution)/shard_map/ppermute | solution.py:42
  34.0 0.1 pad_add_fusion.place
  34.0 2.7 %collective-permute-done.10.refs_6_ = f32[4,2,32,128]{3,2,1,0:T(8,128)S(1)} collective-permute-done((f32[4,2,32,128]{3,2,1,0:T(8,128)S(1)}, f32[4,2,32,128]{3,2,1,0:T(8,128)S(1)}, u32[]{:S(2)}, u32[]{:S(2)}) %collective-permute-start.10) | collective-permute-done | bytes 131104 | tf_op jit(solution)/shard_map/ppermute | solution.py:42
  36.8 0.3 collective-permute-done.11.refs_7_
  37.1 2.1 %collective-permute-done.9.refs_5_ = f32[4,2,32,128]{3,2,1,0:T(8,128)S(1)} collective-permute-done((f32[4,2,32,128]{3,2,1,0:T(8,128)S(1)}, f32[4,2,32,128]{3,2,1,0:T(8,128)S(1)}, u32[]{:S(2)}, u32[]{:S(2)}) %collective-permute-start.9) | collective-permute-done | bytes 131104 | tf_op jit(solution)/shard_map/ppermute | solution.py:42
  39.2 0.8 %collective-permute-done.6.refs_3_ = f32[2,256,128]{2,1,0:T(8,128)S(1)} collective-permute-done((f32[2,256,128]{2,1,0:T(8,128)S(1)}, f32[2,256,128]{2,1,0:T(8,128)S(1)}, u32[]{:S(2)}, u32[]{:S(2)}) %collective-permute-start.6) | collective-permute-done | bytes 262176 | tf_op jit(solution)/shard_map/ppermute | solution.py:42
  40.0 1.6 %shard_map.59 = f32[2,384,128]{2,1,0:T(8,128)S(1)} custom-call(s32[13]{0:T(128)S(1)} %pad_add_fusion.place, f32[2,256,128]{2,1,0:T(8,128)S(1)} %copy-done.1, f32[2,256,128]{2,1,0:T(8,128)S(1)} %collective-permute-done.5.refs_1_, f32[2,256,128]{2,1,0:T(8,128)S(1)} %collective-permute-done.1.refs_2_, f32[2,256,128]{2,1,0:T(8,128)S(1)} %collective-permute-done.6.refs_3_, ...), custom_call_target="tpu_custom_call" | custom-call | tf_op jit(solution)/shard_map/pallas_call | solution.py:100
  41.6 0.1 collective-permute-start.12
  41.7 0.9 %multiply_reduce_fusion.1 = f32[2,128]{1,0:T(2,128)S(1)} fusion(f32[2,128,512]{2,1,0:T(8,128)} %param.6, s32[]{:T(128)S(6)} %select_n.241), kind=kLoop, calls=%fused_computation.6 | loop fusion | flops 65280 | bytes 132100 | tf_op jit(solution)/shard_map/reduce_sum | solution.py:116
  42.6 0.7 %collective-permute-done.12 = f32[2,384,128]{2,1,0:T(8,128)S(1)} collective-permute-done((f32[2,384,128]{2,1,0:T(8,128)S(1)}, f32[2,384,128]{2,1,0:T(8,128)S(1)}, u32[]{:S(2)}, u32[]{:S(2)}) %collective-permute-start.12) | collective-permute-done | bytes 393248 | tf_op jit(solution)/shard_map/ppermute | solution.py:42
  43.5 0.1 multiply_reduce_fusion
  43.6 2.2 %collective-permute-start.13 = (f32[2,40,128]{2,1,0:T(8,128)S(1)}, f32[2,40,128]{2,1,0:T(8,128)S(1)}, u32[]{:S(2)}, u32[]{:S(2)}) collective-permute-start(f32[2,40,128]{2,1,0:T(8,128)S(1)} %get-tuple-element.30), channel_id=1, source_target_pairs={{0,6},{2,0},{4,2},{6,4},{1,7},{3,1},{5,3},{7,5},{8,14},{10,8},{12,... | collective-permute-start | bytes 122888 | tf_op jit(solution)/shard_map/ppermute | solution.py:42
  45.8 1.4 %collective-permute-start.15 = (f32[2,40,128]{2,1,0:T(8,128)S(1)}, f32[2,40,128]{2,1,0:T(8,128)S(1)}, u32[]{:S(2)}, u32[]{:S(2)}) collective-permute-start(f32[2,40,128]{2,1,0:T(8,128)S(1)} %get-tuple-element.28), channel_id=1, source_target_pairs={{0,2},{2,4},{4,6},{6,0},{1,3},{3,5},{5,7},{7,1},{8,10},{10,12},{12... | collective-permute-start | bytes 122888 | tf_op jit(solution)/shard_map/ppermute | solution.py:42
  47.3 0.5 collective-permute-done.13
  47.8 3.2 %collective-permute-done.14 = f32[2,40,128]{2,1,0:T(8,128)S(1)} collective-permute-done((f32[2,40,128]{2,1,0:T(8,128)S(1)}, f32[2,40,128]{2,1,0:T(8,128)S(1)}, u32[]{:S(2)}, u32[]{:S(2)}) %collective-permute-start.14) | collective-permute-done | bytes 40992 | tf_op jit(solution)/shard_map/ppermute | solution.py:42
  50.9 0.7 %collective-permute-done.15 = f32[2,40,128]{2,1,0:T(8,128)S(1)} collective-permute-done((f32[2,40,128]{2,1,0:T(8,128)S(1)}, f32[2,40,128]{2,1,0:T(8,128)S(1)}, u32[]{:S(2)}, u32[]{:S(2)}) %collective-permute-start.15) | collective-permute-done | bytes 40992 | tf_op jit(solution)/shard_map/ppermute | solution.py:42
  51.7 1.5 %collective-permute-start.16 = (f32[2,512]{1,0:T(2,128)S(1)}, f32[2,512]{1,0:T(2,128)S(1)}, u32[]{:S(2)}, u32[]{:S(2)}) collective-permute-start(f32[2,512]{1,0:T(2,128)S(1)} %bitcast.21), channel_id=1, source_target_pairs={{0,8},{8,16},{16,24},{24,0},{1,9},{9,17},{17,25},{25,1},{2,10},{10... | collective-permute-start | bytes 12296 | tf_op jit(solution)/shard_map/ppermute | solution.py:42
  53.2 1.2 %collective-permute-start.17 = (f32[2,512]{1,0:T(2,128)S(1)}, f32[2,512]{1,0:T(2,128)S(1)}, u32[]{:S(2)}, u32[]{:S(2)}) collective-permute-start(f32[2,512]{1,0:T(2,128)S(1)} %bitcast.22), channel_id=1, source_target_pairs={{0,16},{8,24},{16,0},{24,8},{1,17},{9,25},{17,1},{25,9},{2,18},{10... | collective-permute-start | bytes 12296 | tf_op jit(solution)/shard_map/ppermute | solution.py:42
  54.4 1.8 %collective-permute-start.18 = (f32[2,512]{1,0:T(2,128)S(1)}, f32[2,512]{1,0:T(2,128)S(1)}, u32[]{:S(2)}, u32[]{:S(2)}) collective-permute-start(f32[2,512]{1,0:T(2,128)S(1)} %bitcast.23), channel_id=1, source_target_pairs={{0,24},{8,0},{16,8},{24,16},{1,25},{9,1},{17,9},{25,17},{2,26},{10... | collective-permute-start | bytes 12296 | tf_op jit(solution)/shard_map/ppermute | solution.py:42
  56.2 0.7 %slice_negate_fusion = f32[2,32,512]{2,1,0:T(8,128)} fusion(f32[2,40,512]{2,1,0:T(8,128)S(1)} %pad_maximum_fusion.1), kind=kLoop, calls=%fused_computation.4 | loop fusion | flops 32768 | bytes 262144 | tf_op jit(solution)/shard_map/neg | solution.py:132
  56.9 0.0 collective-permute-done.16
  56.9 0.0 collective-permute-done.17
  56.9 1.1 %collective-permute-done.18 = f32[2,512]{1,0:T(2,128)S(1)} collective-permute-done((f32[2,512]{1,0:T(2,128)S(1)}, f32[2,512]{1,0:T(2,128)S(1)}, u32[]{:S(2)}, u32[]{:S(2)}) %collective-permute-start.18) | collective-permute-done | bytes 4128 | tf_op jit(solution)/shard_map/ppermute | solution.py:42
  58.0 0.6 %add_add_fusion.1 = f32[2,512]{1,0:T(2,128)} fusion(f32[2,512]{1,0:T(2,128)S(1)} %collective-permute-done.18, f32[2,512]{1,0:T(2,128)S(1)} %collective-permute-done.17, f32[2,512]{1,0:T(2,128)S(1)} %collective-permute-done.16, f32[2,1,512]{2,1,0:T(1,128)S(1)} %pad_maximum_fusion.7), kind=kLoop, calls=%fused_computation.23 | loop fusion | flops 3072 | bytes 20480 | tf_op jit(solution)/shard_map/add | solution.py:131
  (25 shorter events, 0.3 us)
Async XLA Ops:
  0.6 1.0 %copy-start = (f32[2,128,512]{2,1,0:T(8,128)S(1)}, f32[2,128,512]{2,1,0:T(8,128)}, u32[]{:S(2)}) copy-start(f32[2,128,512]{2,1,0:T(8,128)} %param.5) | copy-start | bytes 1572868
  3.3 3.1 %copy-start.1 = (f32[2,256,128]{2,1,0:T(8,128)S(1)}, f32[2,256,128]{2,1,0:T(8,128)}, u32[]{:S(2)}) copy-start(f32[2,256,128]{2,1,0:T(8,128)} %refs_0_.1) | copy-start | bytes 786436
  3.4 9.4 %collective-permute-start = (f32[2,32,512]{2,1,0:T(8,128)S(1)}, f32[2,32,512]{2,1,0:T(8,128)S(1)}, u32[]{:S(2)}, u32[]{:S(2)}) collective-permute-start(f32[2,32,512]{2,1,0:T(8,128)S(1)} %get-tuple-element.14), channel_id=1, source_target_pairs={{0,8},{8,16},{16,24},{24,0},{1,9},{9,17},{17,25},{25,1},{2,10},{10... | collective-permute-start | bytes 393224 | tf_op jit(solution)/shard_map/ppermute | solution.py:42
  6.4 14.3 %collective-permute-start.1 = (f32[2,256,128]{2,1,0:T(8,128)S(1)}, f32[2,256,128]{2,1,0:T(8,128)S(1)}, u32[]{:S(2)}, u32[]{:S(2)}) collective-permute-start(f32[2,256,128]{2,1,0:T(8,128)S(1)} %copy-done.1), channel_id=1, source_target_pairs={{0,4},{2,6},{4,0},{6,2},{1,5},{3,7},{5,1},{7,3},{8,12},{10,14},{12... | collective-permute-start | bytes 786440 | tf_op jit(solution)/shard_map/ppermute | solution.py:42
  8.9 11.7 %collective-permute-start.2 = (f32[2,32,512]{2,1,0:T(8,128)S(1)}, f32[2,32,512]{2,1,0:T(8,128)S(1)}, u32[]{:S(2)}, u32[]{:S(2)}) collective-permute-start(f32[2,32,512]{2,1,0:T(8,128)S(1)} %get-tuple-element.16), channel_id=1, source_target_pairs={{0,16},{8,24},{16,0},{24,8},{1,17},{9,25},{17,1},{25,9},{2,18},{10... | collective-permute-start | bytes 393224 | tf_op jit(solution)/shard_map/ppermute | solution.py:42
  10.5 10.2 %collective-permute-start.3 = (f32[2,32,512]{2,1,0:T(8,128)S(1)}, f32[2,32,512]{2,1,0:T(8,128)S(1)}, u32[]{:S(2)}, u32[]{:S(2)}) collective-permute-start(f32[2,32,512]{2,1,0:T(8,128)S(1)} %get-tuple-element.15), channel_id=1, source_target_pairs={{0,24},{8,0},{16,8},{24,16},{1,25},{9,1},{17,9},{25,17},{2,26},{10... | collective-permute-start | bytes 393224 | tf_op jit(solution)/shard_map/ppermute | solution.py:42
  11.9 0.7 %copy-start.2 = (s32[2,4]{1,0:T(2,128)S(1)}, s32[2,4]{1,0:T(2,128)}, u32[]{:S(2)}) copy-start(s32[2,4]{1,0:T(2,128)} %param.7) | copy-start | bytes 100
  20.7 5.8 %collective-permute-start.4 = (f32[2,32,128]{2,1,0:T(8,128)S(1)}, f32[2,32,128]{2,1,0:T(8,128)S(1)}, u32[]{:S(2)}, u32[]{:S(2)}) collective-permute-start(f32[2,32,128]{2,1,0:T(8,128)S(1)} %get-tuple-element.27), channel_id=1, source_target_pairs={{0,2},{2,4},{4,6},{6,0},{1,3},{3,5},{5,7},{7,1},{8,10},{10,12},{12... | collective-permute-start | bytes 98312 | tf_op jit(solution)/shard_map/ppermute | solution.py:42
  21.4 8.9 %collective-permute-start.7 = (f32[2,32,128]{2,1,0:T(8,128)S(1)}, f32[2,32,128]{2,1,0:T(8,128)S(1)}, u32[]{:S(2)}, u32[]{:S(2)}) collective-permute-start(f32[2,32,128]{2,1,0:T(8,128)S(1)} %get-tuple-element.26), channel_id=1, source_target_pairs={{0,4},{2,6},{4,0},{6,2},{1,5},{3,7},{5,1},{7,3},{8,12},{10,14},{12... | collective-permute-start | bytes 98312 | tf_op jit(solution)/shard_map/ppermute | solution.py:42
  24.8 5.5 %collective-permute-start.8 = (f32[2,32,128]{2,1,0:T(8,128)S(1)}, f32[2,32,128]{2,1,0:T(8,128)S(1)}, u32[]{:S(2)}, u32[]{:S(2)}) collective-permute-start(f32[2,32,128]{2,1,0:T(8,128)S(1)} %get-tuple-element.25), channel_id=1, source_target_pairs={{0,6},{2,0},{4,2},{6,4},{1,7},{3,1},{5,3},{7,5},{8,14},{10,8},{12,... | collective-permute-start | bytes 98312 | tf_op jit(solution)/shard_map/ppermute | solution.py:42
  26.5 12.7 %collective-permute-start.5 = (f32[2,256,128]{2,1,0:T(8,128)S(1)}, f32[2,256,128]{2,1,0:T(8,128)S(1)}, u32[]{:S(2)}, u32[]{:S(2)}) collective-permute-start(f32[2,256,128]{2,1,0:T(8,128)S(1)} %copy-done.1), channel_id=1, source_target_pairs={{0,2},{2,4},{4,6},{6,0},{1,3},{3,5},{5,7},{7,1},{8,10},{10,12},{12... | collective-permute-start | bytes 786440 | tf_op jit(solution)/shard_map/ppermute | solution.py:42
  26.9 13.1 %collective-permute-start.6 = (f32[2,256,128]{2,1,0:T(8,128)S(1)}, f32[2,256,128]{2,1,0:T(8,128)S(1)}, u32[]{:S(2)}, u32[]{:S(2)}) collective-permute-start(f32[2,256,128]{2,1,0:T(8,128)S(1)} %copy-done.1), channel_id=1, source_target_pairs={{0,6},{2,0},{4,2},{6,4},{1,7},{3,1},{5,3},{7,5},{8,14},{10,8},{12,... | collective-permute-start | bytes 786440 | tf_op jit(solution)/shard_map/ppermute | solution.py:42
  30.3 6.4 %collective-permute-start.10 = (f32[4,2,32,128]{3,2,1,0:T(8,128)S(1)}, f32[4,2,32,128]{3,2,1,0:T(8,128)S(1)}, u32[]{:S(2)}, u32[]{:S(2)}) collective-permute-start(f32[4,2,32,128]{3,2,1,0:T(8,128)S(1)} %pad_maximum_fusion.2.refs_4_), channel_id=1, source_target_pairs={{0,16},{8,24},{16,0},{24,8},{1,17},{9,25},{17,1},{25,9},{2,18},{10... | collective-permute-start | bytes 393224 | tf_op jit(solution)/shard_map/ppermute | solution.py:42
  31.9 5.2 %collective-permute-start.11 = (f32[4,2,32,128]{3,2,1,0:T(8,128)S(1)}, f32[4,2,32,128]{3,2,1,0:T(8,128)S(1)}, u32[]{:S(2)}, u32[]{:S(2)}) collective-permute-start(f32[4,2,32,128]{3,2,1,0:T(8,128)S(1)} %pad_maximum_fusion.2.refs_4_), channel_id=1, source_target_pairs={{0,24},{8,0},{16,8},{24,16},{1,25},{9,1},{17,9},{25,17},{2,26},{10... | collective-permute-start | bytes 393224 | tf_op jit(solution)/shard_map/ppermute | solution.py:42
  33.4 5.9 %collective-permute-start.9 = (f32[4,2,32,128]{3,2,1,0:T(8,128)S(1)}, f32[4,2,32,128]{3,2,1,0:T(8,128)S(1)}, u32[]{:S(2)}, u32[]{:S(2)}) collective-permute-start(f32[4,2,32,128]{3,2,1,0:T(8,128)S(1)} %pad_maximum_fusion.2.refs_4_), channel_id=1, source_target_pairs={{0,8},{8,16},{16,24},{24,0},{1,9},{9,17},{17,25},{25,1},{2,10},{10... | collective-permute-start | bytes 393224 | tf_op jit(solution)/shard_map/ppermute | solution.py:42
  41.6 1.8 %collective-permute-start.12 = (f32[2,384,128]{2,1,0:T(8,128)S(1)}, f32[2,384,128]{2,1,0:T(8,128)S(1)}, u32[]{:S(2)}, u32[]{:S(2)}) collective-permute-start(f32[2,384,128]{2,1,0:T(8,128)S(1)} %shard_map.59), channel_id=1, source_target_pairs={{0,1},{1,0},{2,3},{3,2},{4,5},{5,4},{6,7},{7,6},{8,9},{9,8},{10,11... | collective-permute-start | bytes 1179656 | tf_op jit(solution)/shard_map/ppermute | solution.py:42
  43.6 4.2 %collective-permute-start.13 = (f32[2,40,128]{2,1,0:T(8,128)S(1)}, f32[2,40,128]{2,1,0:T(8,128)S(1)}, u32[]{:S(2)}, u32[]{:S(2)}) collective-permute-start(f32[2,40,128]{2,1,0:T(8,128)S(1)} %get-tuple-element.30), channel_id=1, source_target_pairs={{0,6},{2,0},{4,2},{6,4},{1,7},{3,1},{5,3},{7,5},{8,14},{10,8},{12,... | collective-permute-start | bytes 122888 | tf_op jit(solution)/shard_map/ppermute | solution.py:42
  45.8 5.1 %collective-permute-start.14 = (f32[2,40,128]{2,1,0:T(8,128)S(1)}, f32[2,40,128]{2,1,0:T(8,128)S(1)}, u32[]{:S(2)}, u32[]{:S(2)}) collective-permute-start(f32[2,40,128]{2,1,0:T(8,128)S(1)} %get-tuple-element.29), channel_id=1, source_target_pairs={{0,4},{2,6},{4,0},{6,2},{1,5},{3,7},{5,1},{7,3},{8,12},{10,14},{12... | collective-permute-start | bytes 122888 | tf_op jit(solution)/shard_map/ppermute | solution.py:42
  45.8 5.8 %collective-permute-start.15 = (f32[2,40,128]{2,1,0:T(8,128)S(1)}, f32[2,40,128]{2,1,0:T(8,128)S(1)}, u32[]{:S(2)}, u32[]{:S(2)}) collective-permute-start(f32[2,40,128]{2,1,0:T(8,128)S(1)} %get-tuple-element.28), channel_id=1, source_target_pairs={{0,2},{2,4},{4,6},{6,0},{1,3},{3,5},{5,7},{7,1},{8,10},{10,12},{12... | collective-permute-start | bytes 122888 | tf_op jit(solution)/shard_map/ppermute | solution.py:42
  51.7 5.2 %collective-permute-start.16 = (f32[2,512]{1,0:T(2,128)S(1)}, f32[2,512]{1,0:T(2,128)S(1)}, u32[]{:S(2)}, u32[]{:S(2)}) collective-permute-start(f32[2,512]{1,0:T(2,128)S(1)} %bitcast.21), channel_id=1, source_target_pairs={{0,8},{8,16},{16,24},{24,0},{1,9},{9,17},{17,25},{25,1},{2,10},{10... | collective-permute-start | bytes 12296 | tf_op jit(solution)/shard_map/ppermute | solution.py:42
  53.2 3.6 %collective-permute-start.17 = (f32[2,512]{1,0:T(2,128)S(1)}, f32[2,512]{1,0:T(2,128)S(1)}, u32[]{:S(2)}, u32[]{:S(2)}) collective-permute-start(f32[2,512]{1,0:T(2,128)S(1)} %bitcast.22), channel_id=1, source_target_pairs={{0,16},{8,24},{16,0},{24,8},{1,17},{9,25},{17,1},{25,9},{2,18},{10... | collective-permute-start | bytes 12296 | tf_op jit(solution)/shard_map/ppermute | solution.py:42
  54.4 3.6 %collective-permute-start.18 = (f32[2,512]{1,0:T(2,128)S(1)}, f32[2,512]{1,0:T(2,128)S(1)}, u32[]{:S(2)}, u32[]{:S(2)}) collective-permute-start(f32[2,512]{1,0:T(2,128)S(1)} %bitcast.23), channel_id=1, source_target_pairs={{0,24},{8,0},{16,8},{24,16},{1,25},{9,1},{17,9},{25,17},{2,26},{10... | collective-permute-start | bytes 12296 | tf_op jit(solution)/shard_map/ppermute | solution.py:42

commit v10 on v9

--- a/solution.py
+++ b/solution.py
@@ -72,7 +72,6 @@
             return lax.dynamic_slice_in_dim(partial, r * piece, piece, axis=1)
 
         sums = [shifted(rows_of((row + d) % rows), "row", rows, d) for d in range(1, rows)]
-        sums[0], far = lax.optimization_barrier((sums[0], far))
         scaled = sum(sums, rows_of(row))
 
         def columns_of(array, c):

time: 58.8 us -> 58.2 us (0.990)
  waiting for transfers between devices: 21.7 us -> 19.8 us
  starting transfers between devices: 28.3 us -> 29.6 us
    ppermute x19, waiting for transfers between devices: 21.7 us -> 19.8 us  [shifted(): lax.ppermute(array, axis, [(i, (i + shift) % size) for i in range(size)])]
    ppermute x19, starting transfers between devices: 28.3 us -> 29.6 us  [shifted(): lax.ppermute(array, axis, [(i, (i + shift) % size) for i in range(size)])]
  transfers between devices with their start and end apart: 19 -> 19, of which waited for: 11 -> 12; matrix products, arithmetic and copies ran while one was open for 3% -> 3% of each run, Pallas kernels for 0% -> 0%
where the time goes in v10:
time: 58.2 us; the launch traced here: 58 us
  starting transfers between devices  29.6 us (51%)
  waiting for transfers between devices  19.8 us (34%)
  other arithmetic  2.64 us (5%)
  local copies, waits for them, and re-layouts  1.87 us (3%)
  matrix products  1.62 us (3%)
  Pallas kernels  1.61 us (3%)
  between operations  0.9 us (2%)
    ppermute x19, starting transfers between devices, shifted(): lax.ppermute(array, axis, [(i, (i + shift) % size) for i in range(size)])  29.6 us
    ppermute x19, waiting for transfers between devices, shifted(): lax.ppermute(array, axis, [(i, (i + shift) % size) for i in range(size)])  19.8 us
    unnamed x7, local copies, waits for them, and re-layouts  1.67 us
    dot_general x1, matrix products, per_device(): partial = jnp.einsum('srw,swv->srv', mine, factor_inv, precision=highest)  1.62 us
    pallas_call x1, Pallas kernels, per_device(): pl.pallas_call(functools.partial(multiply_tiles, deep, rows), out_shape=j...  1.61 us
  transfers between devices with their start and end apart: 19, of which 12 were waited for; matrix products, arithmetic and copies ran while one was open for 3% of the time, Pallas kernels for 0%

profile of v10, /device:TPU:0, one launch (start us, length us, event | category | flops | bytes accessed | tf_op | source)
XLA Modules:
  0.0 58.0 jit_solution(12348739302447009193)
XLA Ops:
  0.6 0.0 copy-start
  0.7 1.0 %copy-done = f32[2,128,512]{2,1,0:T(8,128)S(1)} copy-done((f32[2,128,512]{2,1,0:T(8,128)S(1)}, f32[2,128,512]{2,1,0:T(8,128)}, u32[]{:S(2)}) %copy-start) | copy-done | bytes 524312
  1.7 1.6 %fusion = f32[2,128,512]{2,1,0:T(8,128)S(1)} fusion(f32[2,128,512]{2,1,0:T(8,128)} %param.6, f32[2,128,512]{2,1,0:T(8,128)S(1)} %copy-done, s32[]{:T(128)S(6)} %select_n.231), kind=kOutput, calls=%fused_computation.10 | convolution fusion | flops 201326592 | bytes 1179652 | tf_op jit(solution)/shard_map/srw,swv->srv/dot_general | solution.py:69
  3.3 0.0 copy-start.1
  3.4 3.0 %collective-permute-start = (f32[2,32,512]{2,1,0:T(8,128)S(1)}, f32[2,32,512]{2,1,0:T(8,128)S(1)}, u32[]{:S(2)}, u32[]{:S(2)}) collective-permute-start(f32[2,32,512]{2,1,0:T(8,128)S(1)} %get-tuple-element.10), channel_id=1, source_target_pairs={{0,8},{8,16},{16,24},{24,0},{1,9},{9,17},{17,25},{25,1},{2,10},{10... | collective-permute-start | bytes 393224 | tf_op jit(solution)/shard_map/ppermute | solution.py:42
  6.4 1.5 %collective-permute-start.1 = (f32[2,32,512]{2,1,0:T(8,128)S(1)}, f32[2,32,512]{2,1,0:T(8,128)S(1)}, u32[]{:S(2)}, u32[]{:S(2)}) collective-permute-start(f32[2,32,512]{2,1,0:T(8,128)S(1)} %get-tuple-element.12), channel_id=1, source_target_pairs={{0,16},{8,24},{16,0},{24,8},{1,17},{9,25},{17,1},{25,9},{2,18},{10... | collective-permute-start | bytes 393224 | tf_op jit(solution)/shard_map/ppermute | solution.py:42
  7.9 1.4 %collective-permute-start.2 = (f32[2,32,512]{2,1,0:T(8,128)S(1)}, f32[2,32,512]{2,1,0:T(8,128)S(1)}, u32[]{:S(2)}, u32[]{:S(2)}) collective-permute-start(f32[2,32,512]{2,1,0:T(8,128)S(1)} %get-tuple-element.11), channel_id=1, source_target_pairs={{0,24},{8,0},{16,8},{24,16},{1,25},{9,1},{17,9},{25,17},{2,26},{10... | collective-permute-start | bytes 393224 | tf_op jit(solution)/shard_map/ppermute | solution.py:42
  9.3 2.6 %collective-permute-start.5 = (f32[2,256,128]{2,1,0:T(8,128)S(1)}, f32[2,256,128]{2,1,0:T(8,128)S(1)}, u32[]{:S(2)}, u32[]{:S(2)}) collective-permute-start(f32[2,256,128]{2,1,0:T(8,128)S(1)} %copy-done.1), channel_id=1, source_target_pairs={{0,4},{2,6},{4,0},{6,2},{1,5},{3,7},{5,1},{7,3},{8,12},{10,14},{12... | collective-permute-start | bytes 786440 | tf_op jit(solution)/shard_map/ppermute | solution.py:42
  11.9 0.7 %copy-done.2 = s32[2,4]{1,0:T(2,128)S(1)} copy-done((s32[2,4]{1,0:T(2,128)S(1)}, s32[2,4]{1,0:T(2,128)}, u32[]{:S(2)}) %copy-start.2) | copy-done | bytes 56
  12.6 0.1 select_reduce_fusion
  12.7 0.1 sub.51
  12.8 0.0 collective-permute-done
  12.8 0.9 %collective-permute-done.1 = f32[2,32,512]{2,1,0:T(8,128)S(1)} collective-permute-done((f32[2,32,512]{2,1,0:T(8,128)S(1)}, f32[2,32,512]{2,1,0:T(8,128)S(1)}, u32[]{:S(2)}, u32[]{:S(2)}) %collective-permute-start.1) | collective-permute-done | bytes 131104 | tf_op jit(solution)/shard_map/ppermute | solution.py:42
  13.6 0.2 collective-permute-done.2
  13.9 1.6 %collective-permute-start.3 = (f32[2,32,128]{2,1,0:T(8,128)S(1)}, f32[2,32,128]{2,1,0:T(8,128)S(1)}, u32[]{:S(2)}, u32[]{:S(2)}) collective-permute-start(f32[2,32,128]{2,1,0:T(8,128)S(1)} %get-tuple-element.23), channel_id=1, source_target_pairs={{0,2},{2,4},{4,6},{6,0},{1,3},{3,5},{5,7},{7,1},{8,10},{10,12},{12... | collective-permute-start | bytes 98312 | tf_op jit(solution)/shard_map/ppermute | solution.py:42
  15.6 2.6 %collective-permute-start.7 = (f32[2,32,128]{2,1,0:T(8,128)S(1)}, f32[2,32,128]{2,1,0:T(8,128)S(1)}, u32[]{:S(2)}, u32[]{:S(2)}) collective-permute-start(f32[2,32,128]{2,1,0:T(8,128)S(1)} %get-tuple-element.22), channel_id=1, source_target_pairs={{0,4},{2,6},{4,0},{6,2},{1,5},{3,7},{5,1},{7,3},{8,12},{10,14},{12... | collective-permute-start | bytes 98312 | tf_op jit(solution)/shard_map/ppermute | solution.py:42
  18.2 1.3 %collective-permute-start.8 = (f32[2,32,128]{2,1,0:T(8,128)S(1)}, f32[2,32,128]{2,1,0:T(8,128)S(1)}, u32[]{:S(2)}, u32[]{:S(2)}) collective-permute-start(f32[2,32,128]{2,1,0:T(8,128)S(1)} %get-tuple-element.21), channel_id=1, source_target_pairs={{0,6},{2,0},{4,2},{6,4},{1,7},{3,1},{5,3},{7,5},{8,14},{10,8},{12,... | collective-permute-start | bytes 98312 | tf_op jit(solution)/shard_map/ppermute | solution.py:42
  19.5 0.3 collective-permute-done.3
  19.8 6.1 %collective-permute-start.4 = (f32[2,256,128]{2,1,0:T(8,128)S(1)}, f32[2,256,128]{2,1,0:T(8,128)S(1)}, u32[]{:S(2)}, u32[]{:S(2)}) collective-permute-start(f32[2,256,128]{2,1,0:T(8,128)S(1)} %copy-done.1), channel_id=1, source_target_pairs={{0,2},{2,4},{4,6},{6,0},{1,3},{3,5},{5,7},{7,1},{8,10},{10,12},{12... | collective-permute-start | bytes 786440 | tf_op jit(solution)/shard_map/ppermute | solution.py:42
  25.9 0.0 collective-permute-start.6
  25.9 6.0 %collective-permute-done.7 = f32[2,32,128]{2,1,0:T(8,128)S(1)} collective-permute-done((f32[2,32,128]{2,1,0:T(8,128)S(1)}, f32[2,32,128]{2,1,0:T(8,128)S(1)}, u32[]{:S(2)}, u32[]{:S(2)}) %collective-permute-start.7) | collective-permute-done | bytes 32800 | tf_op jit(solution)/shard_map/ppermute | solution.py:42
  31.9 0.0 collective-permute-done.8
  31.9 0.1 collective-permute-start.10
  32.0 2.1 %collective-permute-start.11 = (f32[4,2,32,128]{3,2,1,0:T(8,128)S(1)}, f32[4,2,32,128]{3,2,1,0:T(8,128)S(1)}, u32[]{:S(2)}, u32[]{:S(2)}) collective-permute-start(f32[4,2,32,128]{3,2,1,0:T(8,128)S(1)} %pad_maximum_fusion.2.refs_4_), channel_id=1, source_target_pairs={{0,24},{8,0},{16,8},{24,16},{1,25},{9,1},{17,9},{25,17},{2,26},{10... | collective-permute-start | bytes 393224 | tf_op jit(solution)/shard_map/ppermute | solution.py:42
  34.1 0.0 collective-permute-done.5.refs_2_
  34.1 0.0 collective-permute-start.9
  34.1 0.1 pad_add_fusion.place
  34.2 3.5 %collective-permute-done.10.refs_6_ = f32[4,2,32,128]{3,2,1,0:T(8,128)S(1)} collective-permute-done((f32[4,2,32,128]{3,2,1,0:T(8,128)S(1)}, f32[4,2,32,128]{3,2,1,0:T(8,128)S(1)}, u32[]{:S(2)}, u32[]{:S(2)}) %collective-permute-start.10) | collective-permute-done | bytes 131104 | tf_op jit(solution)/shard_map/ppermute | solution.py:42
  37.8 2.2 %collective-permute-done.9.refs_5_ = f32[4,2,32,128]{3,2,1,0:T(8,128)S(1)} collective-permute-done((f32[4,2,32,128]{3,2,1,0:T(8,128)S(1)}, f32[4,2,32,128]{3,2,1,0:T(8,128)S(1)}, u32[]{:S(2)}, u32[]{:S(2)}) %collective-permute-start.9) | collective-permute-done | bytes 131104 | tf_op jit(solution)/shard_map/ppermute | solution.py:42
  40.0 0.0 collective-permute-done.4.refs_1_
  40.0 1.6 %shard_map.59 = f32[2,384,128]{2,1,0:T(8,128)S(1)} custom-call(s32[13]{0:T(128)S(1)} %pad_add_fusion.place, f32[2,256,128]{2,1,0:T(8,128)S(1)} %copy-done.1, f32[2,256,128]{2,1,0:T(8,128)S(1)} %collective-permute-done.4.refs_1_, f32[2,256,128]{2,1,0:T(8,128)S(1)} %collective-permute-done.5.refs_2_, f32[2,256,128]{2,1,0:T(8,128)S(1)} %collective-permute-done.6.refs_3_, ...), custom_call_target="tpu_custom_call" | custom-call | tf_op jit(solution)/shard_map/pallas_call | solution.py:99
  41.6 0.1 collective-permute-start.12
  41.7 0.9 %multiply_reduce_fusion.1 = f32[2,128]{1,0:T(2,128)S(1)} fusion(f32[2,128,512]{2,1,0:T(8,128)} %param.6, s32[]{:T(128)S(6)} %select_n.241), kind=kLoop, calls=%fused_computation.6 | loop fusion | flops 65280 | bytes 132100 | tf_op jit(solution)/shard_map/reduce_sum | solution.py:115
  42.7 0.7 %collective-permute-done.12 = f32[2,384,128]{2,1,0:T(8,128)S(1)} collective-permute-done((f32[2,384,128]{2,1,0:T(8,128)S(1)}, f32[2,384,128]{2,1,0:T(8,128)S(1)}, u32[]{:S(2)}, u32[]{:S(2)}) %collective-permute-start.12) | collective-permute-done | bytes 393248 | tf_op jit(solution)/shard_map/ppermute | solution.py:42
  43.5 0.1 multiply_reduce_fusion
  43.6 1.6 %collective-permute-start.13 = (f32[2,40,128]{2,1,0:T(8,128)S(1)}, f32[2,40,128]{2,1,0:T(8,128)S(1)}, u32[]{:S(2)}, u32[]{:S(2)}) collective-permute-start(f32[2,40,128]{2,1,0:T(8,128)S(1)} %get-tuple-element.26), channel_id=1, source_target_pairs={{0,6},{2,0},{4,2},{6,4},{1,7},{3,1},{5,3},{7,5},{8,14},{10,8},{12,... | collective-permute-start | bytes 122888 | tf_op jit(solution)/shard_map/ppermute | solution.py:42
  45.2 1.2 %collective-permute-start.14 = (f32[2,40,128]{2,1,0:T(8,128)S(1)}, f32[2,40,128]{2,1,0:T(8,128)S(1)}, u32[]{:S(2)}, u32[]{:S(2)}) collective-permute-start(f32[2,40,128]{2,1,0:T(8,128)S(1)} %get-tuple-element.25), channel_id=1, source_target_pairs={{0,4},{2,6},{4,0},{6,2},{1,5},{3,7},{5,1},{7,3},{8,12},{10,14},{12... | collective-permute-start | bytes 122888 | tf_op jit(solution)/shard_map/ppermute | solution.py:42
  46.4 0.9 %collective-permute-start.15 = (f32[2,40,128]{2,1,0:T(8,128)S(1)}, f32[2,40,128]{2,1,0:T(8,128)S(1)}, u32[]{:S(2)}, u32[]{:S(2)}) collective-permute-start(f32[2,40,128]{2,1,0:T(8,128)S(1)} %get-tuple-element.24), channel_id=1, source_target_pairs={{0,2},{2,4},{4,6},{6,0},{1,3},{3,5},{5,7},{7,1},{8,10},{10,12},{12... | collective-permute-start | bytes 122888 | tf_op jit(solution)/shard_map/ppermute | solution.py:42
  47.3 0.4 collective-permute-done.13
  47.7 3.2 %collective-permute-done.14 = f32[2,40,128]{2,1,0:T(8,128)S(1)} collective-permute-done((f32[2,40,128]{2,1,0:T(8,128)S(1)}, f32[2,40,128]{2,1,0:T(8,128)S(1)}, u32[]{:S(2)}, u32[]{:S(2)}) %collective-permute-start.14) | collective-permute-done | bytes 40992 | tf_op jit(solution)/shard_map/ppermute | solution.py:42
  50.9 1.3 %collective-permute-done.15 = f32[2,40,128]{2,1,0:T(8,128)S(1)} collective-permute-done((f32[2,40,128]{2,1,0:T(8,128)S(1)}, f32[2,40,128]{2,1,0:T(8,128)S(1)}, u32[]{:S(2)}, u32[]{:S(2)}) %collective-permute-start.15) | collective-permute-done | bytes 40992 | tf_op jit(solution)/shard_map/ppermute | solution.py:42
  52.3 0.6 collective-permute-start.16
  52.8 0.6 collective-permute-start.17
  53.4 2.4 %collective-permute-start.18 = (f32[2,512]{1,0:T(2,128)S(1)}, f32[2,512]{1,0:T(2,128)S(1)}, u32[]{:S(2)}, u32[]{:S(2)}) collective-permute-start(f32[2,512]{1,0:T(2,128)S(1)} %bitcast.23), channel_id=1, source_target_pairs={{0,24},{8,0},{16,8},{24,16},{1,25},{9,1},{17,9},{25,17},{2,26},{10... | collective-permute-start | bytes 12296 | tf_op jit(solution)/shard_map/ppermute | solution.py:42
  55.8 0.7 %slice_negate_fusion = f32[2,32,512]{2,1,0:T(8,128)} fusion(f32[2,40,512]{2,1,0:T(8,128)S(1)} %pad_maximum_fusion.1), kind=kLoop, calls=%fused_computation.4 | loop fusion | flops 32768 | bytes 262144 | tf_op jit(solution)/shard_map/neg | solution.py:131
  56.4 0.4 collective-permute-done.16
  56.8 0.6 collective-permute-done.18
  57.4 0.6 %add_add_fusion.1 = f32[2,512]{1,0:T(2,128)} fusion(f32[2,512]{1,0:T(2,128)S(1)} %collective-permute-done.18, f32[2,512]{1,0:T(2,128)S(1)} %collective-permute-done.17, f32[2,512]{1,0:T(2,128)S(1)} %collective-permute-done.16, f32[2,1,512]{2,1,0:T(1,128)S(1)} %pad_maximum_fusion.7), kind=kLoop, calls=%fused_computation.23 | loop fusion | flops 3072 | bytes 20480 | tf_op jit(solution)/shard_map/add | solution.py:130
  (25 shorter events, 0.3 us)
Async XLA Ops:
  0.6 1.0 %copy-start = (f32[2,128,512]{2,1,0:T(8,128)S(1)}, f32[2,128,512]{2,1,0:T(8,128)}, u32[]{:S(2)}) copy-start(f32[2,128,512]{2,1,0:T(8,128)} %param.5) | copy-start | bytes 1572868
  3.3 6.0 %copy-start.1 = (f32[2,256,128]{2,1,0:T(8,128)S(1)}, f32[2,256,128]{2,1,0:T(8,128)}, u32[]{:S(2)}) copy-start(f32[2,256,128]{2,1,0:T(8,128)} %refs_0_.1) | copy-start | bytes 786436
  3.4 9.4 %collective-permute-start = (f32[2,32,512]{2,1,0:T(8,128)S(1)}, f32[2,32,512]{2,1,0:T(8,128)S(1)}, u32[]{:S(2)}, u32[]{:S(2)}) collective-permute-start(f32[2,32,512]{2,1,0:T(8,128)S(1)} %get-tuple-element.10), channel_id=1, source_target_pairs={{0,8},{8,16},{16,24},{24,0},{1,9},{9,17},{17,25},{25,1},{2,10},{10... | collective-permute-start | bytes 393224 | tf_op jit(solution)/shard_map/ppermute | solution.py:42
  6.4 7.3 %collective-permute-start.1 = (f32[2,32,512]{2,1,0:T(8,128)S(1)}, f32[2,32,512]{2,1,0:T(8,128)S(1)}, u32[]{:S(2)}, u32[]{:S(2)}) collective-permute-start(f32[2,32,512]{2,1,0:T(8,128)S(1)} %get-tuple-element.12), channel_id=1, source_target_pairs={{0,16},{8,24},{16,0},{24,8},{1,17},{9,25},{17,1},{25,9},{2,18},{10... | collective-permute-start | bytes 393224 | tf_op jit(solution)/shard_map/ppermute | solution.py:42
  7.9 6.0 %collective-permute-start.2 = (f32[2,32,512]{2,1,0:T(8,128)S(1)}, f32[2,32,512]{2,1,0:T(8,128)S(1)}, u32[]{:S(2)}, u32[]{:S(2)}) collective-permute-start(f32[2,32,512]{2,1,0:T(8,128)S(1)} %get-tuple-element.11), channel_id=1, source_target_pairs={{0,24},{8,0},{16,8},{24,16},{1,25},{9,1},{17,9},{25,17},{2,26},{10... | collective-permute-start | bytes 393224 | tf_op jit(solution)/shard_map/ppermute | solution.py:42
  9.3 24.8 %collective-permute-start.5 = (f32[2,256,128]{2,1,0:T(8,128)S(1)}, f32[2,256,128]{2,1,0:T(8,128)S(1)}, u32[]{:S(2)}, u32[]{:S(2)}) collective-permute-start(f32[2,256,128]{2,1,0:T(8,128)S(1)} %copy-done.1), channel_id=1, source_target_pairs={{0,4},{2,6},{4,0},{6,2},{1,5},{3,7},{5,1},{7,3},{8,12},{10,14},{12... | collective-permute-start | bytes 786440 | tf_op jit(solution)/shard_map/ppermute | solution.py:42
  11.9 0.7 %copy-start.2 = (s32[2,4]{1,0:T(2,128)S(1)}, s32[2,4]{1,0:T(2,128)}, u32[]{:S(2)}) copy-start(s32[2,4]{1,0:T(2,128)} %param.7) | copy-start | bytes 100
  13.9 5.9 %collective-permute-start.3 = (f32[2,32,128]{2,1,0:T(8,128)S(1)}, f32[2,32,128]{2,1,0:T(8,128)S(1)}, u32[]{:S(2)}, u32[]{:S(2)}) collective-permute-start(f32[2,32,128]{2,1,0:T(8,128)S(1)} %get-tuple-element.23), channel_id=1, source_target_pairs={{0,2},{2,4},{4,6},{6,0},{1,3},{3,5},{5,7},{7,1},{8,10},{10,12},{12... | collective-permute-start | bytes 98312 | tf_op jit(solution)/shard_map/ppermute | solution.py:42
  15.6 16.4 %collective-permute-start.7 = (f32[2,32,128]{2,1,0:T(8,128)S(1)}, f32[2,32,128]{2,1,0:T(8,128)S(1)}, u32[]{:S(2)}, u32[]{:S(2)}) collective-permute-start(f32[2,32,128]{2,1,0:T(8,128)S(1)} %get-tuple-element.22), channel_id=1, source_target_pairs={{0,4},{2,6},{4,0},{6,2},{1,5},{3,7},{5,1},{7,3},{8,12},{10,14},{12... | collective-permute-start | bytes 98312 | tf_op jit(solution)/shard_map/ppermute | solution.py:42
  18.2 13.8 %collective-permute-start.8 = (f32[2,32,128]{2,1,0:T(8,128)S(1)}, f32[2,32,128]{2,1,0:T(8,128)S(1)}, u32[]{:S(2)}, u32[]{:S(2)}) collective-permute-start(f32[2,32,128]{2,1,0:T(8,128)S(1)} %get-tuple-element.21), channel_id=1, source_target_pairs={{0,6},{2,0},{4,2},{6,4},{1,7},{3,1},{5,3},{7,5},{8,14},{10,8},{12,... | collective-permute-start | bytes 98312 | tf_op jit(solution)/shard_map/ppermute | solution.py:42
  19.8 20.2 %collective-permute-start.4 = (f32[2,256,128]{2,1,0:T(8,128)S(1)}, f32[2,256,128]{2,1,0:T(8,128)S(1)}, u32[]{:S(2)}, u32[]{:S(2)}) collective-permute-start(f32[2,256,128]{2,1,0:T(8,128)S(1)} %copy-done.1), channel_id=1, source_target_pairs={{0,2},{2,4},{4,6},{6,0},{1,3},{3,5},{5,7},{7,1},{8,10},{10,12},{12... | collective-permute-start | bytes 786440 | tf_op jit(solution)/shard_map/ppermute | solution.py:42
  25.9 14.1 %collective-permute-start.6 = (f32[2,256,128]{2,1,0:T(8,128)S(1)}, f32[2,256,128]{2,1,0:T(8,128)S(1)}, u32[]{:S(2)}, u32[]{:S(2)}) collective-permute-start(f32[2,256,128]{2,1,0:T(8,128)S(1)} %copy-done.1), channel_id=1, source_target_pairs={{0,6},{2,0},{4,2},{6,4},{1,7},{3,1},{5,3},{7,5},{8,14},{10,8},{12,... | collective-permute-start | bytes 786440 | tf_op jit(solution)/shard_map/ppermute | solution.py:42
  31.9 5.8 %collective-permute-start.10 = (f32[4,2,32,128]{3,2,1,0:T(8,128)S(1)}, f32[4,2,32,128]{3,2,1,0:T(8,128)S(1)}, u32[]{:S(2)}, u32[]{:S(2)}) collective-permute-start(f32[4,2,32,128]{3,2,1,0:T(8,128)S(1)} %pad_maximum_fusion.2.refs_4_), channel_id=1, source_target_pairs={{0,16},{8,24},{16,0},{24,8},{1,17},{9,25},{17,1},{25,9},{2,18},{10... | collective-permute-start | bytes 393224 | tf_op jit(solution)/shard_map/ppermute | solution.py:42
  32.0 5.7 %collective-permute-start.11 = (f32[4,2,32,128]{3,2,1,0:T(8,128)S(1)}, f32[4,2,32,128]{3,2,1,0:T(8,128)S(1)}, u32[]{:S(2)}, u32[]{:S(2)}) collective-permute-start(f32[4,2,32,128]{3,2,1,0:T(8,128)S(1)} %pad_maximum_fusion.2.refs_4_), channel_id=1, source_target_pairs={{0,24},{8,0},{16,8},{24,16},{1,25},{9,1},{17,9},{25,17},{2,26},{10... | collective-permute-start | bytes 393224 | tf_op jit(solution)/shard_map/ppermute | solution.py:42
  34.1 5.9 %collective-permute-start.9 = (f32[4,2,32,128]{3,2,1,0:T(8,128)S(1)}, f32[4,2,32,128]{3,2,1,0:T(8,128)S(1)}, u32[]{:S(2)}, u32[]{:S(2)}) collective-permute-start(f32[4,2,32,128]{3,2,1,0:T(8,128)S(1)} %pad_maximum_fusion.2.refs_4_), channel_id=1, source_target_pairs={{0,8},{8,16},{16,24},{24,0},{1,9},{9,17},{17,25},{25,1},{2,10},{10... | collective-permute-start | bytes 393224 | tf_op jit(solution)/shard_map/ppermute | solution.py:42
  41.6 1.8 %collective-permute-start.12 = (f32[2,384,128]{2,1,0:T(8,128)S(1)}, f32[2,384,128]{2,1,0:T(8,128)S(1)}, u32[]{:S(2)}, u32[]{:S(2)}) collective-permute-start(f32[2,384,128]{2,1,0:T(8,128)S(1)} %shard_map.59), channel_id=1, source_target_pairs={{0,1},{1,0},{2,3},{3,2},{4,5},{5,4},{6,7},{7,6},{8,9},{9,8},{10,11... | collective-permute-start | bytes 1179656 | tf_op jit(solution)/shard_map/ppermute | solution.py:42
  43.6 4.1 %collective-permute-start.13 = (f32[2,40,128]{2,1,0:T(8,128)S(1)}, f32[2,40,128]{2,1,0:T(8,128)S(1)}, u32[]{:S(2)}, u32[]{:S(2)}) collective-permute-start(f32[2,40,128]{2,1,0:T(8,128)S(1)} %get-tuple-element.26), channel_id=1, source_target_pairs={{0,6},{2,0},{4,2},{6,4},{1,7},{3,1},{5,3},{7,5},{8,14},{10,8},{12,... | collective-permute-start | bytes 122888 | tf_op jit(solution)/shard_map/ppermute | solution.py:42
  45.2 5.7 %collective-permute-start.14 = (f32[2,40,128]{2,1,0:T(8,128)S(1)}, f32[2,40,128]{2,1,0:T(8,128)S(1)}, u32[]{:S(2)}, u32[]{:S(2)}) collective-permute-start(f32[2,40,128]{2,1,0:T(8,128)S(1)} %get-tuple-element.25), channel_id=1, source_target_pairs={{0,4},{2,6},{4,0},{6,2},{1,5},{3,7},{5,1},{7,3},{8,12},{10,14},{12... | collective-permute-start | bytes 122888 | tf_op jit(solution)/shard_map/ppermute | solution.py:42
  46.4 5.8 %collective-permute-start.15 = (f32[2,40,128]{2,1,0:T(8,128)S(1)}, f32[2,40,128]{2,1,0:T(8,128)S(1)}, u32[]{:S(2)}, u32[]{:S(2)}) collective-permute-start(f32[2,40,128]{2,1,0:T(8,128)S(1)} %get-tuple-element.24), channel_id=1, source_target_pairs={{0,2},{2,4},{4,6},{6,0},{1,3},{3,5},{5,7},{7,1},{8,10},{10,12},{12... | collective-permute-start | bytes 122888 | tf_op jit(solution)/shard_map/ppermute | solution.py:42
  52.3 4.6 %collective-permute-start.16 = (f32[2,512]{1,0:T(2,128)S(1)}, f32[2,512]{1,0:T(2,128)S(1)}, u32[]{:S(2)}, u32[]{:S(2)}) collective-permute-start(f32[2,512]{1,0:T(2,128)S(1)} %bitcast.21), channel_id=1, source_target_pairs={{0,8},{8,16},{16,24},{24,0},{1,9},{9,17},{17,25},{25,1},{2,10},{10... | collective-permute-start | bytes 12296 | tf_op jit(solution)/shard_map/ppermute | solution.py:42
  52.8 4.0 %collective-permute-start.17 = (f32[2,512]{1,0:T(2,128)S(1)}, f32[2,512]{1,0:T(2,128)S(1)}, u32[]{:S(2)}, u32[]{:S(2)}) collective-permute-start(f32[2,512]{1,0:T(2,128)S(1)} %bitcast.22), channel_id=1, source_target_pairs={{0,16},{8,24},{16,0},{24,8},{1,17},{9,25},{17,1},{25,9},{2,18},{10... | collective-permute-start | bytes 12296 | tf_op jit(solution)/shard_map/ppermute | solution.py:42
  53.4 4.0 %collective-permute-start.18 = (f32[2,512]{1,0:T(2,128)S(1)}, f32[2,512]{1,0:T(2,128)S(1)}, u32[]{:S(2)}, u32[]{:S(2)}) collective-permute-start(f32[2,512]{1,0:T(2,128)S(1)} %bitcast.23), channel_id=1, source_target_pairs={{0,24},{8,0},{16,8},{24,16},{1,25},{9,1},{17,9},{25,17},{2,26},{10... | collective-permute-start | bytes 12296 | tf_op jit(solution)/shard_map/ppermute | solution.py:42

commit v11 on v10

--- a/solution.py
+++ b/solution.py
@@ -61,7 +61,7 @@
                 value = jnp.where((place - at) % len(slots) == d, slots[d], value)
             return value
 
-        early = [d for d in range(1, deep) if deep < 4 * d < 3 * deep]
+        early = [d for d in range(1, deep) if not deep < 4 * d < 3 * deep]
         late = [d for d in range(1, deep) if d not in early]
         far = {d: shifted(ancestor, "z", deep, d) for d in early}
 
@@ -72,6 +72,7 @@
             return lax.dynamic_slice_in_dim(partial, r * piece, piece, axis=1)
 
         sums = [shifted(rows_of((row + d) % rows), "row", rows, d) for d in range(1, rows)]
+        sums, far = lax.optimization_barrier((sums, far))
         scaled = sum(sums, rows_of(row))
 
         def columns_of(array, c):

time: 58.2 us -> 57.9 us (level)
  waiting for transfers between devices: 19.8 us -> 21.5 us
  starting transfers between devices: 29.6 us -> 28.6 us
  local copies, waits for them, and re-layouts: 1.87 us -> 0.88 us
    ppermute x19, waiting for transfers between devices: 19.8 us -> 21.5 us  [shifted(): lax.ppermute(array, axis, [(i, (i + shift) % size) for i in range(size)])]
    unnamed x7, local copies, waits for them, and re-layouts: 1.67 us -> 0.69 us
    ppermute x19, starting transfers between devices: 29.6 us -> 28.6 us  [shifted(): lax.ppermute(array, axis, [(i, (i + shift) % size) for i in range(size)])]
  transfers between devices with their start and end apart: 19 -> 19, of which waited for: 12 -> 16; matrix products, arithmetic and copies ran while one was open for 3% -> 6% of each run, Pallas kernels for 0% -> 0%
where the time goes in v11:
time: 57.9 us; the launch traced here: 57.7 us
  starting transfers between devices  28.6 us (49%)
  waiting for transfers between devices  21.5 us (37%)
  other arithmetic  2.64 us (5%)
  matrix products  1.61 us (3%)
  Pallas kernels  1.61 us (3%)
  local copies, waits for them, and re-layouts  0.88 us (2%)
  between operations  0.87 us (2%)
    ppermute x19, starting transfers between devices, shifted(): lax.ppermute(array, axis, [(i, (i + shift) % size) for i in range(size)])  28.6 us
    ppermute x19, waiting for transfers between devices, shifted(): lax.ppermute(array, axis, [(i, (i + shift) % size) for i in range(size)])  21.5 us
    dot_general x1, matrix products, per_device(): partial = jnp.einsum('srw,swv->srv', mine, factor_inv, precision=highest)  1.61 us
    pallas_call x1, Pallas kernels, per_device(): pl.pallas_call(functools.partial(multiply_tiles, deep, rows), out_shape=j...  1.61 us
  transfers between devices with their start and end apart: 19, of which 16 were waited for; matrix products, arithmetic and copies ran while one was open for 6% of the time, Pallas kernels for 0%

profile of v11, /device:TPU:0, one launch (start us, length us, event | category | flops | bytes accessed | tf_op | source)
XLA Modules:
  0.0 57.7 jit_solution(14448800319925263183)
XLA Ops:
  0.6 0.0 copy-start
  0.6 3.1 %collective-permute-start.3 = (f32[2,256,128]{2,1,0:T(8,128)}, f32[2,256,128]{2,1,0:T(8,128)S(1)}, u32[]{:S(2)}, u32[]{:S(2)}) collective-permute-start(f32[2,256,128]{2,1,0:T(8,128)} %refs_0_.1), channel_id=1, source_target_pairs={{0,2},{2,4},{4,6},{6,0},{1,3},{3,5},{5,7},{7,1},{8,10},{10,12},{12... | collective-permute-start | bytes 786440 | tf_op jit(solution)/shard_map/ppermute | solution.py:42
  3.7 2.1 %collective-permute-start.4 = (f32[2,256,128]{2,1,0:T(8,128)}, f32[2,256,128]{2,1,0:T(8,128)S(1)}, u32[]{:S(2)}, u32[]{:S(2)}) collective-permute-start(f32[2,256,128]{2,1,0:T(8,128)} %refs_0_.1), channel_id=1, source_target_pairs={{0,6},{2,0},{4,2},{6,4},{1,7},{3,1},{5,3},{7,5},{8,14},{10,8},{12,... | collective-permute-start | bytes 786440 | tf_op jit(solution)/shard_map/ppermute | solution.py:42
  5.8 1.6 %fusion = f32[2,128,512]{2,1,0:T(8,128)S(1)} fusion(f32[2,128,512]{2,1,0:T(8,128)} %param.6, f32[2,128,512]{2,1,0:T(8,128)S(1)} %copy-done, s32[]{:T(128)S(6)} %select_n.231), kind=kOutput, calls=%fused_computation.10 | convolution fusion | flops 201326592 | bytes 1179652 | tf_op jit(solution)/shard_map/srw,swv->srv/dot_general | solution.py:69
  7.5 1.7 %collective-permute-start = (f32[2,32,512]{2,1,0:T(8,128)S(1)}, f32[2,32,512]{2,1,0:T(8,128)S(1)}, u32[]{:S(2)}, u32[]{:S(2)}) collective-permute-start(f32[2,32,512]{2,1,0:T(8,128)S(1)} %get-tuple-element.22), channel_id=1, source_target_pairs={{0,8},{8,16},{16,24},{24,0},{1,9},{9,17},{17,25},{25,1},{2,10},{10... | collective-permute-start | bytes 393224 | tf_op jit(solution)/shard_map/ppermute | solution.py:42
  9.2 1.5 %collective-permute-start.1 = (f32[2,32,512]{2,1,0:T(8,128)S(1)}, f32[2,32,512]{2,1,0:T(8,128)S(1)}, u32[]{:S(2)}, u32[]{:S(2)}) collective-permute-start(f32[2,32,512]{2,1,0:T(8,128)S(1)} %get-tuple-element.21), channel_id=1, source_target_pairs={{0,16},{8,24},{16,0},{24,8},{1,17},{9,25},{17,1},{25,9},{2,18},{10... | collective-permute-start | bytes 393224 | tf_op jit(solution)/shard_map/ppermute | solution.py:42
  10.7 1.4 %collective-permute-start.2 = (f32[2,32,512]{2,1,0:T(8,128)S(1)}, f32[2,32,512]{2,1,0:T(8,128)S(1)}, u32[]{:S(2)}, u32[]{:S(2)}) collective-permute-start(f32[2,32,512]{2,1,0:T(8,128)S(1)} %get-tuple-element.20), channel_id=1, source_target_pairs={{0,24},{8,0},{16,8},{24,16},{1,25},{9,1},{17,9},{25,17},{2,26},{10... | collective-permute-start | bytes 393224 | tf_op jit(solution)/shard_map/ppermute | solution.py:42
  12.1 0.7 %copy-done.2 = s32[2,4]{1,0:T(2,128)S(1)} copy-done((s32[2,4]{1,0:T(2,128)S(1)}, s32[2,4]{1,0:T(2,128)}, u32[]{:S(2)}) %copy-start.2) | copy-done | bytes 56
  12.8 0.1 select_reduce_fusion
  13.0 0.1 sub.51
  13.0 1.7 %collective-permute-done = f32[2,32,512]{2,1,0:T(8,128)S(1)} collective-permute-done((f32[2,32,512]{2,1,0:T(8,128)S(1)}, f32[2,32,512]{2,1,0:T(8,128)S(1)}, u32[]{:S(2)}, u32[]{:S(2)}) %collective-permute-start) | collective-permute-done | bytes 131104 | tf_op jit(solution)/shard_map/ppermute | solution.py:42
  14.7 1.5 %collective-permute-done.1 = f32[2,32,512]{2,1,0:T(8,128)S(1)} collective-permute-done((f32[2,32,512]{2,1,0:T(8,128)S(1)}, f32[2,32,512]{2,1,0:T(8,128)S(1)}, u32[]{:S(2)}, u32[]{:S(2)}) %collective-permute-start.1) | collective-permute-done | bytes 131104 | tf_op jit(solution)/shard_map/ppermute | solution.py:42
  16.2 0.1 collective-permute-done.2
  16.4 0.0 collective-permute-done.3.refs_1_
  16.4 1.0 %collective-permute-done.4.refs_3_ = f32[2,256,128]{2,1,0:T(8,128)S(1)} collective-permute-done((f32[2,256,128]{2,1,0:T(8,128)}, f32[2,256,128]{2,1,0:T(8,128)S(1)}, u32[]{:S(2)}, u32[]{:S(2)}) %collective-permute-start.4) | collective-permute-done | bytes 262176 | tf_op jit(solution)/shard_map/ppermute | solution.py:42
  17.4 0.0 copy-start.1
  17.4 1.2 %collective-permute-start.5 = (f32[2,32,128]{2,1,0:T(8,128)S(1)}, f32[2,32,128]{2,1,0:T(8,128)S(1)}, u32[]{:S(2)}, u32[]{:S(2)}) collective-permute-start(f32[2,32,128]{2,1,0:T(8,128)S(1)} %get-tuple-element.33), channel_id=1, source_target_pairs={{0,2},{2,4},{4,6},{6,0},{1,3},{3,5},{5,7},{7,1},{8,10},{10,12},{12... | collective-permute-start | bytes 98312 | tf_op jit(solution)/shard_map/ppermute | solution.py:42
  18.6 1.7 %collective-permute-start.7 = (f32[2,32,128]{2,1,0:T(8,128)S(1)}, f32[2,32,128]{2,1,0:T(8,128)S(1)}, u32[]{:S(2)}, u32[]{:S(2)}) collective-permute-start(f32[2,32,128]{2,1,0:T(8,128)S(1)} %get-tuple-element.32), channel_id=1, source_target_pairs={{0,4},{2,6},{4,0},{6,2},{1,5},{3,7},{5,1},{7,3},{8,12},{10,14},{12... | collective-permute-start | bytes 98312 | tf_op jit(solution)/shard_map/ppermute | solution.py:42
  20.3 1.3 %collective-permute-start.8 = (f32[2,32,128]{2,1,0:T(8,128)S(1)}, f32[2,32,128]{2,1,0:T(8,128)S(1)}, u32[]{:S(2)}, u32[]{:S(2)}) collective-permute-start(f32[2,32,128]{2,1,0:T(8,128)S(1)} %get-tuple-element.31), channel_id=1, source_target_pairs={{0,6},{2,0},{4,2},{6,4},{1,7},{3,1},{5,3},{7,5},{8,14},{10,8},{12,... | collective-permute-start | bytes 98312 | tf_op jit(solution)/shard_map/ppermute | solution.py:42
  21.7 1.6 %collective-permute-done.5 = f32[2,32,128]{2,1,0:T(8,128)S(1)} collective-permute-done((f32[2,32,128]{2,1,0:T(8,128)S(1)}, f32[2,32,128]{2,1,0:T(8,128)S(1)}, u32[]{:S(2)}, u32[]{:S(2)}) %collective-permute-start.5) | collective-permute-done | bytes 32800 | tf_op jit(solution)/shard_map/ppermute | solution.py:42
  23.3 0.1 collective-permute-start.6
  23.4 0.8 %collective-permute-done.7 = f32[2,32,128]{2,1,0:T(8,128)S(1)} collective-permute-done((f32[2,32,128]{2,1,0:T(8,128)S(1)}, f32[2,32,128]{2,1,0:T(8,128)S(1)}, u32[]{:S(2)}, u32[]{:S(2)}) %collective-permute-start.7) | collective-permute-done | bytes 32800 | tf_op jit(solution)/shard_map/ppermute | solution.py:42
  24.2 0.2 collective-permute-done.8
  24.5 1.6 %collective-permute-start.10 = (f32[4,2,32,128]{3,2,1,0:T(8,128)S(1)}, f32[4,2,32,128]{3,2,1,0:T(8,128)S(1)}, u32[]{:S(2)}, u32[]{:S(2)}) collective-permute-start(f32[4,2,32,128]{3,2,1,0:T(8,128)S(1)} %pad_maximum_fusion.2.refs_4_), channel_id=1, source_target_pairs={{0,16},{8,24},{16,0},{24,8},{1,17},{9,25},{17,1},{25,9},{2,18},{10... | collective-permute-start | bytes 393224 | tf_op jit(solution)/shard_map/ppermute | solution.py:42
  26.1 1.4 %collective-permute-start.11 = (f32[4,2,32,128]{3,2,1,0:T(8,128)S(1)}, f32[4,2,32,128]{3,2,1,0:T(8,128)S(1)}, u32[]{:S(2)}, u32[]{:S(2)}) collective-permute-start(f32[4,2,32,128]{3,2,1,0:T(8,128)S(1)} %pad_maximum_fusion.2.refs_4_), channel_id=1, source_target_pairs={{0,24},{8,0},{16,8},{24,16},{1,25},{9,1},{17,9},{25,17},{2,26},{10... | collective-permute-start | bytes 393224 | tf_op jit(solution)/shard_map/ppermute | solution.py:42
  27.5 0.6 %collective-permute-start.9 = (f32[4,2,32,128]{3,2,1,0:T(8,128)S(1)}, f32[4,2,32,128]{3,2,1,0:T(8,128)S(1)}, u32[]{:S(2)}, u32[]{:S(2)}) collective-permute-start(f32[4,2,32,128]{3,2,1,0:T(8,128)S(1)} %pad_maximum_fusion.2.refs_4_), channel_id=1, source_target_pairs={{0,8},{8,16},{16,24},{24,0},{1,9},{9,17},{17,25},{25,1},{2,10},{10... | collective-permute-start | bytes 393224 | tf_op jit(solution)/shard_map/ppermute | solution.py:42
  28.1 0.1 pad_add_fusion.place
  28.2 2.7 %collective-permute-done.10.refs_6_ = f32[4,2,32,128]{3,2,1,0:T(8,128)S(1)} collective-permute-done((f32[4,2,32,128]{3,2,1,0:T(8,128)S(1)}, f32[4,2,32,128]{3,2,1,0:T(8,128)S(1)}, u32[]{:S(2)}, u32[]{:S(2)}) %collective-permute-start.10) | collective-permute-done | bytes 131104 | tf_op jit(solution)/shard_map/ppermute | solution.py:42
  30.9 0.1 collective-permute-done.11.refs_7_
  31.0 2.3 %collective-permute-done.9.refs_5_ = f32[4,2,32,128]{3,2,1,0:T(8,128)S(1)} collective-permute-done((f32[4,2,32,128]{3,2,1,0:T(8,128)S(1)}, f32[4,2,32,128]{3,2,1,0:T(8,128)S(1)}, u32[]{:S(2)}, u32[]{:S(2)}) %collective-permute-start.9) | collective-permute-done | bytes 131104 | tf_op jit(solution)/shard_map/ppermute | solution.py:42
  33.4 2.7 %collective-permute-done.6.refs_2_ = f32[2,256,128]{2,1,0:T(8,128)S(1)} collective-permute-done((f32[2,256,128]{2,1,0:T(8,128)S(1)}, f32[2,256,128]{2,1,0:T(8,128)S(1)}, u32[]{:S(2)}, u32[]{:S(2)}) %collective-permute-start.6) | collective-permute-done | bytes 262176 | tf_op jit(solution)/shard_map/ppermute | solution.py:42
  36.1 1.6 %shard_map.59 = f32[2,384,128]{2,1,0:T(8,128)S(1)} custom-call(s32[13]{0:T(128)S(1)} %pad_add_fusion.place, f32[2,256,128]{2,1,0:T(8,128)S(1)} %copy-done.1, f32[2,256,128]{2,1,0:T(8,128)S(1)} %collective-permute-done.3.refs_1_, f32[2,256,128]{2,1,0:T(8,128)S(1)} %collective-permute-done.6.refs_2_, f32[2,256,128]{2,1,0:T(8,128)S(1)} %collective-permute-done.4.refs_3_, ...), custom_call_target="tpu_custom_call" | custom-call | tf_op jit(solution)/shard_map/pallas_call | solution.py:100
  37.7 0.1 collective-permute-start.12
  37.8 0.9 %multiply_reduce_fusion.1 = f32[2,128]{1,0:T(2,128)S(1)} fusion(f32[2,128,512]{2,1,0:T(8,128)} %param.6, s32[]{:T(128)S(6)} %select_n.241), kind=kLoop, calls=%fused_computation.6 | loop fusion | flops 65280 | bytes 132100 | tf_op jit(solution)/shard_map/reduce_sum | solution.py:116
  38.7 0.7 %collective-permute-done.12 = f32[2,384,128]{2,1,0:T(8,128)S(1)} collective-permute-done((f32[2,384,128]{2,1,0:T(8,128)S(1)}, f32[2,384,128]{2,1,0:T(8,128)S(1)}, u32[]{:S(2)}, u32[]{:S(2)}) %collective-permute-start.12) | collective-permute-done | bytes 393248 | tf_op jit(solution)/shard_map/ppermute | solution.py:42
  39.5 0.1 multiply_reduce_fusion
  39.7 5.6 %collective-permute-start.13 = (f32[2,40,128]{2,1,0:T(8,128)S(1)}, f32[2,40,128]{2,1,0:T(8,128)S(1)}, u32[]{:S(2)}, u32[]{:S(2)}) collective-permute-start(f32[2,40,128]{2,1,0:T(8,128)S(1)} %get-tuple-element.36), channel_id=1, source_target_pairs={{0,6},{2,0},{4,2},{6,4},{1,7},{3,1},{5,3},{7,5},{8,14},{10,8},{12,... | collective-permute-start | bytes 122888 | tf_op jit(solution)/shard_map/ppermute | solution.py:42
  45.3 0.1 collective-permute-start.14
  45.4 0.6 %collective-permute-start.15 = (f32[2,40,128]{2,1,0:T(8,128)S(1)}, f32[2,40,128]{2,1,0:T(8,128)S(1)}, u32[]{:S(2)}, u32[]{:S(2)}) collective-permute-start(f32[2,40,128]{2,1,0:T(8,128)S(1)} %get-tuple-element.34), channel_id=1, source_target_pairs={{0,2},{2,4},{4,6},{6,0},{1,3},{3,5},{5,7},{7,1},{8,10},{10,12},{12... | collective-permute-start | bytes 122888 | tf_op jit(solution)/shard_map/ppermute | solution.py:42
  45.9 1.3 %collective-permute-done.13 = f32[2,40,128]{2,1,0:T(8,128)S(1)} collective-permute-done((f32[2,40,128]{2,1,0:T(8,128)S(1)}, f32[2,40,128]{2,1,0:T(8,128)S(1)}, u32[]{:S(2)}, u32[]{:S(2)}) %collective-permute-start.13) | collective-permute-done | bytes 40992 | tf_op jit(solution)/shard_map/ppermute | solution.py:42
  47.2 3.2 %collective-permute-done.14 = f32[2,40,128]{2,1,0:T(8,128)S(1)} collective-permute-done((f32[2,40,128]{2,1,0:T(8,128)S(1)}, f32[2,40,128]{2,1,0:T(8,128)S(1)}, u32[]{:S(2)}, u32[]{:S(2)}) %collective-permute-start.14) | collective-permute-done | bytes 40992 | tf_op jit(solution)/shard_map/ppermute | solution.py:42
  50.4 0.7 %collective-permute-done.15 = f32[2,40,128]{2,1,0:T(8,128)S(1)} collective-permute-done((f32[2,40,128]{2,1,0:T(8,128)S(1)}, f32[2,40,128]{2,1,0:T(8,128)S(1)}, u32[]{:S(2)}, u32[]{:S(2)}) %collective-permute-start.15) | collective-permute-done | bytes 40992 | tf_op jit(solution)/shard_map/ppermute | solution.py:42
  51.2 0.6 collective-permute-start.16
  51.8 1.5 %collective-permute-start.17 = (f32[2,512]{1,0:T(2,128)S(1)}, f32[2,512]{1,0:T(2,128)S(1)}, u32[]{:S(2)}, u32[]{:S(2)}) collective-permute-start(f32[2,512]{1,0:T(2,128)S(1)} %bitcast.22), channel_id=1, source_target_pairs={{0,16},{8,24},{16,0},{24,8},{1,17},{9,25},{17,1},{25,9},{2,18},{10... | collective-permute-start | bytes 12296 | tf_op jit(solution)/shard_map/ppermute | solution.py:42
  53.3 2.4 %collective-permute-start.18 = (f32[2,512]{1,0:T(2,128)S(1)}, f32[2,512]{1,0:T(2,128)S(1)}, u32[]{:S(2)}, u32[]{:S(2)}) collective-permute-start(f32[2,512]{1,0:T(2,128)S(1)} %bitcast.23), channel_id=1, source_target_pairs={{0,24},{8,0},{16,8},{24,16},{1,25},{9,1},{17,9},{25,17},{2,26},{10... | collective-permute-start | bytes 12296 | tf_op jit(solution)/shard_map/ppermute | solution.py:42
  55.7 0.7 %slice_negate_fusion = f32[2,32,512]{2,1,0:T(8,128)} fusion(f32[2,40,512]{2,1,0:T(8,128)S(1)} %pad_maximum_fusion.1), kind=kLoop, calls=%fused_computation.4 | loop fusion | flops 32768 | bytes 262144 | tf_op jit(solution)/shard_map/neg | solution.py:132
  56.4 0.6 %collective-permute-done.18 = f32[2,512]{1,0:T(2,128)S(1)} collective-permute-done((f32[2,512]{1,0:T(2,128)S(1)}, f32[2,512]{1,0:T(2,128)S(1)}, u32[]{:S(2)}, u32[]{:S(2)}) %collective-permute-start.18) | collective-permute-done | bytes 4128 | tf_op jit(solution)/shard_map/ppermute | solution.py:42
  57.1 0.6 %add_add_fusion.1 = f32[2,512]{1,0:T(2,128)} fusion(f32[2,512]{1,0:T(2,128)S(1)} %collective-permute-done.18, f32[2,512]{1,0:T(2,128)S(1)} %collective-permute-done.17, f32[2,512]{1,0:T(2,128)S(1)} %collective-permute-done.16, f32[2,1,512]{2,1,0:T(1,128)S(1)} %pad_maximum_fusion.7), kind=kLoop, calls=%fused_computation.23 | loop fusion | flops 3072 | bytes 20480 | tf_op jit(solution)/shard_map/add | solution.py:131
  (25 shorter events, 0.3 us)
Async XLA Ops:
  0.6 5.2 %copy-start = (f32[2,128,512]{2,1,0:T(8,128)S(1)}, f32[2,128,512]{2,1,0:T(8,128)}, u32[]{:S(2)}) copy-start(f32[2,128,512]{2,1,0:T(8,128)} %param.5) | copy-start | bytes 1572868
  0.6 15.7 %collective-permute-start.3 = (f32[2,256,128]{2,1,0:T(8,128)}, f32[2,256,128]{2,1,0:T(8,128)S(1)}, u32[]{:S(2)}, u32[]{:S(2)}) collective-permute-start(f32[2,256,128]{2,1,0:T(8,128)} %refs_0_.1), channel_id=1, source_target_pairs={{0,2},{2,4},{4,6},{6,0},{1,3},{3,5},{5,7},{7,1},{8,10},{10,12},{12... | collective-permute-start | bytes 786440 | tf_op jit(solution)/shard_map/ppermute | solution.py:42
  3.7 13.6 %collective-permute-start.4 = (f32[2,256,128]{2,1,0:T(8,128)}, f32[2,256,128]{2,1,0:T(8,128)S(1)}, u32[]{:S(2)}, u32[]{:S(2)}) collective-permute-start(f32[2,256,128]{2,1,0:T(8,128)} %refs_0_.1), channel_id=1, source_target_pairs={{0,6},{2,0},{4,2},{6,4},{1,7},{3,1},{5,3},{7,5},{8,14},{10,8},{12,... | collective-permute-start | bytes 786440 | tf_op jit(solution)/shard_map/ppermute | solution.py:42
  7.5 7.2 %collective-permute-start = (f32[2,32,512]{2,1,0:T(8,128)S(1)}, f32[2,32,512]{2,1,0:T(8,128)S(1)}, u32[]{:S(2)}, u32[]{:S(2)}) collective-permute-start(f32[2,32,512]{2,1,0:T(8,128)S(1)} %get-tuple-element.22), channel_id=1, source_target_pairs={{0,8},{8,16},{16,24},{24,0},{1,9},{9,17},{17,25},{25,1},{2,10},{10... | collective-permute-start | bytes 393224 | tf_op jit(solution)/shard_map/ppermute | solution.py:42
  9.2 7.0 %collective-permute-start.1 = (f32[2,32,512]{2,1,0:T(8,128)S(1)}, f32[2,32,512]{2,1,0:T(8,128)S(1)}, u32[]{:S(2)}, u32[]{:S(2)}) collective-permute-start(f32[2,32,512]{2,1,0:T(8,128)S(1)} %get-tuple-element.21), channel_id=1, source_target_pairs={{0,16},{8,24},{16,0},{24,8},{1,17},{9,25},{17,1},{25,9},{2,18},{10... | collective-permute-start | bytes 393224 | tf_op jit(solution)/shard_map/ppermute | solution.py:42
  10.7 5.6 %collective-permute-start.2 = (f32[2,32,512]{2,1,0:T(8,128)S(1)}, f32[2,32,512]{2,1,0:T(8,128)S(1)}, u32[]{:S(2)}, u32[]{:S(2)}) collective-permute-start(f32[2,32,512]{2,1,0:T(8,128)S(1)} %get-tuple-element.20), channel_id=1, source_target_pairs={{0,24},{8,0},{16,8},{24,16},{1,25},{9,1},{17,9},{25,17},{2,26},{10... | collective-permute-start | bytes 393224 | tf_op jit(solution)/shard_map/ppermute | solution.py:42
  12.1 0.7 %copy-start.2 = (s32[2,4]{1,0:T(2,128)S(1)}, s32[2,4]{1,0:T(2,128)}, u32[]{:S(2)}) copy-start(s32[2,4]{1,0:T(2,128)} %param.7) | copy-start | bytes 100
  17.4 6.0 %copy-start.1 = (f32[2,256,128]{2,1,0:T(8,128)S(1)}, f32[2,256,128]{2,1,0:T(8,128)}, u32[]{:S(2)}) copy-start(f32[2,256,128]{2,1,0:T(8,128)} %refs_0_.1) | copy-start | bytes 786436
  17.4 5.9 %collective-permute-start.5 = (f32[2,32,128]{2,1,0:T(8,128)S(1)}, f32[2,32,128]{2,1,0:T(8,128)S(1)}, u32[]{:S(2)}, u32[]{:S(2)}) collective-permute-start(f32[2,32,128]{2,1,0:T(8,128)S(1)} %get-tuple-element.33), channel_id=1, source_target_pairs={{0,2},{2,4},{4,6},{6,0},{1,3},{3,5},{5,7},{7,1},{8,10},{10,12},{12... | collective-permute-start | bytes 98312 | tf_op jit(solution)/shard_map/ppermute | solution.py:42
  18.6 5.6 %collective-permute-start.7 = (f32[2,32,128]{2,1,0:T(8,128)S(1)}, f32[2,32,128]{2,1,0:T(8,128)S(1)}, u32[]{:S(2)}, u32[]{:S(2)}) collective-permute-start(f32[2,32,128]{2,1,0:T(8,128)S(1)} %get-tuple-element.32), channel_id=1, source_target_pairs={{0,4},{2,6},{4,0},{6,2},{1,5},{3,7},{5,1},{7,3},{8,12},{10,14},{12... | collective-permute-start | bytes 98312 | tf_op jit(solution)/shard_map/ppermute | solution.py:42
  20.3 4.1 %collective-permute-start.8 = (f32[2,32,128]{2,1,0:T(8,128)S(1)}, f32[2,32,128]{2,1,0:T(8,128)S(1)}, u32[]{:S(2)}, u32[]{:S(2)}) collective-permute-start(f32[2,32,128]{2,1,0:T(8,128)S(1)} %get-tuple-element.31), channel_id=1, source_target_pairs={{0,6},{2,0},{4,2},{6,4},{1,7},{3,1},{5,3},{7,5},{8,14},{10,8},{12,... | collective-permute-start | bytes 98312 | tf_op jit(solution)/shard_map/ppermute | solution.py:42
  23.3 12.7 %collective-permute-start.6 = (f32[2,256,128]{2,1,0:T(8,128)S(1)}, f32[2,256,128]{2,1,0:T(8,128)S(1)}, u32[]{:S(2)}, u32[]{:S(2)}) collective-permute-start(f32[2,256,128]{2,1,0:T(8,128)S(1)} %copy-done.1), channel_id=1, source_target_pairs={{0,4},{2,6},{4,0},{6,2},{1,5},{3,7},{5,1},{7,3},{8,12},{10,14},{12... | collective-permute-start | bytes 786440 | tf_op jit(solution)/shard_map/ppermute | solution.py:42
  24.5 6.4 %collective-permute-start.10 = (f32[4,2,32,128]{3,2,1,0:T(8,128)S(1)}, f32[4,2,32,128]{3,2,1,0:T(8,128)S(1)}, u32[]{:S(2)}, u32[]{:S(2)}) collective-permute-start(f32[4,2,32,128]{3,2,1,0:T(8,128)S(1)} %pad_maximum_fusion.2.refs_4_), channel_id=1, source_target_pairs={{0,16},{8,24},{16,0},{24,8},{1,17},{9,25},{17,1},{25,9},{2,18},{10... | collective-permute-start | bytes 393224 | tf_op jit(solution)/shard_map/ppermute | solution.py:42
  26.1 5.0 %collective-permute-start.11 = (f32[4,2,32,128]{3,2,1,0:T(8,128)S(1)}, f32[4,2,32,128]{3,2,1,0:T(8,128)S(1)}, u32[]{:S(2)}, u32[]{:S(2)}) collective-permute-start(f32[4,2,32,128]{3,2,1,0:T(8,128)S(1)} %pad_maximum_fusion.2.refs_4_), channel_id=1, source_target_pairs={{0,24},{8,0},{16,8},{24,16},{1,25},{9,1},{17,9},{25,17},{2,26},{10... | collective-permute-start | bytes 393224 | tf_op jit(solution)/shard_map/ppermute | solution.py:42
  27.5 5.9 %collective-permute-start.9 = (f32[4,2,32,128]{3,2,1,0:T(8,128)S(1)}, f32[4,2,32,128]{3,2,1,0:T(8,128)S(1)}, u32[]{:S(2)}, u32[]{:S(2)}) collective-permute-start(f32[4,2,32,128]{3,2,1,0:T(8,128)S(1)} %pad_maximum_fusion.2.refs_4_), channel_id=1, source_target_pairs={{0,8},{8,16},{16,24},{24,0},{1,9},{9,17},{17,25},{25,1},{2,10},{10... | collective-permute-start | bytes 393224 | tf_op jit(solution)/shard_map/ppermute | solution.py:42
  37.7 1.8 %collective-permute-start.12 = (f32[2,384,128]{2,1,0:T(8,128)S(1)}, f32[2,384,128]{2,1,0:T(8,128)S(1)}, u32[]{:S(2)}, u32[]{:S(2)}) collective-permute-start(f32[2,384,128]{2,1,0:T(8,128)S(1)} %shard_map.59), channel_id=1, source_target_pairs={{0,1},{1,0},{2,3},{3,2},{4,5},{5,4},{6,7},{7,6},{8,9},{9,8},{10,11... | collective-permute-start | bytes 1179656 | tf_op jit(solution)/shard_map/ppermute | solution.py:42
  39.7 7.5 %collective-permute-start.13 = (f32[2,40,128]{2,1,0:T(8,128)S(1)}, f32[2,40,128]{2,1,0:T(8,128)S(1)}, u32[]{:S(2)}, u32[]{:S(2)}) collective-permute-start(f32[2,40,128]{2,1,0:T(8,128)S(1)} %get-tuple-element.36), channel_id=1, source_target_pairs={{0,6},{2,0},{4,2},{6,4},{1,7},{3,1},{5,3},{7,5},{8,14},{10,8},{12,... | collective-permute-start | bytes 122888 | tf_op jit(solution)/shard_map/ppermute | solution.py:42
  45.3 5.1 %collective-permute-start.14 = (f32[2,40,128]{2,1,0:T(8,128)S(1)}, f32[2,40,128]{2,1,0:T(8,128)S(1)}, u32[]{:S(2)}, u32[]{:S(2)}) collective-permute-start(f32[2,40,128]{2,1,0:T(8,128)S(1)} %get-tuple-element.35), channel_id=1, source_target_pairs={{0,4},{2,6},{4,0},{6,2},{1,5},{3,7},{5,1},{7,3},{8,12},{10,14},{12... | collective-permute-start | bytes 122888 | tf_op jit(solution)/shard_map/ppermute | solution.py:42
  45.4 5.8 %collective-permute-start.15 = (f32[2,40,128]{2,1,0:T(8,128)S(1)}, f32[2,40,128]{2,1,0:T(8,128)S(1)}, u32[]{:S(2)}, u32[]{:S(2)}) collective-permute-start(f32[2,40,128]{2,1,0:T(8,128)S(1)} %get-tuple-element.34), channel_id=1, source_target_pairs={{0,2},{2,4},{4,6},{6,0},{1,3},{3,5},{5,7},{7,1},{8,10},{10,12},{12... | collective-permute-start | bytes 122888 | tf_op jit(solution)/shard_map/ppermute | solution.py:42
  51.2 5.2 %collective-permute-start.16 = (f32[2,512]{1,0:T(2,128)S(1)}, f32[2,512]{1,0:T(2,128)S(1)}, u32[]{:S(2)}, u32[]{:S(2)}) collective-permute-start(f32[2,512]{1,0:T(2,128)S(1)} %bitcast.21), channel_id=1, source_target_pairs={{0,8},{8,16},{16,24},{24,0},{1,9},{9,17},{17,25},{25,1},{2,10},{10... | collective-permute-start | bytes 12296 | tf_op jit(solution)/shard_map/ppermute | solution.py:42
  51.8 4.6 %collective-permute-start.17 = (f32[2,512]{1,0:T(2,128)S(1)}, f32[2,512]{1,0:T(2,128)S(1)}, u32[]{:S(2)}, u32[]{:S(2)}) collective-permute-start(f32[2,512]{1,0:T(2,128)S(1)} %bitcast.22), channel_id=1, source_target_pairs={{0,16},{8,24},{16,0},{24,8},{1,17},{9,25},{17,1},{25,9},{2,18},{10... | collective-permute-start | bytes 12296 | tf_op jit(solution)/shard_map/ppermute | solution.py:42
  53.3 3.7 %collective-permute-start.18 = (f32[2,512]{1,0:T(2,128)S(1)}, f32[2,512]{1,0:T(2,128)S(1)}, u32[]{:S(2)}, u32[]{:S(2)}) collective-permute-start(f32[2,512]{1,0:T(2,128)S(1)} %bitcast.23), channel_id=1, source_target_pairs={{0,24},{8,0},{16,8},{24,16},{1,25},{9,1},{17,9},{25,17},{2,26},{10... | collective-permute-start | bytes 12296 | tf_op jit(solution)/shard_map/ppermute | solution.py:42

commit v12 on v11

--- a/solution.py
+++ b/solution.py
@@ -82,8 +82,9 @@
         for shift in range(1, deep):
             slots.append(shifted(columns_of(scaled, (z + shift) % deep), "z", deep, shift))
         if deep > 1:
-            slots[1], held_back = lax.optimization_barrier((slots[1], ancestor))
-            far |= {d: shifted(held_back, "z", deep, d) for d in late}
+            slots, far[1] = lax.optimization_barrier((slots, far[1]))
+            for d in late:
+                far[d] = shifted(far[d - 1], "z", deep, 1)
         slots = gathered(jnp.stack(slots), "row", rows)
 
         count = jnp.arange(deep, dtype=jnp.int32)

time: 57.9 us -> 53.4 us (0.922)
  waiting for transfers between devices: 21.5 us -> 17.7 us
  starting transfers between devices: 28.6 us -> 27.8 us
    ppermute x19, waiting for transfers between devices: 21.5 us -> 17.7 us  [shifted(): lax.ppermute(array, axis, [(i, (i + shift) % size) for i in range(size)])]
    ppermute x19, starting transfers between devices: 28.6 us -> 27.8 us  [shifted(): lax.ppermute(array, axis, [(i, (i + shift) % size) for i in range(size)])]
  transfers between devices with their start and end apart: 19 -> 19, of which waited for: 16 -> 15; matrix products, arithmetic and copies ran while one was open for 6% -> 7% of each run, Pallas kernels for 0% -> 0%
where the time goes in v12:
time: 53.4 us; the launch traced here: 53.2 us
  starting transfers between devices  27.8 us (52%)
  waiting for transfers between devices  17.7 us (33%)
  other arithmetic  2.64 us (5%)
  matrix products  1.61 us (3%)
  Pallas kernels  1.61 us (3%)
  local copies, waits for them, and re-layouts  0.88 us (2%)
  between operations  0.87 us (2%)
    ppermute x19, starting transfers between devices, shifted(): lax.ppermute(array, axis, [(i, (i + shift) % size) for i in range(size)])  27.8 us
    ppermute x19, waiting for transfers between devices, shifted(): lax.ppermute(array, axis, [(i, (i + shift) % size) for i in range(size)])  17.7 us
    dot_general x1, matrix products, per_device(): partial = jnp.einsum('srw,swv->srv', mine, factor_inv, precision=highest)  1.61 us
    pallas_call x1, Pallas kernels, per_device(): pl.pallas_call(functools.partial(multiply_tiles, deep, rows), out_shape=j...  1.61 us
  transfers between devices with their start and end apart: 19, of which 15 were waited for; matrix products, arithmetic and copies ran while one was open for 7% of the time, Pallas kernels for 0%

profile of v12, /device:TPU:0, one launch (start us, length us, event | category | flops | bytes accessed | tf_op | source)
XLA Modules:
  0.0 53.2 jit_solution(14648521068649864949)
XLA Ops:
  0.6 0.0 copy-start
  0.6 3.1 %collective-permute-start.3 = (f32[2,256,128]{2,1,0:T(8,128)}, f32[2,256,128]{2,1,0:T(8,128)S(1)}, u32[]{:S(2)}, u32[]{:S(2)}) collective-permute-start(f32[2,256,128]{2,1,0:T(8,128)} %refs_0_.1), channel_id=1, source_target_pairs={{0,2},{2,4},{4,6},{6,0},{1,3},{3,5},{5,7},{7,1},{8,10},{10,12},{12... | collective-permute-start | bytes 786440 | tf_op jit(solution)/shard_map/ppermute | solution.py:42
  3.7 2.1 %collective-permute-start.4 = (f32[2,256,128]{2,1,0:T(8,128)}, f32[2,256,128]{2,1,0:T(8,128)S(1)}, u32[]{:S(2)}, u32[]{:S(2)}) collective-permute-start(f32[2,256,128]{2,1,0:T(8,128)} %refs_0_.1), channel_id=1, source_target_pairs={{0,6},{2,0},{4,2},{6,4},{1,7},{3,1},{5,3},{7,5},{8,14},{10,8},{12,... | collective-permute-start | bytes 786440 | tf_op jit(solution)/shard_map/ppermute | solution.py:42
  5.8 1.6 %fusion = f32[2,128,512]{2,1,0:T(8,128)S(1)} fusion(f32[2,128,512]{2,1,0:T(8,128)} %param.6, f32[2,128,512]{2,1,0:T(8,128)S(1)} %copy-done, s32[]{:T(128)S(6)} %select_n.231), kind=kOutput, calls=%fused_computation.10 | convolution fusion | flops 201326592 | bytes 1179652 | tf_op jit(solution)/shard_map/srw,swv->srv/dot_general | solution.py:69
  7.5 1.7 %collective-permute-start = (f32[2,32,512]{2,1,0:T(8,128)S(1)}, f32[2,32,512]{2,1,0:T(8,128)S(1)}, u32[]{:S(2)}, u32[]{:S(2)}) collective-permute-start(f32[2,32,512]{2,1,0:T(8,128)S(1)} %get-tuple-element.28), channel_id=1, source_target_pairs={{0,8},{8,16},{16,24},{24,0},{1,9},{9,17},{17,25},{25,1},{2,10},{10... | collective-permute-start | bytes 393224 | tf_op jit(solution)/shard_map/ppermute | solution.py:42
  9.2 1.5 %collective-permute-start.1 = (f32[2,32,512]{2,1,0:T(8,128)S(1)}, f32[2,32,512]{2,1,0:T(8,128)S(1)}, u32[]{:S(2)}, u32[]{:S(2)}) collective-permute-start(f32[2,32,512]{2,1,0:T(8,128)S(1)} %get-tuple-element.27), channel_id=1, source_target_pairs={{0,16},{8,24},{16,0},{24,8},{1,17},{9,25},{17,1},{25,9},{2,18},{10... | collective-permute-start | bytes 393224 | tf_op jit(solution)/shard_map/ppermute | solution.py:42
  10.7 1.4 %collective-permute-start.2 = (f32[2,32,512]{2,1,0:T(8,128)S(1)}, f32[2,32,512]{2,1,0:T(8,128)S(1)}, u32[]{:S(2)}, u32[]{:S(2)}) collective-permute-start(f32[2,32,512]{2,1,0:T(8,128)S(1)} %get-tuple-element.26), channel_id=1, source_target_pairs={{0,24},{8,0},{16,8},{24,16},{1,25},{9,1},{17,9},{25,17},{2,26},{10... | collective-permute-start | bytes 393224 | tf_op jit(solution)/shard_map/ppermute | solution.py:42
  12.1 0.7 %copy-done.2 = s32[2,4]{1,0:T(2,128)S(1)} copy-done((s32[2,4]{1,0:T(2,128)S(1)}, s32[2,4]{1,0:T(2,128)}, u32[]{:S(2)}) %copy-start.2) | copy-done | bytes 56
  12.8 0.1 select_reduce_fusion
  13.0 0.1 sub.51
  13.0 1.7 %collective-permute-done = f32[2,32,512]{2,1,0:T(8,128)S(1)} collective-permute-done((f32[2,32,512]{2,1,0:T(8,128)S(1)}, f32[2,32,512]{2,1,0:T(8,128)S(1)}, u32[]{:S(2)}, u32[]{:S(2)}) %collective-permute-start) | collective-permute-done | bytes 131104 | tf_op jit(solution)/shard_map/ppermute | solution.py:42
  14.7 1.5 %collective-permute-done.1 = f32[2,32,512]{2,1,0:T(8,128)S(1)} collective-permute-done((f32[2,32,512]{2,1,0:T(8,128)S(1)}, f32[2,32,512]{2,1,0:T(8,128)S(1)}, u32[]{:S(2)}, u32[]{:S(2)}) %collective-permute-start.1) | collective-permute-done | bytes 131104 | tf_op jit(solution)/shard_map/ppermute | solution.py:42
  16.2 0.1 collective-permute-done.2
  16.4 0.0 collective-permute-done.3.refs_1_
  16.4 1.0 %collective-permute-done.4.refs_3_ = f32[2,256,128]{2,1,0:T(8,128)S(1)} collective-permute-done((f32[2,256,128]{2,1,0:T(8,128)}, f32[2,256,128]{2,1,0:T(8,128)S(1)}, u32[]{:S(2)}, u32[]{:S(2)}) %collective-permute-start.4) | collective-permute-done | bytes 262176 | tf_op jit(solution)/shard_map/ppermute | solution.py:42
  17.4 0.0 copy-start.1
  17.4 1.2 %collective-permute-start.5 = (f32[2,32,128]{2,1,0:T(8,128)S(1)}, f32[2,32,128]{2,1,0:T(8,128)S(1)}, u32[]{:S(2)}, u32[]{:S(2)}) collective-permute-start(f32[2,32,128]{2,1,0:T(8,128)S(1)} %get-tuple-element.38), channel_id=1, source_target_pairs={{0,2},{2,4},{4,6},{6,0},{1,3},{3,5},{5,7},{7,1},{8,10},{10,12},{12... | collective-permute-start | bytes 98312 | tf_op jit(solution)/shard_map/ppermute | solution.py:42
  18.6 1.7 %collective-permute-start.6 = (f32[2,32,128]{2,1,0:T(8,128)S(1)}, f32[2,32,128]{2,1,0:T(8,128)S(1)}, u32[]{:S(2)}, u32[]{:S(2)}) collective-permute-start(f32[2,32,128]{2,1,0:T(8,128)S(1)} %get-tuple-element.37), channel_id=1, source_target_pairs={{0,4},{2,6},{4,0},{6,2},{1,5},{3,7},{5,1},{7,3},{8,12},{10,14},{12... | collective-permute-start | bytes 98312 | tf_op jit(solution)/shard_map/ppermute | solution.py:42
  20.3 1.3 %collective-permute-start.7 = (f32[2,32,128]{2,1,0:T(8,128)S(1)}, f32[2,32,128]{2,1,0:T(8,128)S(1)}, u32[]{:S(2)}, u32[]{:S(2)}) collective-permute-start(f32[2,32,128]{2,1,0:T(8,128)S(1)} %get-tuple-element.36), channel_id=1, source_target_pairs={{0,6},{2,0},{4,2},{6,4},{1,7},{3,1},{5,3},{7,5},{8,14},{10,8},{12,... | collective-permute-start | bytes 98312 | tf_op jit(solution)/shard_map/ppermute | solution.py:42
  21.7 1.6 %collective-permute-done.5 = f32[2,32,128]{2,1,0:T(8,128)S(1)} collective-permute-done((f32[2,32,128]{2,1,0:T(8,128)S(1)}, f32[2,32,128]{2,1,0:T(8,128)S(1)}, u32[]{:S(2)}, u32[]{:S(2)}) %collective-permute-start.5) | collective-permute-done | bytes 32800 | tf_op jit(solution)/shard_map/ppermute | solution.py:42
  23.3 0.9 %collective-permute-done.6 = f32[2,32,128]{2,1,0:T(8,128)S(1)} collective-permute-done((f32[2,32,128]{2,1,0:T(8,128)S(1)}, f32[2,32,128]{2,1,0:T(8,128)S(1)}, u32[]{:S(2)}, u32[]{:S(2)}) %collective-permute-start.6) | collective-permute-done | bytes 32800 | tf_op jit(solution)/shard_map/ppermute | solution.py:42
  24.2 0.2 collective-permute-done.7
  24.5 1.3 %collective-permute-start.8 = (f32[2,256,128]{2,1,0:T(8,128)S(1)}, f32[2,256,128]{2,1,0:T(8,128)S(1)}, u32[]{:S(2)}, u32[]{:S(2)}) collective-permute-start(f32[2,256,128]{2,1,0:T(8,128)S(1)} %collective-permute-done.3.refs_1_), channel_id=1, source_target_pairs={{0,2},{2,4},{4,6},{6,0},{1,3},{3,5},{5,7},{7,1},{8,10},{10,12},{12... | collective-permute-start | bytes 786440 | tf_op jit(solution)/shard_map/ppermute | solution.py:42
  25.8 1.6 %collective-permute-start.10 = (f32[4,2,32,128]{3,2,1,0:T(8,128)S(1)}, f32[4,2,32,128]{3,2,1,0:T(8,128)S(1)}, u32[]{:S(2)}, u32[]{:S(2)}) collective-permute-start(f32[4,2,32,128]{3,2,1,0:T(8,128)S(1)} %pad_maximum_fusion.2.refs_4_), channel_id=1, source_target_pairs={{0,16},{8,24},{16,0},{24,8},{1,17},{9,25},{17,1},{25,9},{2,18},{10... | collective-permute-start | bytes 393224 | tf_op jit(solution)/shard_map/ppermute | solution.py:42
  27.4 1.4 %collective-permute-start.11 = (f32[4,2,32,128]{3,2,1,0:T(8,128)S(1)}, f32[4,2,32,128]{3,2,1,0:T(8,128)S(1)}, u32[]{:S(2)}, u32[]{:S(2)}) collective-permute-start(f32[4,2,32,128]{3,2,1,0:T(8,128)S(1)} %pad_maximum_fusion.2.refs_4_), channel_id=1, source_target_pairs={{0,24},{8,0},{16,8},{24,16},{1,25},{9,1},{17,9},{25,17},{2,26},{10... | collective-permute-start | bytes 393224 | tf_op jit(solution)/shard_map/ppermute | solution.py:42
  28.8 0.6 %collective-permute-start.9 = (f32[4,2,32,128]{3,2,1,0:T(8,128)S(1)}, f32[4,2,32,128]{3,2,1,0:T(8,128)S(1)}, u32[]{:S(2)}, u32[]{:S(2)}) collective-permute-start(f32[4,2,32,128]{3,2,1,0:T(8,128)S(1)} %pad_maximum_fusion.2.refs_4_), channel_id=1, source_target_pairs={{0,8},{8,16},{16,24},{24,0},{1,9},{9,17},{17,25},{25,1},{2,10},{10... | collective-permute-start | bytes 393224 | tf_op jit(solution)/shard_map/ppermute | solution.py:42
  29.4 0.1 pad_add_fusion.place
  29.5 2.5 %collective-permute-done.10.refs_6_ = f32[4,2,32,128]{3,2,1,0:T(8,128)S(1)} collective-permute-done((f32[4,2,32,128]{3,2,1,0:T(8,128)S(1)}, f32[4,2,32,128]{3,2,1,0:T(8,128)S(1)}, u32[]{:S(2)}, u32[]{:S(2)}) %collective-permute-start.10) | collective-permute-done | bytes 131104 | tf_op jit(solution)/shard_map/ppermute | solution.py:42
  32.0 1.2 %collective-permute-done.11.refs_7_ = f32[4,2,32,128]{3,2,1,0:T(8,128)S(1)} collective-permute-done((f32[4,2,32,128]{3,2,1,0:T(8,128)S(1)}, f32[4,2,32,128]{3,2,1,0:T(8,128)S(1)}, u32[]{:S(2)}, u32[]{:S(2)}) %collective-permute-start.11) | collective-permute-done | bytes 131104 | tf_op jit(solution)/shard_map/ppermute | solution.py:42
  33.1 1.6 %collective-permute-done.9.refs_5_ = f32[4,2,32,128]{3,2,1,0:T(8,128)S(1)} collective-permute-done((f32[4,2,32,128]{3,2,1,0:T(8,128)S(1)}, f32[4,2,32,128]{3,2,1,0:T(8,128)S(1)}, u32[]{:S(2)}, u32[]{:S(2)}) %collective-permute-start.9) | collective-permute-done | bytes 131104 | tf_op jit(solution)/shard_map/ppermute | solution.py:42
  34.7 0.0 collective-permute-done.8.refs_2_
  34.7 1.6 %shard_map.59 = f32[2,384,128]{2,1,0:T(8,128)S(1)} custom-call(s32[13]{0:T(128)S(1)} %pad_add_fusion.place, f32[2,256,128]{2,1,0:T(8,128)S(1)} %copy-done.1, f32[2,256,128]{2,1,0:T(8,128)S(1)} %collective-permute-done.3.refs_1_, f32[2,256,128]{2,1,0:T(8,128)S(1)} %collective-permute-done.8.refs_2_, f32[2,256,128]{2,1,0:T(8,128)S(1)} %collective-permute-done.4.refs_3_, ...), custom_call_target="tpu_custom_call" | custom-call | tf_op jit(solution)/shard_map/pallas_call | solution.py:101
  36.3 0.1 collective-permute-start.12
  36.4 0.9 %multiply_reduce_fusion.1 = f32[2,128]{1,0:T(2,128)S(1)} fusion(f32[2,128,512]{2,1,0:T(8,128)} %param.6, s32[]{:T(128)S(6)} %select_n.239), kind=kLoop, calls=%fused_computation.6 | loop fusion | flops 65280 | bytes 132100 | tf_op jit(solution)/shard_map/reduce_sum | solution.py:117
  37.3 0.7 %collective-permute-done.12 = f32[2,384,128]{2,1,0:T(8,128)S(1)} collective-permute-done((f32[2,384,128]{2,1,0:T(8,128)S(1)}, f32[2,384,128]{2,1,0:T(8,128)S(1)}, u32[]{:S(2)}, u32[]{:S(2)}) %collective-permute-start.12) | collective-permute-done | bytes 393248 | tf_op jit(solution)/shard_map/ppermute | solution.py:42
  38.1 0.1 multiply_reduce_fusion
  38.3 2.6 %collective-permute-start.13 = (f32[2,40,128]{2,1,0:T(8,128)S(1)}, f32[2,40,128]{2,1,0:T(8,128)S(1)}, u32[]{:S(2)}, u32[]{:S(2)}) collective-permute-start(f32[2,40,128]{2,1,0:T(8,128)S(1)} %get-tuple-element.42), channel_id=1, source_target_pairs={{0,6},{2,0},{4,2},{6,4},{1,7},{3,1},{5,3},{7,5},{8,14},{10,8},{12,... | collective-permute-start | bytes 122888 | tf_op jit(solution)/shard_map/ppermute | solution.py:42
  40.9 1.7 %collective-permute-start.15 = (f32[2,40,128]{2,1,0:T(8,128)S(1)}, f32[2,40,128]{2,1,0:T(8,128)S(1)}, u32[]{:S(2)}, u32[]{:S(2)}) collective-permute-start(f32[2,40,128]{2,1,0:T(8,128)S(1)} %get-tuple-element.40), channel_id=1, source_target_pairs={{0,2},{2,4},{4,6},{6,0},{1,3},{3,5},{5,7},{7,1},{8,10},{10,12},{12... | collective-permute-start | bytes 122888 | tf_op jit(solution)/shard_map/ppermute | solution.py:42
  42.6 0.1 collective-permute-done.13
  42.7 3.3 %collective-permute-done.14 = f32[2,40,128]{2,1,0:T(8,128)S(1)} collective-permute-done((f32[2,40,128]{2,1,0:T(8,128)S(1)}, f32[2,40,128]{2,1,0:T(8,128)S(1)}, u32[]{:S(2)}, u32[]{:S(2)}) %collective-permute-start.14) | collective-permute-done | bytes 40992 | tf_op jit(solution)/shard_map/ppermute | solution.py:42
  46.0 0.7 %collective-permute-done.15 = f32[2,40,128]{2,1,0:T(8,128)S(1)} collective-permute-done((f32[2,40,128]{2,1,0:T(8,128)S(1)}, f32[2,40,128]{2,1,0:T(8,128)S(1)}, u32[]{:S(2)}, u32[]{:S(2)}) %collective-permute-start.15) | collective-permute-done | bytes 40992 | tf_op jit(solution)/shard_map/ppermute | solution.py:42
  46.7 0.6 %collective-permute-start.16 = (f32[2,512]{1,0:T(2,128)S(1)}, f32[2,512]{1,0:T(2,128)S(1)}, u32[]{:S(2)}, u32[]{:S(2)}) collective-permute-start(f32[2,512]{1,0:T(2,128)S(1)} %bitcast.21), channel_id=1, source_target_pairs={{0,8},{8,16},{16,24},{24,0},{1,9},{9,17},{17,25},{25,1},{2,10},{10... | collective-permute-start | bytes 12296 | tf_op jit(solution)/shard_map/ppermute | solution.py:42
  47.3 1.5 %collective-permute-start.17 = (f32[2,512]{1,0:T(2,128)S(1)}, f32[2,512]{1,0:T(2,128)S(1)}, u32[]{:S(2)}, u32[]{:S(2)}) collective-permute-start(f32[2,512]{1,0:T(2,128)S(1)} %bitcast.22), channel_id=1, source_target_pairs={{0,16},{8,24},{16,0},{24,8},{1,17},{9,25},{17,1},{25,9},{2,18},{10... | collective-permute-start | bytes 12296 | tf_op jit(solution)/shard_map/ppermute | solution.py:42
  48.8 2.4 %collective-permute-start.18 = (f32[2,512]{1,0:T(2,128)S(1)}, f32[2,512]{1,0:T(2,128)S(1)}, u32[]{:S(2)}, u32[]{:S(2)}) collective-permute-start(f32[2,512]{1,0:T(2,128)S(1)} %bitcast.23), channel_id=1, source_target_pairs={{0,24},{8,0},{16,8},{24,16},{1,25},{9,1},{17,9},{25,17},{2,26},{10... | collective-permute-start | bytes 12296 | tf_op jit(solution)/shard_map/ppermute | solution.py:42
  51.3 0.7 %slice_negate_fusion = f32[2,32,512]{2,1,0:T(8,128)} fusion(f32[2,40,512]{2,1,0:T(8,128)S(1)} %pad_maximum_fusion.1), kind=kLoop, calls=%fused_computation.4 | loop fusion | flops 32768 | bytes 262144 | tf_op jit(solution)/shard_map/neg | solution.py:133
  51.9 0.0 collective-permute-done.16
  51.9 0.6 %collective-permute-done.18 = f32[2,512]{1,0:T(2,128)S(1)} collective-permute-done((f32[2,512]{1,0:T(2,128)S(1)}, f32[2,512]{1,0:T(2,128)S(1)}, u32[]{:S(2)}, u32[]{:S(2)}) %collective-permute-start.18) | collective-permute-done | bytes 4128 | tf_op jit(solution)/shard_map/ppermute | solution.py:42
  52.6 0.6 %add_add_fusion.1 = f32[2,512]{1,0:T(2,128)} fusion(f32[2,512]{1,0:T(2,128)S(1)} %collective-permute-done.18, f32[2,512]{1,0:T(2,128)S(1)} %collective-permute-done.17, f32[2,512]{1,0:T(2,128)S(1)} %collective-permute-done.16, f32[2,1,512]{2,1,0:T(1,128)S(1)} %pad_maximum_fusion.7), kind=kLoop, calls=%fused_computation.22 | loop fusion | flops 3072 | bytes 20480 | tf_op jit(solution)/shard_map/add | solution.py:132
  (25 shorter events, 0.3 us)
Async XLA Ops:
  0.6 5.2 %copy-start = (f32[2,128,512]{2,1,0:T(8,128)S(1)}, f32[2,128,512]{2,1,0:T(8,128)}, u32[]{:S(2)}) copy-start(f32[2,128,512]{2,1,0:T(8,128)} %param.5) | copy-start | bytes 1572868
  0.6 15.7 %collective-permute-start.3 = (f32[2,256,128]{2,1,0:T(8,128)}, f32[2,256,128]{2,1,0:T(8,128)S(1)}, u32[]{:S(2)}, u32[]{:S(2)}) collective-permute-start(f32[2,256,128]{2,1,0:T(8,128)} %refs_0_.1), channel_id=1, source_target_pairs={{0,2},{2,4},{4,6},{6,0},{1,3},{3,5},{5,7},{7,1},{8,10},{10,12},{12... | collective-permute-start | bytes 786440 | tf_op jit(solution)/shard_map/ppermute | solution.py:42
  3.7 13.6 %collective-permute-start.4 = (f32[2,256,128]{2,1,0:T(8,128)}, f32[2,256,128]{2,1,0:T(8,128)S(1)}, u32[]{:S(2)}, u32[]{:S(2)}) collective-permute-start(f32[2,256,128]{2,1,0:T(8,128)} %refs_0_.1), channel_id=1, source_target_pairs={{0,6},{2,0},{4,2},{6,4},{1,7},{3,1},{5,3},{7,5},{8,14},{10,8},{12,... | collective-permute-start | bytes 786440 | tf_op jit(solution)/shard_map/ppermute | solution.py:42
  7.5 7.2 %collective-permute-start = (f32[2,32,512]{2,1,0:T(8,128)S(1)}, f32[2,32,512]{2,1,0:T(8,128)S(1)}, u32[]{:S(2)}, u32[]{:S(2)}) collective-permute-start(f32[2,32,512]{2,1,0:T(8,128)S(1)} %get-tuple-element.28), channel_id=1, source_target_pairs={{0,8},{8,16},{16,24},{24,0},{1,9},{9,17},{17,25},{25,1},{2,10},{10... | collective-permute-start | bytes 393224 | tf_op jit(solution)/shard_map/ppermute | solution.py:42
  9.2 7.0 %collective-permute-start.1 = (f32[2,32,512]{2,1,0:T(8,128)S(1)}, f32[2,32,512]{2,1,0:T(8,128)S(1)}, u32[]{:S(2)}, u32[]{:S(2)}) collective-permute-start(f32[2,32,512]{2,1,0:T(8,128)S(1)} %get-tuple-element.27), channel_id=1, source_target_pairs={{0,16},{8,24},{16,0},{24,8},{1,17},{9,25},{17,1},{25,9},{2,18},{10... | collective-permute-start | bytes 393224 | tf_op jit(solution)/shard_map/ppermute | solution.py:42
  10.7 5.6 %collective-permute-start.2 = (f32[2,32,512]{2,1,0:T(8,128)S(1)}, f32[2,32,512]{2,1,0:T(8,128)S(1)}, u32[]{:S(2)}, u32[]{:S(2)}) collective-permute-start(f32[2,32,512]{2,1,0:T(8,128)S(1)} %get-tuple-element.26), channel_id=1, source_target_pairs={{0,24},{8,0},{16,8},{24,16},{1,25},{9,1},{17,9},{25,17},{2,26},{10... | collective-permute-start | bytes 393224 | tf_op jit(solution)/shard_map/ppermute | solution.py:42
  12.1 0.7 %copy-start.2 = (s32[2,4]{1,0:T(2,128)S(1)}, s32[2,4]{1,0:T(2,128)}, u32[]{:S(2)}) copy-start(s32[2,4]{1,0:T(2,128)} %param.7) | copy-start | bytes 100
  17.4 17.3 %copy-start.1 = (f32[2,256,128]{2,1,0:T(8,128)S(1)}, f32[2,256,128]{2,1,0:T(8,128)}, u32[]{:S(2)}) copy-start(f32[2,256,128]{2,1,0:T(8,128)} %refs_0_.1) | copy-start | bytes 786436
  17.4 5.9 %collective-permute-start.5 = (f32[2,32,128]{2,1,0:T(8,128)S(1)}, f32[2,32,128]{2,1,0:T(8,128)S(1)}, u32[]{:S(2)}, u32[]{:S(2)}) collective-permute-start(f32[2,32,128]{2,1,0:T(8,128)S(1)} %get-tuple-element.38), channel_id=1, source_target_pairs={{0,2},{2,4},{4,6},{6,0},{1,3},{3,5},{5,7},{7,1},{8,10},{10,12},{12... | collective-permute-start | bytes 98312 | tf_op jit(solution)/shard_map/ppermute | solution.py:42
  18.6 5.6 %collective-permute-start.6 = (f32[2,32,128]{2,1,0:T(8,128)S(1)}, f32[2,32,128]{2,1,0:T(8,128)S(1)}, u32[]{:S(2)}, u32[]{:S(2)}) collective-permute-start(f32[2,32,128]{2,1,0:T(8,128)S(1)} %get-tuple-element.37), channel_id=1, source_target_pairs={{0,4},{2,6},{4,0},{6,2},{1,5},{3,7},{5,1},{7,3},{8,12},{10,14},{12... | collective-permute-start | bytes 98312 | tf_op jit(solution)/shard_map/ppermute | solution.py:42
  20.3 4.1 %collective-permute-start.7 = (f32[2,32,128]{2,1,0:T(8,128)S(1)}, f32[2,32,128]{2,1,0:T(8,128)S(1)}, u32[]{:S(2)}, u32[]{:S(2)}) collective-permute-start(f32[2,32,128]{2,1,0:T(8,128)S(1)} %get-tuple-element.36), channel_id=1, source_target_pairs={{0,6},{2,0},{4,2},{6,4},{1,7},{3,1},{5,3},{7,5},{8,14},{10,8},{12,... | collective-permute-start | bytes 98312 | tf_op jit(solution)/shard_map/ppermute | solution.py:42
  24.5 10.2 %collective-permute-start.8 = (f32[2,256,128]{2,1,0:T(8,128)S(1)}, f32[2,256,128]{2,1,0:T(8,128)S(1)}, u32[]{:S(2)}, u32[]{:S(2)}) collective-permute-start(f32[2,256,128]{2,1,0:T(8,128)S(1)} %collective-permute-done.3.refs_1_), channel_id=1, source_target_pairs={{0,2},{2,4},{4,6},{6,0},{1,3},{3,5},{5,7},{7,1},{8,10},{10,12},{12... | collective-permute-start | bytes 786440 | tf_op jit(solution)/shard_map/ppermute | solution.py:42
  25.8 6.2 %collective-permute-start.10 = (f32[4,2,32,128]{3,2,1,0:T(8,128)S(1)}, f32[4,2,32,128]{3,2,1,0:T(8,128)S(1)}, u32[]{:S(2)}, u32[]{:S(2)}) collective-permute-start(f32[4,2,32,128]{3,2,1,0:T(8,128)S(1)} %pad_maximum_fusion.2.refs_4_), channel_id=1, source_target_pairs={{0,16},{8,24},{16,0},{24,8},{1,17},{9,25},{17,1},{25,9},{2,18},{10... | collective-permute-start | bytes 393224 | tf_op jit(solution)/shard_map/ppermute | solution.py:42
  27.4 5.7 %collective-permute-start.11 = (f32[4,2,32,128]{3,2,1,0:T(8,128)S(1)}, f32[4,2,32,128]{3,2,1,0:T(8,128)S(1)}, u32[]{:S(2)}, u32[]{:S(2)}) collective-permute-start(f32[4,2,32,128]{3,2,1,0:T(8,128)S(1)} %pad_maximum_fusion.2.refs_4_), channel_id=1, source_target_pairs={{0,24},{8,0},{16,8},{24,16},{1,25},{9,1},{17,9},{25,17},{2,26},{10... | collective-permute-start | bytes 393224 | tf_op jit(solution)/shard_map/ppermute | solution.py:42
  28.8 5.9 %collective-permute-start.9 = (f32[4,2,32,128]{3,2,1,0:T(8,128)S(1)}, f32[4,2,32,128]{3,2,1,0:T(8,128)S(1)}, u32[]{:S(2)}, u32[]{:S(2)}) collective-permute-start(f32[4,2,32,128]{3,2,1,0:T(8,128)S(1)} %pad_maximum_fusion.2.refs_4_), channel_id=1, source_target_pairs={{0,8},{8,16},{16,24},{24,0},{1,9},{9,17},{17,25},{25,1},{2,10},{10... | collective-permute-start | bytes 393224 | tf_op jit(solution)/shard_map/ppermute | solution.py:42
  36.3 1.8 %collective-permute-start.12 = (f32[2,384,128]{2,1,0:T(8,128)S(1)}, f32[2,384,128]{2,1,0:T(8,128)S(1)}, u32[]{:S(2)}, u32[]{:S(2)}) collective-permute-start(f32[2,384,128]{2,1,0:T(8,128)S(1)} %shard_map.59), channel_id=1, source_target_pairs={{0,1},{1,0},{2,3},{3,2},{4,5},{5,4},{6,7},{7,6},{8,9},{9,8},{10,11... | collective-permute-start | bytes 1179656 | tf_op jit(solution)/shard_map/ppermute | solution.py:42
  38.3 4.4 %collective-permute-start.13 = (f32[2,40,128]{2,1,0:T(8,128)S(1)}, f32[2,40,128]{2,1,0:T(8,128)S(1)}, u32[]{:S(2)}, u32[]{:S(2)}) collective-permute-start(f32[2,40,128]{2,1,0:T(8,128)S(1)} %get-tuple-element.42), channel_id=1, source_target_pairs={{0,6},{2,0},{4,2},{6,4},{1,7},{3,1},{5,3},{7,5},{8,14},{10,8},{12,... | collective-permute-start | bytes 122888 | tf_op jit(solution)/shard_map/ppermute | solution.py:42
  40.9 5.1 %collective-permute-start.14 = (f32[2,40,128]{2,1,0:T(8,128)S(1)}, f32[2,40,128]{2,1,0:T(8,128)S(1)}, u32[]{:S(2)}, u32[]{:S(2)}) collective-permute-start(f32[2,40,128]{2,1,0:T(8,128)S(1)} %get-tuple-element.41), channel_id=1, source_target_pairs={{0,4},{2,6},{4,0},{6,2},{1,5},{3,7},{5,1},{7,3},{8,12},{10,14},{12... | collective-permute-start | bytes 122888 | tf_op jit(solution)/shard_map/ppermute | solution.py:42
  40.9 5.8 %collective-permute-start.15 = (f32[2,40,128]{2,1,0:T(8,128)S(1)}, f32[2,40,128]{2,1,0:T(8,128)S(1)}, u32[]{:S(2)}, u32[]{:S(2)}) collective-permute-start(f32[2,40,128]{2,1,0:T(8,128)S(1)} %get-tuple-element.40), channel_id=1, source_target_pairs={{0,2},{2,4},{4,6},{6,0},{1,3},{3,5},{5,7},{7,1},{8,10},{10,12},{12... | collective-permute-start | bytes 122888 | tf_op jit(solution)/shard_map/ppermute | solution.py:42
  46.7 5.2 %collective-permute-start.16 = (f32[2,512]{1,0:T(2,128)S(1)}, f32[2,512]{1,0:T(2,128)S(1)}, u32[]{:S(2)}, u32[]{:S(2)}) collective-permute-start(f32[2,512]{1,0:T(2,128)S(1)} %bitcast.21), channel_id=1, source_target_pairs={{0,8},{8,16},{16,24},{24,0},{1,9},{9,17},{17,25},{25,1},{2,10},{10... | collective-permute-start | bytes 12296 | tf_op jit(solution)/shard_map/ppermute | solution.py:42
  47.3 4.6 %collective-permute-start.17 = (f32[2,512]{1,0:T(2,128)S(1)}, f32[2,512]{1,0:T(2,128)S(1)}, u32[]{:S(2)}, u32[]{:S(2)}) collective-permute-start(f32[2,512]{1,0:T(2,128)S(1)} %bitcast.22), channel_id=1, source_target_pairs={{0,16},{8,24},{16,0},{24,8},{1,17},{9,25},{17,1},{25,9},{2,18},{10... | collective-permute-start | bytes 12296 | tf_op jit(solution)/shard_map/ppermute | solution.py:42
  48.8 3.7 %collective-permute-start.18 = (f32[2,512]{1,0:T(2,128)S(1)}, f32[2,512]{1,0:T(2,128)S(1)}, u32[]{:S(2)}, u32[]{:S(2)}) collective-permute-start(f32[2,512]{1,0:T(2,128)S(1)} %bitcast.23), channel_id=1, source_target_pairs={{0,24},{8,0},{16,8},{24,16},{1,25},{9,1},{17,9},{25,17},{2,26},{10... | collective-permute-start | bytes 12296 | tf_op jit(solution)/shard_map/ppermute | solution.py:42

commit v13 on v11

--- a/solution.py
+++ b/solution.py
@@ -8,6 +8,18 @@
 from jax.sharding import Mesh, PartitionSpec as P
 
 B = 256
+
+
+def scale_pieces(deep, *refs):
+    panels, (factor, out_ref) = refs[:deep], refs[deep:]
+    groups, piece, _ = panels[0].shape
+    for s in range(groups):
+        tall = jnp.concatenate([panel[s] for panel in panels], axis=0)
+        scaled = jnp.dot(
+            tall, factor[s], precision=lax.Precision.HIGHEST, preferred_element_type=jnp.float32
+        )
+        for d in range(deep):
+            out_ref[d, s] = scaled[d * piece : (d + 1) * piece]
 
 
 def multiply_tiles(deep, rows, place, *refs):
@@ -49,7 +61,6 @@
         z = lax.axis_index("z")
         core = lax.axis_index("core")
         groups, chunk, width = panel.shape
-        depth = factor_inv.shape[1]
         part = width // deep
         piece = chunk // rows
         out_rows = ancestor.shape[1] // cols
@@ -65,26 +76,25 @@
         late = [d for d in range(1, deep) if d not in early]
         far = {d: shifted(ancestor, "z", deep, d) for d in early}
 
-        mine = lax.dynamic_slice_in_dim(panel, row * depth, depth, axis=2)
-        partial = jnp.einsum("srw,swv->srv", mine, factor_inv, precision=highest)
+        whole = pl.BlockSpec(memory_space=pltpu.VMEM)
+        scalars = pl.BlockSpec(memory_space=pltpu.SMEM)
+        params = pltpu.CompilerParams(vmem_limit_bytes=32 * 1024 * 1024)
+        quarter = (row - jnp.arange(rows, dtype=jnp.int32)) % rows
 
-        def rows_of(r):
-            return lax.dynamic_slice_in_dim(partial, r * piece, piece, axis=1)
-
-        sums = [shifted(rows_of((row + d) % rows), "row", rows, d) for d in range(1, rows)]
-        sums, far = lax.optimization_barrier((sums, far))
-        scaled = sum(sums, rows_of(row))
-
-        def columns_of(array, c):
-            return lax.dynamic_slice_in_dim(array, c * part, part, axis=2)
-
-        slots = [columns_of(scaled, z)]
-        for shift in range(1, deep):
-            slots.append(shifted(columns_of(scaled, (z + shift) % deep), "z", deep, shift))
-        if deep > 1:
-            slots[1], held_back = lax.optimization_barrier((slots[1], ancestor))
-            far |= {d: shifted(held_back, "z", deep, d) for d in late}
-        slots = gathered(jnp.stack(slots), "row", rows)
+        mine = lax.dynamic_slice_in_dim(panel, row * piece, piece, axis=1)
+        block = lax.dynamic_slice_in_dim(factor_inv, z * part, part, axis=2)
+        panels = gathered(mine, "z", deep)
+        blocks = lax.all_gather(block, "row", axis=1, tiled=True)
+        scaled = pl.pallas_call(
+            functools.partial(scale_pieces, deep),
+            out_shape=jax.ShapeDtypeStruct((deep, groups, piece, part), jnp.float32),
+            in_specs=[whole] * (deep + 1),
+            out_specs=whole,
+            compiler_params=params,
+        )(*panels, blocks)
+        for d in late:
+            far[d] = shifted(far[d - 1], "z", deep, 1)
+        slots = gathered(scaled, "row", rows)
 
         count = jnp.arange(deep, dtype=jnp.int32)
         at = (z - count) % deep
@@ -92,18 +102,16 @@
             jnp.where(pattern[:, :, None] == at, count[:, None], 0), axis=1, dtype=jnp.int32
         )
         from_z = ((z - stored) % deep).reshape(-1)
-        quarter = (row - jnp.arange(rows, dtype=jnp.int32)) % rows
         own_tile = (z - row * tiles - jnp.arange(tiles, dtype=jnp.int32)) % deep
         place = jnp.concatenate([from_z, quarter, own_tile])
         height = ancestor.shape[1]
-        whole = pl.BlockSpec(memory_space=pltpu.VMEM)
         product = pl.pallas_call(
             functools.partial(multiply_tiles, deep, rows),
             out_shape=jax.ShapeDtypeStruct((groups, height + tiles * chunk, part), jnp.float32),
-            in_specs=[pl.BlockSpec(memory_space=pltpu.SMEM)] + [whole] * (deep + rows),
+            in_specs=[scalars] + [whole] * (deep + rows),
             out_specs=whole,
             scratch_shapes=[pltpu.VMEM((groups, deep, chunk, part), jnp.float32)],
-            compiler_params=pltpu.CompilerParams(vmem_limit_bytes=32 * 1024 * 1024),
+            compiler_params=params,
         )(place, ancestor, *[far[d] for d in range(1, deep)], *slots)
         other = shifted(product, "core", cores, 1)
 
@@ -113,7 +121,7 @@
         product = product[:, :height] + other[:, :height]
         halves = [jnp.where(core == 0, own, own_other), jnp.where(core == 0, own_other, own)]
         own = jnp.stack(halves, axis=2).reshape(groups, height, part)
-        squares = jnp.sum(columns_of(factor_inv, z) ** 2, axis=1)
+        squares = jnp.sum(block * block, axis=1)
         term = jnp.sum(own * product, axis=1) + squares
         tail = jnp.broadcast_to(term[:, None], (groups, 8, part))
 

time: 57.9 us -> 69 us (1.19)
  blocking collectives: 0 us -> 10.2 us
  starting transfers between devices: 28.6 us -> 30.8 us
  matrix products: 1.61 us -> 0 us
  waiting for transfers between devices: 21.5 us -> 20.3 us
  local copies, waits for them, and re-layouts: 0.88 us -> 1.85 us
    all_gather x0 -> x1, blocking collectives: none -> 10.2 us  [per_device(): blocks = lax.all_gather(block, 'row', axis=1, tiled=True)]
    ppermute x19 -> x16, starting transfers between devices: 28.6 us -> 30.8 us  [shifted(): lax.ppermute(array, axis, [(i, (i + shift) % size) for i in range(size)])]
    dot_general x1 -> x0, matrix products: 1.61 us -> none  [per_device(): partial = jnp.einsum('srw,swv->srv', mine, factor_inv, precision=highest)]
    ppermute x19 -> x16, waiting for transfers between devices: 21.5 us -> 20.3 us  [shifted(): lax.ppermute(array, axis, [(i, (i + shift) % size) for i in range(size)])]
    unnamed x7, local copies, waits for them, and re-layouts: 0.69 us -> 1.71 us
  transfers between devices with their start and end apart: 19 -> 16, of which waited for: 16 -> 10; matrix products, arithmetic and copies ran while one was open for 6% -> 3% of each run, Pallas kernels for 0% -> 1%
where the time goes in v13:
time: 69 us; the launch traced here: 68.8 us
  starting transfers between devices  30.8 us (45%)
  waiting for transfers between devices  20.3 us (29%)
  blocking collectives  10.2 us (15%)
  other arithmetic  2.6 us (4%)
  Pallas kernels  2.19 us (3%)
  local copies, waits for them, and re-layouts  1.85 us (3%)
  between operations  0.83 us (1%)
    ppermute x16, starting transfers between devices, shifted(): lax.ppermute(array, axis, [(i, (i + shift) % size) for i in range(size)])  30.8 us
    ppermute x16, waiting for transfers between devices, shifted(): lax.ppermute(array, axis, [(i, (i + shift) % size) for i in range(size)])  20.3 us
    all_gather x1, blocking collectives, per_device(): blocks = lax.all_gather(block, 'row', axis=1, tiled=True)  10.2 us
    unnamed x7, local copies, waits for them, and re-layouts  1.71 us
    pallas_call x1, Pallas kernels, per_device(): pl.pallas_call(functools.partial(multiply_tiles, deep, rows), out_shape=j...  1.61 us
  transfers between devices with their start and end apart: 16, of which 10 were waited for; matrix products, arithmetic and copies ran while one was open for 3% of the time, Pallas kernels for 1%

profile of v13, /device:TPU:0, one launch (start us, length us, event | category | flops | bytes accessed | tf_op | source)
XLA Modules:
  0.0 68.8 jit_solution(11998679484517499831)
XLA Ops:
  0.6 0.0 copy-start
  0.6 0.0 copy-start.1
  0.7 1.0 %copy-done = f32[2,128,512]{2,1,0:T(8,128)S(1)} copy-done((f32[2,128,512]{2,1,0:T(8,128)S(1)}, f32[2,128,512]{2,1,0:T(8,128)}, u32[]{:S(2)}) %copy-start) | copy-done | bytes 524312
  1.7 3.1 %collective-permute-start.3 = (f32[2,32,512]{2,1,0:T(8,128)S(1)}, f32[2,32,512]{2,1,0:T(8,128)S(1)}, u32[]{:S(2)}, u32[]{:S(2)}) collective-permute-start(f32[2,32,512]{2,1,0:T(8,128)S(1)} %constant_dynamic-slice_fusion.5.refs_0_), channel_id=1, source_target_pairs={{0,2},{2,4},{4,6},{6,0},{1,3},{3,5},{5,7},{7,1},{8,10},{10,12},{12... | collective-permute-start | bytes 393224 | tf_op jit(solution)/shard_map/ppermute | solution.py:54
  4.8 2.6 %collective-permute-start.4 = (f32[2,32,512]{2,1,0:T(8,128)S(1)}, f32[2,32,512]{2,1,0:T(8,128)S(1)}, u32[]{:S(2)}, u32[]{:S(2)}) collective-permute-start(f32[2,32,512]{2,1,0:T(8,128)S(1)} %constant_dynamic-slice_fusion.5.refs_0_), channel_id=1, source_target_pairs={{0,4},{2,6},{4,0},{6,2},{1,5},{3,7},{5,1},{7,3},{8,12},{10,14},{12... | collective-permute-start | bytes 393224 | tf_op jit(solution)/shard_map/ppermute | solution.py:54
  7.4 1.3 %collective-permute-start.5 = (f32[2,32,512]{2,1,0:T(8,128)S(1)}, f32[2,32,512]{2,1,0:T(8,128)S(1)}, u32[]{:S(2)}, u32[]{:S(2)}) collective-permute-start(f32[2,32,512]{2,1,0:T(8,128)S(1)} %constant_dynamic-slice_fusion.5.refs_0_), channel_id=1, source_target_pairs={{0,6},{2,0},{4,2},{6,4},{1,7},{3,1},{5,3},{7,5},{8,14},{10,8},{12,... | collective-permute-start | bytes 393224 | tf_op jit(solution)/shard_map/ppermute | solution.py:54
  8.7 0.0 copy-done.1
  8.7 0.7 collective-permute-start
  9.4 3.1 %collective-permute-start.2 = (f32[2,256,128]{2,1,0:T(8,128)S(1)}, f32[2,256,128]{2,1,0:T(8,128)S(1)}, u32[]{:S(2)}, u32[]{:S(2)}) collective-permute-start(f32[2,256,128]{2,1,0:T(8,128)S(1)} %copy-done.1), channel_id=1, source_target_pairs={{0,6},{2,0},{4,2},{6,4},{1,7},{3,1},{5,3},{7,5},{8,14},{10,8},{12,... | collective-permute-start | bytes 786440 | tf_op jit(solution)/shard_map/ppermute | solution.py:54
  12.5 0.0 copy-start.2
  12.5 0.7 copy-done.2
  13.2 0.1 select_reduce_fusion
  13.3 0.1 sub.51
  13.4 0.9 %multiply_reduce_fusion.1 = (f32[2,128]{1,0:T(2,128)S(1)}, f32[2,128,128]{2,1,0:T(8,128)S(1)}) fusion(f32[2,128,512]{2,1,0:T(8,128)} %param.6, s32[]{:T(128)S(6)} %select_n.192), kind=kLoop, calls=%fused_computation.5 | loop fusion | flops 65280 | bytes 263172 | tf_op jit(solution)/shard_map/reduce_sum | solution.py:124
  14.4 8.1 %collective-permute-done.refs_1_ = f32[2,256,128]{2,1,0:T(8,128)S(1)} collective-permute-done((f32[2,256,128]{2,1,0:T(8,128)S(1)}, f32[2,256,128]{2,1,0:T(8,128)S(1)}, u32[]{:S(2)}, u32[]{:S(2)}) %collective-permute-start) | collective-permute-done | bytes 262176 | tf_op jit(solution)/shard_map/ppermute | solution.py:54
  22.4 6.4 %collective-permute-start.1 = (f32[2,256,128]{2,1,0:T(8,128)S(1)}, f32[2,256,128]{2,1,0:T(8,128)S(1)}, u32[]{:S(2)}, u32[]{:S(2)}) collective-permute-start(f32[2,256,128]{2,1,0:T(8,128)S(1)} %collective-permute-done.refs_1_), channel_id=1, source_target_pairs={{0,2},{2,4},{4,6},{6,0},{1,3},{3,5},{5,7},{7,1},{8,10},{10,12},{12... | collective-permute-start | bytes 786440 | tf_op jit(solution)/shard_map/ppermute | solution.py:54
  28.8 10.2 %all_gather.3.refs_4_ = f32[2,512,128]{2,1,0:T(8,128)S(1)} all-gather(f32[2,128,128]{2,1,0:T(8,128)S(1)} %get-tuple-element.3), channel_id=1, replica_groups=mesh['row'=4,'z'=4,'core'=2] {'row'}, dimensions={1}, use_global_device_ids=true | all-gather | bytes 655360 | tf_op jit(solution)/shard_map/all_gather | solution.py:87
  39.0 0.0 collective-permute-done.3.refs_1_
  39.0 0.0 collective-permute-done.4.refs_2_
  39.0 0.0 collective-permute-done.5.refs_3_
  39.0 0.6 shard_map.59.refs_4_
  39.6 2.5 %collective-permute-start.6 = (f32[4,2,32,128]{3,2,1,0:T(8,128)S(1)}, f32[4,2,32,128]{3,2,1,0:T(8,128)S(1)}, u32[]{:S(2)}, u32[]{:S(2)}) collective-permute-start(f32[4,2,32,128]{3,2,1,0:T(8,128)S(1)} %shard_map.59.refs_4_), channel_id=1, source_target_pairs={{0,8},{8,16},{16,24},{24,0},{1,9},{9,17},{17,25},{25,1},{2,10},{10... | collective-permute-start | bytes 393224 | tf_op jit(solution)/shard_map/ppermute | solution.py:54
  42.2 0.0 collective-permute-start.7
  42.2 2.5 %collective-permute-start.8 = (f32[4,2,32,128]{3,2,1,0:T(8,128)S(1)}, f32[4,2,32,128]{3,2,1,0:T(8,128)S(1)}, u32[]{:S(2)}, u32[]{:S(2)}) collective-permute-start(f32[4,2,32,128]{3,2,1,0:T(8,128)S(1)} %shard_map.59.refs_4_), channel_id=1, source_target_pairs={{0,24},{8,0},{16,8},{24,16},{1,25},{9,1},{17,9},{25,17},{2,26},{10... | collective-permute-start | bytes 393224 | tf_op jit(solution)/shard_map/ppermute | solution.py:54
  44.6 0.1 pad_add_fusion.place
  44.7 0.8 %collective-permute-done.6.refs_5_ = f32[4,2,32,128]{3,2,1,0:T(8,128)S(1)} collective-permute-done((f32[4,2,32,128]{3,2,1,0:T(8,128)S(1)}, f32[4,2,32,128]{3,2,1,0:T(8,128)S(1)}, u32[]{:S(2)}, u32[]{:S(2)}) %collective-permute-start.6) | collective-permute-done | bytes 131104 | tf_op jit(solution)/shard_map/ppermute | solution.py:54
  45.5 1.6 %collective-permute-done.7.refs_6_ = f32[4,2,32,128]{3,2,1,0:T(8,128)S(1)} collective-permute-done((f32[4,2,32,128]{3,2,1,0:T(8,128)S(1)}, f32[4,2,32,128]{3,2,1,0:T(8,128)S(1)}, u32[]{:S(2)}, u32[]{:S(2)}) %collective-permute-start.7) | collective-permute-done | bytes 131104 | tf_op jit(solution)/shard_map/ppermute | solution.py:54
  47.1 0.4 collective-permute-done.8.refs_7_
  47.5 0.0 collective-permute-done.2.refs_3_
  47.6 0.0 collective-permute-done.1.refs_2_
  47.6 1.6 %shard_map.60 = f32[2,384,128]{2,1,0:T(8,128)S(1)} custom-call(s32[13]{0:T(128)S(1)} %pad_add_fusion.place, f32[2,256,128]{2,1,0:T(8,128)S(1)} %copy-done.1, f32[2,256,128]{2,1,0:T(8,128)S(1)} %collective-permute-done.refs_1_, f32[2,256,128]{2,1,0:T(8,128)S(1)} %collective-permute-done.1.refs_2_, f32[2,256,128]{2,1,0:T(8,128)S(1)} %collective-permute-done.2.refs_3_, ...), custom_call_target="tpu_custom_call" | custom-call | tf_op jit(solution)/shard_map/pallas_call | solution.py:108
  49.2 0.1 collective-permute-start.9
  49.3 1.7 %collective-permute-done.9 = f32[2,384,128]{2,1,0:T(8,128)S(1)} collective-permute-done((f32[2,384,128]{2,1,0:T(8,128)S(1)}, f32[2,384,128]{2,1,0:T(8,128)S(1)}, u32[]{:S(2)}, u32[]{:S(2)}) %collective-permute-start.9) | collective-permute-done | bytes 393248 | tf_op jit(solution)/shard_map/ppermute | solution.py:54
  51.0 0.1 multiply_reduce_fusion
  51.2 1.3 %collective-permute-start.10 = (f32[2,40,128]{2,1,0:T(8,128)S(1)}, f32[2,40,128]{2,1,0:T(8,128)S(1)}, u32[]{:S(2)}, u32[]{:S(2)}) collective-permute-start(f32[2,40,128]{2,1,0:T(8,128)S(1)} %get-tuple-element.17), channel_id=1, source_target_pairs={{0,6},{2,0},{4,2},{6,4},{1,7},{3,1},{5,3},{7,5},{8,14},{10,8},{12,... | collective-permute-start | bytes 122888 | tf_op jit(solution)/shard_map/ppermute | solution.py:54
  52.5 2.7 %collective-permute-start.11 = (f32[2,40,128]{2,1,0:T(8,128)S(1)}, f32[2,40,128]{2,1,0:T(8,128)S(1)}, u32[]{:S(2)}, u32[]{:S(2)}) collective-permute-start(f32[2,40,128]{2,1,0:T(8,128)S(1)} %get-tuple-element.16), channel_id=1, source_target_pairs={{0,4},{2,6},{4,0},{6,2},{1,5},{3,7},{5,1},{7,3},{8,12},{10,14},{12... | collective-permute-start | bytes 122888 | tf_op jit(solution)/shard_map/ppermute | solution.py:54
  55.2 0.0 collective-permute-start.12
  55.2 0.5 collective-permute-done.10
  55.7 2.8 %collective-permute-done.11 = f32[2,40,128]{2,1,0:T(8,128)S(1)} collective-permute-done((f32[2,40,128]{2,1,0:T(8,128)S(1)}, f32[2,40,128]{2,1,0:T(8,128)S(1)}, u32[]{:S(2)}, u32[]{:S(2)}) %collective-permute-start.11) | collective-permute-done | bytes 40992 | tf_op jit(solution)/shard_map/ppermute | solution.py:54
  58.5 2.5 %collective-permute-done.12 = f32[2,40,128]{2,1,0:T(8,128)S(1)} collective-permute-done((f32[2,40,128]{2,1,0:T(8,128)S(1)}, f32[2,40,128]{2,1,0:T(8,128)S(1)}, u32[]{:S(2)}, u32[]{:S(2)}) %collective-permute-start.12) | collective-permute-done | bytes 40992 | tf_op jit(solution)/shard_map/ppermute | solution.py:54
  61.1 2.0 %collective-permute-start.13 = (f32[2,512]{1,0:T(2,128)S(1)}, f32[2,512]{1,0:T(2,128)S(1)}, u32[]{:S(2)}, u32[]{:S(2)}) collective-permute-start(f32[2,512]{1,0:T(2,128)S(1)} %bitcast.12), channel_id=1, source_target_pairs={{0,8},{8,16},{16,24},{24,0},{1,9},{9,17},{17,25},{25,1},{2,10},{10... | collective-permute-start | bytes 12296 | tf_op jit(solution)/shard_map/ppermute | solution.py:54
  63.1 1.5 %collective-permute-start.14 = (f32[2,512]{1,0:T(2,128)S(1)}, f32[2,512]{1,0:T(2,128)S(1)}, u32[]{:S(2)}, u32[]{:S(2)}) collective-permute-start(f32[2,512]{1,0:T(2,128)S(1)} %bitcast.13), channel_id=1, source_target_pairs={{0,16},{8,24},{16,0},{24,8},{1,17},{9,25},{17,1},{25,9},{2,18},{10... | collective-permute-start | bytes 12296 | tf_op jit(solution)/shard_map/ppermute | solution.py:54
  64.6 1.0 %collective-permute-start.15 = (f32[2,512]{1,0:T(2,128)S(1)}, f32[2,512]{1,0:T(2,128)S(1)}, u32[]{:S(2)}, u32[]{:S(2)}) collective-permute-start(f32[2,512]{1,0:T(2,128)S(1)} %bitcast.14), channel_id=1, source_target_pairs={{0,24},{8,0},{16,8},{24,16},{1,25},{9,1},{17,9},{25,17},{2,26},{10... | collective-permute-start | bytes 12296 | tf_op jit(solution)/shard_map/ppermute | solution.py:54
  65.7 0.7 slice_negate_fusion
  66.3 0.0 collective-permute-done.13
  66.3 0.4 collective-permute-done.14
  66.7 1.5 %collective-permute-done.15 = f32[2,512]{1,0:T(2,128)S(1)} collective-permute-done((f32[2,512]{1,0:T(2,128)S(1)}, f32[2,512]{1,0:T(2,128)S(1)}, u32[]{:S(2)}, u32[]{:S(2)}) %collective-permute-start.15) | collective-permute-done | bytes 4128 | tf_op jit(solution)/shard_map/ppermute | solution.py:54
  68.2 0.6 add_add_fusion
  (17 shorter events, 0.2 us)
Async XLA Ops:
  0.6 1.0 %copy-start = (f32[2,128,512]{2,1,0:T(8,128)S(1)}, f32[2,128,512]{2,1,0:T(8,128)}, u32[]{:S(2)}) copy-start(f32[2,128,512]{2,1,0:T(8,128)} %param.5) | copy-start | bytes 1572868
  0.6 8.1 %copy-start.1 = (f32[2,256,128]{2,1,0:T(8,128)S(1)}, f32[2,256,128]{2,1,0:T(8,128)}, u32[]{:S(2)}) copy-start(f32[2,256,128]{2,1,0:T(8,128)} %refs_0_.1) | copy-start | bytes 786436
  1.7 37.3 %collective-permute-start.3 = (f32[2,32,512]{2,1,0:T(8,128)S(1)}, f32[2,32,512]{2,1,0:T(8,128)S(1)}, u32[]{:S(2)}, u32[]{:S(2)}) collective-permute-start(f32[2,32,512]{2,1,0:T(8,128)S(1)} %constant_dynamic-slice_fusion.5.refs_0_), channel_id=1, source_target_pairs={{0,2},{2,4},{4,6},{6,0},{1,3},{3,5},{5,7},{7,1},{8,10},{10,12},{12... | collective-permute-start | bytes 393224 | tf_op jit(solution)/shard_map/ppermute | solution.py:54
  4.8 34.3 %collective-permute-start.4 = (f32[2,32,512]{2,1,0:T(8,128)S(1)}, f32[2,32,512]{2,1,0:T(8,128)S(1)}, u32[]{:S(2)}, u32[]{:S(2)}) collective-permute-start(f32[2,32,512]{2,1,0:T(8,128)S(1)} %constant_dynamic-slice_fusion.5.refs_0_), channel_id=1, source_target_pairs={{0,4},{2,6},{4,0},{6,2},{1,5},{3,7},{5,1},{7,3},{8,12},{10,14},{12... | collective-permute-start | bytes 393224 | tf_op jit(solution)/shard_map/ppermute | solution.py:54
  7.4 31.7 %collective-permute-start.5 = (f32[2,32,512]{2,1,0:T(8,128)S(1)}, f32[2,32,512]{2,1,0:T(8,128)S(1)}, u32[]{:S(2)}, u32[]{:S(2)}) collective-permute-start(f32[2,32,512]{2,1,0:T(8,128)S(1)} %constant_dynamic-slice_fusion.5.refs_0_), channel_id=1, source_target_pairs={{0,6},{2,0},{4,2},{6,4},{1,7},{3,1},{5,3},{7,5},{8,14},{10,8},{12,... | collective-permute-start | bytes 393224 | tf_op jit(solution)/shard_map/ppermute | solution.py:54
  8.7 13.7 %collective-permute-start = (f32[2,256,128]{2,1,0:T(8,128)S(1)}, f32[2,256,128]{2,1,0:T(8,128)S(1)}, u32[]{:S(2)}, u32[]{:S(2)}) collective-permute-start(f32[2,256,128]{2,1,0:T(8,128)S(1)} %copy-done.1), channel_id=1, source_target_pairs={{0,2},{2,4},{4,6},{6,0},{1,3},{3,5},{5,7},{7,1},{8,10},{10,12},{12... | collective-permute-start | bytes 786440 | tf_op jit(solution)/shard_map/ppermute | solution.py:54
  9.4 38.2 %collective-permute-start.2 = (f32[2,256,128]{2,1,0:T(8,128)S(1)}, f32[2,256,128]{2,1,0:T(8,128)S(1)}, u32[]{:S(2)}, u32[]{:S(2)}) collective-permute-start(f32[2,256,128]{2,1,0:T(8,128)S(1)} %copy-done.1), channel_id=1, source_target_pairs={{0,6},{2,0},{4,2},{6,4},{1,7},{3,1},{5,3},{7,5},{8,14},{10,8},{12,... | collective-permute-start | bytes 786440 | tf_op jit(solution)/shard_map/ppermute | solution.py:54
  12.5 0.7 copy-start.2
  22.4 25.1 %collective-permute-start.1 = (f32[2,256,128]{2,1,0:T(8,128)S(1)}, f32[2,256,128]{2,1,0:T(8,128)S(1)}, u32[]{:S(2)}, u32[]{:S(2)}) collective-permute-start(f32[2,256,128]{2,1,0:T(8,128)S(1)} %collective-permute-done.refs_1_), channel_id=1, source_target_pairs={{0,2},{2,4},{4,6},{6,0},{1,3},{3,5},{5,7},{7,1},{8,10},{10,12},{12... | collective-permute-start | bytes 786440 | tf_op jit(solution)/shard_map/ppermute | solution.py:54
  39.6 5.9 %collective-permute-start.6 = (f32[4,2,32,128]{3,2,1,0:T(8,128)S(1)}, f32[4,2,32,128]{3,2,1,0:T(8,128)S(1)}, u32[]{:S(2)}, u32[]{:S(2)}) collective-permute-start(f32[4,2,32,128]{3,2,1,0:T(8,128)S(1)} %shard_map.59.refs_4_), channel_id=1, source_target_pairs={{0,8},{8,16},{16,24},{24,0},{1,9},{9,17},{17,25},{25,1},{2,10},{10... | collective-permute-start | bytes 393224 | tf_op jit(solution)/shard_map/ppermute | solution.py:54
  42.2 5.0 %collective-permute-start.7 = (f32[4,2,32,128]{3,2,1,0:T(8,128)S(1)}, f32[4,2,32,128]{3,2,1,0:T(8,128)S(1)}, u32[]{:S(2)}, u32[]{:S(2)}) collective-permute-start(f32[4,2,32,128]{3,2,1,0:T(8,128)S(1)} %shard_map.59.refs_4_), channel_id=1, source_target_pairs={{0,16},{8,24},{16,0},{24,8},{1,17},{9,25},{17,1},{25,9},{2,18},{10... | collective-permute-start | bytes 393224 | tf_op jit(solution)/shard_map/ppermute | solution.py:54
  42.2 5.4 %collective-permute-start.8 = (f32[4,2,32,128]{3,2,1,0:T(8,128)S(1)}, f32[4,2,32,128]{3,2,1,0:T(8,128)S(1)}, u32[]{:S(2)}, u32[]{:S(2)}) collective-permute-start(f32[4,2,32,128]{3,2,1,0:T(8,128)S(1)} %shard_map.59.refs_4_), channel_id=1, source_target_pairs={{0,24},{8,0},{16,8},{24,16},{1,25},{9,1},{17,9},{25,17},{2,26},{10... | collective-permute-start | bytes 393224 | tf_op jit(solution)/shard_map/ppermute | solution.py:54
  49.2 1.8 %collective-permute-start.9 = (f32[2,384,128]{2,1,0:T(8,128)S(1)}, f32[2,384,128]{2,1,0:T(8,128)S(1)}, u32[]{:S(2)}, u32[]{:S(2)}) collective-permute-start(f32[2,384,128]{2,1,0:T(8,128)S(1)} %shard_map.60), channel_id=1, source_target_pairs={{0,1},{1,0},{2,3},{3,2},{4,5},{5,4},{6,7},{7,6},{8,9},{9,8},{10,11... | collective-permute-start | bytes 1179656 | tf_op jit(solution)/shard_map/ppermute | solution.py:54
  51.2 4.5 %collective-permute-start.10 = (f32[2,40,128]{2,1,0:T(8,128)S(1)}, f32[2,40,128]{2,1,0:T(8,128)S(1)}, u32[]{:S(2)}, u32[]{:S(2)}) collective-permute-start(f32[2,40,128]{2,1,0:T(8,128)S(1)} %get-tuple-element.17), channel_id=1, source_target_pairs={{0,6},{2,0},{4,2},{6,4},{1,7},{3,1},{5,3},{7,5},{8,14},{10,8},{12,... | collective-permute-start | bytes 122888 | tf_op jit(solution)/shard_map/ppermute | solution.py:54
  52.5 6.0 %collective-permute-start.11 = (f32[2,40,128]{2,1,0:T(8,128)S(1)}, f32[2,40,128]{2,1,0:T(8,128)S(1)}, u32[]{:S(2)}, u32[]{:S(2)}) collective-permute-start(f32[2,40,128]{2,1,0:T(8,128)S(1)} %get-tuple-element.16), channel_id=1, source_target_pairs={{0,4},{2,6},{4,0},{6,2},{1,5},{3,7},{5,1},{7,3},{8,12},{10,14},{12... | collective-permute-start | bytes 122888 | tf_op jit(solution)/shard_map/ppermute | solution.py:54
  55.2 5.8 %collective-permute-start.12 = (f32[2,40,128]{2,1,0:T(8,128)S(1)}, f32[2,40,128]{2,1,0:T(8,128)S(1)}, u32[]{:S(2)}, u32[]{:S(2)}) collective-permute-start(f32[2,40,128]{2,1,0:T(8,128)S(1)} %get-tuple-element.15), channel_id=1, source_target_pairs={{0,2},{2,4},{4,6},{6,0},{1,3},{3,5},{5,7},{7,1},{8,10},{10,12},{12... | collective-permute-start | bytes 122888 | tf_op jit(solution)/shard_map/ppermute | solution.py:54
  61.1 5.3 %collective-permute-start.13 = (f32[2,512]{1,0:T(2,128)S(1)}, f32[2,512]{1,0:T(2,128)S(1)}, u32[]{:S(2)}, u32[]{:S(2)}) collective-permute-start(f32[2,512]{1,0:T(2,128)S(1)} %bitcast.12), channel_id=1, source_target_pairs={{0,8},{8,16},{16,24},{24,0},{1,9},{9,17},{17,25},{25,1},{2,10},{10... | collective-permute-start | bytes 12296 | tf_op jit(solution)/shard_map/ppermute | solution.py:54
  63.1 3.6 %collective-permute-start.14 = (f32[2,512]{1,0:T(2,128)S(1)}, f32[2,512]{1,0:T(2,128)S(1)}, u32[]{:S(2)}, u32[]{:S(2)}) collective-permute-start(f32[2,512]{1,0:T(2,128)S(1)} %bitcast.13), channel_id=1, source_target_pairs={{0,16},{8,24},{16,0},{24,8},{1,17},{9,25},{17,1},{25,9},{2,18},{10... | collective-permute-start | bytes 12296 | tf_op jit(solution)/shard_map/ppermute | solution.py:54
  64.6 3.6 %collective-permute-start.15 = (f32[2,512]{1,0:T(2,128)S(1)}, f32[2,512]{1,0:T(2,128)S(1)}, u32[]{:S(2)}, u32[]{:S(2)}) collective-permute-start(f32[2,512]{1,0:T(2,128)S(1)} %bitcast.14), channel_id=1, source_target_pairs={{0,24},{8,0},{16,8},{24,16},{1,25},{9,1},{17,9},{25,17},{2,26},{10... | collective-permute-start | bytes 12296 | tf_op jit(solution)/shard_map/ppermute | solution.py:54

commit v14 on v13

--- a/solution.py
+++ b/solution.py
@@ -10,9 +10,13 @@
 B = 256
 
 
-def scale_pieces(deep, *refs):
-    panels, (factor, out_ref) = refs[:deep], refs[deep:]
+def scale_pieces(deep, rows, place, *refs):
+    panels, blocks, (out_ref, factor) = refs[:deep], refs[deep : deep + rows], refs[deep + rows :]
     groups, piece, _ = panels[0].shape
+    depth = blocks[0].shape[1]
+    for e in range(rows):
+        first = pl.multiple_of(place[e] * depth, depth)
+        factor[:, pl.ds(first, depth)] = blocks[e][...]
     for s in range(groups):
         tall = jnp.concatenate([panel[s] for panel in panels], axis=0)
         scaled = jnp.dot(
@@ -84,14 +88,15 @@
         mine = lax.dynamic_slice_in_dim(panel, row * piece, piece, axis=1)
         block = lax.dynamic_slice_in_dim(factor_inv, z * part, part, axis=2)
         panels = gathered(mine, "z", deep)
-        blocks = lax.all_gather(block, "row", axis=1, tiled=True)
+        blocks = gathered(block, "row", rows)
         scaled = pl.pallas_call(
-            functools.partial(scale_pieces, deep),
+            functools.partial(scale_pieces, deep, rows),
             out_shape=jax.ShapeDtypeStruct((deep, groups, piece, part), jnp.float32),
-            in_specs=[whole] * (deep + 1),
+            in_specs=[scalars] + [whole] * (deep + rows),
             out_specs=whole,
+            scratch_shapes=[pltpu.VMEM((groups, width, part), jnp.float32)],
             compiler_params=params,
-        )(*panels, blocks)
+        )(quarter, *panels, *blocks)
         for d in late:
             far[d] = shifted(far[d - 1], "z", deep, 1)
         slots = gathered(scaled, "row", rows)

time: 69 us -> 58.2 us (0.84)
  blocking collectives: 10.2 us -> 0 us
  waiting for transfers between devices: 20.3 us -> 23.2 us
  starting transfers between devices: 30.8 us -> 28.4 us
  local copies, waits for them, and re-layouts: 1.85 us -> 0.16 us
    all_gather x1 -> x0, blocking collectives: 10.2 us -> none  [per_device(): blocks = lax.all_gather(block, 'row', axis=1, tiled=True)]
    ppermute x16 -> x19, waiting for transfers between devices: 20.3 us -> 23.2 us  [shifted(): lax.ppermute(array, axis, [(i, (i + shift) % size) for i in range(size)])]
    ppermute x16 -> x19, starting transfers between devices: 30.8 us -> 28.4 us  [shifted(): lax.ppermute(array, axis, [(i, (i + shift) % size) for i in range(size)])]
    unnamed x7, local copies, waits for them, and re-layouts: 1.71 us -> 0.02 us
  transfers between devices with their start and end apart: 16 -> 19, of which waited for: 10 -> 9; matrix products, arithmetic and copies ran while one was open for 3% -> 2% of each run, Pallas kernels for 1% -> 2%
where the time goes in v14:
time: 58.2 us; the launch traced here: 58 us
  starting transfers between devices  28.4 us (49%)
  waiting for transfers between devices  23.2 us (40%)
  Pallas kernels  2.76 us (5%)
  other arithmetic  2.67 us (5%)
  between operations  0.85 us (1%)
    ppermute x19, starting transfers between devices, shifted(): lax.ppermute(array, axis, [(i, (i + shift) % size) for i in range(size)])  28.4 us
    ppermute x19, waiting for transfers between devices, shifted(): lax.ppermute(array, axis, [(i, (i + shift) % size) for i in range(size)])  23.2 us
    pallas_call x1, Pallas kernels, per_device(): pl.pallas_call(functools.partial(multiply_tiles, deep, rows), out_shape=j...  1.61 us
  transfers between devices with their start and end apart: 19, of which 9 were waited for; matrix products, arithmetic and copies ran while one was open for 2% of the time, Pallas kernels for 2%

profile of v14, /device:TPU:0, one launch (start us, length us, event | category | flops | bytes accessed | tf_op | source)
XLA Modules:
  0.0 58.0 jit_solution(9316528248097150374)
XLA Ops:
  0.6 0.0 copy-start
  0.7 1.0 %multiply_reduce_fusion.1 = (f32[2,128]{1,0:T(2,128)S(1)}, f32[2,128,128]{2,1,0:T(8,128)S(1)}) fusion(f32[2,128,512]{2,1,0:T(8,128)} %param.6, s32[]{:T(128)S(6)} %select_n.192), kind=kLoop, calls=%fused_computation.5 | loop fusion | flops 65280 | bytes 263172 | tf_op jit(solution)/shard_map/reduce_sum | solution.py:129
  1.7 3.0 %collective-permute-start.6 = (f32[2,128,128]{2,1,0:T(8,128)S(1)}, f32[2,128,128]{2,1,0:T(8,128)S(1)}, u32[]{:S(2)}, u32[]{:S(2)}) collective-permute-start(f32[2,128,128]{2,1,0:T(8,128)S(1)} %get-tuple-element.3.refs_4_), channel_id=1, source_target_pairs={{0,8},{8,16},{16,24},{24,0},{1,9},{9,17},{17,25},{25,1},{2,10},{10... | collective-permute-start | bytes 393224 | tf_op jit(solution)/shard_map/ppermute | solution.py:58
  4.7 1.5 %collective-permute-start.7 = (f32[2,128,128]{2,1,0:T(8,128)S(1)}, f32[2,128,128]{2,1,0:T(8,128)S(1)}, u32[]{:S(2)}, u32[]{:S(2)}) collective-permute-start(f32[2,128,128]{2,1,0:T(8,128)S(1)} %get-tuple-element.3.refs_4_), channel_id=1, source_target_pairs={{0,16},{8,24},{16,0},{24,8},{1,17},{9,25},{17,1},{25,9},{2,18},{10... | collective-permute-start | bytes 393224 | tf_op jit(solution)/shard_map/ppermute | solution.py:58
  6.2 1.4 %collective-permute-start.8 = (f32[2,128,128]{2,1,0:T(8,128)S(1)}, f32[2,128,128]{2,1,0:T(8,128)S(1)}, u32[]{:S(2)}, u32[]{:S(2)}) collective-permute-start(f32[2,128,128]{2,1,0:T(8,128)S(1)} %get-tuple-element.3.refs_4_), channel_id=1, source_target_pairs={{0,24},{8,0},{16,8},{24,16},{1,25},{9,1},{17,9},{25,17},{2,26},{10... | collective-permute-start | bytes 393224 | tf_op jit(solution)/shard_map/ppermute | solution.py:58
  7.6 0.0 copy-start.2
  7.6 1.6 %collective-permute-start.3 = (f32[2,32,512]{2,1,0:T(8,128)S(1)}, f32[2,32,512]{2,1,0:T(8,128)S(1)}, u32[]{:S(2)}, u32[]{:S(2)}) collective-permute-start(f32[2,32,512]{2,1,0:T(8,128)S(1)} %constant_dynamic-slice_fusion.5.refs_0_), channel_id=1, source_target_pairs={{0,2},{2,4},{4,6},{6,0},{1,3},{3,5},{5,7},{7,1},{8,10},{10,12},{12... | collective-permute-start | bytes 393224 | tf_op jit(solution)/shard_map/ppermute | solution.py:58
  9.3 2.6 %collective-permute-start.4 = (f32[2,32,512]{2,1,0:T(8,128)S(1)}, f32[2,32,512]{2,1,0:T(8,128)S(1)}, u32[]{:S(2)}, u32[]{:S(2)}) collective-permute-start(f32[2,32,512]{2,1,0:T(8,128)S(1)} %constant_dynamic-slice_fusion.5.refs_0_), channel_id=1, source_target_pairs={{0,4},{2,6},{4,0},{6,2},{1,5},{3,7},{5,1},{7,3},{8,12},{10,14},{12... | collective-permute-start | bytes 393224 | tf_op jit(solution)/shard_map/ppermute | solution.py:58
  11.9 0.1 select_reduce_fusion
  12.0 0.0 collective-permute-done.6.refs_5_
  12.0 2.1 %collective-permute-start.5 = (f32[2,32,512]{2,1,0:T(8,128)S(1)}, f32[2,32,512]{2,1,0:T(8,128)S(1)}, u32[]{:S(2)}, u32[]{:S(2)}) collective-permute-start(f32[2,32,512]{2,1,0:T(8,128)S(1)} %constant_dynamic-slice_fusion.5.refs_0_), channel_id=1, source_target_pairs={{0,6},{2,0},{4,2},{6,4},{1,7},{3,1},{5,3},{7,5},{8,14},{10,8},{12,... | collective-permute-start | bytes 393224 | tf_op jit(solution)/shard_map/ppermute | solution.py:58
  14.1 0.0 collective-permute-done.7.refs_6_
  14.1 0.0 collective-permute-start
  14.1 0.1 sub.51
  14.2 0.0 collective-permute-done.8.refs_7_
  14.2 3.9 %collective-permute-start.2 = (f32[2,256,128]{2,1,0:T(8,128)S(1)}, f32[2,256,128]{2,1,0:T(8,128)S(1)}, u32[]{:S(2)}, u32[]{:S(2)}) collective-permute-start(f32[2,256,128]{2,1,0:T(8,128)S(1)} %copy-done.1), channel_id=1, source_target_pairs={{0,6},{2,0},{4,2},{6,4},{1,7},{3,1},{5,3},{7,5},{8,14},{10,8},{12,... | collective-permute-start | bytes 786440 | tf_op jit(solution)/shard_map/ppermute | solution.py:58
  18.0 0.0 collective-permute-done.3.refs_1_
  18.0 5.4 %collective-permute-done.4.refs_2_ = f32[2,32,512]{2,1,0:T(8,128)S(1)} collective-permute-done((f32[2,32,512]{2,1,0:T(8,128)S(1)}, f32[2,32,512]{2,1,0:T(8,128)S(1)}, u32[]{:S(2)}, u32[]{:S(2)}) %collective-permute-start.4) | collective-permute-done | bytes 131104 | tf_op jit(solution)/shard_map/ppermute | solution.py:58
  23.5 2.8 %collective-permute-done.5.refs_3_ = f32[2,32,512]{2,1,0:T(8,128)S(1)} collective-permute-done((f32[2,32,512]{2,1,0:T(8,128)S(1)}, f32[2,32,512]{2,1,0:T(8,128)S(1)}, u32[]{:S(2)}, u32[]{:S(2)}) %collective-permute-start.5) | collective-permute-done | bytes 131104 | tf_op jit(solution)/shard_map/ppermute | solution.py:58
  26.3 1.2 %shard_map.59.refs_4_ = f32[4,2,32,128]{3,2,1,0:T(8,128)S(1)} custom-call(s32[4]{0:T(128)S(1)} %and_select_fusion.place, f32[2,32,512]{2,1,0:T(8,128)S(1)} %constant_dynamic-slice_fusion.5.refs_0_, f32[2,32,512]{2,1,0:T(8,128)S(1)} %collective-permute-done.3.refs_1_, f32[2,32,512]{2,1,0:T(8,128)S(1)} %collective-permute-done.4.refs_2_, ...), custom_call_target="tpu_custom_call" | custom-call | tf_op jit(solution)/shard_map/pallas_call | solution.py:92
  27.5 0.5 collective-permute-start.10
  28.0 1.6 %collective-permute-start.11 = (f32[4,2,32,128]{3,2,1,0:T(8,128)S(1)}, f32[4,2,32,128]{3,2,1,0:T(8,128)S(1)}, u32[]{:S(2)}, u32[]{:S(2)}) collective-permute-start(f32[4,2,32,128]{3,2,1,0:T(8,128)S(1)} %shard_map.59.refs_4_), channel_id=1, source_target_pairs={{0,24},{8,0},{16,8},{24,16},{1,25},{9,1},{17,9},{25,17},{2,26},{10... | collective-permute-start | bytes 393224 | tf_op jit(solution)/shard_map/ppermute | solution.py:58
  29.6 0.5 collective-permute-start.9
  30.0 0.0 collective-permute-done.refs_1_
  30.0 2.4 %collective-permute-start.1 = (f32[2,256,128]{2,1,0:T(8,128)S(1)}, f32[2,256,128]{2,1,0:T(8,128)S(1)}, u32[]{:S(2)}, u32[]{:S(2)}) collective-permute-start(f32[2,256,128]{2,1,0:T(8,128)S(1)} %collective-permute-done.refs_1_), channel_id=1, source_target_pairs={{0,2},{2,4},{4,6},{6,0},{1,3},{3,5},{5,7},{7,1},{8,10},{10,12},{12... | collective-permute-start | bytes 786440 | tf_op jit(solution)/shard_map/ppermute | solution.py:58
  32.4 0.1 pad_add_fusion.place
  32.5 0.0 collective-permute-done.10.refs_6_
  32.5 0.5 collective-permute-done.11.refs_7_
  33.0 2.5 %collective-permute-done.9.refs_5_ = f32[4,2,32,128]{3,2,1,0:T(8,128)S(1)} collective-permute-done((f32[4,2,32,128]{3,2,1,0:T(8,128)S(1)}, f32[4,2,32,128]{3,2,1,0:T(8,128)S(1)}, u32[]{:S(2)}, u32[]{:S(2)}) %collective-permute-start.9) | collective-permute-done | bytes 131104 | tf_op jit(solution)/shard_map/ppermute | solution.py:58
  35.5 0.0 collective-permute-done.2.refs_3_
  35.5 4.2 %collective-permute-done.1.refs_2_ = f32[2,256,128]{2,1,0:T(8,128)S(1)} collective-permute-done((f32[2,256,128]{2,1,0:T(8,128)S(1)}, f32[2,256,128]{2,1,0:T(8,128)S(1)}, u32[]{:S(2)}, u32[]{:S(2)}) %collective-permute-start.1) | collective-permute-done | bytes 262176 | tf_op jit(solution)/shard_map/ppermute | solution.py:58
  39.7 1.6 %shard_map.60 = f32[2,384,128]{2,1,0:T(8,128)S(1)} custom-call(s32[13]{0:T(128)S(1)} %pad_add_fusion.place, f32[2,256,128]{2,1,0:T(8,128)S(1)} %copy-done.1, f32[2,256,128]{2,1,0:T(8,128)S(1)} %collective-permute-done.refs_1_, f32[2,256,128]{2,1,0:T(8,128)S(1)} %collective-permute-done.1.refs_2_, f32[2,256,128]{2,1,0:T(8,128)S(1)} %collective-permute-done.2.refs_3_, ...), custom_call_target="tpu_custom_call" | custom-call | tf_op jit(solution)/shard_map/pallas_call | solution.py:113
  41.3 0.1 collective-permute-start.12
  41.4 1.7 %collective-permute-done.12 = f32[2,384,128]{2,1,0:T(8,128)S(1)} collective-permute-done((f32[2,384,128]{2,1,0:T(8,128)S(1)}, f32[2,384,128]{2,1,0:T(8,128)S(1)}, u32[]{:S(2)}, u32[]{:S(2)}) %collective-permute-start.12) | collective-permute-done | bytes 393248 | tf_op jit(solution)/shard_map/ppermute | solution.py:58
  43.2 0.1 multiply_reduce_fusion
  43.3 1.8 %collective-permute-start.13 = (f32[2,40,128]{2,1,0:T(8,128)S(1)}, f32[2,40,128]{2,1,0:T(8,128)S(1)}, u32[]{:S(2)}, u32[]{:S(2)}) collective-permute-start(f32[2,40,128]{2,1,0:T(8,128)S(1)} %get-tuple-element.17), channel_id=1, source_target_pairs={{0,6},{2,0},{4,2},{6,4},{1,7},{3,1},{5,3},{7,5},{8,14},{10,8},{12,... | collective-permute-start | bytes 122888 | tf_op jit(solution)/shard_map/ppermute | solution.py:58
  45.1 0.0 collective-permute-start.14
  45.1 1.3 %collective-permute-start.15 = (f32[2,40,128]{2,1,0:T(8,128)S(1)}, f32[2,40,128]{2,1,0:T(8,128)S(1)}, u32[]{:S(2)}, u32[]{:S(2)}) collective-permute-start(f32[2,40,128]{2,1,0:T(8,128)S(1)} %get-tuple-element.15), channel_id=1, source_target_pairs={{0,2},{2,4},{4,6},{6,0},{1,3},{3,5},{5,7},{7,1},{8,10},{10,12},{12... | collective-permute-start | bytes 122888 | tf_op jit(solution)/shard_map/ppermute | solution.py:58
  46.4 0.9 %collective-permute-done.13 = f32[2,40,128]{2,1,0:T(8,128)S(1)} collective-permute-done((f32[2,40,128]{2,1,0:T(8,128)S(1)}, f32[2,40,128]{2,1,0:T(8,128)S(1)}, u32[]{:S(2)}, u32[]{:S(2)}) %collective-permute-start.13) | collective-permute-done | bytes 40992 | tf_op jit(solution)/shard_map/ppermute | solution.py:58
  47.4 3.7 %collective-permute-done.14 = f32[2,40,128]{2,1,0:T(8,128)S(1)} collective-permute-done((f32[2,40,128]{2,1,0:T(8,128)S(1)}, f32[2,40,128]{2,1,0:T(8,128)S(1)}, u32[]{:S(2)}, u32[]{:S(2)}) %collective-permute-start.14) | collective-permute-done | bytes 40992 | tf_op jit(solution)/shard_map/ppermute | solution.py:58
  51.0 0.0 collective-permute-done.15
  51.1 1.2 %collective-permute-start.16 = (f32[2,512]{1,0:T(2,128)S(1)}, f32[2,512]{1,0:T(2,128)S(1)}, u32[]{:S(2)}, u32[]{:S(2)}) collective-permute-start(f32[2,512]{1,0:T(2,128)S(1)} %bitcast.12), channel_id=1, source_target_pairs={{0,8},{8,16},{16,24},{24,0},{1,9},{9,17},{17,25},{25,1},{2,10},{10... | collective-permute-start | bytes 12296 | tf_op jit(solution)/shard_map/ppermute | solution.py:58
  52.3 1.5 %collective-permute-start.17 = (f32[2,512]{1,0:T(2,128)S(1)}, f32[2,512]{1,0:T(2,128)S(1)}, u32[]{:S(2)}, u32[]{:S(2)}) collective-permute-start(f32[2,512]{1,0:T(2,128)S(1)} %bitcast.13), channel_id=1, source_target_pairs={{0,16},{8,24},{16,0},{24,8},{1,17},{9,25},{17,1},{25,9},{2,18},{10... | collective-permute-start | bytes 12296 | tf_op jit(solution)/shard_map/ppermute | solution.py:58
  53.8 1.4 %collective-permute-start.18 = (f32[2,512]{1,0:T(2,128)S(1)}, f32[2,512]{1,0:T(2,128)S(1)}, u32[]{:S(2)}, u32[]{:S(2)}) collective-permute-start(f32[2,512]{1,0:T(2,128)S(1)} %bitcast.14), channel_id=1, source_target_pairs={{0,24},{8,0},{16,8},{24,16},{1,25},{9,1},{17,9},{25,17},{2,26},{10... | collective-permute-start | bytes 12296 | tf_op jit(solution)/shard_map/ppermute | solution.py:58
  55.3 0.7 %slice_negate_fusion = f32[2,32,512]{2,1,0:T(8,128)} fusion(f32[2,40,512]{2,1,0:T(8,128)S(1)} %pad_maximum_fusion.1), kind=kLoop, calls=%fused_computation.4 | loop fusion | flops 32768 | bytes 262144 | tf_op jit(solution)/shard_map/neg | solution.py:145
  56.0 0.0 collective-permute-done.16
  56.0 1.5 %collective-permute-done.18 = f32[2,512]{1,0:T(2,128)S(1)} collective-permute-done((f32[2,512]{1,0:T(2,128)S(1)}, f32[2,512]{1,0:T(2,128)S(1)}, u32[]{:S(2)}, u32[]{:S(2)}) %collective-permute-start.18) | collective-permute-done | bytes 4128 | tf_op jit(solution)/shard_map/ppermute | solution.py:58
  57.4 0.6 %add_add_fusion = f32[2,512]{1,0:T(2,128)} fusion(f32[2,512]{1,0:T(2,128)S(1)} %collective-permute-done.18, f32[2,512]{1,0:T(2,128)S(1)} %collective-permute-done.17, f32[2,512]{1,0:T(2,128)S(1)} %collective-permute-done.16, f32[2,1,512]{2,1,0:T(1,128)S(1)} %pad_maximum_fusion.6), kind=kLoop, calls=%fused_computation.18 | loop fusion | flops 3072 | bytes 20480 | tf_op jit(solution)/shard_map/add | solution.py:144
  (22 shorter events, 0.2 us)
Async XLA Ops:
  0.6 7.0 %copy-start = (f32[2,128,512]{2,1,0:T(8,128)S(1)}, f32[2,128,512]{2,1,0:T(8,128)}, u32[]{:S(2)}) copy-start(f32[2,128,512]{2,1,0:T(8,128)} %param.5) | copy-start | bytes 1572868
  0.7 13.4 %copy-start.1 = (f32[2,256,128]{2,1,0:T(8,128)S(1)}, f32[2,256,128]{2,1,0:T(8,128)}, u32[]{:S(2)}) copy-start(f32[2,256,128]{2,1,0:T(8,128)} %refs_0_.1) | copy-start | bytes 786436
  1.7 10.3 %collective-permute-start.6 = (f32[2,128,128]{2,1,0:T(8,128)S(1)}, f32[2,128,128]{2,1,0:T(8,128)S(1)}, u32[]{:S(2)}, u32[]{:S(2)}) collective-permute-start(f32[2,128,128]{2,1,0:T(8,128)S(1)} %get-tuple-element.3.refs_4_), channel_id=1, source_target_pairs={{0,8},{8,16},{16,24},{24,0},{1,9},{9,17},{17,25},{25,1},{2,10},{10... | collective-permute-start | bytes 393224 | tf_op jit(solution)/shard_map/ppermute | solution.py:58
  4.7 9.4 %collective-permute-start.7 = (f32[2,128,128]{2,1,0:T(8,128)S(1)}, f32[2,128,128]{2,1,0:T(8,128)S(1)}, u32[]{:S(2)}, u32[]{:S(2)}) collective-permute-start(f32[2,128,128]{2,1,0:T(8,128)S(1)} %get-tuple-element.3.refs_4_), channel_id=1, source_target_pairs={{0,16},{8,24},{16,0},{24,8},{1,17},{9,25},{17,1},{25,9},{2,18},{10... | collective-permute-start | bytes 393224 | tf_op jit(solution)/shard_map/ppermute | solution.py:58
  6.2 8.0 %collective-permute-start.8 = (f32[2,128,128]{2,1,0:T(8,128)S(1)}, f32[2,128,128]{2,1,0:T(8,128)S(1)}, u32[]{:S(2)}, u32[]{:S(2)}) collective-permute-start(f32[2,128,128]{2,1,0:T(8,128)S(1)} %get-tuple-element.3.refs_4_), channel_id=1, source_target_pairs={{0,24},{8,0},{16,8},{24,16},{1,25},{9,1},{17,9},{25,17},{2,26},{10... | collective-permute-start | bytes 393224 | tf_op jit(solution)/shard_map/ppermute | solution.py:58
  7.6 4.2 %copy-start.2 = (s32[2,4]{1,0:T(2,128)S(1)}, s32[2,4]{1,0:T(2,128)}, u32[]{:S(2)}) copy-start(s32[2,4]{1,0:T(2,128)} %param.7) | copy-start | bytes 100
  7.6 10.4 %collective-permute-start.3 = (f32[2,32,512]{2,1,0:T(8,128)S(1)}, f32[2,32,512]{2,1,0:T(8,128)S(1)}, u32[]{:S(2)}, u32[]{:S(2)}) collective-permute-start(f32[2,32,512]{2,1,0:T(8,128)S(1)} %constant_dynamic-slice_fusion.5.refs_0_), channel_id=1, source_target_pairs={{0,2},{2,4},{4,6},{6,0},{1,3},{3,5},{5,7},{7,1},{8,10},{10,12},{12... | collective-permute-start | bytes 393224 | tf_op jit(solution)/shard_map/ppermute | solution.py:58
  9.3 14.2 %collective-permute-start.4 = (f32[2,32,512]{2,1,0:T(8,128)S(1)}, f32[2,32,512]{2,1,0:T(8,128)S(1)}, u32[]{:S(2)}, u32[]{:S(2)}) collective-permute-start(f32[2,32,512]{2,1,0:T(8,128)S(1)} %constant_dynamic-slice_fusion.5.refs_0_), channel_id=1, source_target_pairs={{0,4},{2,6},{4,0},{6,2},{1,5},{3,7},{5,1},{7,3},{8,12},{10,14},{12... | collective-permute-start | bytes 393224 | tf_op jit(solution)/shard_map/ppermute | solution.py:58
  12.0 14.3 %collective-permute-start.5 = (f32[2,32,512]{2,1,0:T(8,128)S(1)}, f32[2,32,512]{2,1,0:T(8,128)S(1)}, u32[]{:S(2)}, u32[]{:S(2)}) collective-permute-start(f32[2,32,512]{2,1,0:T(8,128)S(1)} %constant_dynamic-slice_fusion.5.refs_0_), channel_id=1, source_target_pairs={{0,6},{2,0},{4,2},{6,4},{1,7},{3,1},{5,3},{7,5},{8,14},{10,8},{12,... | collective-permute-start | bytes 393224 | tf_op jit(solution)/shard_map/ppermute | solution.py:58
  14.1 16.0 %collective-permute-start = (f32[2,256,128]{2,1,0:T(8,128)S(1)}, f32[2,256,128]{2,1,0:T(8,128)S(1)}, u32[]{:S(2)}, u32[]{:S(2)}) collective-permute-start(f32[2,256,128]{2,1,0:T(8,128)S(1)} %copy-done.1), channel_id=1, source_target_pairs={{0,2},{2,4},{4,6},{6,0},{1,3},{3,5},{5,7},{7,1},{8,10},{10,12},{12... | collective-permute-start | bytes 786440 | tf_op jit(solution)/shard_map/ppermute | solution.py:58
  14.2 21.3 %collective-permute-start.2 = (f32[2,256,128]{2,1,0:T(8,128)S(1)}, f32[2,256,128]{2,1,0:T(8,128)S(1)}, u32[]{:S(2)}, u32[]{:S(2)}) collective-permute-start(f32[2,256,128]{2,1,0:T(8,128)S(1)} %copy-done.1), channel_id=1, source_target_pairs={{0,6},{2,0},{4,2},{6,4},{1,7},{3,1},{5,3},{7,5},{8,14},{10,8},{12,... | collective-permute-start | bytes 786440 | tf_op jit(solution)/shard_map/ppermute | solution.py:58
  27.5 5.1 %collective-permute-start.10 = (f32[4,2,32,128]{3,2,1,0:T(8,128)S(1)}, f32[4,2,32,128]{3,2,1,0:T(8,128)S(1)}, u32[]{:S(2)}, u32[]{:S(2)}) collective-permute-start(f32[4,2,32,128]{3,2,1,0:T(8,128)S(1)} %shard_map.59.refs_4_), channel_id=1, source_target_pairs={{0,16},{8,24},{16,0},{24,8},{1,17},{9,25},{17,1},{25,9},{2,18},{10... | collective-permute-start | bytes 393224 | tf_op jit(solution)/shard_map/ppermute | solution.py:58
  28.0 5.0 %collective-permute-start.11 = (f32[4,2,32,128]{3,2,1,0:T(8,128)S(1)}, f32[4,2,32,128]{3,2,1,0:T(8,128)S(1)}, u32[]{:S(2)}, u32[]{:S(2)}) collective-permute-start(f32[4,2,32,128]{3,2,1,0:T(8,128)S(1)} %shard_map.59.refs_4_), channel_id=1, source_target_pairs={{0,24},{8,0},{16,8},{24,16},{1,25},{9,1},{17,9},{25,17},{2,26},{10... | collective-permute-start | bytes 393224 | tf_op jit(solution)/shard_map/ppermute | solution.py:58
  29.6 5.9 %collective-permute-start.9 = (f32[4,2,32,128]{3,2,1,0:T(8,128)S(1)}, f32[4,2,32,128]{3,2,1,0:T(8,128)S(1)}, u32[]{:S(2)}, u32[]{:S(2)}) collective-permute-start(f32[4,2,32,128]{3,2,1,0:T(8,128)S(1)} %shard_map.59.refs_4_), channel_id=1, source_target_pairs={{0,8},{8,16},{16,24},{24,0},{1,9},{9,17},{17,25},{25,1},{2,10},{10... | collective-permute-start | bytes 393224 | tf_op jit(solution)/shard_map/ppermute | solution.py:58
  30.0 9.6 %collective-permute-start.1 = (f32[2,256,128]{2,1,0:T(8,128)S(1)}, f32[2,256,128]{2,1,0:T(8,128)S(1)}, u32[]{:S(2)}, u32[]{:S(2)}) collective-permute-start(f32[2,256,128]{2,1,0:T(8,128)S(1)} %collective-permute-done.refs_1_), channel_id=1, source_target_pairs={{0,2},{2,4},{4,6},{6,0},{1,3},{3,5},{5,7},{7,1},{8,10},{10,12},{12... | collective-permute-start | bytes 786440 | tf_op jit(solution)/shard_map/ppermute | solution.py:58
  41.3 1.8 %collective-permute-start.12 = (f32[2,384,128]{2,1,0:T(8,128)S(1)}, f32[2,384,128]{2,1,0:T(8,128)S(1)}, u32[]{:S(2)}, u32[]{:S(2)}) collective-permute-start(f32[2,384,128]{2,1,0:T(8,128)S(1)} %shard_map.60), channel_id=1, source_target_pairs={{0,1},{1,0},{2,3},{3,2},{4,5},{5,4},{6,7},{7,6},{8,9},{9,8},{10,11... | collective-permute-start | bytes 1179656 | tf_op jit(solution)/shard_map/ppermute | solution.py:58
  43.3 4.1 %collective-permute-start.13 = (f32[2,40,128]{2,1,0:T(8,128)S(1)}, f32[2,40,128]{2,1,0:T(8,128)S(1)}, u32[]{:S(2)}, u32[]{:S(2)}) collective-permute-start(f32[2,40,128]{2,1,0:T(8,128)S(1)} %get-tuple-element.17), channel_id=1, source_target_pairs={{0,6},{2,0},{4,2},{6,4},{1,7},{3,1},{5,3},{7,5},{8,14},{10,8},{12,... | collective-permute-start | bytes 122888 | tf_op jit(solution)/shard_map/ppermute | solution.py:58
  45.1 5.9 %collective-permute-start.14 = (f32[2,40,128]{2,1,0:T(8,128)S(1)}, f32[2,40,128]{2,1,0:T(8,128)S(1)}, u32[]{:S(2)}, u32[]{:S(2)}) collective-permute-start(f32[2,40,128]{2,1,0:T(8,128)S(1)} %get-tuple-element.16), channel_id=1, source_target_pairs={{0,4},{2,6},{4,0},{6,2},{1,5},{3,7},{5,1},{7,3},{8,12},{10,14},{12... | collective-permute-start | bytes 122888 | tf_op jit(solution)/shard_map/ppermute | solution.py:58
  45.1 5.9 %collective-permute-start.15 = (f32[2,40,128]{2,1,0:T(8,128)S(1)}, f32[2,40,128]{2,1,0:T(8,128)S(1)}, u32[]{:S(2)}, u32[]{:S(2)}) collective-permute-start(f32[2,40,128]{2,1,0:T(8,128)S(1)} %get-tuple-element.15), channel_id=1, source_target_pairs={{0,2},{2,4},{4,6},{6,0},{1,3},{3,5},{5,7},{7,1},{8,10},{10,12},{12... | collective-permute-start | bytes 122888 | tf_op jit(solution)/shard_map/ppermute | solution.py:58
  51.1 4.8 %collective-permute-start.16 = (f32[2,512]{1,0:T(2,128)S(1)}, f32[2,512]{1,0:T(2,128)S(1)}, u32[]{:S(2)}, u32[]{:S(2)}) collective-permute-start(f32[2,512]{1,0:T(2,128)S(1)} %bitcast.12), channel_id=1, source_target_pairs={{0,8},{8,16},{16,24},{24,0},{1,9},{9,17},{17,25},{25,1},{2,10},{10... | collective-permute-start | bytes 12296 | tf_op jit(solution)/shard_map/ppermute | solution.py:58
  52.3 3.6 %collective-permute-start.17 = (f32[2,512]{1,0:T(2,128)S(1)}, f32[2,512]{1,0:T(2,128)S(1)}, u32[]{:S(2)}, u32[]{:S(2)}) collective-permute-start(f32[2,512]{1,0:T(2,128)S(1)} %bitcast.13), channel_id=1, source_target_pairs={{0,16},{8,24},{16,0},{24,8},{1,17},{9,25},{17,1},{25,9},{2,18},{10... | collective-permute-start | bytes 12296 | tf_op jit(solution)/shard_map/ppermute | solution.py:58
  53.8 3.6 %collective-permute-start.18 = (f32[2,512]{1,0:T(2,128)S(1)}, f32[2,512]{1,0:T(2,128)S(1)}, u32[]{:S(2)}, u32[]{:S(2)}) collective-permute-start(f32[2,512]{1,0:T(2,128)S(1)} %bitcast.14), channel_id=1, source_target_pairs={{0,24},{8,0},{16,8},{24,16},{1,25},{9,1},{17,9},{25,17},{2,26},{10... | collective-permute-start | bytes 12296 | tf_op jit(solution)/shard_map/ppermute | solution.py:58

commit v15 on v12

--- a/solution.py
+++ b/solution.py
@@ -72,7 +72,8 @@
             return lax.dynamic_slice_in_dim(partial, r * piece, piece, axis=1)
 
         sums = [shifted(rows_of((row + d) % rows), "row", rows, d) for d in range(1, rows)]
-        sums, far = lax.optimization_barrier((sums, far))
+        squares = jnp.sum(lax.dynamic_slice_in_dim(factor_inv, z * part, part, axis=2) ** 2, axis=1)
+        sums, squares = lax.optimization_barrier((sums, squares))
         scaled = sum(sums, rows_of(row))
 
         def columns_of(array, c):
@@ -114,23 +115,24 @@
         product = product[:, :height] + other[:, :height]
         halves = [jnp.where(core == 0, own, own_other), jnp.where(core == 0, own_other, own)]
         own = jnp.stack(halves, axis=2).reshape(groups, height, part)
-        squares = jnp.sum(columns_of(factor_inv, z) ** 2, axis=1)
         term = jnp.sum(own * product, axis=1) + squares
-        tail = jnp.broadcast_to(term[:, None], (groups, 8, part))
+        tail = jnp.concatenate([term, jnp.zeros((-groups % 8, part), jnp.float32)])
 
         def rows_for(c):
             block = lax.dynamic_slice_in_dim(product, (c * cores + core) * out_rows, out_rows, axis=1)
-            return jnp.concatenate([block, tail], axis=1)
+            return jnp.concatenate([block.reshape(groups * out_rows, part), tail])
 
         moved = [rows_for(z)]
         for shift in range(1, deep):
             moved.append(shifted(rows_for((z + shift) % deep), "z", deep, shift))
-        moved = jnp.concatenate([picked(moved, z, c) for c in range(deep)], axis=2)
-        local = moved[:, out_rows]
-        total = local
-        for shift in range(1, rows):
-            total = total + shifted(local, "row", rows, shift)
-        return -moved[:, :out_rows], total
+        moved = jnp.concatenate([picked(moved, z, c) for c in range(deep)], axis=1)
+        column_block = -moved[: groups * out_rows].reshape(groups, out_rows, width)
+        total = moved[groups * out_rows : groups * out_rows + groups]
+        step = 1
+        while step < rows:
+            total = total + lax.ppermute(total, "row", [(r, r ^ step) for r in range(rows)])
+            step *= 2
+        return column_block, total
 
     col = ("z", "core")
     in_specs = (P(None, "row", col), P(None, col, None), P(None, "row", None), P())

time: 53.4 us -> 55.8 us (1.045)
  waiting for transfers between devices: 17.7 us -> 22.5 us
  starting transfers between devices: 27.8 us -> 25.2 us
    ppermute x0 -> x2, waiting for transfers between devices: none -> 5.08 us  [per_device(): lax.ppermute(total, 'row', [(r, r ^ step) for r in range(rows)])]
    ppermute x19 -> x16, starting transfers between devices: 27.8 us -> 23.7 us  [shifted(): lax.ppermute(array, axis, [(i, (i + shift) % size) for i in range(size)])]
    ppermute x0 -> x2, starting transfers between devices: none -> 1.52 us  [per_device(): lax.ppermute(total, 'row', [(r, r ^ step) for r in range(rows)])]
    ppermute x19 -> x16, waiting for transfers between devices: 17.7 us -> 17.4 us  [shifted(): lax.ppermute(array, axis, [(i, (i + shift) % size) for i in range(size)])]
  transfers between devices with their start and end apart: 19 -> 18, of which waited for: 15 -> 14; matrix products, arithmetic and copies ran while one was open for 7% -> 7% of each run, Pallas kernels for 0% -> 0%
where the time goes in v15:
time: 55.8 us; the launch traced here: 55.6 us
  starting transfers between devices  25.2 us (45%)
  waiting for transfers between devices  22.5 us (40%)
  other arithmetic  2.84 us (5%)
  matrix products  1.61 us (3%)
  Pallas kernels  1.61 us (3%)
  local copies, waits for them, and re-layouts  0.96 us (2%)
  between operations  0.85 us (2%)
    ppermute x16, starting transfers between devices, shifted(): lax.ppermute(array, axis, [(i, (i + shift) % size) for i in range(size)])  23.7 us
    ppermute x16, waiting for transfers between devices, shifted(): lax.ppermute(array, axis, [(i, (i + shift) % size) for i in range(size)])  17.4 us
    ppermute x2, waiting for transfers between devices, per_device(): lax.ppermute(total, 'row', [(r, r ^ step) for r in range(rows)])  5.08 us
    dot_general x1, matrix products, per_device(): partial = jnp.einsum('srw,swv->srv', mine, factor_inv, precision=highest)  1.61 us
    pallas_call x1, Pallas kernels, per_device(): pl.pallas_call(functools.partial(multiply_tiles, deep, rows), out_shape=j...  1.61 us
    ppermute x2, starting transfers between devices, per_device(): lax.ppermute(total, 'row', [(r, r ^ step) for r in range(rows)])  1.52 us
  transfers between devices with their start and end apart: 18, of which 14 were waited for; matrix products, arithmetic and copies ran while one was open for 7% of the time, Pallas kernels for 0%

profile of v15, /device:TPU:0, one launch (start us, length us, event | category | flops | bytes accessed | tf_op | source)
XLA Modules:
  0.0 55.6 jit_solution(16344020013208204205)
XLA Ops:
  0.6 0.0 copy-start
  0.6 3.1 %collective-permute-start.6 = (f32[2,256,128]{2,1,0:T(8,128)}, f32[2,256,128]{2,1,0:T(8,128)S(1)}, u32[]{:S(2)}, u32[]{:S(2)}) collective-permute-start(f32[2,256,128]{2,1,0:T(8,128)} %refs_0_.1), channel_id=1, source_target_pairs={{0,2},{2,4},{4,6},{6,0},{1,3},{3,5},{5,7},{7,1},{8,10},{10,12},{12... | collective-permute-start | bytes 786440 | tf_op jit(solution)/shard_map/ppermute | solution.py:42
  3.7 2.1 %collective-permute-start.8 = (f32[2,256,128]{2,1,0:T(8,128)}, f32[2,256,128]{2,1,0:T(8,128)S(1)}, u32[]{:S(2)}, u32[]{:S(2)}) collective-permute-start(f32[2,256,128]{2,1,0:T(8,128)} %refs_0_.1), channel_id=1, source_target_pairs={{0,6},{2,0},{4,2},{6,4},{1,7},{3,1},{5,3},{7,5},{8,14},{10,8},{12,... | collective-permute-start | bytes 786440 | tf_op jit(solution)/shard_map/ppermute | solution.py:42
  5.8 1.6 %fusion = f32[2,128,512]{2,1,0:T(8,128)S(1)} fusion(f32[2,128,512]{2,1,0:T(8,128)} %param.6, f32[2,128,512]{2,1,0:T(8,128)S(1)} %copy-done, s32[]{:T(128)S(6)} %select_n.231), kind=kOutput, calls=%fused_computation.10 | convolution fusion | flops 201326592 | bytes 1179652 | tf_op jit(solution)/shard_map/srw,swv->srv/dot_general | solution.py:69
  7.5 1.7 %collective-permute-start = (f32[2,32,512]{2,1,0:T(8,128)S(1)}, f32[2,32,512]{2,1,0:T(8,128)S(1)}, u32[]{:S(2)}, u32[]{:S(2)}) collective-permute-start(f32[2,32,512]{2,1,0:T(8,128)S(1)} %get-tuple-element.26), channel_id=1, source_target_pairs={{0,8},{8,16},{16,24},{24,0},{1,9},{9,17},{17,25},{25,1},{2,10},{10... | collective-permute-start | bytes 393224 | tf_op jit(solution)/shard_map/ppermute | solution.py:42
  9.2 1.5 %collective-permute-start.1 = (f32[2,32,512]{2,1,0:T(8,128)S(1)}, f32[2,32,512]{2,1,0:T(8,128)S(1)}, u32[]{:S(2)}, u32[]{:S(2)}) collective-permute-start(f32[2,32,512]{2,1,0:T(8,128)S(1)} %get-tuple-element.25), channel_id=1, source_target_pairs={{0,16},{8,24},{16,0},{24,8},{1,17},{9,25},{17,1},{25,9},{2,18},{10... | collective-permute-start | bytes 393224 | tf_op jit(solution)/shard_map/ppermute | solution.py:42
  10.7 1.4 %collective-permute-start.2 = (f32[2,32,512]{2,1,0:T(8,128)S(1)}, f32[2,32,512]{2,1,0:T(8,128)S(1)}, u32[]{:S(2)}, u32[]{:S(2)}) collective-permute-start(f32[2,32,512]{2,1,0:T(8,128)S(1)} %get-tuple-element.24), channel_id=1, source_target_pairs={{0,24},{8,0},{16,8},{24,16},{1,25},{9,1},{17,9},{25,17},{2,26},{10... | collective-permute-start | bytes 393224 | tf_op jit(solution)/shard_map/ppermute | solution.py:42
  12.1 0.7 %copy-done.2 = s32[2,4]{1,0:T(2,128)S(1)} copy-done((s32[2,4]{1,0:T(2,128)S(1)}, s32[2,4]{1,0:T(2,128)}, u32[]{:S(2)}) %copy-start.2) | copy-done | bytes 56
  12.8 0.1 select_reduce_fusion
  12.9 0.1 sub.51
  13.0 0.9 %multiply_reduce_fusion.1 = f32[2,128]{1,0:T(2,128)S(1)} fusion(f32[2,128,512]{2,1,0:T(8,128)} %param.6, s32[]{:T(128)S(6)} %select_n.239), kind=kLoop, calls=%fused_computation.9 | loop fusion | flops 65280 | bytes 132100 | tf_op jit(solution)/shard_map/reduce_sum | solution.py:75
  13.9 0.8 %collective-permute-done = f32[2,32,512]{2,1,0:T(8,128)S(1)} collective-permute-done((f32[2,32,512]{2,1,0:T(8,128)S(1)}, f32[2,32,512]{2,1,0:T(8,128)S(1)}, u32[]{:S(2)}, u32[]{:S(2)}) %collective-permute-start) | collective-permute-done | bytes 131104 | tf_op jit(solution)/shard_map/ppermute | solution.py:42
  14.7 1.5 %collective-permute-done.1 = f32[2,32,512]{2,1,0:T(8,128)S(1)} collective-permute-done((f32[2,32,512]{2,1,0:T(8,128)S(1)}, f32[2,32,512]{2,1,0:T(8,128)S(1)}, u32[]{:S(2)}, u32[]{:S(2)}) %collective-permute-start.1) | collective-permute-done | bytes 131104 | tf_op jit(solution)/shard_map/ppermute | solution.py:42
  16.2 0.1 collective-permute-done.2
  16.4 0.0 copy-start.1
  16.4 0.1 collective-permute-start.3
  16.5 2.2 %collective-permute-start.4 = (f32[2,32,128]{2,1,0:T(8,128)S(1)}, f32[2,32,128]{2,1,0:T(8,128)S(1)}, u32[]{:S(2)}, u32[]{:S(2)}) collective-permute-start(f32[2,32,128]{2,1,0:T(8,128)S(1)} %get-tuple-element.35), channel_id=1, source_target_pairs={{0,4},{2,6},{4,0},{6,2},{1,5},{3,7},{5,1},{7,3},{8,12},{10,14},{12... | collective-permute-start | bytes 98312 | tf_op jit(solution)/shard_map/ppermute | solution.py:42
  18.7 1.6 %collective-permute-start.5 = (f32[2,32,128]{2,1,0:T(8,128)S(1)}, f32[2,32,128]{2,1,0:T(8,128)S(1)}, u32[]{:S(2)}, u32[]{:S(2)}) collective-permute-start(f32[2,32,128]{2,1,0:T(8,128)S(1)} %get-tuple-element.34), channel_id=1, source_target_pairs={{0,6},{2,0},{4,2},{6,4},{1,7},{3,1},{5,3},{7,5},{8,14},{10,8},{12,... | collective-permute-start | bytes 98312 | tf_op jit(solution)/shard_map/ppermute | solution.py:42
  20.3 1.9 %collective-permute-done.3 = f32[2,32,128]{2,1,0:T(8,128)S(1)} collective-permute-done((f32[2,32,128]{2,1,0:T(8,128)S(1)}, f32[2,32,128]{2,1,0:T(8,128)S(1)}, u32[]{:S(2)}, u32[]{:S(2)}) %collective-permute-start.3) | collective-permute-done | bytes 32800 | tf_op jit(solution)/shard_map/ppermute | solution.py:42
  22.2 0.5 collective-permute-done.5
  22.8 0.0 collective-permute-done.6.refs_1_
  22.8 2.0 %collective-permute-start.7 = (f32[2,256,128]{2,1,0:T(8,128)S(1)}, f32[2,256,128]{2,1,0:T(8,128)S(1)}, u32[]{:S(2)}, u32[]{:S(2)}) collective-permute-start(f32[2,256,128]{2,1,0:T(8,128)S(1)} %collective-permute-done.6.refs_1_), channel_id=1, source_target_pairs={{0,2},{2,4},{4,6},{6,0},{1,3},{3,5},{5,7},{7,1},{8,10},{10,12},{12... | collective-permute-start | bytes 786440 | tf_op jit(solution)/shard_map/ppermute | solution.py:42
  24.8 1.4 %collective-permute-start.10 = (f32[4,2,32,128]{3,2,1,0:T(8,128)S(1)}, f32[4,2,32,128]{3,2,1,0:T(8,128)S(1)}, u32[]{:S(2)}, u32[]{:S(2)}) collective-permute-start(f32[4,2,32,128]{3,2,1,0:T(8,128)S(1)} %pad_maximum_fusion.2.refs_4_), channel_id=1, source_target_pairs={{0,16},{8,24},{16,0},{24,8},{1,17},{9,25},{17,1},{25,9},{2,18},{10... | collective-permute-start | bytes 393224 | tf_op jit(solution)/shard_map/ppermute | solution.py:42
  26.3 4.4 %collective-permute-start.11 = (f32[4,2,32,128]{3,2,1,0:T(8,128)S(1)}, f32[4,2,32,128]{3,2,1,0:T(8,128)S(1)}, u32[]{:S(2)}, u32[]{:S(2)}) collective-permute-start(f32[4,2,32,128]{3,2,1,0:T(8,128)S(1)} %pad_maximum_fusion.2.refs_4_), channel_id=1, source_target_pairs={{0,24},{8,0},{16,8},{24,16},{1,25},{9,1},{17,9},{25,17},{2,26},{10... | collective-permute-start | bytes 393224 | tf_op jit(solution)/shard_map/ppermute | solution.py:42
  30.7 0.1 pad_add_fusion.place
  30.8 0.3 collective-permute-done.10.refs_6_
  31.1 2.1 %collective-permute-done.11.refs_7_ = f32[4,2,32,128]{3,2,1,0:T(8,128)S(1)} collective-permute-done((f32[4,2,32,128]{3,2,1,0:T(8,128)S(1)}, f32[4,2,32,128]{3,2,1,0:T(8,128)S(1)}, u32[]{:S(2)}, u32[]{:S(2)}) %collective-permute-start.11) | collective-permute-done | bytes 131104 | tf_op jit(solution)/shard_map/ppermute | solution.py:42
  33.2 3.3 %collective-permute-done.9.refs_5_ = f32[4,2,32,128]{3,2,1,0:T(8,128)S(1)} collective-permute-done((f32[4,2,32,128]{3,2,1,0:T(8,128)S(1)}, f32[4,2,32,128]{3,2,1,0:T(8,128)S(1)}, u32[]{:S(2)}, u32[]{:S(2)}) %collective-permute-start.9) | collective-permute-done | bytes 131104 | tf_op jit(solution)/shard_map/ppermute | solution.py:42
  36.5 1.6 %shard_map.59 = f32[2,384,128]{2,1,0:T(8,128)S(1)} custom-call(s32[13]{0:T(128)S(1)} %pad_add_fusion.place, f32[2,256,128]{2,1,0:T(8,128)S(1)} %copy-done.1, f32[2,256,128]{2,1,0:T(8,128)S(1)} %collective-permute-done.6.refs_1_, f32[2,256,128]{2,1,0:T(8,128)S(1)} %collective-permute-done.7.refs_2_, f32[2,256,128]{2,1,0:T(8,128)S(1)} %collective-permute-done.8.refs_3_, ...), custom_call_target="tpu_custom_call" | custom-call | tf_op jit(solution)/shard_map/pallas_call | solution.py:102
  38.1 0.1 collective-permute-start.12
  38.3 0.1 pad.15.clone
  38.3 1.6 %collective-permute-done.12 = f32[2,384,128]{2,1,0:T(8,128)S(1)} collective-permute-done((f32[2,384,128]{2,1,0:T(8,128)S(1)}, f32[2,384,128]{2,1,0:T(8,128)S(1)}, u32[]{:S(2)}, u32[]{:S(2)}) %collective-permute-start.12) | collective-permute-done | bytes 393248 | tf_op jit(solution)/shard_map/ppermute | solution.py:42
  40.0 0.1 multiply_reduce_fusion
  40.1 0.1 fusion.4
  40.2 0.1 collective-permute-start.13
  40.3 1.5 %collective-permute-start.14 = (f32[72,128]{1,0:T(8,128)S(1)}, f32[72,128]{1,0:T(8,128)S(1)}, u32[]{:S(2)}, u32[]{:S(2)}) collective-permute-start(f32[72,128]{1,0:T(8,128)S(1)} %get-tuple-element.39), channel_id=1, source_target_pairs={{0,4},{2,6},{4,0},{6,2},{1,5},{3,7},{5,1},{7,3},{8,12},{10,14},{12... | collective-permute-start | bytes 110600 | tf_op jit(solution)/shard_map/ppermute | solution.py:42
  41.7 0.6 %collective-permute-start.15 = (f32[72,128]{1,0:T(8,128)S(1)}, f32[72,128]{1,0:T(8,128)S(1)}, u32[]{:S(2)}, u32[]{:S(2)}) collective-permute-start(f32[72,128]{1,0:T(8,128)S(1)} %get-tuple-element.38), channel_id=1, source_target_pairs={{0,2},{2,4},{4,6},{6,0},{1,3},{3,5},{5,7},{7,1},{8,10},{10,12},{12... | collective-permute-start | bytes 110600 | tf_op jit(solution)/shard_map/ppermute | solution.py:42
  42.3 2.3 %collective-permute-done.13 = f32[72,128]{1,0:T(8,128)S(1)} collective-permute-done((f32[72,128]{1,0:T(8,128)S(1)}, f32[72,128]{1,0:T(8,128)S(1)}, u32[]{:S(2)}, u32[]{:S(2)}) %collective-permute-start.13) | collective-permute-done | bytes 36896 | tf_op jit(solution)/shard_map/ppermute | solution.py:42
  44.6 1.0 %collective-permute-done.14 = f32[72,128]{1,0:T(8,128)S(1)} collective-permute-done((f32[72,128]{1,0:T(8,128)S(1)}, f32[72,128]{1,0:T(8,128)S(1)}, u32[]{:S(2)}, u32[]{:S(2)}) %collective-permute-start.14) | collective-permute-done | bytes 36896 | tf_op jit(solution)/shard_map/ppermute | solution.py:42
  45.6 1.9 %collective-permute-done.15 = f32[72,128]{1,0:T(8,128)S(1)} collective-permute-done((f32[72,128]{1,0:T(8,128)S(1)}, f32[72,128]{1,0:T(8,128)S(1)}, u32[]{:S(2)}, u32[]{:S(2)}) %collective-permute-start.15) | collective-permute-done | bytes 36896 | tf_op jit(solution)/shard_map/ppermute | solution.py:42
  47.5 0.1 select_select_fusion.2
  47.6 0.1 select_select_fusion.3
  47.7 0.6 %collective-permute-start.16 = (f32[2,512]{1,0:T(2,128)S(1)}, f32[2,512]{1,0:T(2,128)S(1)}, u32[]{:S(2)}, u32[]{:S(2)}) collective-permute-start(f32[2,512]{1,0:T(2,128)S(1)} %pad_maximum_fusion.7), channel_id=1, source_target_pairs={{0,8},{8,0},{16,24},{24,16},{1,9},{9,1},{17,25},{25,17},{2,10},{10... | collective-permute-start | bytes 12296 | tf_op jit(solution)/shard_map/ppermute | solution.py:133
  48.3 3.1 %collective-permute-done.16 = f32[2,512]{1,0:T(2,128)S(1)} collective-permute-done((f32[2,512]{1,0:T(2,128)S(1)}, f32[2,512]{1,0:T(2,128)S(1)}, u32[]{:S(2)}, u32[]{:S(2)}) %collective-permute-start.16) | collective-permute-done | bytes 4128 | tf_op jit(solution)/shard_map/ppermute | solution.py:133
  51.4 0.9 %collective-permute-start.17 = (f32[2,512]{1,0:T(2,128)S(1)}, f32[2,512]{1,0:T(2,128)S(1)}, u32[]{:S(2)}, u32[]{:S(2)}) collective-permute-start(f32[2,512]{1,0:T(2,128)S(1)} %add.208), channel_id=1, source_target_pairs={{0,16},{8,24},{16,0},{24,8},{1,17},{9,25},{17,1},{25,9},{2,18},{10... | collective-permute-start | bytes 12296 | tf_op jit(solution)/shard_map/ppermute | solution.py:133
  52.3 0.7 %slice_negate_fusion = f32[64,512]{1,0:T(8,128)} fusion(f32[72,512]{1,0:T(8,128)S(1)} %pad_maximum_fusion.1), kind=kLoop, calls=%fused_computation.4 | loop fusion | flops 32768 | bytes 262144 | tf_op jit(solution)/shard_map/neg | solution.py:129
  53.0 2.0 %collective-permute-done.17 = f32[2,512]{1,0:T(2,128)S(1)} collective-permute-done((f32[2,512]{1,0:T(2,128)S(1)}, f32[2,512]{1,0:T(2,128)S(1)}, u32[]{:S(2)}, u32[]{:S(2)}) %collective-permute-start.17) | collective-permute-done | bytes 4128 | tf_op jit(solution)/shard_map/ppermute | solution.py:133
  55.0 0.6 %add.209 = f32[2,512]{1,0:T(2,128)} add(f32[2,512]{1,0:T(2,128)S(1)} %add.208, f32[2,512]{1,0:T(2,128)S(1)} %collective-permute-done.17) | non-fusion elementwise | flops 1024 | bytes 12288 | tf_op jit(solution)/shard_map/add | solution.py:133
  (24 shorter events, 0.3 us)
Async XLA Ops:
  0.6 5.2 %copy-start = (f32[2,128,512]{2,1,0:T(8,128)S(1)}, f32[2,128,512]{2,1,0:T(8,128)}, u32[]{:S(2)}) copy-start(f32[2,128,512]{2,1,0:T(8,128)} %param.5) | copy-start | bytes 1572868
  0.6 22.1 %collective-permute-start.6 = (f32[2,256,128]{2,1,0:T(8,128)}, f32[2,256,128]{2,1,0:T(8,128)S(1)}, u32[]{:S(2)}, u32[]{:S(2)}) collective-permute-start(f32[2,256,128]{2,1,0:T(8,128)} %refs_0_.1), channel_id=1, source_target_pairs={{0,2},{2,4},{4,6},{6,0},{1,3},{3,5},{5,7},{7,1},{8,10},{10,12},{12... | collective-permute-start | bytes 786440 | tf_op jit(solution)/shard_map/ppermute | solution.py:42
  3.7 27.0 %collective-permute-start.8 = (f32[2,256,128]{2,1,0:T(8,128)}, f32[2,256,128]{2,1,0:T(8,128)S(1)}, u32[]{:S(2)}, u32[]{:S(2)}) collective-permute-start(f32[2,256,128]{2,1,0:T(8,128)} %refs_0_.1), channel_id=1, source_target_pairs={{0,6},{2,0},{4,2},{6,4},{1,7},{3,1},{5,3},{7,5},{8,14},{10,8},{12,... | collective-permute-start | bytes 786440 | tf_op jit(solution)/shard_map/ppermute | solution.py:42
  7.5 7.2 %collective-permute-start = (f32[2,32,512]{2,1,0:T(8,128)S(1)}, f32[2,32,512]{2,1,0:T(8,128)S(1)}, u32[]{:S(2)}, u32[]{:S(2)}) collective-permute-start(f32[2,32,512]{2,1,0:T(8,128)S(1)} %get-tuple-element.26), channel_id=1, source_target_pairs={{0,8},{8,16},{16,24},{24,0},{1,9},{9,17},{17,25},{25,1},{2,10},{10... | collective-permute-start | bytes 393224 | tf_op jit(solution)/shard_map/ppermute | solution.py:42
  9.2 7.0 %collective-permute-start.1 = (f32[2,32,512]{2,1,0:T(8,128)S(1)}, f32[2,32,512]{2,1,0:T(8,128)S(1)}, u32[]{:S(2)}, u32[]{:S(2)}) collective-permute-start(f32[2,32,512]{2,1,0:T(8,128)S(1)} %get-tuple-element.25), channel_id=1, source_target_pairs={{0,16},{8,24},{16,0},{24,8},{1,17},{9,25},{17,1},{25,9},{2,18},{10... | collective-permute-start | bytes 393224 | tf_op jit(solution)/shard_map/ppermute | solution.py:42
  10.7 5.6 %collective-permute-start.2 = (f32[2,32,512]{2,1,0:T(8,128)S(1)}, f32[2,32,512]{2,1,0:T(8,128)S(1)}, u32[]{:S(2)}, u32[]{:S(2)}) collective-permute-start(f32[2,32,512]{2,1,0:T(8,128)S(1)} %get-tuple-element.24), channel_id=1, source_target_pairs={{0,24},{8,0},{16,8},{24,16},{1,25},{9,1},{17,9},{25,17},{2,26},{10... | collective-permute-start | bytes 393224 | tf_op jit(solution)/shard_map/ppermute | solution.py:42
  12.1 0.7 %copy-start.2 = (s32[2,4]{1,0:T(2,128)S(1)}, s32[2,4]{1,0:T(2,128)}, u32[]{:S(2)}) copy-start(s32[2,4]{1,0:T(2,128)} %param.7) | copy-start | bytes 100
  16.4 20.1 %copy-start.1 = (f32[2,256,128]{2,1,0:T(8,128)S(1)}, f32[2,256,128]{2,1,0:T(8,128)}, u32[]{:S(2)}) copy-start(f32[2,256,128]{2,1,0:T(8,128)} %refs_0_.1) | copy-start | bytes 786436
  16.4 5.8 %collective-permute-start.3 = (f32[2,32,128]{2,1,0:T(8,128)S(1)}, f32[2,32,128]{2,1,0:T(8,128)S(1)}, u32[]{:S(2)}, u32[]{:S(2)}) collective-permute-start(f32[2,32,128]{2,1,0:T(8,128)S(1)} %get-tuple-element.36), channel_id=1, source_target_pairs={{0,2},{2,4},{4,6},{6,0},{1,3},{3,5},{5,7},{7,1},{8,10},{10,12},{12... | collective-permute-start | bytes 98312 | tf_op jit(solution)/shard_map/ppermute | solution.py:42
  16.5 5.7 %collective-permute-start.4 = (f32[2,32,128]{2,1,0:T(8,128)S(1)}, f32[2,32,128]{2,1,0:T(8,128)S(1)}, u32[]{:S(2)}, u32[]{:S(2)}) collective-permute-start(f32[2,32,128]{2,1,0:T(8,128)S(1)} %get-tuple-element.35), channel_id=1, source_target_pairs={{0,4},{2,6},{4,0},{6,2},{1,5},{3,7},{5,1},{7,3},{8,12},{10,14},{12... | collective-permute-start | bytes 98312 | tf_op jit(solution)/shard_map/ppermute | solution.py:42
  18.7 4.0 %collective-permute-start.5 = (f32[2,32,128]{2,1,0:T(8,128)S(1)}, f32[2,32,128]{2,1,0:T(8,128)S(1)}, u32[]{:S(2)}, u32[]{:S(2)}) collective-permute-start(f32[2,32,128]{2,1,0:T(8,128)S(1)} %get-tuple-element.34), channel_id=1, source_target_pairs={{0,6},{2,0},{4,2},{6,4},{1,7},{3,1},{5,3},{7,5},{8,14},{10,8},{12,... | collective-permute-start | bytes 98312 | tf_op jit(solution)/shard_map/ppermute | solution.py:42
  22.8 13.7 %collective-permute-start.7 = (f32[2,256,128]{2,1,0:T(8,128)S(1)}, f32[2,256,128]{2,1,0:T(8,128)S(1)}, u32[]{:S(2)}, u32[]{:S(2)}) collective-permute-start(f32[2,256,128]{2,1,0:T(8,128)S(1)} %collective-permute-done.6.refs_1_), channel_id=1, source_target_pairs={{0,2},{2,4},{4,6},{6,0},{1,3},{3,5},{5,7},{7,1},{8,10},{10,12},{12... | collective-permute-start | bytes 786440 | tf_op jit(solution)/shard_map/ppermute | solution.py:42
  24.8 6.3 %collective-permute-start.10 = (f32[4,2,32,128]{3,2,1,0:T(8,128)S(1)}, f32[4,2,32,128]{3,2,1,0:T(8,128)S(1)}, u32[]{:S(2)}, u32[]{:S(2)}) collective-permute-start(f32[4,2,32,128]{3,2,1,0:T(8,128)S(1)} %pad_maximum_fusion.2.refs_4_), channel_id=1, source_target_pairs={{0,16},{8,24},{16,0},{24,8},{1,17},{9,25},{17,1},{25,9},{2,18},{10... | collective-permute-start | bytes 393224 | tf_op jit(solution)/shard_map/ppermute | solution.py:42
  26.3 6.9 %collective-permute-start.11 = (f32[4,2,32,128]{3,2,1,0:T(8,128)S(1)}, f32[4,2,32,128]{3,2,1,0:T(8,128)S(1)}, u32[]{:S(2)}, u32[]{:S(2)}) collective-permute-start(f32[4,2,32,128]{3,2,1,0:T(8,128)S(1)} %pad_maximum_fusion.2.refs_4_), channel_id=1, source_target_pairs={{0,24},{8,0},{16,8},{24,16},{1,25},{9,1},{17,9},{25,17},{2,26},{10... | collective-permute-start | bytes 393224 | tf_op jit(solution)/shard_map/ppermute | solution.py:42
  30.7 5.9 %collective-permute-start.9 = (f32[4,2,32,128]{3,2,1,0:T(8,128)S(1)}, f32[4,2,32,128]{3,2,1,0:T(8,128)S(1)}, u32[]{:S(2)}, u32[]{:S(2)}) collective-permute-start(f32[4,2,32,128]{3,2,1,0:T(8,128)S(1)} %pad_maximum_fusion.2.refs_4_), channel_id=1, source_target_pairs={{0,8},{8,16},{16,24},{24,0},{1,9},{9,17},{17,25},{25,1},{2,10},{10... | collective-permute-start | bytes 393224 | tf_op jit(solution)/shard_map/ppermute | solution.py:42
  38.1 1.8 %collective-permute-start.12 = (f32[2,384,128]{2,1,0:T(8,128)S(1)}, f32[2,384,128]{2,1,0:T(8,128)S(1)}, u32[]{:S(2)}, u32[]{:S(2)}) collective-permute-start(f32[2,384,128]{2,1,0:T(8,128)S(1)} %shard_map.59), channel_id=1, source_target_pairs={{0,1},{1,0},{2,3},{3,2},{4,5},{5,4},{6,7},{7,6},{8,9},{9,8},{10,11... | collective-permute-start | bytes 1179656 | tf_op jit(solution)/shard_map/ppermute | solution.py:42
  40.2 4.4 %collective-permute-start.13 = (f32[72,128]{1,0:T(8,128)S(1)}, f32[72,128]{1,0:T(8,128)S(1)}, u32[]{:S(2)}, u32[]{:S(2)}) collective-permute-start(f32[72,128]{1,0:T(8,128)S(1)} %get-tuple-element.40), channel_id=1, source_target_pairs={{0,6},{2,0},{4,2},{6,4},{1,7},{3,1},{5,3},{7,5},{8,14},{10,8},{12,... | collective-permute-start | bytes 110600 | tf_op jit(solution)/shard_map/ppermute | solution.py:42
  40.3 5.3 %collective-permute-start.14 = (f32[72,128]{1,0:T(8,128)S(1)}, f32[72,128]{1,0:T(8,128)S(1)}, u32[]{:S(2)}, u32[]{:S(2)}) collective-permute-start(f32[72,128]{1,0:T(8,128)S(1)} %get-tuple-element.39), channel_id=1, source_target_pairs={{0,4},{2,6},{4,0},{6,2},{1,5},{3,7},{5,1},{7,3},{8,12},{10,14},{12... | collective-permute-start | bytes 110600 | tf_op jit(solution)/shard_map/ppermute | solution.py:42
  41.7 5.8 %collective-permute-start.15 = (f32[72,128]{1,0:T(8,128)S(1)}, f32[72,128]{1,0:T(8,128)S(1)}, u32[]{:S(2)}, u32[]{:S(2)}) collective-permute-start(f32[72,128]{1,0:T(8,128)S(1)} %get-tuple-element.38), channel_id=1, source_target_pairs={{0,2},{2,4},{4,6},{6,0},{1,3},{3,5},{5,7},{7,1},{8,10},{10,12},{12... | collective-permute-start | bytes 110600 | tf_op jit(solution)/shard_map/ppermute | solution.py:42
  47.7 3.7 %collective-permute-start.16 = (f32[2,512]{1,0:T(2,128)S(1)}, f32[2,512]{1,0:T(2,128)S(1)}, u32[]{:S(2)}, u32[]{:S(2)}) collective-permute-start(f32[2,512]{1,0:T(2,128)S(1)} %pad_maximum_fusion.7), channel_id=1, source_target_pairs={{0,8},{8,0},{16,24},{24,16},{1,9},{9,1},{17,25},{25,17},{2,10},{10... | collective-permute-start | bytes 12296 | tf_op jit(solution)/shard_map/ppermute | solution.py:133
  51.4 3.6 %collective-permute-start.17 = (f32[2,512]{1,0:T(2,128)S(1)}, f32[2,512]{1,0:T(2,128)S(1)}, u32[]{:S(2)}, u32[]{:S(2)}) collective-permute-start(f32[2,512]{1,0:T(2,128)S(1)} %add.208), channel_id=1, source_target_pairs={{0,16},{8,24},{16,0},{24,8},{1,17},{9,25},{17,1},{25,9},{2,18},{10... | collective-permute-start | bytes 12296 | tf_op jit(solution)/shard_map/ppermute | solution.py:133

commit v16 on v15

--- a/solution.py
+++ b/solution.py
@@ -73,7 +73,7 @@
 
         sums = [shifted(rows_of((row + d) % rows), "row", rows, d) for d in range(1, rows)]
         squares = jnp.sum(lax.dynamic_slice_in_dim(factor_inv, z * part, part, axis=2) ** 2, axis=1)
-        sums, squares = lax.optimization_barrier((sums, squares))
+        sums, squares, far = lax.optimization_barrier((sums, squares, far))
         scaled = sum(sums, rows_of(row))
 
         def columns_of(array, c):
@@ -128,10 +128,9 @@
         moved = jnp.concatenate([picked(moved, z, c) for c in range(deep)], axis=1)
         column_block = -moved[: groups * out_rows].reshape(groups, out_rows, width)
         total = moved[groups * out_rows : groups * out_rows + groups]
-        step = 1
-        while step < rows:
-            total = total + lax.ppermute(total, "row", [(r, r ^ step) for r in range(rows)])
-            step *= 2
+        local = total
+        for shift in range(1, rows):
+            total = total + shifted(local, "row", rows, shift)
         return column_block, total
 
     col = ("z", "core")

time: 55.8 us -> 53.5 us (0.959)
  waiting for transfers between devices: 22.5 us -> 17.6 us
  starting transfers between devices: 25.2 us -> 27.8 us
    ppermute x2 -> x0, waiting for transfers between devices: 5.08 us -> none  [per_device(): lax.ppermute(total, 'row', [(r, r ^ step) for r in range(rows)])]
    ppermute x16 -> x19, starting transfers between devices: 23.7 us -> 27.8 us  [shifted(): lax.ppermute(array, axis, [(i, (i + shift) % size) for i in range(size)])]
    ppermute x2 -> x0, starting transfers between devices: 1.52 us -> none  [per_device(): lax.ppermute(total, 'row', [(r, r ^ step) for r in range(rows)])]
    ppermute x16 -> x19, waiting for transfers between devices: 17.4 us -> 17.6 us  [shifted(): lax.ppermute(array, axis, [(i, (i + shift) % size) for i in range(size)])]
  transfers between devices with their start and end apart: 18 -> 19, of which waited for: 14 -> 14; matrix products, arithmetic and copies ran while one was open for 7% -> 7% of each run, Pallas kernels for 0% -> 0%
where the time goes in v16:
time: 53.5 us; the launch traced here: 53.3 us
  starting transfers between devices  27.8 us (52%)
  waiting for transfers between devices  17.6 us (33%)
  other arithmetic  2.83 us (5%)
  matrix products  1.61 us (3%)
  Pallas kernels  1.61 us (3%)
  local copies, waits for them, and re-layouts  0.95 us (2%)
  between operations  0.87 us (2%)
    ppermute x19, starting transfers between devices, shifted(): lax.ppermute(array, axis, [(i, (i + shift) % size) for i in range(size)])  27.8 us
    ppermute x19, waiting for transfers between devices, shifted(): lax.ppermute(array, axis, [(i, (i + shift) % size) for i in range(size)])  17.6 us
    dot_general x1, matrix products, per_device(): partial = jnp.einsum('srw,swv->srv', mine, factor_inv, precision=highest)  1.61 us
    pallas_call x1, Pallas kernels, per_device(): pl.pallas_call(functools.partial(multiply_tiles, deep, rows), out_shape=j...  1.61 us
  transfers between devices with their start and end apart: 19, of which 14 were waited for; matrix products, arithmetic and copies ran while one was open for 7% of the time, Pallas kernels for 0%

profile of v16, /device:TPU:0, one launch (start us, length us, event | category | flops | bytes accessed | tf_op | source)
XLA Modules:
  0.0 53.3 jit_solution(3761679682143579477)
XLA Ops:
  0.6 0.0 copy-start
  0.6 3.1 %collective-permute-start.3 = (f32[2,256,128]{2,1,0:T(8,128)}, f32[2,256,128]{2,1,0:T(8,128)S(1)}, u32[]{:S(2)}, u32[]{:S(2)}) collective-permute-start(f32[2,256,128]{2,1,0:T(8,128)} %refs_0_.1), channel_id=1, source_target_pairs={{0,2},{2,4},{4,6},{6,0},{1,3},{3,5},{5,7},{7,1},{8,10},{10,12},{12... | collective-permute-start | bytes 786440 | tf_op jit(solution)/shard_map/ppermute | solution.py:42
  3.7 2.1 %collective-permute-start.4 = (f32[2,256,128]{2,1,0:T(8,128)}, f32[2,256,128]{2,1,0:T(8,128)S(1)}, u32[]{:S(2)}, u32[]{:S(2)}) collective-permute-start(f32[2,256,128]{2,1,0:T(8,128)} %refs_0_.1), channel_id=1, source_target_pairs={{0,6},{2,0},{4,2},{6,4},{1,7},{3,1},{5,3},{7,5},{8,14},{10,8},{12,... | collective-permute-start | bytes 786440 | tf_op jit(solution)/shard_map/ppermute | solution.py:42
  5.8 1.6 %fusion = f32[2,128,512]{2,1,0:T(8,128)S(1)} fusion(f32[2,128,512]{2,1,0:T(8,128)} %param.6, f32[2,128,512]{2,1,0:T(8,128)S(1)} %copy-done, s32[]{:T(128)S(6)} %select_n.231), kind=kOutput, calls=%fused_computation.10 | convolution fusion | flops 201326592 | bytes 1179652 | tf_op jit(solution)/shard_map/srw,swv->srv/dot_general | solution.py:69
  7.5 1.7 %collective-permute-start = (f32[2,32,512]{2,1,0:T(8,128)S(1)}, f32[2,32,512]{2,1,0:T(8,128)S(1)}, u32[]{:S(2)}, u32[]{:S(2)}) collective-permute-start(f32[2,32,512]{2,1,0:T(8,128)S(1)} %get-tuple-element.30), channel_id=1, source_target_pairs={{0,8},{8,16},{16,24},{24,0},{1,9},{9,17},{17,25},{25,1},{2,10},{10... | collective-permute-start | bytes 393224 | tf_op jit(solution)/shard_map/ppermute | solution.py:42
  9.2 1.5 %collective-permute-start.1 = (f32[2,32,512]{2,1,0:T(8,128)S(1)}, f32[2,32,512]{2,1,0:T(8,128)S(1)}, u32[]{:S(2)}, u32[]{:S(2)}) collective-permute-start(f32[2,32,512]{2,1,0:T(8,128)S(1)} %get-tuple-element.29), channel_id=1, source_target_pairs={{0,16},{8,24},{16,0},{24,8},{1,17},{9,25},{17,1},{25,9},{2,18},{10... | collective-permute-start | bytes 393224 | tf_op jit(solution)/shard_map/ppermute | solution.py:42
  10.7 1.4 %collective-permute-start.2 = (f32[2,32,512]{2,1,0:T(8,128)S(1)}, f32[2,32,512]{2,1,0:T(8,128)S(1)}, u32[]{:S(2)}, u32[]{:S(2)}) collective-permute-start(f32[2,32,512]{2,1,0:T(8,128)S(1)} %get-tuple-element.28), channel_id=1, source_target_pairs={{0,24},{8,0},{16,8},{24,16},{1,25},{9,1},{17,9},{25,17},{2,26},{10... | collective-permute-start | bytes 393224 | tf_op jit(solution)/shard_map/ppermute | solution.py:42
  12.1 0.7 %copy-done.2 = s32[2,4]{1,0:T(2,128)S(1)} copy-done((s32[2,4]{1,0:T(2,128)S(1)}, s32[2,4]{1,0:T(2,128)}, u32[]{:S(2)}) %copy-start.2) | copy-done | bytes 56
  12.8 0.1 select_reduce_fusion
  13.0 0.1 sub.51
  13.0 0.9 %multiply_reduce_fusion.1 = f32[2,128]{1,0:T(2,128)S(1)} fusion(f32[2,128,512]{2,1,0:T(8,128)} %param.6, s32[]{:T(128)S(6)} %select_n.239), kind=kLoop, calls=%fused_computation.9 | loop fusion | flops 65280 | bytes 132100 | tf_op jit(solution)/shard_map/reduce_sum | solution.py:75
  14.0 0.7 %collective-permute-done = f32[2,32,512]{2,1,0:T(8,128)S(1)} collective-permute-done((f32[2,32,512]{2,1,0:T(8,128)S(1)}, f32[2,32,512]{2,1,0:T(8,128)S(1)}, u32[]{:S(2)}, u32[]{:S(2)}) %collective-permute-start) | collective-permute-done | bytes 131104 | tf_op jit(solution)/shard_map/ppermute | solution.py:42
  14.7 1.5 %collective-permute-done.1 = f32[2,32,512]{2,1,0:T(8,128)S(1)} collective-permute-done((f32[2,32,512]{2,1,0:T(8,128)S(1)}, f32[2,32,512]{2,1,0:T(8,128)S(1)}, u32[]{:S(2)}, u32[]{:S(2)}) %collective-permute-start.1) | collective-permute-done | bytes 131104 | tf_op jit(solution)/shard_map/ppermute | solution.py:42
  16.2 0.1 collective-permute-done.2
  16.4 1.0 %collective-permute-done.4.refs_3_ = f32[2,256,128]{2,1,0:T(8,128)S(1)} collective-permute-done((f32[2,256,128]{2,1,0:T(8,128)}, f32[2,256,128]{2,1,0:T(8,128)S(1)}, u32[]{:S(2)}, u32[]{:S(2)}) %collective-permute-start.4) | collective-permute-done | bytes 262176 | tf_op jit(solution)/shard_map/ppermute | solution.py:42
  17.4 0.0 copy-start.1
  17.4 1.2 %collective-permute-start.5 = (f32[2,32,128]{2,1,0:T(8,128)S(1)}, f32[2,32,128]{2,1,0:T(8,128)S(1)}, u32[]{:S(2)}, u32[]{:S(2)}) collective-permute-start(f32[2,32,128]{2,1,0:T(8,128)S(1)} %get-tuple-element.40), channel_id=1, source_target_pairs={{0,2},{2,4},{4,6},{6,0},{1,3},{3,5},{5,7},{7,1},{8,10},{10,12},{12... | collective-permute-start | bytes 98312 | tf_op jit(solution)/shard_map/ppermute | solution.py:42
  18.6 1.7 %collective-permute-start.6 = (f32[2,32,128]{2,1,0:T(8,128)S(1)}, f32[2,32,128]{2,1,0:T(8,128)S(1)}, u32[]{:S(2)}, u32[]{:S(2)}) collective-permute-start(f32[2,32,128]{2,1,0:T(8,128)S(1)} %get-tuple-element.39), channel_id=1, source_target_pairs={{0,4},{2,6},{4,0},{6,2},{1,5},{3,7},{5,1},{7,3},{8,12},{10,14},{12... | collective-permute-start | bytes 98312 | tf_op jit(solution)/shard_map/ppermute | solution.py:42
  20.3 1.3 %collective-permute-start.7 = (f32[2,32,128]{2,1,0:T(8,128)S(1)}, f32[2,32,128]{2,1,0:T(8,128)S(1)}, u32[]{:S(2)}, u32[]{:S(2)}) collective-permute-start(f32[2,32,128]{2,1,0:T(8,128)S(1)} %get-tuple-element.38), channel_id=1, source_target_pairs={{0,6},{2,0},{4,2},{6,4},{1,7},{3,1},{5,3},{7,5},{8,14},{10,8},{12,... | collective-permute-start | bytes 98312 | tf_op jit(solution)/shard_map/ppermute | solution.py:42
  21.7 1.6 %collective-permute-done.5 = f32[2,32,128]{2,1,0:T(8,128)S(1)} collective-permute-done((f32[2,32,128]{2,1,0:T(8,128)S(1)}, f32[2,32,128]{2,1,0:T(8,128)S(1)}, u32[]{:S(2)}, u32[]{:S(2)}) %collective-permute-start.5) | collective-permute-done | bytes 32800 | tf_op jit(solution)/shard_map/ppermute | solution.py:42
  23.3 0.9 %collective-permute-done.6 = f32[2,32,128]{2,1,0:T(8,128)S(1)} collective-permute-done((f32[2,32,128]{2,1,0:T(8,128)S(1)}, f32[2,32,128]{2,1,0:T(8,128)S(1)}, u32[]{:S(2)}, u32[]{:S(2)}) %collective-permute-start.6) | collective-permute-done | bytes 32800 | tf_op jit(solution)/shard_map/ppermute | solution.py:42
  24.2 0.2 collective-permute-done.7
  24.5 1.3 %collective-permute-start.8 = (f32[2,256,128]{2,1,0:T(8,128)S(1)}, f32[2,256,128]{2,1,0:T(8,128)S(1)}, u32[]{:S(2)}, u32[]{:S(2)}) collective-permute-start(f32[2,256,128]{2,1,0:T(8,128)S(1)} %collective-permute-done.3.refs_1_), channel_id=1, source_target_pairs={{0,2},{2,4},{4,6},{6,0},{1,3},{3,5},{5,7},{7,1},{8,10},{10,12},{12... | collective-permute-start | bytes 786440 | tf_op jit(solution)/shard_map/ppermute | solution.py:42
  25.8 1.6 %collective-permute-start.10 = (f32[4,2,32,128]{3,2,1,0:T(8,128)S(1)}, f32[4,2,32,128]{3,2,1,0:T(8,128)S(1)}, u32[]{:S(2)}, u32[]{:S(2)}) collective-permute-start(f32[4,2,32,128]{3,2,1,0:T(8,128)S(1)} %pad_maximum_fusion.2.refs_4_), channel_id=1, source_target_pairs={{0,16},{8,24},{16,0},{24,8},{1,17},{9,25},{17,1},{25,9},{2,18},{10... | collective-permute-start | bytes 393224 | tf_op jit(solution)/shard_map/ppermute | solution.py:42
  27.4 1.4 %collective-permute-start.11 = (f32[4,2,32,128]{3,2,1,0:T(8,128)S(1)}, f32[4,2,32,128]{3,2,1,0:T(8,128)S(1)}, u32[]{:S(2)}, u32[]{:S(2)}) collective-permute-start(f32[4,2,32,128]{3,2,1,0:T(8,128)S(1)} %pad_maximum_fusion.2.refs_4_), channel_id=1, source_target_pairs={{0,24},{8,0},{16,8},{24,16},{1,25},{9,1},{17,9},{25,17},{2,26},{10... | collective-permute-start | bytes 393224 | tf_op jit(solution)/shard_map/ppermute | solution.py:42
  28.8 0.6 %collective-permute-start.9 = (f32[4,2,32,128]{3,2,1,0:T(8,128)S(1)}, f32[4,2,32,128]{3,2,1,0:T(8,128)S(1)}, u32[]{:S(2)}, u32[]{:S(2)}) collective-permute-start(f32[4,2,32,128]{3,2,1,0:T(8,128)S(1)} %pad_maximum_fusion.2.refs_4_), channel_id=1, source_target_pairs={{0,8},{8,16},{16,24},{24,0},{1,9},{9,17},{17,25},{25,1},{2,10},{10... | collective-permute-start | bytes 393224 | tf_op jit(solution)/shard_map/ppermute | solution.py:42
  29.4 0.1 pad_add_fusion.place
  29.5 2.5 %collective-permute-done.10.refs_6_ = f32[4,2,32,128]{3,2,1,0:T(8,128)S(1)} collective-permute-done((f32[4,2,32,128]{3,2,1,0:T(8,128)S(1)}, f32[4,2,32,128]{3,2,1,0:T(8,128)S(1)}, u32[]{:S(2)}, u32[]{:S(2)}) %collective-permute-start.10) | collective-permute-done | bytes 131104 | tf_op jit(solution)/shard_map/ppermute | solution.py:42
  32.0 1.2 %collective-permute-done.11.refs_7_ = f32[4,2,32,128]{3,2,1,0:T(8,128)S(1)} collective-permute-done((f32[4,2,32,128]{3,2,1,0:T(8,128)S(1)}, f32[4,2,32,128]{3,2,1,0:T(8,128)S(1)}, u32[]{:S(2)}, u32[]{:S(2)}) %collective-permute-start.11) | collective-permute-done | bytes 131104 | tf_op jit(solution)/shard_map/ppermute | solution.py:42
  33.1 1.6 %collective-permute-done.9.refs_5_ = f32[4,2,32,128]{3,2,1,0:T(8,128)S(1)} collective-permute-done((f32[4,2,32,128]{3,2,1,0:T(8,128)S(1)}, f32[4,2,32,128]{3,2,1,0:T(8,128)S(1)}, u32[]{:S(2)}, u32[]{:S(2)}) %collective-permute-start.9) | collective-permute-done | bytes 131104 | tf_op jit(solution)/shard_map/ppermute | solution.py:42
  34.7 1.6 %shard_map.59 = f32[2,384,128]{2,1,0:T(8,128)S(1)} custom-call(s32[13]{0:T(128)S(1)} %pad_add_fusion.place, f32[2,256,128]{2,1,0:T(8,128)S(1)} %copy-done.1, f32[2,256,128]{2,1,0:T(8,128)S(1)} %collective-permute-done.3.refs_1_, f32[2,256,128]{2,1,0:T(8,128)S(1)} %collective-permute-done.8.refs_2_, f32[2,256,128]{2,1,0:T(8,128)S(1)} %collective-permute-done.4.refs_3_, ...), custom_call_target="tpu_custom_call" | custom-call | tf_op jit(solution)/shard_map/pallas_call | solution.py:102
  36.3 0.1 collective-permute-start.12
  36.4 0.1 pad.15.clone
  36.5 1.6 %collective-permute-done.12 = f32[2,384,128]{2,1,0:T(8,128)S(1)} collective-permute-done((f32[2,384,128]{2,1,0:T(8,128)S(1)}, f32[2,384,128]{2,1,0:T(8,128)S(1)}, u32[]{:S(2)}, u32[]{:S(2)}) %collective-permute-start.12) | collective-permute-done | bytes 393248 | tf_op jit(solution)/shard_map/ppermute | solution.py:42
  38.1 0.1 multiply_reduce_fusion
  38.3 0.1 fusion.4
  38.4 2.6 %collective-permute-start.13 = (f32[72,128]{1,0:T(8,128)S(1)}, f32[72,128]{1,0:T(8,128)S(1)}, u32[]{:S(2)}, u32[]{:S(2)}) collective-permute-start(f32[72,128]{1,0:T(8,128)S(1)} %get-tuple-element.44), channel_id=1, source_target_pairs={{0,6},{2,0},{4,2},{6,4},{1,7},{3,1},{5,3},{7,5},{8,14},{10,8},{12,... | collective-permute-start | bytes 110600 | tf_op jit(solution)/shard_map/ppermute | solution.py:42
  40.9 1.7 %collective-permute-start.15 = (f32[72,128]{1,0:T(8,128)S(1)}, f32[72,128]{1,0:T(8,128)S(1)}, u32[]{:S(2)}, u32[]{:S(2)}) collective-permute-start(f32[72,128]{1,0:T(8,128)S(1)} %get-tuple-element.42), channel_id=1, source_target_pairs={{0,2},{2,4},{4,6},{6,0},{1,3},{3,5},{5,7},{7,1},{8,10},{10,12},{12... | collective-permute-start | bytes 110600 | tf_op jit(solution)/shard_map/ppermute | solution.py:42
  42.6 3.3 %collective-permute-done.14 = f32[72,128]{1,0:T(8,128)S(1)} collective-permute-done((f32[72,128]{1,0:T(8,128)S(1)}, f32[72,128]{1,0:T(8,128)S(1)}, u32[]{:S(2)}, u32[]{:S(2)}) %collective-permute-start.14) | collective-permute-done | bytes 36896 | tf_op jit(solution)/shard_map/ppermute | solution.py:42
  46.0 0.7 %collective-permute-done.15 = f32[72,128]{1,0:T(8,128)S(1)} collective-permute-done((f32[72,128]{1,0:T(8,128)S(1)}, f32[72,128]{1,0:T(8,128)S(1)}, u32[]{:S(2)}, u32[]{:S(2)}) %collective-permute-start.15) | collective-permute-done | bytes 36896 | tf_op jit(solution)/shard_map/ppermute | solution.py:42
  46.7 0.1 select_select_fusion.2
  46.8 0.1 select_select_fusion.3
  46.9 0.6 %collective-permute-start.16 = (f32[2,512]{1,0:T(2,128)S(1)}, f32[2,512]{1,0:T(2,128)S(1)}, u32[]{:S(2)}, u32[]{:S(2)}) collective-permute-start(f32[2,512]{1,0:T(2,128)S(1)} %pad_maximum_fusion.7), channel_id=1, source_target_pairs={{0,8},{8,16},{16,24},{24,0},{1,9},{9,17},{17,25},{25,1},{2,10},{10... | collective-permute-start | bytes 12296 | tf_op jit(solution)/shard_map/ppermute | solution.py:42
  47.4 1.5 %collective-permute-start.17 = (f32[2,512]{1,0:T(2,128)S(1)}, f32[2,512]{1,0:T(2,128)S(1)}, u32[]{:S(2)}, u32[]{:S(2)}) collective-permute-start(f32[2,512]{1,0:T(2,128)S(1)} %pad_maximum_fusion.7), channel_id=1, source_target_pairs={{0,16},{8,24},{16,0},{24,8},{1,17},{9,25},{17,1},{25,9},{2,18},{10... | collective-permute-start | bytes 12296 | tf_op jit(solution)/shard_map/ppermute | solution.py:42
  49.0 2.4 %collective-permute-start.18 = (f32[2,512]{1,0:T(2,128)S(1)}, f32[2,512]{1,0:T(2,128)S(1)}, u32[]{:S(2)}, u32[]{:S(2)}) collective-permute-start(f32[2,512]{1,0:T(2,128)S(1)} %pad_maximum_fusion.7), channel_id=1, source_target_pairs={{0,24},{8,0},{16,8},{24,16},{1,25},{9,1},{17,9},{25,17},{2,26},{10... | collective-permute-start | bytes 12296 | tf_op jit(solution)/shard_map/ppermute | solution.py:42
  51.4 0.7 %slice_negate_fusion = f32[64,512]{1,0:T(8,128)} fusion(f32[72,512]{1,0:T(8,128)S(1)} %pad_maximum_fusion.1), kind=kLoop, calls=%fused_computation.4 | loop fusion | flops 32768 | bytes 262144 | tf_op jit(solution)/shard_map/neg | solution.py:129
  52.1 0.6 %collective-permute-done.18 = f32[2,512]{1,0:T(2,128)S(1)} collective-permute-done((f32[2,512]{1,0:T(2,128)S(1)}, f32[2,512]{1,0:T(2,128)S(1)}, u32[]{:S(2)}, u32[]{:S(2)}) %collective-permute-start.18) | collective-permute-done | bytes 4128 | tf_op jit(solution)/shard_map/ppermute | solution.py:42
  52.7 0.6 %add_add_fusion.1 = f32[2,512]{1,0:T(2,128)} fusion(f32[2,512]{1,0:T(2,128)S(1)} %collective-permute-done.18, f32[2,512]{1,0:T(2,128)S(1)} %collective-permute-done.17, f32[2,512]{1,0:T(2,128)S(1)} %pad_maximum_fusion.7, f32[2,512]{1,0:T(2,128)S(1)} %collective-permute-done.16), kind=kLoop, calls=%fused_computation.25 | loop fusion | flops 3072 | bytes 20480 | tf_op jit(solution)/shard_map/add | solution.py:133
  (25 shorter events, 0.3 us)
Async XLA Ops:
  0.6 5.2 %copy-start = (f32[2,128,512]{2,1,0:T(8,128)S(1)}, f32[2,128,512]{2,1,0:T(8,128)}, u32[]{:S(2)}) copy-start(f32[2,128,512]{2,1,0:T(8,128)} %param.5) | copy-start | bytes 1572868
  0.6 15.7 %collective-permute-start.3 = (f32[2,256,128]{2,1,0:T(8,128)}, f32[2,256,128]{2,1,0:T(8,128)S(1)}, u32[]{:S(2)}, u32[]{:S(2)}) collective-permute-start(f32[2,256,128]{2,1,0:T(8,128)} %refs_0_.1), channel_id=1, source_target_pairs={{0,2},{2,4},{4,6},{6,0},{1,3},{3,5},{5,7},{7,1},{8,10},{10,12},{12... | collective-permute-start | bytes 786440 | tf_op jit(solution)/shard_map/ppermute | solution.py:42
  3.7 13.6 %collective-permute-start.4 = (f32[2,256,128]{2,1,0:T(8,128)}, f32[2,256,128]{2,1,0:T(8,128)S(1)}, u32[]{:S(2)}, u32[]{:S(2)}) collective-permute-start(f32[2,256,128]{2,1,0:T(8,128)} %refs_0_.1), channel_id=1, source_target_pairs={{0,6},{2,0},{4,2},{6,4},{1,7},{3,1},{5,3},{7,5},{8,14},{10,8},{12,... | collective-permute-start | bytes 786440 | tf_op jit(solution)/shard_map/ppermute | solution.py:42
  7.5 7.2 %collective-permute-start = (f32[2,32,512]{2,1,0:T(8,128)S(1)}, f32[2,32,512]{2,1,0:T(8,128)S(1)}, u32[]{:S(2)}, u32[]{:S(2)}) collective-permute-start(f32[2,32,512]{2,1,0:T(8,128)S(1)} %get-tuple-element.30), channel_id=1, source_target_pairs={{0,8},{8,16},{16,24},{24,0},{1,9},{9,17},{17,25},{25,1},{2,10},{10... | collective-permute-start | bytes 393224 | tf_op jit(solution)/shard_map/ppermute | solution.py:42
  9.2 7.0 %collective-permute-start.1 = (f32[2,32,512]{2,1,0:T(8,128)S(1)}, f32[2,32,512]{2,1,0:T(8,128)S(1)}, u32[]{:S(2)}, u32[]{:S(2)}) collective-permute-start(f32[2,32,512]{2,1,0:T(8,128)S(1)} %get-tuple-element.29), channel_id=1, source_target_pairs={{0,16},{8,24},{16,0},{24,8},{1,17},{9,25},{17,1},{25,9},{2,18},{10... | collective-permute-start | bytes 393224 | tf_op jit(solution)/shard_map/ppermute | solution.py:42
  10.7 5.6 %collective-permute-start.2 = (f32[2,32,512]{2,1,0:T(8,128)S(1)}, f32[2,32,512]{2,1,0:T(8,128)S(1)}, u32[]{:S(2)}, u32[]{:S(2)}) collective-permute-start(f32[2,32,512]{2,1,0:T(8,128)S(1)} %get-tuple-element.28), channel_id=1, source_target_pairs={{0,24},{8,0},{16,8},{24,16},{1,25},{9,1},{17,9},{25,17},{2,26},{10... | collective-permute-start | bytes 393224 | tf_op jit(solution)/shard_map/ppermute | solution.py:42
  12.1 0.7 %copy-start.2 = (s32[2,4]{1,0:T(2,128)S(1)}, s32[2,4]{1,0:T(2,128)}, u32[]{:S(2)}) copy-start(s32[2,4]{1,0:T(2,128)} %param.7) | copy-start | bytes 100
  17.4 17.3 %copy-start.1 = (f32[2,256,128]{2,1,0:T(8,128)S(1)}, f32[2,256,128]{2,1,0:T(8,128)}, u32[]{:S(2)}) copy-start(f32[2,256,128]{2,1,0:T(8,128)} %refs_0_.1) | copy-start | bytes 786436
  17.4 5.9 %collective-permute-start.5 = (f32[2,32,128]{2,1,0:T(8,128)S(1)}, f32[2,32,128]{2,1,0:T(8,128)S(1)}, u32[]{:S(2)}, u32[]{:S(2)}) collective-permute-start(f32[2,32,128]{2,1,0:T(8,128)S(1)} %get-tuple-element.40), channel_id=1, source_target_pairs={{0,2},{2,4},{4,6},{6,0},{1,3},{3,5},{5,7},{7,1},{8,10},{10,12},{12... | collective-permute-start | bytes 98312 | tf_op jit(solution)/shard_map/ppermute | solution.py:42
  18.6 5.6 %collective-permute-start.6 = (f32[2,32,128]{2,1,0:T(8,128)S(1)}, f32[2,32,128]{2,1,0:T(8,128)S(1)}, u32[]{:S(2)}, u32[]{:S(2)}) collective-permute-start(f32[2,32,128]{2,1,0:T(8,128)S(1)} %get-tuple-element.39), channel_id=1, source_target_pairs={{0,4},{2,6},{4,0},{6,2},{1,5},{3,7},{5,1},{7,3},{8,12},{10,14},{12... | collective-permute-start | bytes 98312 | tf_op jit(solution)/shard_map/ppermute | solution.py:42
  20.3 4.1 %collective-permute-start.7 = (f32[2,32,128]{2,1,0:T(8,128)S(1)}, f32[2,32,128]{2,1,0:T(8,128)S(1)}, u32[]{:S(2)}, u32[]{:S(2)}) collective-permute-start(f32[2,32,128]{2,1,0:T(8,128)S(1)} %get-tuple-element.38), channel_id=1, source_target_pairs={{0,6},{2,0},{4,2},{6,4},{1,7},{3,1},{5,3},{7,5},{8,14},{10,8},{12,... | collective-permute-start | bytes 98312 | tf_op jit(solution)/shard_map/ppermute | solution.py:42
  24.5 10.2 %collective-permute-start.8 = (f32[2,256,128]{2,1,0:T(8,128)S(1)}, f32[2,256,128]{2,1,0:T(8,128)S(1)}, u32[]{:S(2)}, u32[]{:S(2)}) collective-permute-start(f32[2,256,128]{2,1,0:T(8,128)S(1)} %collective-permute-done.3.refs_1_), channel_id=1, source_target_pairs={{0,2},{2,4},{4,6},{6,0},{1,3},{3,5},{5,7},{7,1},{8,10},{10,12},{12... | collective-permute-start | bytes 786440 | tf_op jit(solution)/shard_map/ppermute | solution.py:42
  25.8 6.2 %collective-permute-start.10 = (f32[4,2,32,128]{3,2,1,0:T(8,128)S(1)}, f32[4,2,32,128]{3,2,1,0:T(8,128)S(1)}, u32[]{:S(2)}, u32[]{:S(2)}) collective-permute-start(f32[4,2,32,128]{3,2,1,0:T(8,128)S(1)} %pad_maximum_fusion.2.refs_4_), channel_id=1, source_target_pairs={{0,16},{8,24},{16,0},{24,8},{1,17},{9,25},{17,1},{25,9},{2,18},{10... | collective-permute-start | bytes 393224 | tf_op jit(solution)/shard_map/ppermute | solution.py:42
  27.4 5.7 %collective-permute-start.11 = (f32[4,2,32,128]{3,2,1,0:T(8,128)S(1)}, f32[4,2,32,128]{3,2,1,0:T(8,128)S(1)}, u32[]{:S(2)}, u32[]{:S(2)}) collective-permute-start(f32[4,2,32,128]{3,2,1,0:T(8,128)S(1)} %pad_maximum_fusion.2.refs_4_), channel_id=1, source_target_pairs={{0,24},{8,0},{16,8},{24,16},{1,25},{9,1},{17,9},{25,17},{2,26},{10... | collective-permute-start | bytes 393224 | tf_op jit(solution)/shard_map/ppermute | solution.py:42
  28.8 5.9 %collective-permute-start.9 = (f32[4,2,32,128]{3,2,1,0:T(8,128)S(1)}, f32[4,2,32,128]{3,2,1,0:T(8,128)S(1)}, u32[]{:S(2)}, u32[]{:S(2)}) collective-permute-start(f32[4,2,32,128]{3,2,1,0:T(8,128)S(1)} %pad_maximum_fusion.2.refs_4_), channel_id=1, source_target_pairs={{0,8},{8,16},{16,24},{24,0},{1,9},{9,17},{17,25},{25,1},{2,10},{10... | collective-permute-start | bytes 393224 | tf_op jit(solution)/shard_map/ppermute | solution.py:42
  36.3 1.8 %collective-permute-start.12 = (f32[2,384,128]{2,1,0:T(8,128)S(1)}, f32[2,384,128]{2,1,0:T(8,128)S(1)}, u32[]{:S(2)}, u32[]{:S(2)}) collective-permute-start(f32[2,384,128]{2,1,0:T(8,128)S(1)} %shard_map.59), channel_id=1, source_target_pairs={{0,1},{1,0},{2,3},{3,2},{4,5},{5,4},{6,7},{7,6},{8,9},{9,8},{10,11... | collective-permute-start | bytes 1179656 | tf_op jit(solution)/shard_map/ppermute | solution.py:42
  38.4 4.3 %collective-permute-start.13 = (f32[72,128]{1,0:T(8,128)S(1)}, f32[72,128]{1,0:T(8,128)S(1)}, u32[]{:S(2)}, u32[]{:S(2)}) collective-permute-start(f32[72,128]{1,0:T(8,128)S(1)} %get-tuple-element.44), channel_id=1, source_target_pairs={{0,6},{2,0},{4,2},{6,4},{1,7},{3,1},{5,3},{7,5},{8,14},{10,8},{12,... | collective-permute-start | bytes 110600 | tf_op jit(solution)/shard_map/ppermute | solution.py:42
  40.9 5.0 %collective-permute-start.14 = (f32[72,128]{1,0:T(8,128)S(1)}, f32[72,128]{1,0:T(8,128)S(1)}, u32[]{:S(2)}, u32[]{:S(2)}) collective-permute-start(f32[72,128]{1,0:T(8,128)S(1)} %get-tuple-element.43), channel_id=1, source_target_pairs={{0,4},{2,6},{4,0},{6,2},{1,5},{3,7},{5,1},{7,3},{8,12},{10,14},{12... | collective-permute-start | bytes 110600 | tf_op jit(solution)/shard_map/ppermute | solution.py:42
  40.9 5.8 %collective-permute-start.15 = (f32[72,128]{1,0:T(8,128)S(1)}, f32[72,128]{1,0:T(8,128)S(1)}, u32[]{:S(2)}, u32[]{:S(2)}) collective-permute-start(f32[72,128]{1,0:T(8,128)S(1)} %get-tuple-element.42), channel_id=1, source_target_pairs={{0,2},{2,4},{4,6},{6,0},{1,3},{3,5},{5,7},{7,1},{8,10},{10,12},{12... | collective-permute-start | bytes 110600 | tf_op jit(solution)/shard_map/ppermute | solution.py:42
  46.9 5.2 %collective-permute-start.16 = (f32[2,512]{1,0:T(2,128)S(1)}, f32[2,512]{1,0:T(2,128)S(1)}, u32[]{:S(2)}, u32[]{:S(2)}) collective-permute-start(f32[2,512]{1,0:T(2,128)S(1)} %pad_maximum_fusion.7), channel_id=1, source_target_pairs={{0,8},{8,16},{16,24},{24,0},{1,9},{9,17},{17,25},{25,1},{2,10},{10... | collective-permute-start | bytes 12296 | tf_op jit(solution)/shard_map/ppermute | solution.py:42
  47.4 4.6 %collective-permute-start.17 = (f32[2,512]{1,0:T(2,128)S(1)}, f32[2,512]{1,0:T(2,128)S(1)}, u32[]{:S(2)}, u32[]{:S(2)}) collective-permute-start(f32[2,512]{1,0:T(2,128)S(1)} %pad_maximum_fusion.7), channel_id=1, source_target_pairs={{0,16},{8,24},{16,0},{24,8},{1,17},{9,25},{17,1},{25,9},{2,18},{10... | collective-permute-start | bytes 12296 | tf_op jit(solution)/shard_map/ppermute | solution.py:42
  49.0 3.7 %collective-permute-start.18 = (f32[2,512]{1,0:T(2,128)S(1)}, f32[2,512]{1,0:T(2,128)S(1)}, u32[]{:S(2)}, u32[]{:S(2)}) collective-permute-start(f32[2,512]{1,0:T(2,128)S(1)} %pad_maximum_fusion.7), channel_id=1, source_target_pairs={{0,24},{8,0},{16,8},{24,16},{1,25},{9,1},{17,9},{25,17},{2,26},{10... | collective-permute-start | bytes 12296 | tf_op jit(solution)/shard_map/ppermute | solution.py:42

commit v17 on v16

--- a/solution.py
+++ b/solution.py
@@ -63,17 +63,19 @@
 
         early = [d for d in range(1, deep) if not deep < 4 * d < 3 * deep]
         late = [d for d in range(1, deep) if d not in early]
-        far = {d: shifted(ancestor, "z", deep, d) for d in early}
+        far = {d: shifted(ancestor, "z", deep, d) for d in early[:1]}
 
         mine = lax.dynamic_slice_in_dim(panel, row * depth, depth, axis=2)
         partial = jnp.einsum("srw,swv->srv", mine, factor_inv, precision=highest)
+        partial, held_back = lax.optimization_barrier((partial, ancestor))
+        far |= {d: shifted(held_back, "z", deep, d) for d in early[1:]}
 
         def rows_of(r):
             return lax.dynamic_slice_in_dim(partial, r * piece, piece, axis=1)
 
         sums = [shifted(rows_of((row + d) % rows), "row", rows, d) for d in range(1, rows)]
         squares = jnp.sum(lax.dynamic_slice_in_dim(factor_inv, z * part, part, axis=2) ** 2, axis=1)
-        sums, squares, far = lax.optimization_barrier((sums, squares, far))
+        sums, squares = lax.optimization_barrier((sums, squares))
         scaled = sum(sums, rows_of(row))
 
         def columns_of(array, c):

time: 53.5 us -> 51.3 us (0.959)
  waiting for transfers between devices: 17.6 us -> 13.9 us
  starting transfers between devices: 27.8 us -> 29.4 us
    ppermute x19, waiting for transfers between devices: 17.6 us -> 13.9 us  [shifted(): lax.ppermute(array, axis, [(i, (i + shift) % size) for i in range(size)])]
    ppermute x19, starting transfers between devices: 27.8 us -> 29.4 us  [shifted(): lax.ppermute(array, axis, [(i, (i + shift) % size) for i in range(size)])]
  transfers between devices with their start and end apart: 19 -> 19, of which waited for: 14 -> 10; matrix products, arithmetic and copies ran while one was open for 7% -> 7% of each run, Pallas kernels for 0% -> 0%
where the time goes in v17:
time: 51.3 us; the launch traced here: 51.1 us
  starting transfers between devices  29.4 us (57%)
  waiting for transfers between devices  13.9 us (27%)
  other arithmetic  2.84 us (6%)
  matrix products  1.62 us (3%)
  Pallas kernels  1.61 us (3%)
  local copies, waits for them, and re-layouts  0.95 us (2%)
  between operations  0.86 us (2%)
    ppermute x19, starting transfers between devices, shifted(): lax.ppermute(array, axis, [(i, (i + shift) % size) for i in range(size)])  29.4 us
    ppermute x19, waiting for transfers between devices, shifted(): lax.ppermute(array, axis, [(i, (i + shift) % size) for i in range(size)])  13.9 us
    dot_general x1, matrix products, per_device(): partial = jnp.einsum('srw,swv->srv', mine, factor_inv, precision=highest)  1.62 us
    pallas_call x1, Pallas kernels, per_device(): pl.pallas_call(functools.partial(multiply_tiles, deep, rows), out_shape=j...  1.61 us
  transfers between devices with their start and end apart: 19, of which 10 were waited for; matrix products, arithmetic and copies ran while one was open for 7% of the time, Pallas kernels for 0%

profile of v17, /device:TPU:0, one launch (start us, length us, event | category | flops | bytes accessed | tf_op | source)
XLA Modules:
  0.0 51.1 jit_solution(2069412226036514354)
XLA Ops:
  0.6 0.0 copy-start
  0.6 3.1 %collective-permute-start.6 = (f32[2,256,128]{2,1,0:T(8,128)}, f32[2,256,128]{2,1,0:T(8,128)S(1)}, u32[]{:S(2)}, u32[]{:S(2)}) collective-permute-start(f32[2,256,128]{2,1,0:T(8,128)} %refs_0_.1), channel_id=1, source_target_pairs={{0,2},{2,4},{4,6},{6,0},{1,3},{3,5},{5,7},{7,1},{8,10},{10,12},{12... | collective-permute-start | bytes 786440 | tf_op jit(solution)/shard_map/ppermute | solution.py:42
  3.7 1.6 %fusion = f32[2,128,512]{2,1,0:T(8,128)S(1)} fusion(f32[2,128,512]{2,1,0:T(8,128)} %param.6, f32[2,128,512]{2,1,0:T(8,128)S(1)} %copy-done, s32[]{:T(128)S(6)} %select_n.231), kind=kOutput, calls=%fused_computation.10 | convolution fusion | flops 201326592 | bytes 1179652 | tf_op jit(solution)/shard_map/srw,swv->srv/dot_general | solution.py:69
  5.4 0.0 copy-start.1
  5.4 1.5 %collective-permute-start = (f32[2,32,512]{2,1,0:T(8,128)S(1)}, f32[2,32,512]{2,1,0:T(8,128)S(1)}, u32[]{:S(2)}, u32[]{:S(2)}) collective-permute-start(f32[2,32,512]{2,1,0:T(8,128)S(1)} %get-tuple-element.30), channel_id=1, source_target_pairs={{0,8},{8,16},{16,24},{24,0},{1,9},{9,17},{17,25},{25,1},{2,10},{10... | collective-permute-start | bytes 393224 | tf_op jit(solution)/shard_map/ppermute | solution.py:42
  7.0 1.5 %collective-permute-start.1 = (f32[2,32,512]{2,1,0:T(8,128)S(1)}, f32[2,32,512]{2,1,0:T(8,128)S(1)}, u32[]{:S(2)}, u32[]{:S(2)}) collective-permute-start(f32[2,32,512]{2,1,0:T(8,128)S(1)} %get-tuple-element.29), channel_id=1, source_target_pairs={{0,16},{8,24},{16,0},{24,8},{1,17},{9,25},{17,1},{25,9},{2,18},{10... | collective-permute-start | bytes 393224 | tf_op jit(solution)/shard_map/ppermute | solution.py:42
  8.5 1.4 %collective-permute-start.2 = (f32[2,32,512]{2,1,0:T(8,128)S(1)}, f32[2,32,512]{2,1,0:T(8,128)S(1)}, u32[]{:S(2)}, u32[]{:S(2)}) collective-permute-start(f32[2,32,512]{2,1,0:T(8,128)S(1)} %get-tuple-element.28), channel_id=1, source_target_pairs={{0,24},{8,0},{16,8},{24,16},{1,25},{9,1},{17,9},{25,17},{2,26},{10... | collective-permute-start | bytes 393224 | tf_op jit(solution)/shard_map/ppermute | solution.py:42
  9.9 3.0 %collective-permute-start.8 = (f32[2,256,128]{2,1,0:T(8,128)S(1)}, f32[2,256,128]{2,1,0:T(8,128)S(1)}, u32[]{:S(2)}, u32[]{:S(2)}) collective-permute-start(f32[2,256,128]{2,1,0:T(8,128)S(1)} %copy-done.1), channel_id=1, source_target_pairs={{0,6},{2,0},{4,2},{6,4},{1,7},{3,1},{5,3},{7,5},{8,14},{10,8},{12,... | collective-permute-start | bytes 786440 | tf_op jit(solution)/shard_map/ppermute | solution.py:42
  12.9 0.7 %copy-done.2 = s32[2,4]{1,0:T(2,128)S(1)} copy-done((s32[2,4]{1,0:T(2,128)S(1)}, s32[2,4]{1,0:T(2,128)}, u32[]{:S(2)}) %copy-start.2) | copy-done | bytes 56
  13.6 0.1 select_reduce_fusion
  13.7 0.1 sub.51
  13.8 0.9 %multiply_reduce_fusion.1 = f32[2,128]{1,0:T(2,128)S(1)} fusion(f32[2,128,512]{2,1,0:T(8,128)} %param.6, s32[]{:T(128)S(6)} %select_n.239), kind=kLoop, calls=%fused_computation.9 | loop fusion | flops 65280 | bytes 132100 | tf_op jit(solution)/shard_map/reduce_sum | solution.py:77
  14.7 0.0 collective-permute-done.1
  14.7 0.0 collective-permute-done.2
  14.8 1.1 %collective-permute-start.3 = (f32[2,32,128]{2,1,0:T(8,128)S(1)}, f32[2,32,128]{2,1,0:T(8,128)S(1)}, u32[]{:S(2)}, u32[]{:S(2)}) collective-permute-start(f32[2,32,128]{2,1,0:T(8,128)S(1)} %get-tuple-element.40), channel_id=1, source_target_pairs={{0,2},{2,4},{4,6},{6,0},{1,3},{3,5},{5,7},{7,1},{8,10},{10,12},{12... | collective-permute-start | bytes 98312 | tf_op jit(solution)/shard_map/ppermute | solution.py:42
  15.9 2.3 %collective-permute-start.4 = (f32[2,32,128]{2,1,0:T(8,128)S(1)}, f32[2,32,128]{2,1,0:T(8,128)S(1)}, u32[]{:S(2)}, u32[]{:S(2)}) collective-permute-start(f32[2,32,128]{2,1,0:T(8,128)S(1)} %get-tuple-element.39), channel_id=1, source_target_pairs={{0,4},{2,6},{4,0},{6,2},{1,5},{3,7},{5,1},{7,3},{8,12},{10,14},{12... | collective-permute-start | bytes 98312 | tf_op jit(solution)/shard_map/ppermute | solution.py:42
  18.2 1.7 %collective-permute-start.5 = (f32[2,32,128]{2,1,0:T(8,128)S(1)}, f32[2,32,128]{2,1,0:T(8,128)S(1)}, u32[]{:S(2)}, u32[]{:S(2)}) collective-permute-start(f32[2,32,128]{2,1,0:T(8,128)S(1)} %get-tuple-element.38), channel_id=1, source_target_pairs={{0,6},{2,0},{4,2},{6,4},{1,7},{3,1},{5,3},{7,5},{8,14},{10,8},{12,... | collective-permute-start | bytes 98312 | tf_op jit(solution)/shard_map/ppermute | solution.py:42
  19.9 1.1 %collective-permute-done.3 = f32[2,32,128]{2,1,0:T(8,128)S(1)} collective-permute-done((f32[2,32,128]{2,1,0:T(8,128)S(1)}, f32[2,32,128]{2,1,0:T(8,128)S(1)}, u32[]{:S(2)}, u32[]{:S(2)}) %collective-permute-start.3) | collective-permute-done | bytes 32800 | tf_op jit(solution)/shard_map/ppermute | solution.py:42
  20.9 0.4 collective-permute-done.4
  21.3 0.8 %collective-permute-done.5 = f32[2,32,128]{2,1,0:T(8,128)S(1)} collective-permute-done((f32[2,32,128]{2,1,0:T(8,128)S(1)}, f32[2,32,128]{2,1,0:T(8,128)S(1)}, u32[]{:S(2)}, u32[]{:S(2)}) %collective-permute-start.5) | collective-permute-done | bytes 32800 | tf_op jit(solution)/shard_map/ppermute | solution.py:42
  22.1 0.0 collective-permute-done.6.refs_1_
  22.1 1.1 %collective-permute-start.7 = (f32[2,256,128]{2,1,0:T(8,128)S(1)}, f32[2,256,128]{2,1,0:T(8,128)S(1)}, u32[]{:S(2)}, u32[]{:S(2)}) collective-permute-start(f32[2,256,128]{2,1,0:T(8,128)S(1)} %collective-permute-done.6.refs_1_), channel_id=1, source_target_pairs={{0,2},{2,4},{4,6},{6,0},{1,3},{3,5},{5,7},{7,1},{8,10},{10,12},{12... | collective-permute-start | bytes 786440 | tf_op jit(solution)/shard_map/ppermute | solution.py:42
  23.2 1.0 %collective-permute-start.10 = (f32[4,2,32,128]{3,2,1,0:T(8,128)S(1)}, f32[4,2,32,128]{3,2,1,0:T(8,128)S(1)}, u32[]{:S(2)}, u32[]{:S(2)}) collective-permute-start(f32[4,2,32,128]{3,2,1,0:T(8,128)S(1)} %pad_maximum_fusion.2.refs_4_), channel_id=1, source_target_pairs={{0,16},{8,24},{16,0},{24,8},{1,17},{9,25},{17,1},{25,9},{2,18},{10... | collective-permute-start | bytes 393224 | tf_op jit(solution)/shard_map/ppermute | solution.py:42
  24.2 1.7 %collective-permute-start.11 = (f32[4,2,32,128]{3,2,1,0:T(8,128)S(1)}, f32[4,2,32,128]{3,2,1,0:T(8,128)S(1)}, u32[]{:S(2)}, u32[]{:S(2)}) collective-permute-start(f32[4,2,32,128]{3,2,1,0:T(8,128)S(1)} %pad_maximum_fusion.2.refs_4_), channel_id=1, source_target_pairs={{0,24},{8,0},{16,8},{24,16},{1,25},{9,1},{17,9},{25,17},{2,26},{10... | collective-permute-start | bytes 393224 | tf_op jit(solution)/shard_map/ppermute | solution.py:42
  25.9 0.3 collective-permute-start.9
  26.2 0.1 pad_add_fusion.place
  26.3 3.2 %collective-permute-done.10.refs_6_ = f32[4,2,32,128]{3,2,1,0:T(8,128)S(1)} collective-permute-done((f32[4,2,32,128]{3,2,1,0:T(8,128)S(1)}, f32[4,2,32,128]{3,2,1,0:T(8,128)S(1)}, u32[]{:S(2)}, u32[]{:S(2)}) %collective-permute-start.10) | collective-permute-done | bytes 131104 | tf_op jit(solution)/shard_map/ppermute | solution.py:42
  29.5 2.3 %collective-permute-done.9.refs_5_ = f32[4,2,32,128]{3,2,1,0:T(8,128)S(1)} collective-permute-done((f32[4,2,32,128]{3,2,1,0:T(8,128)S(1)}, f32[4,2,32,128]{3,2,1,0:T(8,128)S(1)}, u32[]{:S(2)}, u32[]{:S(2)}) %collective-permute-start.9) | collective-permute-done | bytes 131104 | tf_op jit(solution)/shard_map/ppermute | solution.py:42
  31.8 1.6 %shard_map.59 = f32[2,384,128]{2,1,0:T(8,128)S(1)} custom-call(s32[13]{0:T(128)S(1)} %pad_add_fusion.place, f32[2,256,128]{2,1,0:T(8,128)S(1)} %copy-done.1, f32[2,256,128]{2,1,0:T(8,128)S(1)} %collective-permute-done.6.refs_1_, f32[2,256,128]{2,1,0:T(8,128)S(1)} %collective-permute-done.7.refs_2_, f32[2,256,128]{2,1,0:T(8,128)S(1)} %collective-permute-done.8.refs_3_, ...), custom_call_target="tpu_custom_call" | custom-call | tf_op jit(solution)/shard_map/pallas_call | solution.py:104
  33.4 0.1 collective-permute-start.12
  33.5 0.1 pad.15.clone
  33.6 1.6 %collective-permute-done.12 = f32[2,384,128]{2,1,0:T(8,128)S(1)} collective-permute-done((f32[2,384,128]{2,1,0:T(8,128)S(1)}, f32[2,384,128]{2,1,0:T(8,128)S(1)}, u32[]{:S(2)}, u32[]{:S(2)}) %collective-permute-start.12) | collective-permute-done | bytes 393248 | tf_op jit(solution)/shard_map/ppermute | solution.py:42
  35.3 0.1 multiply_reduce_fusion
  35.4 0.1 fusion.4
  35.5 3.3 %collective-permute-start.13 = (f32[72,128]{1,0:T(8,128)S(1)}, f32[72,128]{1,0:T(8,128)S(1)}, u32[]{:S(2)}, u32[]{:S(2)}) collective-permute-start(f32[72,128]{1,0:T(8,128)S(1)} %get-tuple-element.44), channel_id=1, source_target_pairs={{0,6},{2,0},{4,2},{6,4},{1,7},{3,1},{5,3},{7,5},{8,14},{10,8},{12,... | collective-permute-start | bytes 110600 | tf_op jit(solution)/shard_map/ppermute | solution.py:42
  38.8 0.6 %collective-permute-start.14 = (f32[72,128]{1,0:T(8,128)S(1)}, f32[72,128]{1,0:T(8,128)S(1)}, u32[]{:S(2)}, u32[]{:S(2)}) collective-permute-start(f32[72,128]{1,0:T(8,128)S(1)} %get-tuple-element.43), channel_id=1, source_target_pairs={{0,4},{2,6},{4,0},{6,2},{1,5},{3,7},{5,1},{7,3},{8,12},{10,14},{12... | collective-permute-start | bytes 110600 | tf_op jit(solution)/shard_map/ppermute | solution.py:42
  39.5 1.9 %collective-permute-start.15 = (f32[72,128]{1,0:T(8,128)S(1)}, f32[72,128]{1,0:T(8,128)S(1)}, u32[]{:S(2)}, u32[]{:S(2)}) collective-permute-start(f32[72,128]{1,0:T(8,128)S(1)} %get-tuple-element.42), channel_id=1, source_target_pairs={{0,2},{2,4},{4,6},{6,0},{1,3},{3,5},{5,7},{7,1},{8,10},{10,12},{12... | collective-permute-start | bytes 110600 | tf_op jit(solution)/shard_map/ppermute | solution.py:42
  41.4 2.3 %collective-permute-done.14 = f32[72,128]{1,0:T(8,128)S(1)} collective-permute-done((f32[72,128]{1,0:T(8,128)S(1)}, f32[72,128]{1,0:T(8,128)S(1)}, u32[]{:S(2)}, u32[]{:S(2)}) %collective-permute-start.14) | collective-permute-done | bytes 36896 | tf_op jit(solution)/shard_map/ppermute | solution.py:42
  43.7 1.5 %collective-permute-done.15 = f32[72,128]{1,0:T(8,128)S(1)} collective-permute-done((f32[72,128]{1,0:T(8,128)S(1)}, f32[72,128]{1,0:T(8,128)S(1)}, u32[]{:S(2)}, u32[]{:S(2)}) %collective-permute-start.15) | collective-permute-done | bytes 36896 | tf_op jit(solution)/shard_map/ppermute | solution.py:42
  45.2 0.1 select_select_fusion.2
  45.3 0.1 select_select_fusion.3
  45.4 0.6 %collective-permute-start.16 = (f32[2,512]{1,0:T(2,128)S(1)}, f32[2,512]{1,0:T(2,128)S(1)}, u32[]{:S(2)}, u32[]{:S(2)}) collective-permute-start(f32[2,512]{1,0:T(2,128)S(1)} %pad_maximum_fusion.7), channel_id=1, source_target_pairs={{0,8},{8,16},{16,24},{24,0},{1,9},{9,17},{17,25},{25,1},{2,10},{10... | collective-permute-start | bytes 12296 | tf_op jit(solution)/shard_map/ppermute | solution.py:42
  46.0 0.7 %collective-permute-start.17 = (f32[2,512]{1,0:T(2,128)S(1)}, f32[2,512]{1,0:T(2,128)S(1)}, u32[]{:S(2)}, u32[]{:S(2)}) collective-permute-start(f32[2,512]{1,0:T(2,128)S(1)} %pad_maximum_fusion.7), channel_id=1, source_target_pairs={{0,16},{8,24},{16,0},{24,8},{1,17},{9,25},{17,1},{25,9},{2,18},{10... | collective-permute-start | bytes 12296 | tf_op jit(solution)/shard_map/ppermute | solution.py:42
  46.7 2.4 %collective-permute-start.18 = (f32[2,512]{1,0:T(2,128)S(1)}, f32[2,512]{1,0:T(2,128)S(1)}, u32[]{:S(2)}, u32[]{:S(2)}) collective-permute-start(f32[2,512]{1,0:T(2,128)S(1)} %pad_maximum_fusion.7), channel_id=1, source_target_pairs={{0,24},{8,0},{16,8},{24,16},{1,25},{9,1},{17,9},{25,17},{2,26},{10... | collective-permute-start | bytes 12296 | tf_op jit(solution)/shard_map/ppermute | solution.py:42
  49.1 0.7 %slice_negate_fusion = f32[64,512]{1,0:T(8,128)} fusion(f32[72,512]{1,0:T(8,128)S(1)} %pad_maximum_fusion.1), kind=kLoop, calls=%fused_computation.4 | loop fusion | flops 32768 | bytes 262144 | tf_op jit(solution)/shard_map/neg | solution.py:131
  49.8 0.2 collective-permute-done.16
  50.0 0.6 %collective-permute-done.18 = f32[2,512]{1,0:T(2,128)S(1)} collective-permute-done((f32[2,512]{1,0:T(2,128)S(1)}, f32[2,512]{1,0:T(2,128)S(1)}, u32[]{:S(2)}, u32[]{:S(2)}) %collective-permute-start.18) | collective-permute-done | bytes 4128 | tf_op jit(solution)/shard_map/ppermute | solution.py:42
  50.5 0.6 %add_add_fusion.1 = f32[2,512]{1,0:T(2,128)} fusion(f32[2,512]{1,0:T(2,128)S(1)} %collective-permute-done.18, f32[2,512]{1,0:T(2,128)S(1)} %collective-permute-done.17, f32[2,512]{1,0:T(2,128)S(1)} %pad_maximum_fusion.7, f32[2,512]{1,0:T(2,128)S(1)} %collective-permute-done.16), kind=kLoop, calls=%fused_computation.25 | loop fusion | flops 3072 | bytes 20480 | tf_op jit(solution)/shard_map/add | solution.py:135
  (25 shorter events, 0.3 us)
Async XLA Ops:
  0.6 3.1 %copy-start = (f32[2,128,512]{2,1,0:T(8,128)S(1)}, f32[2,128,512]{2,1,0:T(8,128)}, u32[]{:S(2)}) copy-start(f32[2,128,512]{2,1,0:T(8,128)} %param.5) | copy-start | bytes 1572868
  0.6 21.4 %collective-permute-start.6 = (f32[2,256,128]{2,1,0:T(8,128)}, f32[2,256,128]{2,1,0:T(8,128)S(1)}, u32[]{:S(2)}, u32[]{:S(2)}) collective-permute-start(f32[2,256,128]{2,1,0:T(8,128)} %refs_0_.1), channel_id=1, source_target_pairs={{0,2},{2,4},{4,6},{6,0},{1,3},{3,5},{5,7},{7,1},{8,10},{10,12},{12... | collective-permute-start | bytes 786440 | tf_op jit(solution)/shard_map/ppermute | solution.py:42
  5.4 4.6 %copy-start.1 = (f32[2,256,128]{2,1,0:T(8,128)S(1)}, f32[2,256,128]{2,1,0:T(8,128)}, u32[]{:S(2)}) copy-start(f32[2,256,128]{2,1,0:T(8,128)} %refs_0_.1) | copy-start | bytes 786436
  5.4 9.3 %collective-permute-start = (f32[2,32,512]{2,1,0:T(8,128)S(1)}, f32[2,32,512]{2,1,0:T(8,128)S(1)}, u32[]{:S(2)}, u32[]{:S(2)}) collective-permute-start(f32[2,32,512]{2,1,0:T(8,128)S(1)} %get-tuple-element.30), channel_id=1, source_target_pairs={{0,8},{8,16},{16,24},{24,0},{1,9},{9,17},{17,25},{25,1},{2,10},{10... | collective-permute-start | bytes 393224 | tf_op jit(solution)/shard_map/ppermute | solution.py:42
  7.0 7.8 %collective-permute-start.1 = (f32[2,32,512]{2,1,0:T(8,128)S(1)}, f32[2,32,512]{2,1,0:T(8,128)S(1)}, u32[]{:S(2)}, u32[]{:S(2)}) collective-permute-start(f32[2,32,512]{2,1,0:T(8,128)S(1)} %get-tuple-element.29), channel_id=1, source_target_pairs={{0,16},{8,24},{16,0},{24,8},{1,17},{9,25},{17,1},{25,9},{2,18},{10... | collective-permute-start | bytes 393224 | tf_op jit(solution)/shard_map/ppermute | solution.py:42
  8.5 6.3 %collective-permute-start.2 = (f32[2,32,512]{2,1,0:T(8,128)S(1)}, f32[2,32,512]{2,1,0:T(8,128)S(1)}, u32[]{:S(2)}, u32[]{:S(2)}) collective-permute-start(f32[2,32,512]{2,1,0:T(8,128)S(1)} %get-tuple-element.28), channel_id=1, source_target_pairs={{0,24},{8,0},{16,8},{24,16},{1,25},{9,1},{17,9},{25,17},{2,26},{10... | collective-permute-start | bytes 393224 | tf_op jit(solution)/shard_map/ppermute | solution.py:42
  9.9 16.4 %collective-permute-start.8 = (f32[2,256,128]{2,1,0:T(8,128)S(1)}, f32[2,256,128]{2,1,0:T(8,128)S(1)}, u32[]{:S(2)}, u32[]{:S(2)}) collective-permute-start(f32[2,256,128]{2,1,0:T(8,128)S(1)} %copy-done.1), channel_id=1, source_target_pairs={{0,6},{2,0},{4,2},{6,4},{1,7},{3,1},{5,3},{7,5},{8,14},{10,8},{12,... | collective-permute-start | bytes 786440 | tf_op jit(solution)/shard_map/ppermute | solution.py:42
  12.9 0.7 %copy-start.2 = (s32[2,4]{1,0:T(2,128)S(1)}, s32[2,4]{1,0:T(2,128)}, u32[]{:S(2)}) copy-start(s32[2,4]{1,0:T(2,128)} %param.7) | copy-start | bytes 100
  14.8 6.1 %collective-permute-start.3 = (f32[2,32,128]{2,1,0:T(8,128)S(1)}, f32[2,32,128]{2,1,0:T(8,128)S(1)}, u32[]{:S(2)}, u32[]{:S(2)}) collective-permute-start(f32[2,32,128]{2,1,0:T(8,128)S(1)} %get-tuple-element.40), channel_id=1, source_target_pairs={{0,2},{2,4},{4,6},{6,0},{1,3},{3,5},{5,7},{7,1},{8,10},{10,12},{12... | collective-permute-start | bytes 98312 | tf_op jit(solution)/shard_map/ppermute | solution.py:42
  15.9 5.4 %collective-permute-start.4 = (f32[2,32,128]{2,1,0:T(8,128)S(1)}, f32[2,32,128]{2,1,0:T(8,128)S(1)}, u32[]{:S(2)}, u32[]{:S(2)}) collective-permute-start(f32[2,32,128]{2,1,0:T(8,128)S(1)} %get-tuple-element.39), channel_id=1, source_target_pairs={{0,4},{2,6},{4,0},{6,2},{1,5},{3,7},{5,1},{7,3},{8,12},{10,14},{12... | collective-permute-start | bytes 98312 | tf_op jit(solution)/shard_map/ppermute | solution.py:42
  18.2 3.9 %collective-permute-start.5 = (f32[2,32,128]{2,1,0:T(8,128)S(1)}, f32[2,32,128]{2,1,0:T(8,128)S(1)}, u32[]{:S(2)}, u32[]{:S(2)}) collective-permute-start(f32[2,32,128]{2,1,0:T(8,128)S(1)} %get-tuple-element.38), channel_id=1, source_target_pairs={{0,6},{2,0},{4,2},{6,4},{1,7},{3,1},{5,3},{7,5},{8,14},{10,8},{12,... | collective-permute-start | bytes 98312 | tf_op jit(solution)/shard_map/ppermute | solution.py:42
  22.1 9.7 %collective-permute-start.7 = (f32[2,256,128]{2,1,0:T(8,128)S(1)}, f32[2,256,128]{2,1,0:T(8,128)S(1)}, u32[]{:S(2)}, u32[]{:S(2)}) collective-permute-start(f32[2,256,128]{2,1,0:T(8,128)S(1)} %collective-permute-done.6.refs_1_), channel_id=1, source_target_pairs={{0,2},{2,4},{4,6},{6,0},{1,3},{3,5},{5,7},{7,1},{8,10},{10,12},{12... | collective-permute-start | bytes 786440 | tf_op jit(solution)/shard_map/ppermute | solution.py:42
  23.2 6.3 %collective-permute-start.10 = (f32[4,2,32,128]{3,2,1,0:T(8,128)S(1)}, f32[4,2,32,128]{3,2,1,0:T(8,128)S(1)}, u32[]{:S(2)}, u32[]{:S(2)}) collective-permute-start(f32[4,2,32,128]{3,2,1,0:T(8,128)S(1)} %pad_maximum_fusion.2.refs_4_), channel_id=1, source_target_pairs={{0,16},{8,24},{16,0},{24,8},{1,17},{9,25},{17,1},{25,9},{2,18},{10... | collective-permute-start | bytes 393224 | tf_op jit(solution)/shard_map/ppermute | solution.py:42
  24.2 5.3 %collective-permute-start.11 = (f32[4,2,32,128]{3,2,1,0:T(8,128)S(1)}, f32[4,2,32,128]{3,2,1,0:T(8,128)S(1)}, u32[]{:S(2)}, u32[]{:S(2)}) collective-permute-start(f32[4,2,32,128]{3,2,1,0:T(8,128)S(1)} %pad_maximum_fusion.2.refs_4_), channel_id=1, source_target_pairs={{0,24},{8,0},{16,8},{24,16},{1,25},{9,1},{17,9},{25,17},{2,26},{10... | collective-permute-start | bytes 393224 | tf_op jit(solution)/shard_map/ppermute | solution.py:42
  25.9 5.9 %collective-permute-start.9 = (f32[4,2,32,128]{3,2,1,0:T(8,128)S(1)}, f32[4,2,32,128]{3,2,1,0:T(8,128)S(1)}, u32[]{:S(2)}, u32[]{:S(2)}) collective-permute-start(f32[4,2,32,128]{3,2,1,0:T(8,128)S(1)} %pad_maximum_fusion.2.refs_4_), channel_id=1, source_target_pairs={{0,8},{8,16},{16,24},{24,0},{1,9},{9,17},{17,25},{25,1},{2,10},{10... | collective-permute-start | bytes 393224 | tf_op jit(solution)/shard_map/ppermute | solution.py:42
  33.4 1.8 %collective-permute-start.12 = (f32[2,384,128]{2,1,0:T(8,128)S(1)}, f32[2,384,128]{2,1,0:T(8,128)S(1)}, u32[]{:S(2)}, u32[]{:S(2)}) collective-permute-start(f32[2,384,128]{2,1,0:T(8,128)S(1)} %shard_map.59), channel_id=1, source_target_pairs={{0,1},{1,0},{2,3},{3,2},{4,5},{5,4},{6,7},{7,6},{8,9},{9,8},{10,11... | collective-permute-start | bytes 1179656 | tf_op jit(solution)/shard_map/ppermute | solution.py:42
  35.5 5.9 %collective-permute-start.13 = (f32[72,128]{1,0:T(8,128)S(1)}, f32[72,128]{1,0:T(8,128)S(1)}, u32[]{:S(2)}, u32[]{:S(2)}) collective-permute-start(f32[72,128]{1,0:T(8,128)S(1)} %get-tuple-element.44), channel_id=1, source_target_pairs={{0,6},{2,0},{4,2},{6,4},{1,7},{3,1},{5,3},{7,5},{8,14},{10,8},{12,... | collective-permute-start | bytes 110600 | tf_op jit(solution)/shard_map/ppermute | solution.py:42
  38.8 4.9 %collective-permute-start.14 = (f32[72,128]{1,0:T(8,128)S(1)}, f32[72,128]{1,0:T(8,128)S(1)}, u32[]{:S(2)}, u32[]{:S(2)}) collective-permute-start(f32[72,128]{1,0:T(8,128)S(1)} %get-tuple-element.43), channel_id=1, source_target_pairs={{0,4},{2,6},{4,0},{6,2},{1,5},{3,7},{5,1},{7,3},{8,12},{10,14},{12... | collective-permute-start | bytes 110600 | tf_op jit(solution)/shard_map/ppermute | solution.py:42
  39.5 5.8 %collective-permute-start.15 = (f32[72,128]{1,0:T(8,128)S(1)}, f32[72,128]{1,0:T(8,128)S(1)}, u32[]{:S(2)}, u32[]{:S(2)}) collective-permute-start(f32[72,128]{1,0:T(8,128)S(1)} %get-tuple-element.42), channel_id=1, source_target_pairs={{0,2},{2,4},{4,6},{6,0},{1,3},{3,5},{5,7},{7,1},{8,10},{10,12},{12... | collective-permute-start | bytes 110600 | tf_op jit(solution)/shard_map/ppermute | solution.py:42
  45.4 4.6 %collective-permute-start.16 = (f32[2,512]{1,0:T(2,128)S(1)}, f32[2,512]{1,0:T(2,128)S(1)}, u32[]{:S(2)}, u32[]{:S(2)}) collective-permute-start(f32[2,512]{1,0:T(2,128)S(1)} %pad_maximum_fusion.7), channel_id=1, source_target_pairs={{0,8},{8,16},{16,24},{24,0},{1,9},{9,17},{17,25},{25,1},{2,10},{10... | collective-permute-start | bytes 12296 | tf_op jit(solution)/shard_map/ppermute | solution.py:42
  46.0 4.0 %collective-permute-start.17 = (f32[2,512]{1,0:T(2,128)S(1)}, f32[2,512]{1,0:T(2,128)S(1)}, u32[]{:S(2)}, u32[]{:S(2)}) collective-permute-start(f32[2,512]{1,0:T(2,128)S(1)} %pad_maximum_fusion.7), channel_id=1, source_target_pairs={{0,16},{8,24},{16,0},{24,8},{1,17},{9,25},{17,1},{25,9},{2,18},{10... | collective-permute-start | bytes 12296 | tf_op jit(solution)/shard_map/ppermute | solution.py:42
  46.7 3.9 %collective-permute-start.18 = (f32[2,512]{1,0:T(2,128)S(1)}, f32[2,512]{1,0:T(2,128)S(1)}, u32[]{:S(2)}, u32[]{:S(2)}) collective-permute-start(f32[2,512]{1,0:T(2,128)S(1)} %pad_maximum_fusion.7), channel_id=1, source_target_pairs={{0,24},{8,0},{16,8},{24,16},{1,25},{9,1},{17,9},{25,17},{2,26},{10... | collective-permute-start | bytes 12296 | tf_op jit(solution)/shard_map/ppermute | solution.py:42

commit v18 on v17

--- a/solution.py
+++ b/solution.py
@@ -85,9 +85,8 @@
         for shift in range(1, deep):
             slots.append(shifted(columns_of(scaled, (z + shift) % deep), "z", deep, shift))
         if deep > 1:
-            slots, far[1] = lax.optimization_barrier((slots, far[1]))
-            for d in late:
-                far[d] = shifted(far[d - 1], "z", deep, 1)
+            for d in reversed(late):
+                far[d] = shifted(far[d + 1], "z", deep, deep - 1)
         slots = gathered(jnp.stack(slots), "row", rows)
 
         count = jnp.arange(deep, dtype=jnp.int32)

time: 51.3 us -> 51.1 us (level)
  waiting for transfers between devices: 13.9 us -> 13.3 us
    ppermute x19, waiting for transfers between devices: 13.9 us -> 13.3 us  [shifted(): lax.ppermute(array, axis, [(i, (i + shift) % size) for i in range(size)])]
  transfers between devices with their start and end apart: 19 -> 19, of which waited for: 10 -> 8; matrix products, arithmetic and copies ran while one was open for 7% -> 7% of each run, Pallas kernels for 0% -> 0%
where the time goes in v18:
time: 51.1 us; the launch traced here: 50.9 us
  starting transfers between devices  29.7 us (58%)
  waiting for transfers between devices  13.3 us (26%)
  other arithmetic  2.84 us (6%)
  matrix products  1.62 us (3%)
  Pallas kernels  1.61 us (3%)
  local copies, waits for them, and re-layouts  0.95 us (2%)
  between operations  0.87 us (2%)
    ppermute x19, starting transfers between devices, shifted(): lax.ppermute(array, axis, [(i, (i + shift) % size) for i in range(size)])  29.7 us
    ppermute x19, waiting for transfers between devices, shifted(): lax.ppermute(array, axis, [(i, (i + shift) % size) for i in range(size)])  13.3 us
    dot_general x1, matrix products, per_device(): partial = jnp.einsum('srw,swv->srv', mine, factor_inv, precision=highest)  1.62 us
    pallas_call x1, Pallas kernels, per_device(): pl.pallas_call(functools.partial(multiply_tiles, deep, rows), out_shape=j...  1.61 us
  transfers between devices with their start and end apart: 19, of which 8 were waited for; matrix products, arithmetic and copies ran while one was open for 7% of the time, Pallas kernels for 0%

profile of v18, /device:TPU:0, one launch (start us, length us, event | category | flops | bytes accessed | tf_op | source)
XLA Modules:
  0.0 50.9 jit_solution(16458683034215387861)
XLA Ops:
  0.6 0.0 copy-start
  0.6 3.1 %collective-permute-start = (f32[2,256,128]{2,1,0:T(8,128)}, f32[2,256,128]{2,1,0:T(8,128)S(1)}, u32[]{:S(2)}, u32[]{:S(2)}) collective-permute-start(f32[2,256,128]{2,1,0:T(8,128)} %refs_0_.1), channel_id=1, source_target_pairs={{0,2},{2,4},{4,6},{6,0},{1,3},{3,5},{5,7},{7,1},{8,10},{10,12},{12... | collective-permute-start | bytes 786440 | tf_op jit(solution)/shard_map/ppermute | solution.py:42
  3.7 1.6 %fusion = f32[2,128,512]{2,1,0:T(8,128)S(1)} fusion(f32[2,128,512]{2,1,0:T(8,128)} %param.6, f32[2,128,512]{2,1,0:T(8,128)S(1)} %copy-done, s32[]{:T(128)S(6)} %select_n.231), kind=kOutput, calls=%fused_computation.10 | convolution fusion | flops 201326592 | bytes 1179652 | tf_op jit(solution)/shard_map/srw,swv->srv/dot_general | solution.py:69
  5.4 0.0 copy-start.1
  5.4 1.5 %collective-permute-start.3 = (f32[2,32,512]{2,1,0:T(8,128)S(1)}, f32[2,32,512]{2,1,0:T(8,128)S(1)}, u32[]{:S(2)}, u32[]{:S(2)}) collective-permute-start(f32[2,32,512]{2,1,0:T(8,128)S(1)} %get-tuple-element.20), channel_id=1, source_target_pairs={{0,8},{8,16},{16,24},{24,0},{1,9},{9,17},{17,25},{25,1},{2,10},{10... | collective-permute-start | bytes 393224 | tf_op jit(solution)/shard_map/ppermute | solution.py:42
  7.0 1.5 %collective-permute-start.4 = (f32[2,32,512]{2,1,0:T(8,128)S(1)}, f32[2,32,512]{2,1,0:T(8,128)S(1)}, u32[]{:S(2)}, u32[]{:S(2)}) collective-permute-start(f32[2,32,512]{2,1,0:T(8,128)S(1)} %get-tuple-element.19), channel_id=1, source_target_pairs={{0,16},{8,24},{16,0},{24,8},{1,17},{9,25},{17,1},{25,9},{2,18},{10... | collective-permute-start | bytes 393224 | tf_op jit(solution)/shard_map/ppermute | solution.py:42
  8.5 1.4 %collective-permute-start.5 = (f32[2,32,512]{2,1,0:T(8,128)S(1)}, f32[2,32,512]{2,1,0:T(8,128)S(1)}, u32[]{:S(2)}, u32[]{:S(2)}) collective-permute-start(f32[2,32,512]{2,1,0:T(8,128)S(1)} %get-tuple-element.18), channel_id=1, source_target_pairs={{0,24},{8,0},{16,8},{24,16},{1,25},{9,1},{17,9},{25,17},{2,26},{10... | collective-permute-start | bytes 393224 | tf_op jit(solution)/shard_map/ppermute | solution.py:42
  9.9 3.0 %collective-permute-start.1 = (f32[2,256,128]{2,1,0:T(8,128)S(1)}, f32[2,256,128]{2,1,0:T(8,128)S(1)}, u32[]{:S(2)}, u32[]{:S(2)}) collective-permute-start(f32[2,256,128]{2,1,0:T(8,128)S(1)} %copy-done.1), channel_id=1, source_target_pairs={{0,6},{2,0},{4,2},{6,4},{1,7},{3,1},{5,3},{7,5},{8,14},{10,8},{12,... | collective-permute-start | bytes 786440 | tf_op jit(solution)/shard_map/ppermute | solution.py:42
  12.9 0.7 %copy-done.2 = s32[2,4]{1,0:T(2,128)S(1)} copy-done((s32[2,4]{1,0:T(2,128)S(1)}, s32[2,4]{1,0:T(2,128)}, u32[]{:S(2)}) %copy-start.2) | copy-done | bytes 56
  13.6 0.1 select_reduce_fusion
  13.7 0.1 sub.51
  13.8 0.9 %multiply_reduce_fusion.1 = f32[2,128]{1,0:T(2,128)S(1)} fusion(f32[2,128,512]{2,1,0:T(8,128)} %param.6, s32[]{:T(128)S(6)} %select_n.239), kind=kLoop, calls=%fused_computation.9 | loop fusion | flops 65280 | bytes 132100 | tf_op jit(solution)/shard_map/reduce_sum | solution.py:77
  14.7 0.0 collective-permute-done.4
  14.7 0.0 collective-permute-done.5
  14.8 1.1 %collective-permute-start.6 = (f32[2,32,128]{2,1,0:T(8,128)S(1)}, f32[2,32,128]{2,1,0:T(8,128)S(1)}, u32[]{:S(2)}, u32[]{:S(2)}) collective-permute-start(f32[2,32,128]{2,1,0:T(8,128)S(1)} %get-tuple-element.31), channel_id=1, source_target_pairs={{0,2},{2,4},{4,6},{6,0},{1,3},{3,5},{5,7},{7,1},{8,10},{10,12},{12... | collective-permute-start | bytes 98312 | tf_op jit(solution)/shard_map/ppermute | solution.py:42
  15.9 2.3 %collective-permute-start.7 = (f32[2,32,128]{2,1,0:T(8,128)S(1)}, f32[2,32,128]{2,1,0:T(8,128)S(1)}, u32[]{:S(2)}, u32[]{:S(2)}) collective-permute-start(f32[2,32,128]{2,1,0:T(8,128)S(1)} %get-tuple-element.30), channel_id=1, source_target_pairs={{0,4},{2,6},{4,0},{6,2},{1,5},{3,7},{5,1},{7,3},{8,12},{10,14},{12... | collective-permute-start | bytes 98312 | tf_op jit(solution)/shard_map/ppermute | solution.py:42
  18.2 1.7 %collective-permute-start.8 = (f32[2,32,128]{2,1,0:T(8,128)S(1)}, f32[2,32,128]{2,1,0:T(8,128)S(1)}, u32[]{:S(2)}, u32[]{:S(2)}) collective-permute-start(f32[2,32,128]{2,1,0:T(8,128)S(1)} %get-tuple-element.29), channel_id=1, source_target_pairs={{0,6},{2,0},{4,2},{6,4},{1,7},{3,1},{5,3},{7,5},{8,14},{10,8},{12,... | collective-permute-start | bytes 98312 | tf_op jit(solution)/shard_map/ppermute | solution.py:42
  19.9 0.0 collective-permute-done.1.refs_3_
  19.9 2.6 %collective-permute-start.2 = (f32[2,256,128]{2,1,0:T(8,128)S(1)}, f32[2,256,128]{2,1,0:T(8,128)S(1)}, u32[]{:S(2)}, u32[]{:S(2)}) collective-permute-start(f32[2,256,128]{2,1,0:T(8,128)S(1)} %collective-permute-done.1.refs_3_), channel_id=1, source_target_pairs={{0,6},{2,0},{4,2},{6,4},{1,7},{3,1},{5,3},{7,5},{8,14},{10,8},{12,... | collective-permute-start | bytes 786440 | tf_op jit(solution)/shard_map/ppermute | solution.py:42
  22.5 0.0 collective-permute-done.7
  22.5 0.0 collective-permute-done.8
  22.5 1.5 %collective-permute-start.10 = (f32[4,2,32,128]{3,2,1,0:T(8,128)S(1)}, f32[4,2,32,128]{3,2,1,0:T(8,128)S(1)}, u32[]{:S(2)}, u32[]{:S(2)}) collective-permute-start(f32[4,2,32,128]{3,2,1,0:T(8,128)S(1)} %pad_maximum_fusion.2.refs_4_), channel_id=1, source_target_pairs={{0,16},{8,24},{16,0},{24,8},{1,17},{9,25},{17,1},{25,9},{2,18},{10... | collective-permute-start | bytes 393224 | tf_op jit(solution)/shard_map/ppermute | solution.py:42
  24.0 1.8 %collective-permute-start.11 = (f32[4,2,32,128]{3,2,1,0:T(8,128)S(1)}, f32[4,2,32,128]{3,2,1,0:T(8,128)S(1)}, u32[]{:S(2)}, u32[]{:S(2)}) collective-permute-start(f32[4,2,32,128]{3,2,1,0:T(8,128)S(1)} %pad_maximum_fusion.2.refs_4_), channel_id=1, source_target_pairs={{0,24},{8,0},{16,8},{24,16},{1,25},{9,1},{17,9},{25,17},{2,26},{10... | collective-permute-start | bytes 393224 | tf_op jit(solution)/shard_map/ppermute | solution.py:42
  25.8 0.2 collective-permute-start.9
  26.0 0.1 pad_add_fusion.place
  26.1 2.8 %collective-permute-done.10.refs_6_ = f32[4,2,32,128]{3,2,1,0:T(8,128)S(1)} collective-permute-done((f32[4,2,32,128]{3,2,1,0:T(8,128)S(1)}, f32[4,2,32,128]{3,2,1,0:T(8,128)S(1)}, u32[]{:S(2)}, u32[]{:S(2)}) %collective-permute-start.10) | collective-permute-done | bytes 131104 | tf_op jit(solution)/shard_map/ppermute | solution.py:42
  28.9 0.0 collective-permute-done.11.refs_7_
  29.0 2.7 %collective-permute-done.9.refs_5_ = f32[4,2,32,128]{3,2,1,0:T(8,128)S(1)} collective-permute-done((f32[4,2,32,128]{3,2,1,0:T(8,128)S(1)}, f32[4,2,32,128]{3,2,1,0:T(8,128)S(1)}, u32[]{:S(2)}, u32[]{:S(2)}) %collective-permute-start.9) | collective-permute-done | bytes 131104 | tf_op jit(solution)/shard_map/ppermute | solution.py:42
  31.7 1.6 %shard_map.59 = f32[2,384,128]{2,1,0:T(8,128)S(1)} custom-call(s32[13]{0:T(128)S(1)} %pad_add_fusion.place, f32[2,256,128]{2,1,0:T(8,128)S(1)} %copy-done.1, f32[2,256,128]{2,1,0:T(8,128)S(1)} %collective-permute-done.refs_1_, f32[2,256,128]{2,1,0:T(8,128)S(1)} %collective-permute-done.2.refs_2_, f32[2,256,128]{2,1,0:T(8,128)S(1)} %collective-permute-done.1.refs_3_, ...), custom_call_target="tpu_custom_call" | custom-call | tf_op jit(solution)/shard_map/pallas_call | solution.py:103
  33.3 0.1 collective-permute-start.12
  33.4 0.1 pad.15.clone
  33.5 1.6 %collective-permute-done.12 = f32[2,384,128]{2,1,0:T(8,128)S(1)} collective-permute-done((f32[2,384,128]{2,1,0:T(8,128)S(1)}, f32[2,384,128]{2,1,0:T(8,128)S(1)}, u32[]{:S(2)}, u32[]{:S(2)}) %collective-permute-start.12) | collective-permute-done | bytes 393248 | tf_op jit(solution)/shard_map/ppermute | solution.py:42
  35.1 0.1 multiply_reduce_fusion
  35.3 0.1 fusion.4
  35.4 3.9 %collective-permute-start.13 = (f32[72,128]{1,0:T(8,128)S(1)}, f32[72,128]{1,0:T(8,128)S(1)}, u32[]{:S(2)}, u32[]{:S(2)}) collective-permute-start(f32[72,128]{1,0:T(8,128)S(1)} %get-tuple-element.34), channel_id=1, source_target_pairs={{0,6},{2,0},{4,2},{6,4},{1,7},{3,1},{5,3},{7,5},{8,14},{10,8},{12,... | collective-permute-start | bytes 110600 | tf_op jit(solution)/shard_map/ppermute | solution.py:42
  39.2 0.6 %collective-permute-start.15 = (f32[72,128]{1,0:T(8,128)S(1)}, f32[72,128]{1,0:T(8,128)S(1)}, u32[]{:S(2)}, u32[]{:S(2)}) collective-permute-start(f32[72,128]{1,0:T(8,128)S(1)} %get-tuple-element.32), channel_id=1, source_target_pairs={{0,2},{2,4},{4,6},{6,0},{1,3},{3,5},{5,7},{7,1},{8,10},{10,12},{12... | collective-permute-start | bytes 110600 | tf_op jit(solution)/shard_map/ppermute | solution.py:42
  39.9 1.2 %collective-permute-done.13 = f32[72,128]{1,0:T(8,128)S(1)} collective-permute-done((f32[72,128]{1,0:T(8,128)S(1)}, f32[72,128]{1,0:T(8,128)S(1)}, u32[]{:S(2)}, u32[]{:S(2)}) %collective-permute-start.13) | collective-permute-done | bytes 36896 | tf_op jit(solution)/shard_map/ppermute | solution.py:42
  41.1 3.2 %collective-permute-done.14 = f32[72,128]{1,0:T(8,128)S(1)} collective-permute-done((f32[72,128]{1,0:T(8,128)S(1)}, f32[72,128]{1,0:T(8,128)S(1)}, u32[]{:S(2)}, u32[]{:S(2)}) %collective-permute-start.14) | collective-permute-done | bytes 36896 | tf_op jit(solution)/shard_map/ppermute | solution.py:42
  44.3 0.7 %collective-permute-done.15 = f32[72,128]{1,0:T(8,128)S(1)} collective-permute-done((f32[72,128]{1,0:T(8,128)S(1)}, f32[72,128]{1,0:T(8,128)S(1)}, u32[]{:S(2)}, u32[]{:S(2)}) %collective-permute-start.15) | collective-permute-done | bytes 36896 | tf_op jit(solution)/shard_map/ppermute | solution.py:42
  45.0 0.1 select_select_fusion.2
  45.1 0.1 select_select_fusion.3
  45.2 0.2 collective-permute-start.16
  45.4 1.0 %collective-permute-start.17 = (f32[2,512]{1,0:T(2,128)S(1)}, f32[2,512]{1,0:T(2,128)S(1)}, u32[]{:S(2)}, u32[]{:S(2)}) collective-permute-start(f32[2,512]{1,0:T(2,128)S(1)} %pad_maximum_fusion.7), channel_id=1, source_target_pairs={{0,16},{8,24},{16,0},{24,8},{1,17},{9,25},{17,1},{25,9},{2,18},{10... | collective-permute-start | bytes 12296 | tf_op jit(solution)/shard_map/ppermute | solution.py:42
  46.4 2.2 %collective-permute-start.18 = (f32[2,512]{1,0:T(2,128)S(1)}, f32[2,512]{1,0:T(2,128)S(1)}, u32[]{:S(2)}, u32[]{:S(2)}) collective-permute-start(f32[2,512]{1,0:T(2,128)S(1)} %pad_maximum_fusion.7), channel_id=1, source_target_pairs={{0,24},{8,0},{16,8},{24,16},{1,25},{9,1},{17,9},{25,17},{2,26},{10... | collective-permute-start | bytes 12296 | tf_op jit(solution)/shard_map/ppermute | solution.py:42
  48.6 0.7 %slice_negate_fusion = f32[64,512]{1,0:T(8,128)} fusion(f32[72,512]{1,0:T(8,128)S(1)} %pad_maximum_fusion.1), kind=kLoop, calls=%fused_computation.4 | loop fusion | flops 32768 | bytes 262144 | tf_op jit(solution)/shard_map/neg | solution.py:130
  49.3 0.5 collective-permute-done.16
  49.7 0.6 %collective-permute-done.18 = f32[2,512]{1,0:T(2,128)S(1)} collective-permute-done((f32[2,512]{1,0:T(2,128)S(1)}, f32[2,512]{1,0:T(2,128)S(1)}, u32[]{:S(2)}, u32[]{:S(2)}) %collective-permute-start.18) | collective-permute-done | bytes 4128 | tf_op jit(solution)/shard_map/ppermute | solution.py:42
  50.3 0.6 %add_add_fusion.1 = f32[2,512]{1,0:T(2,128)} fusion(f32[2,512]{1,0:T(2,128)S(1)} %collective-permute-done.18, f32[2,512]{1,0:T(2,128)S(1)} %collective-permute-done.17, f32[2,512]{1,0:T(2,128)S(1)} %pad_maximum_fusion.7, f32[2,512]{1,0:T(2,128)S(1)} %collective-permute-done.16), kind=kLoop, calls=%fused_computation.26 | loop fusion | flops 3072 | bytes 20480 | tf_op jit(solution)/shard_map/add | solution.py:134
  (25 shorter events, 0.3 us)
Async XLA Ops:
  0.6 3.1 %copy-start = (f32[2,128,512]{2,1,0:T(8,128)S(1)}, f32[2,128,512]{2,1,0:T(8,128)}, u32[]{:S(2)}) copy-start(f32[2,128,512]{2,1,0:T(8,128)} %param.5) | copy-start | bytes 1572868
  0.6 25.5 %collective-permute-start = (f32[2,256,128]{2,1,0:T(8,128)}, f32[2,256,128]{2,1,0:T(8,128)S(1)}, u32[]{:S(2)}, u32[]{:S(2)}) collective-permute-start(f32[2,256,128]{2,1,0:T(8,128)} %refs_0_.1), channel_id=1, source_target_pairs={{0,2},{2,4},{4,6},{6,0},{1,3},{3,5},{5,7},{7,1},{8,10},{10,12},{12... | collective-permute-start | bytes 786440 | tf_op jit(solution)/shard_map/ppermute | solution.py:42
  5.4 4.6 %copy-start.1 = (f32[2,256,128]{2,1,0:T(8,128)S(1)}, f32[2,256,128]{2,1,0:T(8,128)}, u32[]{:S(2)}) copy-start(f32[2,256,128]{2,1,0:T(8,128)} %refs_0_.1) | copy-start | bytes 786436
  5.4 9.3 %collective-permute-start.3 = (f32[2,32,512]{2,1,0:T(8,128)S(1)}, f32[2,32,512]{2,1,0:T(8,128)S(1)}, u32[]{:S(2)}, u32[]{:S(2)}) collective-permute-start(f32[2,32,512]{2,1,0:T(8,128)S(1)} %get-tuple-element.20), channel_id=1, source_target_pairs={{0,8},{8,16},{16,24},{24,0},{1,9},{9,17},{17,25},{25,1},{2,10},{10... | collective-permute-start | bytes 393224 | tf_op jit(solution)/shard_map/ppermute | solution.py:42
  7.0 7.8 %collective-permute-start.4 = (f32[2,32,512]{2,1,0:T(8,128)S(1)}, f32[2,32,512]{2,1,0:T(8,128)S(1)}, u32[]{:S(2)}, u32[]{:S(2)}) collective-permute-start(f32[2,32,512]{2,1,0:T(8,128)S(1)} %get-tuple-element.19), channel_id=1, source_target_pairs={{0,16},{8,24},{16,0},{24,8},{1,17},{9,25},{17,1},{25,9},{2,18},{10... | collective-permute-start | bytes 393224 | tf_op jit(solution)/shard_map/ppermute | solution.py:42
  8.5 6.3 %collective-permute-start.5 = (f32[2,32,512]{2,1,0:T(8,128)S(1)}, f32[2,32,512]{2,1,0:T(8,128)S(1)}, u32[]{:S(2)}, u32[]{:S(2)}) collective-permute-start(f32[2,32,512]{2,1,0:T(8,128)S(1)} %get-tuple-element.18), channel_id=1, source_target_pairs={{0,24},{8,0},{16,8},{24,16},{1,25},{9,1},{17,9},{25,17},{2,26},{10... | collective-permute-start | bytes 393224 | tf_op jit(solution)/shard_map/ppermute | solution.py:42
  9.9 9.9 %collective-permute-start.1 = (f32[2,256,128]{2,1,0:T(8,128)S(1)}, f32[2,256,128]{2,1,0:T(8,128)S(1)}, u32[]{:S(2)}, u32[]{:S(2)}) collective-permute-start(f32[2,256,128]{2,1,0:T(8,128)S(1)} %copy-done.1), channel_id=1, source_target_pairs={{0,6},{2,0},{4,2},{6,4},{1,7},{3,1},{5,3},{7,5},{8,14},{10,8},{12,... | collective-permute-start | bytes 786440 | tf_op jit(solution)/shard_map/ppermute | solution.py:42
  12.9 0.7 %copy-start.2 = (s32[2,4]{1,0:T(2,128)S(1)}, s32[2,4]{1,0:T(2,128)}, u32[]{:S(2)}) copy-start(s32[2,4]{1,0:T(2,128)} %param.7) | copy-start | bytes 100
  14.8 7.6 %collective-permute-start.6 = (f32[2,32,128]{2,1,0:T(8,128)S(1)}, f32[2,32,128]{2,1,0:T(8,128)S(1)}, u32[]{:S(2)}, u32[]{:S(2)}) collective-permute-start(f32[2,32,128]{2,1,0:T(8,128)S(1)} %get-tuple-element.31), channel_id=1, source_target_pairs={{0,2},{2,4},{4,6},{6,0},{1,3},{3,5},{5,7},{7,1},{8,10},{10,12},{12... | collective-permute-start | bytes 98312 | tf_op jit(solution)/shard_map/ppermute | solution.py:42
  15.9 6.5 %collective-permute-start.7 = (f32[2,32,128]{2,1,0:T(8,128)S(1)}, f32[2,32,128]{2,1,0:T(8,128)S(1)}, u32[]{:S(2)}, u32[]{:S(2)}) collective-permute-start(f32[2,32,128]{2,1,0:T(8,128)S(1)} %get-tuple-element.30), channel_id=1, source_target_pairs={{0,4},{2,6},{4,0},{6,2},{1,5},{3,7},{5,1},{7,3},{8,12},{10,14},{12... | collective-permute-start | bytes 98312 | tf_op jit(solution)/shard_map/ppermute | solution.py:42
  18.2 4.3 %collective-permute-start.8 = (f32[2,32,128]{2,1,0:T(8,128)S(1)}, f32[2,32,128]{2,1,0:T(8,128)S(1)}, u32[]{:S(2)}, u32[]{:S(2)}) collective-permute-start(f32[2,32,128]{2,1,0:T(8,128)S(1)} %get-tuple-element.29), channel_id=1, source_target_pairs={{0,6},{2,0},{4,2},{6,4},{1,7},{3,1},{5,3},{7,5},{8,14},{10,8},{12,... | collective-permute-start | bytes 98312 | tf_op jit(solution)/shard_map/ppermute | solution.py:42
  19.9 11.8 %collective-permute-start.2 = (f32[2,256,128]{2,1,0:T(8,128)S(1)}, f32[2,256,128]{2,1,0:T(8,128)S(1)}, u32[]{:S(2)}, u32[]{:S(2)}) collective-permute-start(f32[2,256,128]{2,1,0:T(8,128)S(1)} %collective-permute-done.1.refs_3_), channel_id=1, source_target_pairs={{0,6},{2,0},{4,2},{6,4},{1,7},{3,1},{5,3},{7,5},{8,14},{10,8},{12,... | collective-permute-start | bytes 786440 | tf_op jit(solution)/shard_map/ppermute | solution.py:42
  22.5 6.4 %collective-permute-start.10 = (f32[4,2,32,128]{3,2,1,0:T(8,128)S(1)}, f32[4,2,32,128]{3,2,1,0:T(8,128)S(1)}, u32[]{:S(2)}, u32[]{:S(2)}) collective-permute-start(f32[4,2,32,128]{3,2,1,0:T(8,128)S(1)} %pad_maximum_fusion.2.refs_4_), channel_id=1, source_target_pairs={{0,16},{8,24},{16,0},{24,8},{1,17},{9,25},{17,1},{25,9},{2,18},{10... | collective-permute-start | bytes 393224 | tf_op jit(solution)/shard_map/ppermute | solution.py:42
  24.0 5.0 %collective-permute-start.11 = (f32[4,2,32,128]{3,2,1,0:T(8,128)S(1)}, f32[4,2,32,128]{3,2,1,0:T(8,128)S(1)}, u32[]{:S(2)}, u32[]{:S(2)}) collective-permute-start(f32[4,2,32,128]{3,2,1,0:T(8,128)S(1)} %pad_maximum_fusion.2.refs_4_), channel_id=1, source_target_pairs={{0,24},{8,0},{16,8},{24,16},{1,25},{9,1},{17,9},{25,17},{2,26},{10... | collective-permute-start | bytes 393224 | tf_op jit(solution)/shard_map/ppermute | solution.py:42
  25.8 5.9 %collective-permute-start.9 = (f32[4,2,32,128]{3,2,1,0:T(8,128)S(1)}, f32[4,2,32,128]{3,2,1,0:T(8,128)S(1)}, u32[]{:S(2)}, u32[]{:S(2)}) collective-permute-start(f32[4,2,32,128]{3,2,1,0:T(8,128)S(1)} %pad_maximum_fusion.2.refs_4_), channel_id=1, source_target_pairs={{0,8},{8,16},{16,24},{24,0},{1,9},{9,17},{17,25},{25,1},{2,10},{10... | collective-permute-start | bytes 393224 | tf_op jit(solution)/shard_map/ppermute | solution.py:42
  33.3 1.8 %collective-permute-start.12 = (f32[2,384,128]{2,1,0:T(8,128)S(1)}, f32[2,384,128]{2,1,0:T(8,128)S(1)}, u32[]{:S(2)}, u32[]{:S(2)}) collective-permute-start(f32[2,384,128]{2,1,0:T(8,128)S(1)} %shard_map.59), channel_id=1, source_target_pairs={{0,1},{1,0},{2,3},{3,2},{4,5},{5,4},{6,7},{7,6},{8,9},{9,8},{10,11... | collective-permute-start | bytes 1179656 | tf_op jit(solution)/shard_map/ppermute | solution.py:42
  35.4 5.7 %collective-permute-start.13 = (f32[72,128]{1,0:T(8,128)S(1)}, f32[72,128]{1,0:T(8,128)S(1)}, u32[]{:S(2)}, u32[]{:S(2)}) collective-permute-start(f32[72,128]{1,0:T(8,128)S(1)} %get-tuple-element.34), channel_id=1, source_target_pairs={{0,6},{2,0},{4,2},{6,4},{1,7},{3,1},{5,3},{7,5},{8,14},{10,8},{12,... | collective-permute-start | bytes 110600 | tf_op jit(solution)/shard_map/ppermute | solution.py:42
  39.2 5.0 %collective-permute-start.14 = (f32[72,128]{1,0:T(8,128)S(1)}, f32[72,128]{1,0:T(8,128)S(1)}, u32[]{:S(2)}, u32[]{:S(2)}) collective-permute-start(f32[72,128]{1,0:T(8,128)S(1)} %get-tuple-element.33), channel_id=1, source_target_pairs={{0,4},{2,6},{4,0},{6,2},{1,5},{3,7},{5,1},{7,3},{8,12},{10,14},{12... | collective-permute-start | bytes 110600 | tf_op jit(solution)/shard_map/ppermute | solution.py:42
  39.2 5.8 %collective-permute-start.15 = (f32[72,128]{1,0:T(8,128)S(1)}, f32[72,128]{1,0:T(8,128)S(1)}, u32[]{:S(2)}, u32[]{:S(2)}) collective-permute-start(f32[72,128]{1,0:T(8,128)S(1)} %get-tuple-element.32), channel_id=1, source_target_pairs={{0,2},{2,4},{4,6},{6,0},{1,3},{3,5},{5,7},{7,1},{8,10},{10,12},{12... | collective-permute-start | bytes 110600 | tf_op jit(solution)/shard_map/ppermute | solution.py:42
  45.2 4.6 %collective-permute-start.16 = (f32[2,512]{1,0:T(2,128)S(1)}, f32[2,512]{1,0:T(2,128)S(1)}, u32[]{:S(2)}, u32[]{:S(2)}) collective-permute-start(f32[2,512]{1,0:T(2,128)S(1)} %pad_maximum_fusion.7), channel_id=1, source_target_pairs={{0,8},{8,16},{16,24},{24,0},{1,9},{9,17},{17,25},{25,1},{2,10},{10... | collective-permute-start | bytes 12296 | tf_op jit(solution)/shard_map/ppermute | solution.py:42
  45.4 4.4 %collective-permute-start.17 = (f32[2,512]{1,0:T(2,128)S(1)}, f32[2,512]{1,0:T(2,128)S(1)}, u32[]{:S(2)}, u32[]{:S(2)}) collective-permute-start(f32[2,512]{1,0:T(2,128)S(1)} %pad_maximum_fusion.7), channel_id=1, source_target_pairs={{0,16},{8,24},{16,0},{24,8},{1,17},{9,25},{17,1},{25,9},{2,18},{10... | collective-permute-start | bytes 12296 | tf_op jit(solution)/shard_map/ppermute | solution.py:42
  46.4 3.9 %collective-permute-start.18 = (f32[2,512]{1,0:T(2,128)S(1)}, f32[2,512]{1,0:T(2,128)S(1)}, u32[]{:S(2)}, u32[]{:S(2)}) collective-permute-start(f32[2,512]{1,0:T(2,128)S(1)} %pad_maximum_fusion.7), channel_id=1, source_target_pairs={{0,24},{8,0},{16,8},{24,16},{1,25},{9,1},{17,9},{25,17},{2,26},{10... | collective-permute-start | bytes 12296 | tf_op jit(solution)/shard_map/ppermute | solution.py:42

commit v19 on v18

--- a/solution.py
+++ b/solution.py
@@ -41,8 +41,11 @@
     def shifted(array, axis, size, shift):
         return lax.ppermute(array, axis, [(i, (i + shift) % size) for i in range(size)])
 
+    def traded(array, axis, size, other):
+        return lax.ppermute(array, axis, [(i, i ^ other) for i in range(size)])
+
     def gathered(array, axis, size):
-        return [array] + [shifted(array, axis, size, d) for d in range(1, size)]
+        return [array] + [traded(array, axis, size, d) for d in range(1, size)]
 
     def per_device(ancestor, panel, factor_inv, pattern):
         row = lax.axis_index("row")
@@ -58,7 +61,7 @@
         def picked(slots, place, at):
             value = slots[0]
             for d in range(1, len(slots)):
-                value = jnp.where((place - at) % len(slots) == d, slots[d], value)
+                value = jnp.where(place ^ at == d, slots[d], value)
             return value
 
         early = [d for d in range(1, deep) if not deep < 4 * d < 3 * deep]
@@ -73,7 +76,7 @@
         def rows_of(r):
             return lax.dynamic_slice_in_dim(partial, r * piece, piece, axis=1)
 
-        sums = [shifted(rows_of((row + d) % rows), "row", rows, d) for d in range(1, rows)]
+        sums = [traded(rows_of(row ^ d), "row", rows, d) for d in range(1, rows)]
         squares = jnp.sum(lax.dynamic_slice_in_dim(factor_inv, z * part, part, axis=2) ** 2, axis=1)
         sums, squares = lax.optimization_barrier((sums, squares))
         scaled = sum(sums, rows_of(row))
@@ -82,8 +85,8 @@
             return lax.dynamic_slice_in_dim(array, c * part, part, axis=2)
 
         slots = [columns_of(scaled, z)]
-        for shift in range(1, deep):
-            slots.append(shifted(columns_of(scaled, (z + shift) % deep), "z", deep, shift))
+        for d in range(1, deep):
+            slots.append(traded(columns_of(scaled, z ^ d), "z", deep, d))
         if deep > 1:
             for d in reversed(late):
                 far[d] = shifted(far[d + 1], "z", deep, deep - 1)
@@ -94,8 +97,8 @@
         stored = jnp.sum(
             jnp.where(pattern[:, :, None] == at, count[:, None], 0), axis=1, dtype=jnp.int32
         )
-        from_z = ((z - stored) % deep).reshape(-1)
-        quarter = (row - jnp.arange(rows, dtype=jnp.int32)) % rows
+        from_z = (z ^ stored).reshape(-1)
+        quarter = row ^ jnp.arange(rows, dtype=jnp.int32)
         own_tile = (z - row * tiles - jnp.arange(tiles, dtype=jnp.int32)) % deep
         place = jnp.concatenate([from_z, quarter, own_tile])
         height = ancestor.shape[1]
@@ -124,14 +127,14 @@
             return jnp.concatenate([block.reshape(groups * out_rows, part), tail])
 
         moved = [rows_for(z)]
-        for shift in range(1, deep):
-            moved.append(shifted(rows_for((z + shift) % deep), "z", deep, shift))
+        for d in range(1, deep):
+            moved.append(traded(rows_for(z ^ d), "z", deep, d))
         moved = jnp.concatenate([picked(moved, z, c) for c in range(deep)], axis=1)
         column_block = -moved[: groups * out_rows].reshape(groups, out_rows, width)
         total = moved[groups * out_rows : groups * out_rows + groups]
         local = total
-        for shift in range(1, rows):
-            total = total + shifted(local, "row", rows, shift)
+        for d in range(1, rows):
+            total = total + traded(local, "row", rows, d)
         return column_block, total
 
     col = ("z", "core")

time: 51.1 us -> 50.4 us (0.986)
  waiting for transfers between devices: 13.3 us -> 14.4 us
  starting transfers between devices: 29.7 us -> 28.7 us
  local copies, waits for them, and re-layouts: 0.95 us -> 0.29 us
    ppermute x19 -> x4, starting transfers between devices: 29.7 us -> 9.15 us  [shifted(): lax.ppermute(array, axis, [(i, (i + shift) % size) for i in range(size)])]
    ppermute x0 -> x15, starting transfers between devices: none -> 19.6 us  [traded(): return lax.ppermute(array, axis, [(i, i ^ other) for i in range(size)])]
    ppermute x0 -> x15, waiting for transfers between devices: none -> 12.8 us  [traded(): return lax.ppermute(array, axis, [(i, i ^ other) for i in range(size)])]
    ppermute x19 -> x4, waiting for transfers between devices: 13.3 us -> 1.59 us  [shifted(): lax.ppermute(array, axis, [(i, (i + shift) % size) for i in range(size)])]
    unnamed x6, local copies, waits for them, and re-layouts: 0.68 us -> 0.02 us
  transfers between devices with their start and end apart: 19 -> 19, of which waited for: 8 -> 12; matrix products, arithmetic and copies ran while one was open for 7% -> 7% of each run, Pallas kernels for 0% -> 0%
where the time goes in v19:
time: 50.4 us; the launch traced here: 50.3 us
  starting transfers between devices  28.7 us (57%)
  waiting for transfers between devices  14.4 us (29%)
  other arithmetic  2.83 us (6%)
  matrix products  1.62 us (3%)
  Pallas kernels  1.61 us (3%)
  between operations  0.85 us (2%)
    ppermute x15, starting transfers between devices, traded(): return lax.ppermute(array, axis, [(i, i ^ other) for i in range(size)])  19.6 us
    ppermute x15, waiting for transfers between devices, traded(): return lax.ppermute(array, axis, [(i, i ^ other) for i in range(size)])  12.8 us
    ppermute x4, starting transfers between devices, shifted(): lax.ppermute(array, axis, [(i, (i + shift) % size) for i in range(size)])  9.15 us
    dot_general x1, matrix products, per_device(): partial = jnp.einsum('srw,swv->srv', mine, factor_inv, precision=highest)  1.62 us
    pallas_call x1, Pallas kernels, per_device(): pl.pallas_call(functools.partial(multiply_tiles, deep, rows), out_shape=j...  1.61 us
    ppermute x4, waiting for transfers between devices, shifted(): lax.ppermute(array, axis, [(i, (i + shift) % size) for i in range(size)])  1.59 us
  transfers between devices with their start and end apart: 19, of which 12 were waited for; matrix products, arithmetic and copies ran while one was open for 7% of the time, Pallas kernels for 0%

profile of v19, /device:TPU:0, one launch (start us, length us, event | category | flops | bytes accessed | tf_op | source)
XLA Modules:
  0.0 50.3 jit_solution(12203949848375977541)
XLA Ops:
  0.6 0.0 copy-start
  0.6 3.1 %collective-permute-start = (f32[2,256,128]{2,1,0:T(8,128)}, f32[2,256,128]{2,1,0:T(8,128)S(1)}, u32[]{:S(2)}, u32[]{:S(2)}) collective-permute-start(f32[2,256,128]{2,1,0:T(8,128)} %refs_0_.1), channel_id=1, source_target_pairs={{0,2},{2,4},{4,6},{6,0},{1,3},{3,5},{5,7},{7,1},{8,10},{10,12},{12... | collective-permute-start | bytes 786440 | tf_op jit(solution)/shard_map/ppermute | solution.py:42
  3.7 1.6 %fusion = f32[2,128,512]{2,1,0:T(8,128)S(1)} fusion(f32[2,128,512]{2,1,0:T(8,128)} %param.6, f32[2,128,512]{2,1,0:T(8,128)S(1)} %copy-done, s32[]{:T(128)S(6)} %select_n.153), kind=kOutput, calls=%fused_computation.10 | convolution fusion | flops 201326592 | bytes 1179652 | tf_op jit(solution)/shard_map/srw,swv->srv/dot_general | solution.py:72
  5.4 0.0 copy-start.1
  5.4 1.6 %collective-permute-start.3 = (f32[2,32,512]{2,1,0:T(8,128)S(1)}, f32[2,32,512]{2,1,0:T(8,128)S(1)}, u32[]{:S(2)}, u32[]{:S(2)}) collective-permute-start(f32[2,32,512]{2,1,0:T(8,128)S(1)} %get-tuple-element.20), channel_id=1, source_target_pairs={{0,8},{8,0},{16,24},{24,16},{1,9},{9,1},{17,25},{25,17},{2,10},{10... | collective-permute-start | bytes 393224 | tf_op jit(solution)/shard_map/ppermute | solution.py:45
  7.0 1.5 %collective-permute-start.4 = (f32[2,32,512]{2,1,0:T(8,128)S(1)}, f32[2,32,512]{2,1,0:T(8,128)S(1)}, u32[]{:S(2)}, u32[]{:S(2)}) collective-permute-start(f32[2,32,512]{2,1,0:T(8,128)S(1)} %get-tuple-element.19), channel_id=1, source_target_pairs={{0,16},{8,24},{16,0},{24,8},{1,17},{9,25},{17,1},{25,9},{2,18},{10... | collective-permute-start | bytes 393224 | tf_op jit(solution)/shard_map/ppermute | solution.py:45
  8.5 0.5 collective-permute-start.5
  9.0 3.0 %collective-permute-start.1 = (f32[2,256,128]{2,1,0:T(8,128)S(1)}, f32[2,256,128]{2,1,0:T(8,128)S(1)}, u32[]{:S(2)}, u32[]{:S(2)}) collective-permute-start(f32[2,256,128]{2,1,0:T(8,128)S(1)} %copy-done.1), channel_id=1, source_target_pairs={{0,6},{2,0},{4,2},{6,4},{1,7},{3,1},{5,3},{7,5},{8,14},{10,8},{12,... | collective-permute-start | bytes 786440 | tf_op jit(solution)/shard_map/ppermute | solution.py:42
  12.0 0.9 %multiply_reduce_fusion.1 = f32[2,128]{1,0:T(2,128)S(1)} fusion(f32[2,128,512]{2,1,0:T(8,128)} %param.6, s32[]{:T(128)S(6)} %select_n.158), kind=kLoop, calls=%fused_computation.9 | loop fusion | flops 65280 | bytes 132100 | tf_op jit(solution)/shard_map/reduce_sum | solution.py:80
  12.9 0.1 select_reduce_fusion
  13.0 1.7 %collective-permute-done.4 = f32[2,32,512]{2,1,0:T(8,128)S(1)} collective-permute-done((f32[2,32,512]{2,1,0:T(8,128)S(1)}, f32[2,32,512]{2,1,0:T(8,128)S(1)}, u32[]{:S(2)}, u32[]{:S(2)}) %collective-permute-start.4) | collective-permute-done | bytes 131104 | tf_op jit(solution)/shard_map/ppermute | solution.py:45
  14.8 0.0 collective-permute-done.5
  14.8 1.6 %collective-permute-start.6 = (f32[2,32,128]{2,1,0:T(8,128)S(1)}, f32[2,32,128]{2,1,0:T(8,128)S(1)}, u32[]{:S(2)}, u32[]{:S(2)}) collective-permute-start(f32[2,32,128]{2,1,0:T(8,128)S(1)} %get-tuple-element.31), channel_id=1, source_target_pairs={{0,2},{2,0},{4,6},{6,4},{1,3},{3,1},{5,7},{7,5},{8,10},{10,8},{12,... | collective-permute-start | bytes 98312 | tf_op jit(solution)/shard_map/ppermute | solution.py:45
  16.5 2.0 %collective-permute-start.7 = (f32[2,32,128]{2,1,0:T(8,128)S(1)}, f32[2,32,128]{2,1,0:T(8,128)S(1)}, u32[]{:S(2)}, u32[]{:S(2)}) collective-permute-start(f32[2,32,128]{2,1,0:T(8,128)S(1)} %get-tuple-element.30), channel_id=1, source_target_pairs={{0,4},{2,6},{4,0},{6,2},{1,5},{3,7},{5,1},{7,3},{8,12},{10,14},{12... | collective-permute-start | bytes 98312 | tf_op jit(solution)/shard_map/ppermute | solution.py:45
  18.5 0.8 %collective-permute-start.8 = (f32[2,32,128]{2,1,0:T(8,128)S(1)}, f32[2,32,128]{2,1,0:T(8,128)S(1)}, u32[]{:S(2)}, u32[]{:S(2)}) collective-permute-start(f32[2,32,128]{2,1,0:T(8,128)S(1)} %get-tuple-element.29), channel_id=1, source_target_pairs={{0,6},{2,4},{4,2},{6,0},{1,7},{3,5},{5,3},{7,1},{8,14},{10,12},{12... | collective-permute-start | bytes 98312 | tf_op jit(solution)/shard_map/ppermute | solution.py:45
  19.3 3.0 %collective-permute-start.2 = (f32[2,256,128]{2,1,0:T(8,128)S(1)}, f32[2,256,128]{2,1,0:T(8,128)S(1)}, u32[]{:S(2)}, u32[]{:S(2)}) collective-permute-start(f32[2,256,128]{2,1,0:T(8,128)S(1)} %collective-permute-done.1.refs_3_), channel_id=1, source_target_pairs={{0,6},{2,0},{4,2},{6,4},{1,7},{3,1},{5,3},{7,5},{8,14},{10,8},{12,... | collective-permute-start | bytes 786440 | tf_op jit(solution)/shard_map/ppermute | solution.py:42
  22.3 0.0 collective-permute-done.6
  22.3 0.1 collective-permute-done.7
  22.4 2.2 %collective-permute-done.8 = f32[2,32,128]{2,1,0:T(8,128)S(1)} collective-permute-done((f32[2,32,128]{2,1,0:T(8,128)S(1)}, f32[2,32,128]{2,1,0:T(8,128)S(1)}, u32[]{:S(2)}, u32[]{:S(2)}) %collective-permute-start.8) | collective-permute-done | bytes 32800 | tf_op jit(solution)/shard_map/ppermute | solution.py:45
  24.6 1.3 %collective-permute-start.10 = (f32[4,2,32,128]{3,2,1,0:T(8,128)S(1)}, f32[4,2,32,128]{3,2,1,0:T(8,128)S(1)}, u32[]{:S(2)}, u32[]{:S(2)}) collective-permute-start(f32[4,2,32,128]{3,2,1,0:T(8,128)S(1)} %pad_maximum_fusion.2.refs_4_), channel_id=1, source_target_pairs={{0,16},{8,24},{16,0},{24,8},{1,17},{9,25},{17,1},{25,9},{2,18},{10... | collective-permute-start | bytes 393224 | tf_op jit(solution)/shard_map/ppermute | solution.py:45
  25.9 1.5 %collective-permute-start.11 = (f32[4,2,32,128]{3,2,1,0:T(8,128)S(1)}, f32[4,2,32,128]{3,2,1,0:T(8,128)S(1)}, u32[]{:S(2)}, u32[]{:S(2)}) collective-permute-start(f32[4,2,32,128]{3,2,1,0:T(8,128)S(1)} %pad_maximum_fusion.2.refs_4_), channel_id=1, source_target_pairs={{0,24},{8,16},{16,8},{24,0},{1,25},{9,17},{17,9},{25,1},{2,26},{10... | collective-permute-start | bytes 393224 | tf_op jit(solution)/shard_map/ppermute | solution.py:45
  27.4 0.8 %collective-permute-start.9 = (f32[4,2,32,128]{3,2,1,0:T(8,128)S(1)}, f32[4,2,32,128]{3,2,1,0:T(8,128)S(1)}, u32[]{:S(2)}, u32[]{:S(2)}) collective-permute-start(f32[4,2,32,128]{3,2,1,0:T(8,128)S(1)} %pad_maximum_fusion.2.refs_4_), channel_id=1, source_target_pairs={{0,8},{8,0},{16,24},{24,16},{1,9},{9,1},{17,25},{25,17},{2,10},{10... | collective-permute-start | bytes 393224 | tf_op jit(solution)/shard_map/ppermute | solution.py:45
  28.2 0.1 xor.48
  28.3 0.1 pad_add_fusion.place
  28.3 1.3 %collective-permute-done.10.refs_6_ = f32[4,2,32,128]{3,2,1,0:T(8,128)S(1)} collective-permute-done((f32[4,2,32,128]{3,2,1,0:T(8,128)S(1)}, f32[4,2,32,128]{3,2,1,0:T(8,128)S(1)}, u32[]{:S(2)}, u32[]{:S(2)}) %collective-permute-start.10) | collective-permute-done | bytes 131104 | tf_op jit(solution)/shard_map/ppermute | solution.py:45
  29.6 2.1 %collective-permute-done.11.refs_7_ = f32[4,2,32,128]{3,2,1,0:T(8,128)S(1)} collective-permute-done((f32[4,2,32,128]{3,2,1,0:T(8,128)S(1)}, f32[4,2,32,128]{3,2,1,0:T(8,128)S(1)}, u32[]{:S(2)}, u32[]{:S(2)}) %collective-permute-start.11) | collective-permute-done | bytes 131104 | tf_op jit(solution)/shard_map/ppermute | solution.py:45
  31.8 0.7 %collective-permute-done.9.refs_5_ = f32[4,2,32,128]{3,2,1,0:T(8,128)S(1)} collective-permute-done((f32[4,2,32,128]{3,2,1,0:T(8,128)S(1)}, f32[4,2,32,128]{3,2,1,0:T(8,128)S(1)}, u32[]{:S(2)}, u32[]{:S(2)}) %collective-permute-start.9) | collective-permute-done | bytes 131104 | tf_op jit(solution)/shard_map/ppermute | solution.py:45
  32.5 1.6 %shard_map.59 = f32[2,384,128]{2,1,0:T(8,128)S(1)} custom-call(s32[13]{0:T(128)S(1)} %pad_add_fusion.place, f32[2,256,128]{2,1,0:T(8,128)S(1)} %copy-done.1, f32[2,256,128]{2,1,0:T(8,128)S(1)} %collective-permute-done.refs_1_, f32[2,256,128]{2,1,0:T(8,128)S(1)} %collective-permute-done.2.refs_2_, f32[2,256,128]{2,1,0:T(8,128)S(1)} %collective-permute-done.1.refs_3_, ...), custom_call_target="tpu_custom_call" | custom-call | tf_op jit(solution)/shard_map/pallas_call | solution.py:106
  34.1 0.1 collective-permute-start.12
  34.3 0.1 pad.15.clone
  34.3 1.6 %collective-permute-done.12 = f32[2,384,128]{2,1,0:T(8,128)S(1)} collective-permute-done((f32[2,384,128]{2,1,0:T(8,128)S(1)}, f32[2,384,128]{2,1,0:T(8,128)S(1)}, u32[]{:S(2)}, u32[]{:S(2)}) %collective-permute-start.12) | collective-permute-done | bytes 393248 | tf_op jit(solution)/shard_map/ppermute | solution.py:42
  36.0 0.1 multiply_reduce_fusion
  36.1 0.1 fusion.4
  36.2 0.9 %collective-permute-start.13 = (f32[72,128]{1,0:T(8,128)S(1)}, f32[72,128]{1,0:T(8,128)S(1)}, u32[]{:S(2)}, u32[]{:S(2)}) collective-permute-start(f32[72,128]{1,0:T(8,128)S(1)} %get-tuple-element.34), channel_id=1, source_target_pairs={{0,6},{2,4},{4,2},{6,0},{1,7},{3,5},{5,3},{7,1},{8,14},{10,12},{12... | collective-permute-start | bytes 110600 | tf_op jit(solution)/shard_map/ppermute | solution.py:45
  37.1 1.7 %collective-permute-start.14 = (f32[72,128]{1,0:T(8,128)S(1)}, f32[72,128]{1,0:T(8,128)S(1)}, u32[]{:S(2)}, u32[]{:S(2)}) collective-permute-start(f32[72,128]{1,0:T(8,128)S(1)} %get-tuple-element.33), channel_id=1, source_target_pairs={{0,4},{2,6},{4,0},{6,2},{1,5},{3,7},{5,1},{7,3},{8,12},{10,14},{12... | collective-permute-start | bytes 110600 | tf_op jit(solution)/shard_map/ppermute | solution.py:45
  38.8 1.9 %collective-permute-start.15 = (f32[72,128]{1,0:T(8,128)S(1)}, f32[72,128]{1,0:T(8,128)S(1)}, u32[]{:S(2)}, u32[]{:S(2)}) collective-permute-start(f32[72,128]{1,0:T(8,128)S(1)} %get-tuple-element.32), channel_id=1, source_target_pairs={{0,2},{2,0},{4,6},{6,4},{1,3},{3,1},{5,7},{7,5},{8,10},{10,8},{12,... | collective-permute-start | bytes 110600 | tf_op jit(solution)/shard_map/ppermute | solution.py:45
  40.7 1.4 %collective-permute-done.13 = f32[72,128]{1,0:T(8,128)S(1)} collective-permute-done((f32[72,128]{1,0:T(8,128)S(1)}, f32[72,128]{1,0:T(8,128)S(1)}, u32[]{:S(2)}, u32[]{:S(2)}) %collective-permute-start.13) | collective-permute-done | bytes 36896 | tf_op jit(solution)/shard_map/ppermute | solution.py:45
  42.1 0.7 %collective-permute-done.14 = f32[72,128]{1,0:T(8,128)S(1)} collective-permute-done((f32[72,128]{1,0:T(8,128)S(1)}, f32[72,128]{1,0:T(8,128)S(1)}, u32[]{:S(2)}, u32[]{:S(2)}) %collective-permute-start.14) | collective-permute-done | bytes 36896 | tf_op jit(solution)/shard_map/ppermute | solution.py:45
  42.7 0.3 collective-permute-done.15
  43.0 0.1 select_select_fusion.2
  43.1 0.1 select_select_fusion.3
  43.2 1.0 %collective-permute-start.16 = (f32[2,512]{1,0:T(2,128)S(1)}, f32[2,512]{1,0:T(2,128)S(1)}, u32[]{:S(2)}, u32[]{:S(2)}) collective-permute-start(f32[2,512]{1,0:T(2,128)S(1)} %pad_maximum_fusion.7), channel_id=1, source_target_pairs={{0,8},{8,0},{16,24},{24,16},{1,9},{9,1},{17,25},{25,17},{2,10},{10... | collective-permute-start | bytes 12296 | tf_op jit(solution)/shard_map/ppermute | solution.py:45
  44.2 0.9 %collective-permute-start.17 = (f32[2,512]{1,0:T(2,128)S(1)}, f32[2,512]{1,0:T(2,128)S(1)}, u32[]{:S(2)}, u32[]{:S(2)}) collective-permute-start(f32[2,512]{1,0:T(2,128)S(1)} %pad_maximum_fusion.7), channel_id=1, source_target_pairs={{0,16},{8,24},{16,0},{24,8},{1,17},{9,25},{17,1},{25,9},{2,18},{10... | collective-permute-start | bytes 12296 | tf_op jit(solution)/shard_map/ppermute | solution.py:45
  45.1 1.6 %collective-permute-start.18 = (f32[2,512]{1,0:T(2,128)S(1)}, f32[2,512]{1,0:T(2,128)S(1)}, u32[]{:S(2)}, u32[]{:S(2)}) collective-permute-start(f32[2,512]{1,0:T(2,128)S(1)} %pad_maximum_fusion.7), channel_id=1, source_target_pairs={{0,24},{8,16},{16,8},{24,0},{1,25},{9,17},{17,9},{25,1},{2,26},{10... | collective-permute-start | bytes 12296 | tf_op jit(solution)/shard_map/ppermute | solution.py:45
  46.8 0.7 %slice_negate_fusion = f32[64,512]{1,0:T(8,128)} fusion(f32[72,512]{1,0:T(8,128)S(1)} %pad_maximum_fusion.1), kind=kLoop, calls=%fused_computation.4 | loop fusion | flops 32768 | bytes 262144 | tf_op jit(solution)/shard_map/neg | solution.py:133
  47.4 0.4 collective-permute-done.17
  47.9 1.8 %collective-permute-done.18 = f32[2,512]{1,0:T(2,128)S(1)} collective-permute-done((f32[2,512]{1,0:T(2,128)S(1)}, f32[2,512]{1,0:T(2,128)S(1)}, u32[]{:S(2)}, u32[]{:S(2)}) %collective-permute-start.18) | collective-permute-done | bytes 4128 | tf_op jit(solution)/shard_map/ppermute | solution.py:45
  49.7 0.6 %add_add_fusion.1 = f32[2,512]{1,0:T(2,128)} fusion(f32[2,512]{1,0:T(2,128)S(1)} %collective-permute-done.18, f32[2,512]{1,0:T(2,128)S(1)} %collective-permute-done.17, f32[2,512]{1,0:T(2,128)S(1)} %pad_maximum_fusion.7, f32[2,512]{1,0:T(2,128)S(1)} %collective-permute-done.16), kind=kLoop, calls=%fused_computation.26 | loop fusion | flops 3072 | bytes 20480 | tf_op jit(solution)/shard_map/add | solution.py:137
  (24 shorter events, 0.3 us)
Async XLA Ops:
  0.6 3.1 %copy-start = (f32[2,128,512]{2,1,0:T(8,128)S(1)}, f32[2,128,512]{2,1,0:T(8,128)}, u32[]{:S(2)}) copy-start(f32[2,128,512]{2,1,0:T(8,128)} %param.5) | copy-start | bytes 1572868
  0.6 27.7 %collective-permute-start = (f32[2,256,128]{2,1,0:T(8,128)}, f32[2,256,128]{2,1,0:T(8,128)S(1)}, u32[]{:S(2)}, u32[]{:S(2)}) collective-permute-start(f32[2,256,128]{2,1,0:T(8,128)} %refs_0_.1), channel_id=1, source_target_pairs={{0,2},{2,4},{4,6},{6,0},{1,3},{3,5},{5,7},{7,1},{8,10},{10,12},{12... | collective-permute-start | bytes 786440 | tf_op jit(solution)/shard_map/ppermute | solution.py:42
  5.4 3.6 %copy-start.1 = (f32[2,256,128]{2,1,0:T(8,128)S(1)}, f32[2,256,128]{2,1,0:T(8,128)}, u32[]{:S(2)}) copy-start(f32[2,256,128]{2,1,0:T(8,128)} %refs_0_.1) | copy-start | bytes 786436
  5.4 7.6 %collective-permute-start.3 = (f32[2,32,512]{2,1,0:T(8,128)S(1)}, f32[2,32,512]{2,1,0:T(8,128)S(1)}, u32[]{:S(2)}, u32[]{:S(2)}) collective-permute-start(f32[2,32,512]{2,1,0:T(8,128)S(1)} %get-tuple-element.20), channel_id=1, source_target_pairs={{0,8},{8,0},{16,24},{24,16},{1,9},{9,1},{17,25},{25,17},{2,10},{10... | collective-permute-start | bytes 393224 | tf_op jit(solution)/shard_map/ppermute | solution.py:45
  7.0 7.8 %collective-permute-start.4 = (f32[2,32,512]{2,1,0:T(8,128)S(1)}, f32[2,32,512]{2,1,0:T(8,128)S(1)}, u32[]{:S(2)}, u32[]{:S(2)}) collective-permute-start(f32[2,32,512]{2,1,0:T(8,128)S(1)} %get-tuple-element.19), channel_id=1, source_target_pairs={{0,16},{8,24},{16,0},{24,8},{1,17},{9,25},{17,1},{25,9},{2,18},{10... | collective-permute-start | bytes 393224 | tf_op jit(solution)/shard_map/ppermute | solution.py:45
  8.5 6.3 %collective-permute-start.5 = (f32[2,32,512]{2,1,0:T(8,128)S(1)}, f32[2,32,512]{2,1,0:T(8,128)S(1)}, u32[]{:S(2)}, u32[]{:S(2)}) collective-permute-start(f32[2,32,512]{2,1,0:T(8,128)S(1)} %get-tuple-element.18), channel_id=1, source_target_pairs={{0,24},{8,16},{16,8},{24,0},{1,25},{9,17},{17,9},{25,1},{2,26},{10... | collective-permute-start | bytes 393224 | tf_op jit(solution)/shard_map/ppermute | solution.py:45
  9.0 10.3 %collective-permute-start.1 = (f32[2,256,128]{2,1,0:T(8,128)S(1)}, f32[2,256,128]{2,1,0:T(8,128)S(1)}, u32[]{:S(2)}, u32[]{:S(2)}) collective-permute-start(f32[2,256,128]{2,1,0:T(8,128)S(1)} %copy-done.1), channel_id=1, source_target_pairs={{0,6},{2,0},{4,2},{6,4},{1,7},{3,1},{5,3},{7,5},{8,14},{10,8},{12,... | collective-permute-start | bytes 786440 | tf_op jit(solution)/shard_map/ppermute | solution.py:42
  12.0 1.0 %copy-start.2 = (s32[2,4]{1,0:T(2,128)S(1)}, s32[2,4]{1,0:T(2,128)}, u32[]{:S(2)}) copy-start(s32[2,4]{1,0:T(2,128)} %param.7) | copy-start | bytes 100
  14.8 7.5 %collective-permute-start.6 = (f32[2,32,128]{2,1,0:T(8,128)S(1)}, f32[2,32,128]{2,1,0:T(8,128)S(1)}, u32[]{:S(2)}, u32[]{:S(2)}) collective-permute-start(f32[2,32,128]{2,1,0:T(8,128)S(1)} %get-tuple-element.31), channel_id=1, source_target_pairs={{0,2},{2,0},{4,6},{6,4},{1,3},{3,1},{5,7},{7,5},{8,10},{10,8},{12,... | collective-permute-start | bytes 98312 | tf_op jit(solution)/shard_map/ppermute | solution.py:45
  16.5 5.9 %collective-permute-start.7 = (f32[2,32,128]{2,1,0:T(8,128)S(1)}, f32[2,32,128]{2,1,0:T(8,128)S(1)}, u32[]{:S(2)}, u32[]{:S(2)}) collective-permute-start(f32[2,32,128]{2,1,0:T(8,128)S(1)} %get-tuple-element.30), channel_id=1, source_target_pairs={{0,4},{2,6},{4,0},{6,2},{1,5},{3,7},{5,1},{7,3},{8,12},{10,14},{12... | collective-permute-start | bytes 98312 | tf_op jit(solution)/shard_map/ppermute | solution.py:45
  18.5 6.1 %collective-permute-start.8 = (f32[2,32,128]{2,1,0:T(8,128)S(1)}, f32[2,32,128]{2,1,0:T(8,128)S(1)}, u32[]{:S(2)}, u32[]{:S(2)}) collective-permute-start(f32[2,32,128]{2,1,0:T(8,128)S(1)} %get-tuple-element.29), channel_id=1, source_target_pairs={{0,6},{2,4},{4,2},{6,0},{1,7},{3,5},{5,3},{7,1},{8,14},{10,12},{12... | collective-permute-start | bytes 98312 | tf_op jit(solution)/shard_map/ppermute | solution.py:45
  19.3 13.2 %collective-permute-start.2 = (f32[2,256,128]{2,1,0:T(8,128)S(1)}, f32[2,256,128]{2,1,0:T(8,128)S(1)}, u32[]{:S(2)}, u32[]{:S(2)}) collective-permute-start(f32[2,256,128]{2,1,0:T(8,128)S(1)} %collective-permute-done.1.refs_3_), channel_id=1, source_target_pairs={{0,6},{2,0},{4,2},{6,4},{1,7},{3,1},{5,3},{7,5},{8,14},{10,8},{12,... | collective-permute-start | bytes 786440 | tf_op jit(solution)/shard_map/ppermute | solution.py:42
  24.6 5.0 %collective-permute-start.10 = (f32[4,2,32,128]{3,2,1,0:T(8,128)S(1)}, f32[4,2,32,128]{3,2,1,0:T(8,128)S(1)}, u32[]{:S(2)}, u32[]{:S(2)}) collective-permute-start(f32[4,2,32,128]{3,2,1,0:T(8,128)S(1)} %pad_maximum_fusion.2.refs_4_), channel_id=1, source_target_pairs={{0,16},{8,24},{16,0},{24,8},{1,17},{9,25},{17,1},{25,9},{2,18},{10... | collective-permute-start | bytes 393224 | tf_op jit(solution)/shard_map/ppermute | solution.py:45
  25.9 5.9 %collective-permute-start.11 = (f32[4,2,32,128]{3,2,1,0:T(8,128)S(1)}, f32[4,2,32,128]{3,2,1,0:T(8,128)S(1)}, u32[]{:S(2)}, u32[]{:S(2)}) collective-permute-start(f32[4,2,32,128]{3,2,1,0:T(8,128)S(1)} %pad_maximum_fusion.2.refs_4_), channel_id=1, source_target_pairs={{0,24},{8,16},{16,8},{24,0},{1,25},{9,17},{17,9},{25,1},{2,26},{10... | collective-permute-start | bytes 393224 | tf_op jit(solution)/shard_map/ppermute | solution.py:45
  27.4 5.2 %collective-permute-start.9 = (f32[4,2,32,128]{3,2,1,0:T(8,128)S(1)}, f32[4,2,32,128]{3,2,1,0:T(8,128)S(1)}, u32[]{:S(2)}, u32[]{:S(2)}) collective-permute-start(f32[4,2,32,128]{3,2,1,0:T(8,128)S(1)} %pad_maximum_fusion.2.refs_4_), channel_id=1, source_target_pairs={{0,8},{8,0},{16,24},{24,16},{1,9},{9,1},{17,25},{25,17},{2,10},{10... | collective-permute-start | bytes 393224 | tf_op jit(solution)/shard_map/ppermute | solution.py:45
  34.1 1.8 %collective-permute-start.12 = (f32[2,384,128]{2,1,0:T(8,128)S(1)}, f32[2,384,128]{2,1,0:T(8,128)S(1)}, u32[]{:S(2)}, u32[]{:S(2)}) collective-permute-start(f32[2,384,128]{2,1,0:T(8,128)S(1)} %shard_map.59), channel_id=1, source_target_pairs={{0,1},{1,0},{2,3},{3,2},{4,5},{5,4},{6,7},{7,6},{8,9},{9,8},{10,11... | collective-permute-start | bytes 1179656 | tf_op jit(solution)/shard_map/ppermute | solution.py:42
  36.2 5.9 %collective-permute-start.13 = (f32[72,128]{1,0:T(8,128)S(1)}, f32[72,128]{1,0:T(8,128)S(1)}, u32[]{:S(2)}, u32[]{:S(2)}) collective-permute-start(f32[72,128]{1,0:T(8,128)S(1)} %get-tuple-element.34), channel_id=1, source_target_pairs={{0,6},{2,4},{4,2},{6,0},{1,7},{3,5},{5,3},{7,1},{8,14},{10,12},{12... | collective-permute-start | bytes 110600 | tf_op jit(solution)/shard_map/ppermute | solution.py:45
  37.1 5.7 %collective-permute-start.14 = (f32[72,128]{1,0:T(8,128)S(1)}, f32[72,128]{1,0:T(8,128)S(1)}, u32[]{:S(2)}, u32[]{:S(2)}) collective-permute-start(f32[72,128]{1,0:T(8,128)S(1)} %get-tuple-element.33), channel_id=1, source_target_pairs={{0,4},{2,6},{4,0},{6,2},{1,5},{3,7},{5,1},{7,3},{8,12},{10,14},{12... | collective-permute-start | bytes 110600 | tf_op jit(solution)/shard_map/ppermute | solution.py:45
  38.8 4.2 %collective-permute-start.15 = (f32[72,128]{1,0:T(8,128)S(1)}, f32[72,128]{1,0:T(8,128)S(1)}, u32[]{:S(2)}, u32[]{:S(2)}) collective-permute-start(f32[72,128]{1,0:T(8,128)S(1)} %get-tuple-element.32), channel_id=1, source_target_pairs={{0,2},{2,0},{4,6},{6,4},{1,3},{3,1},{5,7},{7,5},{8,10},{10,8},{12,... | collective-permute-start | bytes 110600 | tf_op jit(solution)/shard_map/ppermute | solution.py:45
  43.2 4.2 %collective-permute-start.16 = (f32[2,512]{1,0:T(2,128)S(1)}, f32[2,512]{1,0:T(2,128)S(1)}, u32[]{:S(2)}, u32[]{:S(2)}) collective-permute-start(f32[2,512]{1,0:T(2,128)S(1)} %pad_maximum_fusion.7), channel_id=1, source_target_pairs={{0,8},{8,0},{16,24},{24,16},{1,9},{9,1},{17,25},{25,17},{2,10},{10... | collective-permute-start | bytes 12296 | tf_op jit(solution)/shard_map/ppermute | solution.py:45
  44.2 3.6 %collective-permute-start.17 = (f32[2,512]{1,0:T(2,128)S(1)}, f32[2,512]{1,0:T(2,128)S(1)}, u32[]{:S(2)}, u32[]{:S(2)}) collective-permute-start(f32[2,512]{1,0:T(2,128)S(1)} %pad_maximum_fusion.7), channel_id=1, source_target_pairs={{0,16},{8,24},{16,0},{24,8},{1,17},{9,25},{17,1},{25,9},{2,18},{10... | collective-permute-start | bytes 12296 | tf_op jit(solution)/shard_map/ppermute | solution.py:45
  45.1 4.5 %collective-permute-start.18 = (f32[2,512]{1,0:T(2,128)S(1)}, f32[2,512]{1,0:T(2,128)S(1)}, u32[]{:S(2)}, u32[]{:S(2)}) collective-permute-start(f32[2,512]{1,0:T(2,128)S(1)} %pad_maximum_fusion.7), channel_id=1, source_target_pairs={{0,24},{8,16},{16,8},{24,0},{1,25},{9,17},{17,9},{25,1},{2,26},{10... | collective-permute-start | bytes 12296 | tf_op jit(solution)/shard_map/ppermute | solution.py:45

commit v20 on v19

--- a/solution.py
+++ b/solution.py
@@ -45,7 +45,7 @@
         return lax.ppermute(array, axis, [(i, i ^ other) for i in range(size)])
 
     def gathered(array, axis, size):
-        return [array] + [traded(array, axis, size, d) for d in range(1, size)]
+        return [array] + [traded(array, axis, size, d) for d in reversed(range(1, size))][::-1]
 
     def per_device(ancestor, panel, factor_inv, pattern):
         row = lax.axis_index("row")
@@ -76,7 +76,7 @@
         def rows_of(r):
             return lax.dynamic_slice_in_dim(partial, r * piece, piece, axis=1)
 
-        sums = [traded(rows_of(row ^ d), "row", rows, d) for d in range(1, rows)]
+        sums = [traded(rows_of(row ^ d), "row", rows, d) for d in reversed(range(1, rows))]
         squares = jnp.sum(lax.dynamic_slice_in_dim(factor_inv, z * part, part, axis=2) ** 2, axis=1)
         sums, squares = lax.optimization_barrier((sums, squares))
         scaled = sum(sums, rows_of(row))
@@ -84,9 +84,8 @@
         def columns_of(array, c):
             return lax.dynamic_slice_in_dim(array, c * part, part, axis=2)
 
-        slots = [columns_of(scaled, z)]
-        for d in range(1, deep):
-            slots.append(traded(columns_of(scaled, z ^ d), "z", deep, d))
+        slots = [traded(columns_of(scaled, z ^ d), "z", deep, d) for d in reversed(range(1, deep))]
+        slots = [columns_of(scaled, z)] + slots[::-1]
         if deep > 1:
             for d in reversed(late):
                 far[d] = shifted(far[d + 1], "z", deep, deep - 1)
@@ -126,14 +125,13 @@
             block = lax.dynamic_slice_in_dim(product, (c * cores + core) * out_rows, out_rows, axis=1)
             return jnp.concatenate([block.reshape(groups * out_rows, part), tail])
 
-        moved = [rows_for(z)]
-        for d in range(1, deep):
-            moved.append(traded(rows_for(z ^ d), "z", deep, d))
+        moved = [traded(rows_for(z ^ d), "z", deep, d) for d in reversed(range(1, deep))]
+        moved = [rows_for(z)] + moved[::-1]
         moved = jnp.concatenate([picked(moved, z, c) for c in range(deep)], axis=1)
         column_block = -moved[: groups * out_rows].reshape(groups, out_rows, width)
         total = moved[groups * out_rows : groups * out_rows + groups]
         local = total
-        for d in range(1, rows):
+        for d in reversed(range(1, rows)):
             total = total + traded(local, "row", rows, d)
         return column_block, total
 

time: 50.4 us -> 50.2 us (level)
  waiting for transfers between devices: 14.4 us -> 13.8 us
    ppermute x15, waiting for transfers between devices: 12.8 us -> 12.2 us  [traded(): return lax.ppermute(array, axis, [(i, i ^ other) for i in range(size)])]
where the time goes in v20:
time: 50.2 us; the launch traced here: 50 us
  starting transfers between devices  29 us (58%)
  waiting for transfers between devices  13.8 us (27%)
  other arithmetic  2.83 us (6%)
  matrix products  1.62 us (3%)
  Pallas kernels  1.61 us (3%)
  between operations  0.85 us (2%)
    ppermute x15, starting transfers between devices, traded(): return lax.ppermute(array, axis, [(i, i ^ other) for i in range(size)])  19.6 us
    ppermute x15, waiting for transfers between devices, traded(): return lax.ppermute(array, axis, [(i, i ^ other) for i in range(size)])  12.2 us
    ppermute x4, starting transfers between devices, shifted(): lax.ppermute(array, axis, [(i, (i + shift) % size) for i in range(size)])  9.42 us
    dot_general x1, matrix products, per_device(): partial = jnp.einsum('srw,swv->srv', mine, factor_inv, precision=highest)  1.62 us
    pallas_call x1, Pallas kernels, per_device(): pl.pallas_call(functools.partial(multiply_tiles, deep, rows), out_shape=j...  1.61 us
    ppermute x4, waiting for transfers between devices, shifted(): lax.ppermute(array, axis, [(i, (i + shift) % size) for i in range(size)])  1.59 us
  transfers between devices with their start and end apart: 19, of which 12 were waited for; matrix products, arithmetic and copies ran while one was open for 7% of the time, Pallas kernels for 0%

profile of v20, /device:TPU:0, one launch (start us, length us, event | category | flops | bytes accessed | tf_op | source)
XLA Modules:
  0.0 50.0 jit_solution(7373800696069605307)
XLA Ops:
  0.6 0.0 copy-start
  0.6 3.1 %collective-permute-start = (f32[2,256,128]{2,1,0:T(8,128)}, f32[2,256,128]{2,1,0:T(8,128)S(1)}, u32[]{:S(2)}, u32[]{:S(2)}) collective-permute-start(f32[2,256,128]{2,1,0:T(8,128)} %refs_0_.1), channel_id=1, source_target_pairs={{0,2},{2,4},{4,6},{6,0},{1,3},{3,5},{5,7},{7,1},{8,10},{10,12},{12... | collective-permute-start | bytes 786440 | tf_op jit(solution)/shard_map/ppermute | solution.py:42
  3.7 1.6 %fusion = f32[2,128,512]{2,1,0:T(8,128)S(1)} fusion(f32[2,128,512]{2,1,0:T(8,128)} %param.6, f32[2,128,512]{2,1,0:T(8,128)S(1)} %copy-done, s32[]{:T(128)S(6)} %select_n.153), kind=kOutput, calls=%fused_computation.10 | convolution fusion | flops 201326592 | bytes 1179652 | tf_op jit(solution)/shard_map/srw,swv->srv/dot_general | solution.py:72
  5.4 0.0 copy-start.1
  5.4 2.5 %collective-permute-start.3 = (f32[2,32,512]{2,1,0:T(8,128)S(1)}, f32[2,32,512]{2,1,0:T(8,128)S(1)}, u32[]{:S(2)}, u32[]{:S(2)}) collective-permute-start(f32[2,32,512]{2,1,0:T(8,128)S(1)} %get-tuple-element.20), channel_id=1, source_target_pairs={{0,24},{8,16},{16,8},{24,0},{1,25},{9,17},{17,9},{25,1},{2,26},{10... | collective-permute-start | bytes 393224 | tf_op jit(solution)/shard_map/ppermute | solution.py:45
  7.9 0.5 %collective-permute-start.4 = (f32[2,32,512]{2,1,0:T(8,128)S(1)}, f32[2,32,512]{2,1,0:T(8,128)S(1)}, u32[]{:S(2)}, u32[]{:S(2)}) collective-permute-start(f32[2,32,512]{2,1,0:T(8,128)S(1)} %get-tuple-element.19), channel_id=1, source_target_pairs={{0,16},{8,24},{16,0},{24,8},{1,17},{9,25},{17,1},{25,9},{2,18},{10... | collective-permute-start | bytes 393224 | tf_op jit(solution)/shard_map/ppermute | solution.py:45
  8.4 0.5 %collective-permute-start.5 = (f32[2,32,512]{2,1,0:T(8,128)S(1)}, f32[2,32,512]{2,1,0:T(8,128)S(1)}, u32[]{:S(2)}, u32[]{:S(2)}) collective-permute-start(f32[2,32,512]{2,1,0:T(8,128)S(1)} %get-tuple-element.18), channel_id=1, source_target_pairs={{0,8},{8,0},{16,24},{24,16},{1,9},{9,1},{17,25},{25,17},{2,10},{10... | collective-permute-start | bytes 393224 | tf_op jit(solution)/shard_map/ppermute | solution.py:45
  9.0 3.0 %collective-permute-start.1 = (f32[2,256,128]{2,1,0:T(8,128)S(1)}, f32[2,256,128]{2,1,0:T(8,128)S(1)}, u32[]{:S(2)}, u32[]{:S(2)}) collective-permute-start(f32[2,256,128]{2,1,0:T(8,128)S(1)} %copy-done.1), channel_id=1, source_target_pairs={{0,6},{2,0},{4,2},{6,4},{1,7},{3,1},{5,3},{7,5},{8,14},{10,8},{12,... | collective-permute-start | bytes 786440 | tf_op jit(solution)/shard_map/ppermute | solution.py:42
  12.0 0.9 %multiply_reduce_fusion.1 = f32[2,128]{1,0:T(2,128)S(1)} fusion(f32[2,128,512]{2,1,0:T(8,128)} %param.6, s32[]{:T(128)S(6)} %select_n.158), kind=kLoop, calls=%fused_computation.9 | loop fusion | flops 65280 | bytes 132100 | tf_op jit(solution)/shard_map/reduce_sum | solution.py:80
  12.9 0.1 select_reduce_fusion
  13.0 1.1 %collective-permute-done.4 = f32[2,32,512]{2,1,0:T(8,128)S(1)} collective-permute-done((f32[2,32,512]{2,1,0:T(8,128)S(1)}, f32[2,32,512]{2,1,0:T(8,128)S(1)}, u32[]{:S(2)}, u32[]{:S(2)}) %collective-permute-start.4) | collective-permute-done | bytes 131104 | tf_op jit(solution)/shard_map/ppermute | solution.py:45
  14.1 0.1 collective-permute-done.5
  14.3 1.6 %collective-permute-start.6 = (f32[2,32,128]{2,1,0:T(8,128)S(1)}, f32[2,32,128]{2,1,0:T(8,128)S(1)}, u32[]{:S(2)}, u32[]{:S(2)}) collective-permute-start(f32[2,32,128]{2,1,0:T(8,128)S(1)} %get-tuple-element.31), channel_id=1, source_target_pairs={{0,2},{2,0},{4,6},{6,4},{1,3},{3,1},{5,7},{7,5},{8,10},{10,8},{12,... | collective-permute-start | bytes 98312 | tf_op jit(solution)/shard_map/ppermute | solution.py:45
  15.9 2.3 %collective-permute-start.7 = (f32[2,32,128]{2,1,0:T(8,128)S(1)}, f32[2,32,128]{2,1,0:T(8,128)S(1)}, u32[]{:S(2)}, u32[]{:S(2)}) collective-permute-start(f32[2,32,128]{2,1,0:T(8,128)S(1)} %get-tuple-element.30), channel_id=1, source_target_pairs={{0,4},{2,6},{4,0},{6,2},{1,5},{3,7},{5,1},{7,3},{8,12},{10,14},{12... | collective-permute-start | bytes 98312 | tf_op jit(solution)/shard_map/ppermute | solution.py:45
  18.2 0.6 %collective-permute-start.8 = (f32[2,32,128]{2,1,0:T(8,128)S(1)}, f32[2,32,128]{2,1,0:T(8,128)S(1)}, u32[]{:S(2)}, u32[]{:S(2)}) collective-permute-start(f32[2,32,128]{2,1,0:T(8,128)S(1)} %get-tuple-element.29), channel_id=1, source_target_pairs={{0,6},{2,4},{4,2},{6,0},{1,7},{3,5},{5,3},{7,1},{8,14},{10,12},{12... | collective-permute-start | bytes 98312 | tf_op jit(solution)/shard_map/ppermute | solution.py:45
  18.8 0.0 collective-permute-done.1.refs_3_
  18.8 3.3 %collective-permute-start.2 = (f32[2,256,128]{2,1,0:T(8,128)S(1)}, f32[2,256,128]{2,1,0:T(8,128)S(1)}, u32[]{:S(2)}, u32[]{:S(2)}) collective-permute-start(f32[2,256,128]{2,1,0:T(8,128)S(1)} %collective-permute-done.1.refs_3_), channel_id=1, source_target_pairs={{0,6},{2,0},{4,2},{6,4},{1,7},{3,1},{5,3},{7,5},{8,14},{10,8},{12,... | collective-permute-start | bytes 786440 | tf_op jit(solution)/shard_map/ppermute | solution.py:42
  22.0 0.0 collective-permute-done.6
  22.0 2.3 %collective-permute-done.8 = f32[2,32,128]{2,1,0:T(8,128)S(1)} collective-permute-done((f32[2,32,128]{2,1,0:T(8,128)S(1)}, f32[2,32,128]{2,1,0:T(8,128)S(1)}, u32[]{:S(2)}, u32[]{:S(2)}) %collective-permute-start.8) | collective-permute-done | bytes 32800 | tf_op jit(solution)/shard_map/ppermute | solution.py:45
  24.3 1.5 %collective-permute-start.10 = (f32[4,2,32,128]{3,2,1,0:T(8,128)S(1)}, f32[4,2,32,128]{3,2,1,0:T(8,128)S(1)}, u32[]{:S(2)}, u32[]{:S(2)}) collective-permute-start(f32[4,2,32,128]{3,2,1,0:T(8,128)S(1)} %pad_maximum_fusion.2.refs_4_), channel_id=1, source_target_pairs={{0,16},{8,24},{16,0},{24,8},{1,17},{9,25},{17,1},{25,9},{2,18},{10... | collective-permute-start | bytes 393224 | tf_op jit(solution)/shard_map/ppermute | solution.py:45
  25.9 1.5 %collective-permute-start.11 = (f32[4,2,32,128]{3,2,1,0:T(8,128)S(1)}, f32[4,2,32,128]{3,2,1,0:T(8,128)S(1)}, u32[]{:S(2)}, u32[]{:S(2)}) collective-permute-start(f32[4,2,32,128]{3,2,1,0:T(8,128)S(1)} %pad_maximum_fusion.2.refs_4_), channel_id=1, source_target_pairs={{0,24},{8,16},{16,8},{24,0},{1,25},{9,17},{17,9},{25,1},{2,26},{10... | collective-permute-start | bytes 393224 | tf_op jit(solution)/shard_map/ppermute | solution.py:45
  27.4 0.5 collective-permute-start.9
  27.9 0.1 xor.48
  28.0 0.1 pad_add_fusion.place
  28.1 1.9 %collective-permute-done.10.refs_6_ = f32[4,2,32,128]{3,2,1,0:T(8,128)S(1)} collective-permute-done((f32[4,2,32,128]{3,2,1,0:T(8,128)S(1)}, f32[4,2,32,128]{3,2,1,0:T(8,128)S(1)}, u32[]{:S(2)}, u32[]{:S(2)}) %collective-permute-start.10) | collective-permute-done | bytes 131104 | tf_op jit(solution)/shard_map/ppermute | solution.py:45
  29.9 1.8 %collective-permute-done.11.refs_7_ = f32[4,2,32,128]{3,2,1,0:T(8,128)S(1)} collective-permute-done((f32[4,2,32,128]{3,2,1,0:T(8,128)S(1)}, f32[4,2,32,128]{3,2,1,0:T(8,128)S(1)}, u32[]{:S(2)}, u32[]{:S(2)}) %collective-permute-start.11) | collective-permute-done | bytes 131104 | tf_op jit(solution)/shard_map/ppermute | solution.py:45
  31.7 0.6 %collective-permute-done.9.refs_5_ = f32[4,2,32,128]{3,2,1,0:T(8,128)S(1)} collective-permute-done((f32[4,2,32,128]{3,2,1,0:T(8,128)S(1)}, f32[4,2,32,128]{3,2,1,0:T(8,128)S(1)}, u32[]{:S(2)}, u32[]{:S(2)}) %collective-permute-start.9) | collective-permute-done | bytes 131104 | tf_op jit(solution)/shard_map/ppermute | solution.py:45
  32.4 1.6 %shard_map.59 = f32[2,384,128]{2,1,0:T(8,128)S(1)} custom-call(s32[13]{0:T(128)S(1)} %pad_add_fusion.place, f32[2,256,128]{2,1,0:T(8,128)S(1)} %copy-done.1, f32[2,256,128]{2,1,0:T(8,128)S(1)} %collective-permute-done.refs_1_, f32[2,256,128]{2,1,0:T(8,128)S(1)} %collective-permute-done.2.refs_2_, f32[2,256,128]{2,1,0:T(8,128)S(1)} %collective-permute-done.1.refs_3_, ...), custom_call_target="tpu_custom_call" | custom-call | tf_op jit(solution)/shard_map/pallas_call | solution.py:105
  34.0 0.1 collective-permute-start.12
  34.1 0.1 pad.15.clone
  34.2 1.6 %collective-permute-done.12 = f32[2,384,128]{2,1,0:T(8,128)S(1)} collective-permute-done((f32[2,384,128]{2,1,0:T(8,128)S(1)}, f32[2,384,128]{2,1,0:T(8,128)S(1)}, u32[]{:S(2)}, u32[]{:S(2)}) %collective-permute-start.12) | collective-permute-done | bytes 393248 | tf_op jit(solution)/shard_map/ppermute | solution.py:42
  35.9 0.1 multiply_reduce_fusion
  36.0 0.1 fusion.4
  36.1 0.2 collective-permute-start.13
  36.3 0.6 %collective-permute-start.14 = (f32[72,128]{1,0:T(8,128)S(1)}, f32[72,128]{1,0:T(8,128)S(1)}, u32[]{:S(2)}, u32[]{:S(2)}) collective-permute-start(f32[72,128]{1,0:T(8,128)S(1)} %get-tuple-element.33), channel_id=1, source_target_pairs={{0,4},{2,6},{4,0},{6,2},{1,5},{3,7},{5,1},{7,3},{8,12},{10,14},{12... | collective-permute-start | bytes 110600 | tf_op jit(solution)/shard_map/ppermute | solution.py:45
  36.9 3.6 %collective-permute-start.15 = (f32[72,128]{1,0:T(8,128)S(1)}, f32[72,128]{1,0:T(8,128)S(1)}, u32[]{:S(2)}, u32[]{:S(2)}) collective-permute-start(f32[72,128]{1,0:T(8,128)S(1)} %get-tuple-element.32), channel_id=1, source_target_pairs={{0,2},{2,0},{4,6},{6,4},{1,3},{3,1},{5,7},{7,5},{8,10},{10,8},{12,... | collective-permute-start | bytes 110600 | tf_op jit(solution)/shard_map/ppermute | solution.py:45
  40.5 1.7 %collective-permute-done.13 = f32[72,128]{1,0:T(8,128)S(1)} collective-permute-done((f32[72,128]{1,0:T(8,128)S(1)}, f32[72,128]{1,0:T(8,128)S(1)}, u32[]{:S(2)}, u32[]{:S(2)}) %collective-permute-start.13) | collective-permute-done | bytes 36896 | tf_op jit(solution)/shard_map/ppermute | solution.py:45
  42.3 0.4 collective-permute-done.15
  42.6 0.1 select_select_fusion.2
  42.7 0.1 select_select_fusion.3
  42.8 1.6 %collective-permute-start.16 = (f32[2,512]{1,0:T(2,128)S(1)}, f32[2,512]{1,0:T(2,128)S(1)}, u32[]{:S(2)}, u32[]{:S(2)}) collective-permute-start(f32[2,512]{1,0:T(2,128)S(1)} %pad_maximum_fusion.7), channel_id=1, source_target_pairs={{0,24},{8,16},{16,8},{24,0},{1,25},{9,17},{17,9},{25,1},{2,26},{10... | collective-permute-start | bytes 12296 | tf_op jit(solution)/shard_map/ppermute | solution.py:45
  44.5 1.3 %collective-permute-start.17 = (f32[2,512]{1,0:T(2,128)S(1)}, f32[2,512]{1,0:T(2,128)S(1)}, u32[]{:S(2)}, u32[]{:S(2)}) collective-permute-start(f32[2,512]{1,0:T(2,128)S(1)} %pad_maximum_fusion.7), channel_id=1, source_target_pairs={{0,16},{8,24},{16,0},{24,8},{1,17},{9,25},{17,1},{25,9},{2,18},{10... | collective-permute-start | bytes 12296 | tf_op jit(solution)/shard_map/ppermute | solution.py:45
  45.8 0.6 %collective-permute-start.18 = (f32[2,512]{1,0:T(2,128)S(1)}, f32[2,512]{1,0:T(2,128)S(1)}, u32[]{:S(2)}, u32[]{:S(2)}) collective-permute-start(f32[2,512]{1,0:T(2,128)S(1)} %pad_maximum_fusion.7), channel_id=1, source_target_pairs={{0,8},{8,0},{16,24},{24,16},{1,9},{9,1},{17,25},{25,17},{2,10},{10... | collective-permute-start | bytes 12296 | tf_op jit(solution)/shard_map/ppermute | solution.py:45
  46.4 0.7 %slice_negate_fusion = f32[64,512]{1,0:T(8,128)} fusion(f32[72,512]{1,0:T(8,128)S(1)} %pad_maximum_fusion.1), kind=kLoop, calls=%fused_computation.4 | loop fusion | flops 32768 | bytes 262144 | tf_op jit(solution)/shard_map/neg | solution.py:131
  47.1 0.3 collective-permute-done.16
  47.4 0.7 %collective-permute-done.17 = f32[2,512]{1,0:T(2,128)S(1)} collective-permute-done((f32[2,512]{1,0:T(2,128)S(1)}, f32[2,512]{1,0:T(2,128)S(1)}, u32[]{:S(2)}, u32[]{:S(2)}) %collective-permute-start.17) | collective-permute-done | bytes 4128 | tf_op jit(solution)/shard_map/ppermute | solution.py:45
  48.1 1.3 %collective-permute-done.18 = f32[2,512]{1,0:T(2,128)S(1)} collective-permute-done((f32[2,512]{1,0:T(2,128)S(1)}, f32[2,512]{1,0:T(2,128)S(1)}, u32[]{:S(2)}, u32[]{:S(2)}) %collective-permute-start.18) | collective-permute-done | bytes 4128 | tf_op jit(solution)/shard_map/ppermute | solution.py:45
  49.4 0.6 %add_add_fusion.1 = f32[2,512]{1,0:T(2,128)} fusion(f32[2,512]{1,0:T(2,128)S(1)} %collective-permute-done.18, f32[2,512]{1,0:T(2,128)S(1)} %collective-permute-done.17, f32[2,512]{1,0:T(2,128)S(1)} %pad_maximum_fusion.7, f32[2,512]{1,0:T(2,128)S(1)} %collective-permute-done.16), kind=kLoop, calls=%fused_computation.26 | loop fusion | flops 3072 | bytes 20480 | tf_op jit(solution)/shard_map/add | solution.py:135
  (24 shorter events, 0.3 us)
Async XLA Ops:
  0.6 3.1 %copy-start = (f32[2,128,512]{2,1,0:T(8,128)S(1)}, f32[2,128,512]{2,1,0:T(8,128)}, u32[]{:S(2)}) copy-start(f32[2,128,512]{2,1,0:T(8,128)} %param.5) | copy-start | bytes 1572868
  0.6 27.4 %collective-permute-start = (f32[2,256,128]{2,1,0:T(8,128)}, f32[2,256,128]{2,1,0:T(8,128)S(1)}, u32[]{:S(2)}, u32[]{:S(2)}) collective-permute-start(f32[2,256,128]{2,1,0:T(8,128)} %refs_0_.1), channel_id=1, source_target_pairs={{0,2},{2,4},{4,6},{6,0},{1,3},{3,5},{5,7},{7,1},{8,10},{10,12},{12... | collective-permute-start | bytes 786440 | tf_op jit(solution)/shard_map/ppermute | solution.py:42
  5.4 3.6 %copy-start.1 = (f32[2,256,128]{2,1,0:T(8,128)S(1)}, f32[2,256,128]{2,1,0:T(8,128)}, u32[]{:S(2)}) copy-start(f32[2,256,128]{2,1,0:T(8,128)} %refs_0_.1) | copy-start | bytes 786436
  5.4 7.6 %collective-permute-start.3 = (f32[2,32,512]{2,1,0:T(8,128)S(1)}, f32[2,32,512]{2,1,0:T(8,128)S(1)}, u32[]{:S(2)}, u32[]{:S(2)}) collective-permute-start(f32[2,32,512]{2,1,0:T(8,128)S(1)} %get-tuple-element.20), channel_id=1, source_target_pairs={{0,24},{8,16},{16,8},{24,0},{1,25},{9,17},{17,9},{25,1},{2,26},{10... | collective-permute-start | bytes 393224 | tf_op jit(solution)/shard_map/ppermute | solution.py:45
  7.9 6.2 %collective-permute-start.4 = (f32[2,32,512]{2,1,0:T(8,128)S(1)}, f32[2,32,512]{2,1,0:T(8,128)S(1)}, u32[]{:S(2)}, u32[]{:S(2)}) collective-permute-start(f32[2,32,512]{2,1,0:T(8,128)S(1)} %get-tuple-element.19), channel_id=1, source_target_pairs={{0,16},{8,24},{16,0},{24,8},{1,17},{9,25},{17,1},{25,9},{2,18},{10... | collective-permute-start | bytes 393224 | tf_op jit(solution)/shard_map/ppermute | solution.py:45
  8.4 5.8 %collective-permute-start.5 = (f32[2,32,512]{2,1,0:T(8,128)S(1)}, f32[2,32,512]{2,1,0:T(8,128)S(1)}, u32[]{:S(2)}, u32[]{:S(2)}) collective-permute-start(f32[2,32,512]{2,1,0:T(8,128)S(1)} %get-tuple-element.18), channel_id=1, source_target_pairs={{0,8},{8,0},{16,24},{24,16},{1,9},{9,1},{17,25},{25,17},{2,10},{10... | collective-permute-start | bytes 393224 | tf_op jit(solution)/shard_map/ppermute | solution.py:45
  9.0 9.8 %collective-permute-start.1 = (f32[2,256,128]{2,1,0:T(8,128)S(1)}, f32[2,256,128]{2,1,0:T(8,128)S(1)}, u32[]{:S(2)}, u32[]{:S(2)}) collective-permute-start(f32[2,256,128]{2,1,0:T(8,128)S(1)} %copy-done.1), channel_id=1, source_target_pairs={{0,6},{2,0},{4,2},{6,4},{1,7},{3,1},{5,3},{7,5},{8,14},{10,8},{12,... | collective-permute-start | bytes 786440 | tf_op jit(solution)/shard_map/ppermute | solution.py:42
  12.0 1.0 %copy-start.2 = (s32[2,4]{1,0:T(2,128)S(1)}, s32[2,4]{1,0:T(2,128)}, u32[]{:S(2)}) copy-start(s32[2,4]{1,0:T(2,128)} %param.7) | copy-start | bytes 100
  14.3 7.7 %collective-permute-start.6 = (f32[2,32,128]{2,1,0:T(8,128)S(1)}, f32[2,32,128]{2,1,0:T(8,128)S(1)}, u32[]{:S(2)}, u32[]{:S(2)}) collective-permute-start(f32[2,32,128]{2,1,0:T(8,128)S(1)} %get-tuple-element.31), channel_id=1, source_target_pairs={{0,2},{2,0},{4,6},{6,4},{1,3},{3,1},{5,7},{7,5},{8,10},{10,8},{12,... | collective-permute-start | bytes 98312 | tf_op jit(solution)/shard_map/ppermute | solution.py:45
  15.9 6.1 %collective-permute-start.7 = (f32[2,32,128]{2,1,0:T(8,128)S(1)}, f32[2,32,128]{2,1,0:T(8,128)S(1)}, u32[]{:S(2)}, u32[]{:S(2)}) collective-permute-start(f32[2,32,128]{2,1,0:T(8,128)S(1)} %get-tuple-element.30), channel_id=1, source_target_pairs={{0,4},{2,6},{4,0},{6,2},{1,5},{3,7},{5,1},{7,3},{8,12},{10,14},{12... | collective-permute-start | bytes 98312 | tf_op jit(solution)/shard_map/ppermute | solution.py:45
  18.2 6.1 %collective-permute-start.8 = (f32[2,32,128]{2,1,0:T(8,128)S(1)}, f32[2,32,128]{2,1,0:T(8,128)S(1)}, u32[]{:S(2)}, u32[]{:S(2)}) collective-permute-start(f32[2,32,128]{2,1,0:T(8,128)S(1)} %get-tuple-element.29), channel_id=1, source_target_pairs={{0,6},{2,4},{4,2},{6,0},{1,7},{3,5},{5,3},{7,1},{8,14},{10,12},{12... | collective-permute-start | bytes 98312 | tf_op jit(solution)/shard_map/ppermute | solution.py:45
  18.8 13.6 %collective-permute-start.2 = (f32[2,256,128]{2,1,0:T(8,128)S(1)}, f32[2,256,128]{2,1,0:T(8,128)S(1)}, u32[]{:S(2)}, u32[]{:S(2)}) collective-permute-start(f32[2,256,128]{2,1,0:T(8,128)S(1)} %collective-permute-done.1.refs_3_), channel_id=1, source_target_pairs={{0,6},{2,0},{4,2},{6,4},{1,7},{3,1},{5,3},{7,5},{8,14},{10,8},{12,... | collective-permute-start | bytes 786440 | tf_op jit(solution)/shard_map/ppermute | solution.py:42
  24.3 5.6 %collective-permute-start.10 = (f32[4,2,32,128]{3,2,1,0:T(8,128)S(1)}, f32[4,2,32,128]{3,2,1,0:T(8,128)S(1)}, u32[]{:S(2)}, u32[]{:S(2)}) collective-permute-start(f32[4,2,32,128]{3,2,1,0:T(8,128)S(1)} %pad_maximum_fusion.2.refs_4_), channel_id=1, source_target_pairs={{0,16},{8,24},{16,0},{24,8},{1,17},{9,25},{17,1},{25,9},{2,18},{10... | collective-permute-start | bytes 393224 | tf_op jit(solution)/shard_map/ppermute | solution.py:45
  25.9 5.9 %collective-permute-start.11 = (f32[4,2,32,128]{3,2,1,0:T(8,128)S(1)}, f32[4,2,32,128]{3,2,1,0:T(8,128)S(1)}, u32[]{:S(2)}, u32[]{:S(2)}) collective-permute-start(f32[4,2,32,128]{3,2,1,0:T(8,128)S(1)} %pad_maximum_fusion.2.refs_4_), channel_id=1, source_target_pairs={{0,24},{8,16},{16,8},{24,0},{1,25},{9,17},{17,9},{25,1},{2,26},{10... | collective-permute-start | bytes 393224 | tf_op jit(solution)/shard_map/ppermute | solution.py:45
  27.4 5.0 %collective-permute-start.9 = (f32[4,2,32,128]{3,2,1,0:T(8,128)S(1)}, f32[4,2,32,128]{3,2,1,0:T(8,128)S(1)}, u32[]{:S(2)}, u32[]{:S(2)}) collective-permute-start(f32[4,2,32,128]{3,2,1,0:T(8,128)S(1)} %pad_maximum_fusion.2.refs_4_), channel_id=1, source_target_pairs={{0,8},{8,0},{16,24},{24,16},{1,9},{9,1},{17,25},{25,17},{2,10},{10... | collective-permute-start | bytes 393224 | tf_op jit(solution)/shard_map/ppermute | solution.py:45
  34.0 1.8 %collective-permute-start.12 = (f32[2,384,128]{2,1,0:T(8,128)S(1)}, f32[2,384,128]{2,1,0:T(8,128)S(1)}, u32[]{:S(2)}, u32[]{:S(2)}) collective-permute-start(f32[2,384,128]{2,1,0:T(8,128)S(1)} %shard_map.59), channel_id=1, source_target_pairs={{0,1},{1,0},{2,3},{3,2},{4,5},{5,4},{6,7},{7,6},{8,9},{9,8},{10,11... | collective-permute-start | bytes 1179656 | tf_op jit(solution)/shard_map/ppermute | solution.py:42
  36.1 6.2 %collective-permute-start.13 = (f32[72,128]{1,0:T(8,128)S(1)}, f32[72,128]{1,0:T(8,128)S(1)}, u32[]{:S(2)}, u32[]{:S(2)}) collective-permute-start(f32[72,128]{1,0:T(8,128)S(1)} %get-tuple-element.34), channel_id=1, source_target_pairs={{0,6},{2,4},{4,2},{6,0},{1,7},{3,5},{5,3},{7,1},{8,14},{10,12},{12... | collective-permute-start | bytes 110600 | tf_op jit(solution)/shard_map/ppermute | solution.py:45
  36.3 6.0 %collective-permute-start.14 = (f32[72,128]{1,0:T(8,128)S(1)}, f32[72,128]{1,0:T(8,128)S(1)}, u32[]{:S(2)}, u32[]{:S(2)}) collective-permute-start(f32[72,128]{1,0:T(8,128)S(1)} %get-tuple-element.33), channel_id=1, source_target_pairs={{0,4},{2,6},{4,0},{6,2},{1,5},{3,7},{5,1},{7,3},{8,12},{10,14},{12... | collective-permute-start | bytes 110600 | tf_op jit(solution)/shard_map/ppermute | solution.py:45
  36.9 5.7 %collective-permute-start.15 = (f32[72,128]{1,0:T(8,128)S(1)}, f32[72,128]{1,0:T(8,128)S(1)}, u32[]{:S(2)}, u32[]{:S(2)}) collective-permute-start(f32[72,128]{1,0:T(8,128)S(1)} %get-tuple-element.32), channel_id=1, source_target_pairs={{0,2},{2,0},{4,6},{6,4},{1,3},{3,1},{5,7},{7,5},{8,10},{10,8},{12,... | collective-permute-start | bytes 110600 | tf_op jit(solution)/shard_map/ppermute | solution.py:45
  42.8 4.6 %collective-permute-start.16 = (f32[2,512]{1,0:T(2,128)S(1)}, f32[2,512]{1,0:T(2,128)S(1)}, u32[]{:S(2)}, u32[]{:S(2)}) collective-permute-start(f32[2,512]{1,0:T(2,128)S(1)} %pad_maximum_fusion.7), channel_id=1, source_target_pairs={{0,24},{8,16},{16,8},{24,0},{1,25},{9,17},{17,9},{25,1},{2,26},{10... | collective-permute-start | bytes 12296 | tf_op jit(solution)/shard_map/ppermute | solution.py:45
  44.5 3.6 %collective-permute-start.17 = (f32[2,512]{1,0:T(2,128)S(1)}, f32[2,512]{1,0:T(2,128)S(1)}, u32[]{:S(2)}, u32[]{:S(2)}) collective-permute-start(f32[2,512]{1,0:T(2,128)S(1)} %pad_maximum_fusion.7), channel_id=1, source_target_pairs={{0,16},{8,24},{16,0},{24,8},{1,17},{9,25},{17,1},{25,9},{2,18},{10... | collective-permute-start | bytes 12296 | tf_op jit(solution)/shard_map/ppermute | solution.py:45
  45.8 3.6 %collective-permute-start.18 = (f32[2,512]{1,0:T(2,128)S(1)}, f32[2,512]{1,0:T(2,128)S(1)}, u32[]{:S(2)}, u32[]{:S(2)}) collective-permute-start(f32[2,512]{1,0:T(2,128)S(1)} %pad_maximum_fusion.7), channel_id=1, source_target_pairs={{0,8},{8,0},{16,24},{24,16},{1,9},{9,1},{17,25},{25,17},{2,10},{10... | collective-permute-start | bytes 12296 | tf_op jit(solution)/shard_map/ppermute | solution.py:45

commit v21 on v20

--- a/solution.py
+++ b/solution.py
@@ -38,9 +38,6 @@
     fine = Mesh(mesh.devices.reshape(rows, deep, cores), ("row", "z", "core"))
     highest = lax.Precision.HIGHEST
 
-    def shifted(array, axis, size, shift):
-        return lax.ppermute(array, axis, [(i, (i + shift) % size) for i in range(size)])
-
     def traded(array, axis, size, other):
         return lax.ppermute(array, axis, [(i, i ^ other) for i in range(size)])
 
@@ -64,14 +61,12 @@
                 value = jnp.where(place ^ at == d, slots[d], value)
             return value
 
-        early = [d for d in range(1, deep) if not deep < 4 * d < 3 * deep]
-        late = [d for d in range(1, deep) if d not in early]
-        far = {d: shifted(ancestor, "z", deep, d) for d in early[:1]}
+        far = {d: traded(ancestor, "z", deep, d) for d in range(2, deep, 2)}
 
         mine = lax.dynamic_slice_in_dim(panel, row * depth, depth, axis=2)
         partial = jnp.einsum("srw,swv->srv", mine, factor_inv, precision=highest)
         partial, held_back = lax.optimization_barrier((partial, ancestor))
-        far |= {d: shifted(held_back, "z", deep, d) for d in early[1:]}
+        far |= {d: traded(held_back, "z", deep, d) for d in range(1, min(deep, 2))}
 
         def rows_of(r):
             return lax.dynamic_slice_in_dim(partial, r * piece, piece, axis=1)
@@ -86,19 +81,17 @@
 
         slots = [traded(columns_of(scaled, z ^ d), "z", deep, d) for d in reversed(range(1, deep))]
         slots = [columns_of(scaled, z)] + slots[::-1]
-        if deep > 1:
-            for d in reversed(late):
-                far[d] = shifted(far[d + 1], "z", deep, deep - 1)
+        far |= {d: traded(far[d - 1], "z", deep, 1) for d in range(3, deep, 2)}
         slots = gathered(jnp.stack(slots), "row", rows)
 
         count = jnp.arange(deep, dtype=jnp.int32)
-        at = (z - count) % deep
+        at = z ^ count
         stored = jnp.sum(
             jnp.where(pattern[:, :, None] == at, count[:, None], 0), axis=1, dtype=jnp.int32
         )
         from_z = (z ^ stored).reshape(-1)
         quarter = row ^ jnp.arange(rows, dtype=jnp.int32)
-        own_tile = (z - row * tiles - jnp.arange(tiles, dtype=jnp.int32)) % deep
+        own_tile = z ^ (row * tiles + jnp.arange(tiles, dtype=jnp.int32))
         place = jnp.concatenate([from_z, quarter, own_tile])
         height = ancestor.shape[1]
         whole = pl.BlockSpec(memory_space=pltpu.VMEM)
@@ -110,7 +103,7 @@
             scratch_shapes=[pltpu.VMEM((groups, deep, chunk, part), jnp.float32)],
             compiler_params=pltpu.CompilerParams(vmem_limit_bytes=32 * 1024 * 1024),
         )(place, ancestor, *[far[d] for d in range(1, deep)], *slots)
-        other = shifted(product, "core", cores, 1)
+        other = traded(product, "core", cores, 1)
 
         own, own_other = [
             array[:, height:].reshape(groups, tiles, chunk, part) for array in (product, other)

time: 50.2 us -> 52.4 us (1.044)
  waiting for transfers between devices: 13.8 us -> 19.1 us
  starting transfers between devices: 29 us -> 26 us
    ppermute x4 -> x0, starting transfers between devices: 9.42 us -> none  [shifted(): lax.ppermute(array, axis, [(i, (i + shift) % size) for i in range(size)])]
    ppermute x15 -> x19, waiting for transfers between devices: 12.2 us -> 19.1 us  [traded(): return lax.ppermute(array, axis, [(i, i ^ other) for i in range(size)])]
    ppermute x15 -> x19, starting transfers between devices: 19.6 us -> 26 us  [traded(): return lax.ppermute(array, axis, [(i, i ^ other) for i in range(size)])]
    ppermute x4 -> x0, waiting for transfers between devices: 1.59 us -> none  [shifted(): lax.ppermute(array, axis, [(i, (i + shift) % size) for i in range(size)])]
  transfers between devices with their start and end apart: 19 -> 19, of which waited for: 12 -> 13; matrix products, arithmetic and copies ran while one was open for 7% -> 7% of each run, Pallas kernels for 0% -> 0%
where the time goes in v21:
time: 52.4 us; the launch traced here: 52.3 us
  starting transfers between devices  26 us (50%)
  waiting for transfers between devices  19.1 us (36%)
  other arithmetic  2.83 us (5%)
  matrix products  1.61 us (3%)
  Pallas kernels  1.61 us (3%)
  between operations  0.85 us (2%)
    ppermute x19, starting transfers between devices, traded(): return lax.ppermute(array, axis, [(i, i ^ other) for i in range(size)])  26 us
    ppermute x19, waiting for transfers between devices, traded(): return lax.ppermute(array, axis, [(i, i ^ other) for i in range(size)])  19.1 us
    dot_general x1, matrix products, per_device(): partial = jnp.einsum('srw,swv->srv', mine, factor_inv, precision=highest)  1.61 us
    pallas_call x1, Pallas kernels, per_device(): pl.pallas_call(functools.partial(multiply_tiles, deep, rows), out_shape=j...  1.61 us
  transfers between devices with their start and end apart: 19, of which 13 were waited for; matrix products, arithmetic and copies ran while one was open for 7% of the time, Pallas kernels for 0%

profile of v21, /device:TPU:0, one launch (start us, length us, event | category | flops | bytes accessed | tf_op | source)
XLA Modules:
  0.0 52.3 jit_solution(16517154724369418867)
XLA Ops:
  0.6 0.0 copy-start
  0.6 4.1 %collective-permute-start.1 = (f32[2,256,128]{2,1,0:T(8,128)}, f32[2,256,128]{2,1,0:T(8,128)S(1)}, u32[]{:S(2)}, u32[]{:S(2)}) collective-permute-start(f32[2,256,128]{2,1,0:T(8,128)} %refs_0_.1), channel_id=1, source_target_pairs={{0,4},{2,6},{4,0},{6,2},{1,5},{3,7},{5,1},{7,3},{8,12},{10,14},{12... | collective-permute-start | bytes 786440 | tf_op jit(solution)/shard_map/ppermute | solution.py:42
  4.7 1.6 %fusion = f32[2,128,512]{2,1,0:T(8,128)S(1)} fusion(f32[2,128,512]{2,1,0:T(8,128)} %param.6, f32[2,128,512]{2,1,0:T(8,128)S(1)} %copy-done, s32[]{:T(128)S(6)} %select_n.134), kind=kOutput, calls=%fused_computation.10 | convolution fusion | flops 201326592 | bytes 1179652 | tf_op jit(solution)/shard_map/srw,swv->srv/dot_general | solution.py:67
  6.4 0.0 copy-start.1
  6.4 2.5 %collective-permute-start.3 = (f32[2,32,512]{2,1,0:T(8,128)S(1)}, f32[2,32,512]{2,1,0:T(8,128)S(1)}, u32[]{:S(2)}, u32[]{:S(2)}) collective-permute-start(f32[2,32,512]{2,1,0:T(8,128)S(1)} %get-tuple-element.20), channel_id=1, source_target_pairs={{0,24},{8,16},{16,8},{24,0},{1,25},{9,17},{17,9},{25,1},{2,26},{10... | collective-permute-start | bytes 393224 | tf_op jit(solution)/shard_map/ppermute | solution.py:42
  9.0 0.5 collective-permute-start.4
  9.5 0.5 %collective-permute-start.5 = (f32[2,32,512]{2,1,0:T(8,128)S(1)}, f32[2,32,512]{2,1,0:T(8,128)S(1)}, u32[]{:S(2)}, u32[]{:S(2)}) collective-permute-start(f32[2,32,512]{2,1,0:T(8,128)S(1)} %get-tuple-element.18), channel_id=1, source_target_pairs={{0,8},{8,0},{16,24},{24,16},{1,9},{9,1},{17,25},{25,17},{2,10},{10... | collective-permute-start | bytes 393224 | tf_op jit(solution)/shard_map/ppermute | solution.py:42
  10.0 1.6 %collective-permute-start = (f32[2,256,128]{2,1,0:T(8,128)S(1)}, f32[2,256,128]{2,1,0:T(8,128)S(1)}, u32[]{:S(2)}, u32[]{:S(2)}) collective-permute-start(f32[2,256,128]{2,1,0:T(8,128)S(1)} %copy-done.1), channel_id=1, source_target_pairs={{0,2},{2,0},{4,6},{6,4},{1,3},{3,1},{5,7},{7,5},{8,10},{10,8},{12,... | collective-permute-start | bytes 786440 | tf_op jit(solution)/shard_map/ppermute | solution.py:42
  11.6 0.9 %multiply_reduce_fusion.1 = f32[2,128]{1,0:T(2,128)S(1)} fusion(f32[2,128,512]{2,1,0:T(8,128)} %param.6, s32[]{:T(128)S(6)} %select_n.139), kind=kLoop, calls=%fused_computation.9 | loop fusion | flops 65280 | bytes 132100 | tf_op jit(solution)/shard_map/reduce_sum | solution.py:75
  12.5 0.1 select_reduce_fusion
  12.6 0.3 collective-permute-done.3
  12.9 2.3 %collective-permute-done.4 = f32[2,32,512]{2,1,0:T(8,128)S(1)} collective-permute-done((f32[2,32,512]{2,1,0:T(8,128)S(1)}, f32[2,32,512]{2,1,0:T(8,128)S(1)}, u32[]{:S(2)}, u32[]{:S(2)}) %collective-permute-start.4) | collective-permute-done | bytes 131104 | tf_op jit(solution)/shard_map/ppermute | solution.py:42
  15.2 0.1 collective-permute-done.5
  15.3 1.6 %collective-permute-start.6 = (f32[2,32,128]{2,1,0:T(8,128)S(1)}, f32[2,32,128]{2,1,0:T(8,128)S(1)}, u32[]{:S(2)}, u32[]{:S(2)}) collective-permute-start(f32[2,32,128]{2,1,0:T(8,128)S(1)} %get-tuple-element.31), channel_id=1, source_target_pairs={{0,2},{2,0},{4,6},{6,4},{1,3},{3,1},{5,7},{7,5},{8,10},{10,8},{12,... | collective-permute-start | bytes 98312 | tf_op jit(solution)/shard_map/ppermute | solution.py:42
  17.0 1.2 %collective-permute-start.7 = (f32[2,32,128]{2,1,0:T(8,128)S(1)}, f32[2,32,128]{2,1,0:T(8,128)S(1)}, u32[]{:S(2)}, u32[]{:S(2)}) collective-permute-start(f32[2,32,128]{2,1,0:T(8,128)S(1)} %get-tuple-element.30), channel_id=1, source_target_pairs={{0,4},{2,6},{4,0},{6,2},{1,5},{3,7},{5,1},{7,3},{8,12},{10,14},{12... | collective-permute-start | bytes 98312 | tf_op jit(solution)/shard_map/ppermute | solution.py:42
  18.2 1.6 %collective-permute-start.8 = (f32[2,32,128]{2,1,0:T(8,128)S(1)}, f32[2,32,128]{2,1,0:T(8,128)S(1)}, u32[]{:S(2)}, u32[]{:S(2)}) collective-permute-start(f32[2,32,128]{2,1,0:T(8,128)S(1)} %get-tuple-element.29), channel_id=1, source_target_pairs={{0,6},{2,4},{4,2},{6,0},{1,7},{3,5},{5,3},{7,1},{8,14},{10,12},{12... | collective-permute-start | bytes 98312 | tf_op jit(solution)/shard_map/ppermute | solution.py:42
  19.8 0.0 collective-permute-done.1.refs_2_
  19.8 0.7 %collective-permute-start.2 = (f32[2,256,128]{2,1,0:T(8,128)S(1)}, f32[2,256,128]{2,1,0:T(8,128)S(1)}, u32[]{:S(2)}, u32[]{:S(2)}) collective-permute-start(f32[2,256,128]{2,1,0:T(8,128)S(1)} %collective-permute-done.1.refs_2_), channel_id=1, source_target_pairs={{0,2},{2,0},{4,6},{6,4},{1,3},{3,1},{5,7},{7,5},{8,10},{10,8},{12,... | collective-permute-start | bytes 786440 | tf_op jit(solution)/shard_map/ppermute | solution.py:42
  20.5 4.1 %collective-permute-done.6 = f32[2,32,128]{2,1,0:T(8,128)S(1)} collective-permute-done((f32[2,32,128]{2,1,0:T(8,128)S(1)}, f32[2,32,128]{2,1,0:T(8,128)S(1)}, u32[]{:S(2)}, u32[]{:S(2)}) %collective-permute-start.6) | collective-permute-done | bytes 32800 | tf_op jit(solution)/shard_map/ppermute | solution.py:42
  24.5 0.0 collective-permute-done.8
  24.6 1.7 %collective-permute-start.10 = (f32[4,2,32,128]{3,2,1,0:T(8,128)S(1)}, f32[4,2,32,128]{3,2,1,0:T(8,128)S(1)}, u32[]{:S(2)}, u32[]{:S(2)}) collective-permute-start(f32[4,2,32,128]{3,2,1,0:T(8,128)S(1)} %pad_maximum_fusion.2.refs_4_), channel_id=1, source_target_pairs={{0,16},{8,24},{16,0},{24,8},{1,17},{9,25},{17,1},{25,9},{2,18},{10... | collective-permute-start | bytes 393224 | tf_op jit(solution)/shard_map/ppermute | solution.py:42
  26.2 1.4 %collective-permute-start.11 = (f32[4,2,32,128]{3,2,1,0:T(8,128)S(1)}, f32[4,2,32,128]{3,2,1,0:T(8,128)S(1)}, u32[]{:S(2)}, u32[]{:S(2)}) collective-permute-start(f32[4,2,32,128]{3,2,1,0:T(8,128)S(1)} %pad_maximum_fusion.2.refs_4_), channel_id=1, source_target_pairs={{0,24},{8,16},{16,8},{24,0},{1,25},{9,17},{17,9},{25,1},{2,26},{10... | collective-permute-start | bytes 393224 | tf_op jit(solution)/shard_map/ppermute | solution.py:42
  27.7 0.4 collective-permute-start.9
  28.1 0.1 xor.67
  28.2 0.1 pad_add_fusion.place
  28.3 1.6 %collective-permute-done.10.refs_6_ = f32[4,2,32,128]{3,2,1,0:T(8,128)S(1)} collective-permute-done((f32[4,2,32,128]{3,2,1,0:T(8,128)S(1)}, f32[4,2,32,128]{3,2,1,0:T(8,128)S(1)}, u32[]{:S(2)}, u32[]{:S(2)}) %collective-permute-start.10) | collective-permute-done | bytes 131104 | tf_op jit(solution)/shard_map/ppermute | solution.py:42
  29.9 2.2 %collective-permute-done.11.refs_7_ = f32[4,2,32,128]{3,2,1,0:T(8,128)S(1)} collective-permute-done((f32[4,2,32,128]{3,2,1,0:T(8,128)S(1)}, f32[4,2,32,128]{3,2,1,0:T(8,128)S(1)}, u32[]{:S(2)}, u32[]{:S(2)}) %collective-permute-start.11) | collective-permute-done | bytes 131104 | tf_op jit(solution)/shard_map/ppermute | solution.py:42
  32.1 0.5 %collective-permute-done.9.refs_5_ = f32[4,2,32,128]{3,2,1,0:T(8,128)S(1)} collective-permute-done((f32[4,2,32,128]{3,2,1,0:T(8,128)S(1)}, f32[4,2,32,128]{3,2,1,0:T(8,128)S(1)}, u32[]{:S(2)}, u32[]{:S(2)}) %collective-permute-start.9) | collective-permute-done | bytes 131104 | tf_op jit(solution)/shard_map/ppermute | solution.py:42
  32.7 1.6 %shard_map.59 = f32[2,384,128]{2,1,0:T(8,128)S(1)} custom-call(s32[13]{0:T(128)S(1)} %pad_add_fusion.place, f32[2,256,128]{2,1,0:T(8,128)S(1)} %copy-done.1, f32[2,256,128]{2,1,0:T(8,128)S(1)} %collective-permute-done.refs_1_, f32[2,256,128]{2,1,0:T(8,128)S(1)} %collective-permute-done.1.refs_2_, f32[2,256,128]{2,1,0:T(8,128)S(1)} %collective-permute-done.2.refs_3_, ...), custom_call_target="tpu_custom_call" | custom-call | tf_op jit(solution)/shard_map/pallas_call | solution.py:98
  34.3 0.1 collective-permute-start.12
  34.4 0.1 pad.15.clone
  34.5 1.6 %collective-permute-done.12 = f32[2,384,128]{2,1,0:T(8,128)S(1)} collective-permute-done((f32[2,384,128]{2,1,0:T(8,128)S(1)}, f32[2,384,128]{2,1,0:T(8,128)S(1)}, u32[]{:S(2)}, u32[]{:S(2)}) %collective-permute-start.12) | collective-permute-done | bytes 393248 | tf_op jit(solution)/shard_map/ppermute | solution.py:42
  36.1 0.1 multiply_reduce_fusion
  36.3 0.1 fusion.4
  36.3 3.7 %collective-permute-start.13 = (f32[72,128]{1,0:T(8,128)S(1)}, f32[72,128]{1,0:T(8,128)S(1)}, u32[]{:S(2)}, u32[]{:S(2)}) collective-permute-start(f32[72,128]{1,0:T(8,128)S(1)} %get-tuple-element.34), channel_id=1, source_target_pairs={{0,6},{2,4},{4,2},{6,0},{1,7},{3,5},{5,3},{7,1},{8,14},{10,12},{12... | collective-permute-start | bytes 110600 | tf_op jit(solution)/shard_map/ppermute | solution.py:42
  40.1 0.7 %collective-permute-start.15 = (f32[72,128]{1,0:T(8,128)S(1)}, f32[72,128]{1,0:T(8,128)S(1)}, u32[]{:S(2)}, u32[]{:S(2)}) collective-permute-start(f32[72,128]{1,0:T(8,128)S(1)} %get-tuple-element.32), channel_id=1, source_target_pairs={{0,2},{2,0},{4,6},{6,4},{1,3},{3,1},{5,7},{7,5},{8,10},{10,8},{12,... | collective-permute-start | bytes 110600 | tf_op jit(solution)/shard_map/ppermute | solution.py:42
  40.8 1.5 %collective-permute-done.13 = f32[72,128]{1,0:T(8,128)S(1)} collective-permute-done((f32[72,128]{1,0:T(8,128)S(1)}, f32[72,128]{1,0:T(8,128)S(1)}, u32[]{:S(2)}, u32[]{:S(2)}) %collective-permute-start.13) | collective-permute-done | bytes 36896 | tf_op jit(solution)/shard_map/ppermute | solution.py:42
  42.3 2.6 %collective-permute-done.14 = f32[72,128]{1,0:T(8,128)S(1)} collective-permute-done((f32[72,128]{1,0:T(8,128)S(1)}, f32[72,128]{1,0:T(8,128)S(1)}, u32[]{:S(2)}, u32[]{:S(2)}) %collective-permute-start.14) | collective-permute-done | bytes 36896 | tf_op jit(solution)/shard_map/ppermute | solution.py:42
  44.9 0.1 select_select_fusion.2
  45.0 0.1 select_select_fusion.3
  45.1 2.4 %collective-permute-start.16 = (f32[2,512]{1,0:T(2,128)S(1)}, f32[2,512]{1,0:T(2,128)S(1)}, u32[]{:S(2)}, u32[]{:S(2)}) collective-permute-start(f32[2,512]{1,0:T(2,128)S(1)} %pad_maximum_fusion.7), channel_id=1, source_target_pairs={{0,24},{8,16},{16,8},{24,0},{1,25},{9,17},{17,9},{25,1},{2,26},{10... | collective-permute-start | bytes 12296 | tf_op jit(solution)/shard_map/ppermute | solution.py:42
  47.5 0.5 collective-permute-start.17
  48.1 0.6 %collective-permute-start.18 = (f32[2,512]{1,0:T(2,128)S(1)}, f32[2,512]{1,0:T(2,128)S(1)}, u32[]{:S(2)}, u32[]{:S(2)}) collective-permute-start(f32[2,512]{1,0:T(2,128)S(1)} %pad_maximum_fusion.7), channel_id=1, source_target_pairs={{0,8},{8,0},{16,24},{24,16},{1,9},{9,1},{17,25},{25,17},{2,10},{10... | collective-permute-start | bytes 12296 | tf_op jit(solution)/shard_map/ppermute | solution.py:42
  48.7 0.7 %slice_negate_fusion = f32[64,512]{1,0:T(8,128)} fusion(f32[72,512]{1,0:T(8,128)S(1)} %pad_maximum_fusion.1), kind=kLoop, calls=%fused_computation.4 | loop fusion | flops 32768 | bytes 262144 | tf_op jit(solution)/shard_map/neg | solution.py:124
  49.4 0.3 collective-permute-done.16
  49.7 1.5 %collective-permute-done.17 = f32[2,512]{1,0:T(2,128)S(1)} collective-permute-done((f32[2,512]{1,0:T(2,128)S(1)}, f32[2,512]{1,0:T(2,128)S(1)}, u32[]{:S(2)}, u32[]{:S(2)}) %collective-permute-start.17) | collective-permute-done | bytes 4128 | tf_op jit(solution)/shard_map/ppermute | solution.py:42
  51.2 0.5 collective-permute-done.18
  51.7 0.6 %add_add_fusion.1 = f32[2,512]{1,0:T(2,128)} fusion(f32[2,512]{1,0:T(2,128)S(1)} %collective-permute-done.18, f32[2,512]{1,0:T(2,128)S(1)} %collective-permute-done.17, f32[2,512]{1,0:T(2,128)S(1)} %pad_maximum_fusion.7, f32[2,512]{1,0:T(2,128)S(1)} %collective-permute-done.16), kind=kLoop, calls=%fused_computation.26 | loop fusion | flops 3072 | bytes 20480 | tf_op jit(solution)/shard_map/add | solution.py:128
  (24 shorter events, 0.3 us)
Async XLA Ops:
  0.6 4.1 %copy-start = (f32[2,128,512]{2,1,0:T(8,128)S(1)}, f32[2,128,512]{2,1,0:T(8,128)}, u32[]{:S(2)}) copy-start(f32[2,128,512]{2,1,0:T(8,128)} %param.5) | copy-start | bytes 1572868
  0.6 19.1 %collective-permute-start.1 = (f32[2,256,128]{2,1,0:T(8,128)}, f32[2,256,128]{2,1,0:T(8,128)S(1)}, u32[]{:S(2)}, u32[]{:S(2)}) collective-permute-start(f32[2,256,128]{2,1,0:T(8,128)} %refs_0_.1), channel_id=1, source_target_pairs={{0,4},{2,6},{4,0},{6,2},{1,5},{3,7},{5,1},{7,3},{8,12},{10,14},{12... | collective-permute-start | bytes 786440 | tf_op jit(solution)/shard_map/ppermute | solution.py:42
  6.4 3.6 %copy-start.1 = (f32[2,256,128]{2,1,0:T(8,128)S(1)}, f32[2,256,128]{2,1,0:T(8,128)}, u32[]{:S(2)}) copy-start(f32[2,256,128]{2,1,0:T(8,128)} %refs_0_.1) | copy-start | bytes 786436
  6.4 6.5 %collective-permute-start.3 = (f32[2,32,512]{2,1,0:T(8,128)S(1)}, f32[2,32,512]{2,1,0:T(8,128)S(1)}, u32[]{:S(2)}, u32[]{:S(2)}) collective-permute-start(f32[2,32,512]{2,1,0:T(8,128)S(1)} %get-tuple-element.20), channel_id=1, source_target_pairs={{0,24},{8,16},{16,8},{24,0},{1,25},{9,17},{17,9},{25,1},{2,26},{10... | collective-permute-start | bytes 393224 | tf_op jit(solution)/shard_map/ppermute | solution.py:42
  9.0 6.2 %collective-permute-start.4 = (f32[2,32,512]{2,1,0:T(8,128)S(1)}, f32[2,32,512]{2,1,0:T(8,128)S(1)}, u32[]{:S(2)}, u32[]{:S(2)}) collective-permute-start(f32[2,32,512]{2,1,0:T(8,128)S(1)} %get-tuple-element.19), channel_id=1, source_target_pairs={{0,16},{8,24},{16,0},{24,8},{1,17},{9,25},{17,1},{25,9},{2,18},{10... | collective-permute-start | bytes 393224 | tf_op jit(solution)/shard_map/ppermute | solution.py:42
  9.5 5.8 %collective-permute-start.5 = (f32[2,32,512]{2,1,0:T(8,128)S(1)}, f32[2,32,512]{2,1,0:T(8,128)S(1)}, u32[]{:S(2)}, u32[]{:S(2)}) collective-permute-start(f32[2,32,512]{2,1,0:T(8,128)S(1)} %get-tuple-element.18), channel_id=1, source_target_pairs={{0,8},{8,0},{16,24},{24,16},{1,9},{9,1},{17,25},{25,17},{2,10},{10... | collective-permute-start | bytes 393224 | tf_op jit(solution)/shard_map/ppermute | solution.py:42
  10.0 18.3 %collective-permute-start = (f32[2,256,128]{2,1,0:T(8,128)S(1)}, f32[2,256,128]{2,1,0:T(8,128)S(1)}, u32[]{:S(2)}, u32[]{:S(2)}) collective-permute-start(f32[2,256,128]{2,1,0:T(8,128)S(1)} %copy-done.1), channel_id=1, source_target_pairs={{0,2},{2,0},{4,6},{6,4},{1,3},{3,1},{5,7},{7,5},{8,10},{10,8},{12,... | collective-permute-start | bytes 786440 | tf_op jit(solution)/shard_map/ppermute | solution.py:42
  11.6 1.0 %copy-start.2 = (s32[2,4]{1,0:T(2,128)S(1)}, s32[2,4]{1,0:T(2,128)}, u32[]{:S(2)}) copy-start(s32[2,4]{1,0:T(2,128)} %param.7) | copy-start | bytes 100
  15.3 9.2 %collective-permute-start.6 = (f32[2,32,128]{2,1,0:T(8,128)S(1)}, f32[2,32,128]{2,1,0:T(8,128)S(1)}, u32[]{:S(2)}, u32[]{:S(2)}) collective-permute-start(f32[2,32,128]{2,1,0:T(8,128)S(1)} %get-tuple-element.31), channel_id=1, source_target_pairs={{0,2},{2,0},{4,6},{6,4},{1,3},{3,1},{5,7},{7,5},{8,10},{10,8},{12,... | collective-permute-start | bytes 98312 | tf_op jit(solution)/shard_map/ppermute | solution.py:42
  17.0 7.6 %collective-permute-start.7 = (f32[2,32,128]{2,1,0:T(8,128)S(1)}, f32[2,32,128]{2,1,0:T(8,128)S(1)}, u32[]{:S(2)}, u32[]{:S(2)}) collective-permute-start(f32[2,32,128]{2,1,0:T(8,128)S(1)} %get-tuple-element.30), channel_id=1, source_target_pairs={{0,4},{2,6},{4,0},{6,2},{1,5},{3,7},{5,1},{7,3},{8,12},{10,14},{12... | collective-permute-start | bytes 98312 | tf_op jit(solution)/shard_map/ppermute | solution.py:42
  18.2 6.3 %collective-permute-start.8 = (f32[2,32,128]{2,1,0:T(8,128)S(1)}, f32[2,32,128]{2,1,0:T(8,128)S(1)}, u32[]{:S(2)}, u32[]{:S(2)}) collective-permute-start(f32[2,32,128]{2,1,0:T(8,128)S(1)} %get-tuple-element.29), channel_id=1, source_target_pairs={{0,6},{2,4},{4,2},{6,0},{1,7},{3,5},{5,3},{7,1},{8,14},{10,12},{12... | collective-permute-start | bytes 98312 | tf_op jit(solution)/shard_map/ppermute | solution.py:42
  19.8 12.9 %collective-permute-start.2 = (f32[2,256,128]{2,1,0:T(8,128)S(1)}, f32[2,256,128]{2,1,0:T(8,128)S(1)}, u32[]{:S(2)}, u32[]{:S(2)}) collective-permute-start(f32[2,256,128]{2,1,0:T(8,128)S(1)} %collective-permute-done.1.refs_2_), channel_id=1, source_target_pairs={{0,2},{2,0},{4,6},{6,4},{1,3},{3,1},{5,7},{7,5},{8,10},{10,8},{12,... | collective-permute-start | bytes 786440 | tf_op jit(solution)/shard_map/ppermute | solution.py:42
  24.6 5.3 %collective-permute-start.10 = (f32[4,2,32,128]{3,2,1,0:T(8,128)S(1)}, f32[4,2,32,128]{3,2,1,0:T(8,128)S(1)}, u32[]{:S(2)}, u32[]{:S(2)}) collective-permute-start(f32[4,2,32,128]{3,2,1,0:T(8,128)S(1)} %pad_maximum_fusion.2.refs_4_), channel_id=1, source_target_pairs={{0,16},{8,24},{16,0},{24,8},{1,17},{9,25},{17,1},{25,9},{2,18},{10... | collective-permute-start | bytes 393224 | tf_op jit(solution)/shard_map/ppermute | solution.py:42
  26.2 5.9 %collective-permute-start.11 = (f32[4,2,32,128]{3,2,1,0:T(8,128)S(1)}, f32[4,2,32,128]{3,2,1,0:T(8,128)S(1)}, u32[]{:S(2)}, u32[]{:S(2)}) collective-permute-start(f32[4,2,32,128]{3,2,1,0:T(8,128)S(1)} %pad_maximum_fusion.2.refs_4_), channel_id=1, source_target_pairs={{0,24},{8,16},{16,8},{24,0},{1,25},{9,17},{17,9},{25,1},{2,26},{10... | collective-permute-start | bytes 393224 | tf_op jit(solution)/shard_map/ppermute | solution.py:42
  27.7 5.0 %collective-permute-start.9 = (f32[4,2,32,128]{3,2,1,0:T(8,128)S(1)}, f32[4,2,32,128]{3,2,1,0:T(8,128)S(1)}, u32[]{:S(2)}, u32[]{:S(2)}) collective-permute-start(f32[4,2,32,128]{3,2,1,0:T(8,128)S(1)} %pad_maximum_fusion.2.refs_4_), channel_id=1, source_target_pairs={{0,8},{8,0},{16,24},{24,16},{1,9},{9,1},{17,25},{25,17},{2,10},{10... | collective-permute-start | bytes 393224 | tf_op jit(solution)/shard_map/ppermute | solution.py:42
  34.3 1.8 %collective-permute-start.12 = (f32[2,384,128]{2,1,0:T(8,128)S(1)}, f32[2,384,128]{2,1,0:T(8,128)S(1)}, u32[]{:S(2)}, u32[]{:S(2)}) collective-permute-start(f32[2,384,128]{2,1,0:T(8,128)S(1)} %shard_map.59), channel_id=1, source_target_pairs={{0,1},{1,0},{2,3},{3,2},{4,5},{5,4},{6,7},{7,6},{8,9},{9,8},{10,11... | collective-permute-start | bytes 1179656 | tf_op jit(solution)/shard_map/ppermute | solution.py:42
  36.3 5.9 %collective-permute-start.13 = (f32[72,128]{1,0:T(8,128)S(1)}, f32[72,128]{1,0:T(8,128)S(1)}, u32[]{:S(2)}, u32[]{:S(2)}) collective-permute-start(f32[72,128]{1,0:T(8,128)S(1)} %get-tuple-element.34), channel_id=1, source_target_pairs={{0,6},{2,4},{4,2},{6,0},{1,7},{3,5},{5,3},{7,1},{8,14},{10,12},{12... | collective-permute-start | bytes 110600 | tf_op jit(solution)/shard_map/ppermute | solution.py:42
  40.1 4.9 %collective-permute-start.14 = (f32[72,128]{1,0:T(8,128)S(1)}, f32[72,128]{1,0:T(8,128)S(1)}, u32[]{:S(2)}, u32[]{:S(2)}) collective-permute-start(f32[72,128]{1,0:T(8,128)S(1)} %get-tuple-element.33), channel_id=1, source_target_pairs={{0,4},{2,6},{4,0},{6,2},{1,5},{3,7},{5,1},{7,3},{8,12},{10,14},{12... | collective-permute-start | bytes 110600 | tf_op jit(solution)/shard_map/ppermute | solution.py:42
  40.1 4.9 %collective-permute-start.15 = (f32[72,128]{1,0:T(8,128)S(1)}, f32[72,128]{1,0:T(8,128)S(1)}, u32[]{:S(2)}, u32[]{:S(2)}) collective-permute-start(f32[72,128]{1,0:T(8,128)S(1)} %get-tuple-element.32), channel_id=1, source_target_pairs={{0,2},{2,0},{4,6},{6,4},{1,3},{3,1},{5,7},{7,5},{8,10},{10,8},{12,... | collective-permute-start | bytes 110600 | tf_op jit(solution)/shard_map/ppermute | solution.py:42
  45.1 4.6 %collective-permute-start.16 = (f32[2,512]{1,0:T(2,128)S(1)}, f32[2,512]{1,0:T(2,128)S(1)}, u32[]{:S(2)}, u32[]{:S(2)}) collective-permute-start(f32[2,512]{1,0:T(2,128)S(1)} %pad_maximum_fusion.7), channel_id=1, source_target_pairs={{0,24},{8,16},{16,8},{24,0},{1,25},{9,17},{17,9},{25,1},{2,26},{10... | collective-permute-start | bytes 12296 | tf_op jit(solution)/shard_map/ppermute | solution.py:42
  47.5 3.6 %collective-permute-start.17 = (f32[2,512]{1,0:T(2,128)S(1)}, f32[2,512]{1,0:T(2,128)S(1)}, u32[]{:S(2)}, u32[]{:S(2)}) collective-permute-start(f32[2,512]{1,0:T(2,128)S(1)} %pad_maximum_fusion.7), channel_id=1, source_target_pairs={{0,16},{8,24},{16,0},{24,8},{1,17},{9,25},{17,1},{25,9},{2,18},{10... | collective-permute-start | bytes 12296 | tf_op jit(solution)/shard_map/ppermute | solution.py:42
  48.1 3.6 %collective-permute-start.18 = (f32[2,512]{1,0:T(2,128)S(1)}, f32[2,512]{1,0:T(2,128)S(1)}, u32[]{:S(2)}, u32[]{:S(2)}) collective-permute-start(f32[2,512]{1,0:T(2,128)S(1)} %pad_maximum_fusion.7), channel_id=1, source_target_pairs={{0,8},{8,0},{16,24},{24,16},{1,9},{9,1},{17,25},{25,17},{2,10},{10... | collective-permute-start | bytes 12296 | tf_op jit(solution)/shard_map/ppermute | solution.py:42

commit v22 on v19

--- a/solution.py
+++ b/solution.py
@@ -25,7 +25,7 @@
         wide = jnp.concatenate([piece_ref[s] for piece_ref in far], axis=1)
         tall = spread[s].reshape(deep * chunk, spread.shape[3])
         out_ref[s, :height] = jnp.dot(
-            wide, tall, precision=lax.Precision.HIGHEST, preferred_element_type=jnp.float32
+            wide, tall, precision=lax.Precision.HIGH, preferred_element_type=jnp.float32
         )
         for t in range(tiles):
             own = spread[s, place[groups * deep + rows + t]]
@@ -36,7 +36,7 @@
     rows, cols = mesh.shape["row"], mesh.shape["col"]
     cores, deep = 2, cols // 2
     fine = Mesh(mesh.devices.reshape(rows, deep, cores), ("row", "z", "core"))
-    highest = lax.Precision.HIGHEST
+    high = lax.Precision.HIGH
 
     def shifted(array, axis, size, shift):
         return lax.ppermute(array, axis, [(i, (i + shift) % size) for i in range(size)])
@@ -69,7 +69,7 @@
         far = {d: shifted(ancestor, "z", deep, d) for d in early[:1]}
 
         mine = lax.dynamic_slice_in_dim(panel, row * depth, depth, axis=2)
-        partial = jnp.einsum("srw,swv->srv", mine, factor_inv, precision=highest)
+        partial = jnp.einsum("srw,swv->srv", mine, factor_inv, precision=high)
         partial, held_back = lax.optimization_barrier((partial, ancestor))
         far |= {d: shifted(held_back, "z", deep, d) for d in early[1:]}
 

time: 50.4 us -> 49.8 us (0.988)
  no operation moved by 1% of the time
where the time goes in v22:
time: 49.8 us; the launch traced here: 49.6 us
  starting transfers between devices  28.7 us (58%)
  waiting for transfers between devices  14.4 us (29%)
  other arithmetic  2.83 us (6%)
  matrix products  1.42 us (3%)
  Pallas kernels  1.16 us (2%)
  between operations  0.85 us (2%)
    ppermute x15, starting transfers between devices, traded(): return lax.ppermute(array, axis, [(i, i ^ other) for i in range(size)])  19.6 us
    ppermute x15, waiting for transfers between devices, traded(): return lax.ppermute(array, axis, [(i, i ^ other) for i in range(size)])  12.8 us
    ppermute x4, starting transfers between devices, shifted(): lax.ppermute(array, axis, [(i, (i + shift) % size) for i in range(size)])  9.15 us
    ppermute x4, waiting for transfers between devices, shifted(): lax.ppermute(array, axis, [(i, (i + shift) % size) for i in range(size)])  1.59 us
    dot_general x1, matrix products, per_device(): partial = jnp.einsum('srw,swv->srv', mine, factor_inv, precision=high)  1.42 us
    pallas_call x1, Pallas kernels, per_device(): pl.pallas_call(functools.partial(multiply_tiles, deep, rows), out_shape=j...  1.16 us
  transfers between devices with their start and end apart: 19, of which 12 were waited for; matrix products, arithmetic and copies ran while one was open for 7% of the time, Pallas kernels for 0%

profile of v22, /device:TPU:0, one launch (start us, length us, event | category | flops | bytes accessed | tf_op | source)
XLA Modules:
  0.0 49.6 jit_solution(7624951114353801573)
XLA Ops:
  0.6 0.0 copy-start
  0.6 3.1 %collective-permute-start = (f32[2,256,128]{2,1,0:T(8,128)}, f32[2,256,128]{2,1,0:T(8,128)S(1)}, u32[]{:S(2)}, u32[]{:S(2)}) collective-permute-start(f32[2,256,128]{2,1,0:T(8,128)} %refs_0_.1), channel_id=1, source_target_pairs={{0,2},{2,4},{4,6},{6,0},{1,3},{3,5},{5,7},{7,1},{8,10},{10,12},{12... | collective-permute-start | bytes 786440 | tf_op jit(solution)/shard_map/ppermute | solution.py:42
  3.7 1.4 %fusion = f32[2,128,512]{2,1,0:T(8,128)S(1)} fusion(f32[2,128,512]{2,1,0:T(8,128)} %param.6, f32[2,128,512]{2,1,0:T(8,128)S(1)} %copy-done, s32[]{:T(128)S(6)} %select_n.153), kind=kOutput, calls=%fused_computation.10 | convolution fusion | flops 100663296 | bytes 1179652 | tf_op jit(solution)/shard_map/srw,swv->srv/dot_general | solution.py:72
  5.2 0.0 copy-start.1
  5.2 1.6 %collective-permute-start.3 = (f32[2,32,512]{2,1,0:T(8,128)S(1)}, f32[2,32,512]{2,1,0:T(8,128)S(1)}, u32[]{:S(2)}, u32[]{:S(2)}) collective-permute-start(f32[2,32,512]{2,1,0:T(8,128)S(1)} %get-tuple-element.20), channel_id=1, source_target_pairs={{0,8},{8,0},{16,24},{24,16},{1,9},{9,1},{17,25},{25,17},{2,10},{10... | collective-permute-start | bytes 393224 | tf_op jit(solution)/shard_map/ppermute | solution.py:45
  6.8 1.5 %collective-permute-start.4 = (f32[2,32,512]{2,1,0:T(8,128)S(1)}, f32[2,32,512]{2,1,0:T(8,128)S(1)}, u32[]{:S(2)}, u32[]{:S(2)}) collective-permute-start(f32[2,32,512]{2,1,0:T(8,128)S(1)} %get-tuple-element.19), channel_id=1, source_target_pairs={{0,16},{8,24},{16,0},{24,8},{1,17},{9,25},{17,1},{25,9},{2,18},{10... | collective-permute-start | bytes 393224 | tf_op jit(solution)/shard_map/ppermute | solution.py:45
  8.3 0.5 collective-permute-start.5
  8.8 3.0 %collective-permute-start.1 = (f32[2,256,128]{2,1,0:T(8,128)S(1)}, f32[2,256,128]{2,1,0:T(8,128)S(1)}, u32[]{:S(2)}, u32[]{:S(2)}) collective-permute-start(f32[2,256,128]{2,1,0:T(8,128)S(1)} %copy-done.1), channel_id=1, source_target_pairs={{0,6},{2,0},{4,2},{6,4},{1,7},{3,1},{5,3},{7,5},{8,14},{10,8},{12,... | collective-permute-start | bytes 786440 | tf_op jit(solution)/shard_map/ppermute | solution.py:42
  11.8 0.9 %multiply_reduce_fusion.1 = f32[2,128]{1,0:T(2,128)S(1)} fusion(f32[2,128,512]{2,1,0:T(8,128)} %param.6, s32[]{:T(128)S(6)} %select_n.158), kind=kLoop, calls=%fused_computation.9 | loop fusion | flops 65280 | bytes 132100 | tf_op jit(solution)/shard_map/reduce_sum | solution.py:80
  12.8 0.1 select_reduce_fusion
  12.8 0.0 collective-permute-done.3
  12.8 1.7 %collective-permute-done.4 = f32[2,32,512]{2,1,0:T(8,128)S(1)} collective-permute-done((f32[2,32,512]{2,1,0:T(8,128)S(1)}, f32[2,32,512]{2,1,0:T(8,128)S(1)}, u32[]{:S(2)}, u32[]{:S(2)}) %collective-permute-start.4) | collective-permute-done | bytes 131104 | tf_op jit(solution)/shard_map/ppermute | solution.py:45
  14.6 0.0 collective-permute-done.5
  14.6 1.6 %collective-permute-start.6 = (f32[2,32,128]{2,1,0:T(8,128)S(1)}, f32[2,32,128]{2,1,0:T(8,128)S(1)}, u32[]{:S(2)}, u32[]{:S(2)}) collective-permute-start(f32[2,32,128]{2,1,0:T(8,128)S(1)} %get-tuple-element.31), channel_id=1, source_target_pairs={{0,2},{2,0},{4,6},{6,4},{1,3},{3,1},{5,7},{7,5},{8,10},{10,8},{12,... | collective-permute-start | bytes 98312 | tf_op jit(solution)/shard_map/ppermute | solution.py:45
  16.3 2.0 %collective-permute-start.7 = (f32[2,32,128]{2,1,0:T(8,128)S(1)}, f32[2,32,128]{2,1,0:T(8,128)S(1)}, u32[]{:S(2)}, u32[]{:S(2)}) collective-permute-start(f32[2,32,128]{2,1,0:T(8,128)S(1)} %get-tuple-element.30), channel_id=1, source_target_pairs={{0,4},{2,6},{4,0},{6,2},{1,5},{3,7},{5,1},{7,3},{8,12},{10,14},{12... | collective-permute-start | bytes 98312 | tf_op jit(solution)/shard_map/ppermute | solution.py:45
  18.3 0.8 %collective-permute-start.8 = (f32[2,32,128]{2,1,0:T(8,128)S(1)}, f32[2,32,128]{2,1,0:T(8,128)S(1)}, u32[]{:S(2)}, u32[]{:S(2)}) collective-permute-start(f32[2,32,128]{2,1,0:T(8,128)S(1)} %get-tuple-element.29), channel_id=1, source_target_pairs={{0,6},{2,4},{4,2},{6,0},{1,7},{3,5},{5,3},{7,1},{8,14},{10,12},{12... | collective-permute-start | bytes 98312 | tf_op jit(solution)/shard_map/ppermute | solution.py:45
  19.1 3.0 %collective-permute-start.2 = (f32[2,256,128]{2,1,0:T(8,128)S(1)}, f32[2,256,128]{2,1,0:T(8,128)S(1)}, u32[]{:S(2)}, u32[]{:S(2)}) collective-permute-start(f32[2,256,128]{2,1,0:T(8,128)S(1)} %collective-permute-done.1.refs_3_), channel_id=1, source_target_pairs={{0,6},{2,0},{4,2},{6,4},{1,7},{3,1},{5,3},{7,5},{8,14},{10,8},{12,... | collective-permute-start | bytes 786440 | tf_op jit(solution)/shard_map/ppermute | solution.py:42
  22.1 0.1 collective-permute-done.7
  22.2 2.2 %collective-permute-done.8 = f32[2,32,128]{2,1,0:T(8,128)S(1)} collective-permute-done((f32[2,32,128]{2,1,0:T(8,128)S(1)}, f32[2,32,128]{2,1,0:T(8,128)S(1)}, u32[]{:S(2)}, u32[]{:S(2)}) %collective-permute-start.8) | collective-permute-done | bytes 32800 | tf_op jit(solution)/shard_map/ppermute | solution.py:45
  24.4 1.3 %collective-permute-start.10 = (f32[4,2,32,128]{3,2,1,0:T(8,128)S(1)}, f32[4,2,32,128]{3,2,1,0:T(8,128)S(1)}, u32[]{:S(2)}, u32[]{:S(2)}) collective-permute-start(f32[4,2,32,128]{3,2,1,0:T(8,128)S(1)} %pad_maximum_fusion.2.refs_4_), channel_id=1, source_target_pairs={{0,16},{8,24},{16,0},{24,8},{1,17},{9,25},{17,1},{25,9},{2,18},{10... | collective-permute-start | bytes 393224 | tf_op jit(solution)/shard_map/ppermute | solution.py:45
  25.7 1.5 %collective-permute-start.11 = (f32[4,2,32,128]{3,2,1,0:T(8,128)S(1)}, f32[4,2,32,128]{3,2,1,0:T(8,128)S(1)}, u32[]{:S(2)}, u32[]{:S(2)}) collective-permute-start(f32[4,2,32,128]{3,2,1,0:T(8,128)S(1)} %pad_maximum_fusion.2.refs_4_), channel_id=1, source_target_pairs={{0,24},{8,16},{16,8},{24,0},{1,25},{9,17},{17,9},{25,1},{2,26},{10... | collective-permute-start | bytes 393224 | tf_op jit(solution)/shard_map/ppermute | solution.py:45
  27.2 0.8 %collective-permute-start.9 = (f32[4,2,32,128]{3,2,1,0:T(8,128)S(1)}, f32[4,2,32,128]{3,2,1,0:T(8,128)S(1)}, u32[]{:S(2)}, u32[]{:S(2)}) collective-permute-start(f32[4,2,32,128]{3,2,1,0:T(8,128)S(1)} %pad_maximum_fusion.2.refs_4_), channel_id=1, source_target_pairs={{0,8},{8,0},{16,24},{24,16},{1,9},{9,1},{17,25},{25,17},{2,10},{10... | collective-permute-start | bytes 393224 | tf_op jit(solution)/shard_map/ppermute | solution.py:45
  28.0 0.1 xor.48
  28.1 0.1 pad_add_fusion.place
  28.1 1.3 %collective-permute-done.10.refs_6_ = f32[4,2,32,128]{3,2,1,0:T(8,128)S(1)} collective-permute-done((f32[4,2,32,128]{3,2,1,0:T(8,128)S(1)}, f32[4,2,32,128]{3,2,1,0:T(8,128)S(1)}, u32[]{:S(2)}, u32[]{:S(2)}) %collective-permute-start.10) | collective-permute-done | bytes 131104 | tf_op jit(solution)/shard_map/ppermute | solution.py:45
  29.5 2.1 %collective-permute-done.11.refs_7_ = f32[4,2,32,128]{3,2,1,0:T(8,128)S(1)} collective-permute-done((f32[4,2,32,128]{3,2,1,0:T(8,128)S(1)}, f32[4,2,32,128]{3,2,1,0:T(8,128)S(1)}, u32[]{:S(2)}, u32[]{:S(2)}) %collective-permute-start.11) | collective-permute-done | bytes 131104 | tf_op jit(solution)/shard_map/ppermute | solution.py:45
  31.6 0.7 %collective-permute-done.9.refs_5_ = f32[4,2,32,128]{3,2,1,0:T(8,128)S(1)} collective-permute-done((f32[4,2,32,128]{3,2,1,0:T(8,128)S(1)}, f32[4,2,32,128]{3,2,1,0:T(8,128)S(1)}, u32[]{:S(2)}, u32[]{:S(2)}) %collective-permute-start.9) | collective-permute-done | bytes 131104 | tf_op jit(solution)/shard_map/ppermute | solution.py:45
  32.3 1.2 %shard_map.59 = f32[2,384,128]{2,1,0:T(8,128)S(1)} custom-call(s32[13]{0:T(128)S(1)} %pad_add_fusion.place, f32[2,256,128]{2,1,0:T(8,128)S(1)} %copy-done.1, f32[2,256,128]{2,1,0:T(8,128)S(1)} %collective-permute-done.refs_1_, f32[2,256,128]{2,1,0:T(8,128)S(1)} %collective-permute-done.2.refs_2_, f32[2,256,128]{2,1,0:T(8,128)S(1)} %collective-permute-done.1.refs_3_, ...), custom_call_target="tpu_custom_call" | custom-call | tf_op jit(solution)/shard_map/pallas_call | solution.py:106
  33.5 0.1 collective-permute-start.12
  33.6 0.1 pad.15.clone
  33.7 1.6 %collective-permute-done.12 = f32[2,384,128]{2,1,0:T(8,128)S(1)} collective-permute-done((f32[2,384,128]{2,1,0:T(8,128)S(1)}, f32[2,384,128]{2,1,0:T(8,128)S(1)}, u32[]{:S(2)}, u32[]{:S(2)}) %collective-permute-start.12) | collective-permute-done | bytes 393248 | tf_op jit(solution)/shard_map/ppermute | solution.py:42
  35.4 0.1 multiply_reduce_fusion
  35.5 0.1 fusion.4
  35.6 0.9 %collective-permute-start.13 = (f32[72,128]{1,0:T(8,128)S(1)}, f32[72,128]{1,0:T(8,128)S(1)}, u32[]{:S(2)}, u32[]{:S(2)}) collective-permute-start(f32[72,128]{1,0:T(8,128)S(1)} %get-tuple-element.34), channel_id=1, source_target_pairs={{0,6},{2,4},{4,2},{6,0},{1,7},{3,5},{5,3},{7,1},{8,14},{10,12},{12... | collective-permute-start | bytes 110600 | tf_op jit(solution)/shard_map/ppermute | solution.py:45
  36.4 1.7 %collective-permute-start.14 = (f32[72,128]{1,0:T(8,128)S(1)}, f32[72,128]{1,0:T(8,128)S(1)}, u32[]{:S(2)}, u32[]{:S(2)}) collective-permute-start(f32[72,128]{1,0:T(8,128)S(1)} %get-tuple-element.33), channel_id=1, source_target_pairs={{0,4},{2,6},{4,0},{6,2},{1,5},{3,7},{5,1},{7,3},{8,12},{10,14},{12... | collective-permute-start | bytes 110600 | tf_op jit(solution)/shard_map/ppermute | solution.py:45
  38.2 1.9 %collective-permute-start.15 = (f32[72,128]{1,0:T(8,128)S(1)}, f32[72,128]{1,0:T(8,128)S(1)}, u32[]{:S(2)}, u32[]{:S(2)}) collective-permute-start(f32[72,128]{1,0:T(8,128)S(1)} %get-tuple-element.32), channel_id=1, source_target_pairs={{0,2},{2,0},{4,6},{6,4},{1,3},{3,1},{5,7},{7,5},{8,10},{10,8},{12,... | collective-permute-start | bytes 110600 | tf_op jit(solution)/shard_map/ppermute | solution.py:45
  40.0 1.4 %collective-permute-done.13 = f32[72,128]{1,0:T(8,128)S(1)} collective-permute-done((f32[72,128]{1,0:T(8,128)S(1)}, f32[72,128]{1,0:T(8,128)S(1)}, u32[]{:S(2)}, u32[]{:S(2)}) %collective-permute-start.13) | collective-permute-done | bytes 36896 | tf_op jit(solution)/shard_map/ppermute | solution.py:45
  41.4 0.7 %collective-permute-done.14 = f32[72,128]{1,0:T(8,128)S(1)} collective-permute-done((f32[72,128]{1,0:T(8,128)S(1)}, f32[72,128]{1,0:T(8,128)S(1)}, u32[]{:S(2)}, u32[]{:S(2)}) %collective-permute-start.14) | collective-permute-done | bytes 36896 | tf_op jit(solution)/shard_map/ppermute | solution.py:45
  42.1 0.3 collective-permute-done.15
  42.4 0.1 select_select_fusion.2
  42.5 0.1 select_select_fusion.3
  42.6 1.0 %collective-permute-start.16 = (f32[2,512]{1,0:T(2,128)S(1)}, f32[2,512]{1,0:T(2,128)S(1)}, u32[]{:S(2)}, u32[]{:S(2)}) collective-permute-start(f32[2,512]{1,0:T(2,128)S(1)} %pad_maximum_fusion.7), channel_id=1, source_target_pairs={{0,8},{8,0},{16,24},{24,16},{1,9},{9,1},{17,25},{25,17},{2,10},{10... | collective-permute-start | bytes 12296 | tf_op jit(solution)/shard_map/ppermute | solution.py:45
  43.6 0.9 %collective-permute-start.17 = (f32[2,512]{1,0:T(2,128)S(1)}, f32[2,512]{1,0:T(2,128)S(1)}, u32[]{:S(2)}, u32[]{:S(2)}) collective-permute-start(f32[2,512]{1,0:T(2,128)S(1)} %pad_maximum_fusion.7), channel_id=1, source_target_pairs={{0,16},{8,24},{16,0},{24,8},{1,17},{9,25},{17,1},{25,9},{2,18},{10... | collective-permute-start | bytes 12296 | tf_op jit(solution)/shard_map/ppermute | solution.py:45
  44.5 1.6 %collective-permute-start.18 = (f32[2,512]{1,0:T(2,128)S(1)}, f32[2,512]{1,0:T(2,128)S(1)}, u32[]{:S(2)}, u32[]{:S(2)}) collective-permute-start(f32[2,512]{1,0:T(2,128)S(1)} %pad_maximum_fusion.7), channel_id=1, source_target_pairs={{0,24},{8,16},{16,8},{24,0},{1,25},{9,17},{17,9},{25,1},{2,26},{10... | collective-permute-start | bytes 12296 | tf_op jit(solution)/shard_map/ppermute | solution.py:45
  46.1 0.7 %slice_negate_fusion = f32[64,512]{1,0:T(8,128)} fusion(f32[72,512]{1,0:T(8,128)S(1)} %pad_maximum_fusion.1), kind=kLoop, calls=%fused_computation.4 | loop fusion | flops 32768 | bytes 262144 | tf_op jit(solution)/shard_map/neg | solution.py:133
  46.8 0.4 collective-permute-done.17
  47.2 1.8 %collective-permute-done.18 = f32[2,512]{1,0:T(2,128)S(1)} collective-permute-done((f32[2,512]{1,0:T(2,128)S(1)}, f32[2,512]{1,0:T(2,128)S(1)}, u32[]{:S(2)}, u32[]{:S(2)}) %collective-permute-start.18) | collective-permute-done | bytes 4128 | tf_op jit(solution)/shard_map/ppermute | solution.py:45
  49.0 0.6 %add_add_fusion.1 = f32[2,512]{1,0:T(2,128)} fusion(f32[2,512]{1,0:T(2,128)S(1)} %collective-permute-done.18, f32[2,512]{1,0:T(2,128)S(1)} %collective-permute-done.17, f32[2,512]{1,0:T(2,128)S(1)} %pad_maximum_fusion.7, f32[2,512]{1,0:T(2,128)S(1)} %collective-permute-done.16), kind=kLoop, calls=%fused_computation.26 | loop fusion | flops 3072 | bytes 20480 | tf_op jit(solution)/shard_map/add | solution.py:137
  (24 shorter events, 0.3 us)
Async XLA Ops:
  0.6 3.1 %copy-start = (f32[2,128,512]{2,1,0:T(8,128)S(1)}, f32[2,128,512]{2,1,0:T(8,128)}, u32[]{:S(2)}) copy-start(f32[2,128,512]{2,1,0:T(8,128)} %param.5) | copy-start | bytes 1572868
  0.6 27.5 %collective-permute-start = (f32[2,256,128]{2,1,0:T(8,128)}, f32[2,256,128]{2,1,0:T(8,128)S(1)}, u32[]{:S(2)}, u32[]{:S(2)}) collective-permute-start(f32[2,256,128]{2,1,0:T(8,128)} %refs_0_.1), channel_id=1, source_target_pairs={{0,2},{2,4},{4,6},{6,0},{1,3},{3,5},{5,7},{7,1},{8,10},{10,12},{12... | collective-permute-start | bytes 786440 | tf_op jit(solution)/shard_map/ppermute | solution.py:42
  5.2 3.6 %copy-start.1 = (f32[2,256,128]{2,1,0:T(8,128)S(1)}, f32[2,256,128]{2,1,0:T(8,128)}, u32[]{:S(2)}) copy-start(f32[2,256,128]{2,1,0:T(8,128)} %refs_0_.1) | copy-start | bytes 786436
  5.2 7.6 %collective-permute-start.3 = (f32[2,32,512]{2,1,0:T(8,128)S(1)}, f32[2,32,512]{2,1,0:T(8,128)S(1)}, u32[]{:S(2)}, u32[]{:S(2)}) collective-permute-start(f32[2,32,512]{2,1,0:T(8,128)S(1)} %get-tuple-element.20), channel_id=1, source_target_pairs={{0,8},{8,0},{16,24},{24,16},{1,9},{9,1},{17,25},{25,17},{2,10},{10... | collective-permute-start | bytes 393224 | tf_op jit(solution)/shard_map/ppermute | solution.py:45
  6.8 7.8 %collective-permute-start.4 = (f32[2,32,512]{2,1,0:T(8,128)S(1)}, f32[2,32,512]{2,1,0:T(8,128)S(1)}, u32[]{:S(2)}, u32[]{:S(2)}) collective-permute-start(f32[2,32,512]{2,1,0:T(8,128)S(1)} %get-tuple-element.19), channel_id=1, source_target_pairs={{0,16},{8,24},{16,0},{24,8},{1,17},{9,25},{17,1},{25,9},{2,18},{10... | collective-permute-start | bytes 393224 | tf_op jit(solution)/shard_map/ppermute | solution.py:45
  8.3 6.3 %collective-permute-start.5 = (f32[2,32,512]{2,1,0:T(8,128)S(1)}, f32[2,32,512]{2,1,0:T(8,128)S(1)}, u32[]{:S(2)}, u32[]{:S(2)}) collective-permute-start(f32[2,32,512]{2,1,0:T(8,128)S(1)} %get-tuple-element.18), channel_id=1, source_target_pairs={{0,24},{8,16},{16,8},{24,0},{1,25},{9,17},{17,9},{25,1},{2,26},{10... | collective-permute-start | bytes 393224 | tf_op jit(solution)/shard_map/ppermute | solution.py:45
  8.8 10.3 %collective-permute-start.1 = (f32[2,256,128]{2,1,0:T(8,128)S(1)}, f32[2,256,128]{2,1,0:T(8,128)S(1)}, u32[]{:S(2)}, u32[]{:S(2)}) collective-permute-start(f32[2,256,128]{2,1,0:T(8,128)S(1)} %copy-done.1), channel_id=1, source_target_pairs={{0,6},{2,0},{4,2},{6,4},{1,7},{3,1},{5,3},{7,5},{8,14},{10,8},{12,... | collective-permute-start | bytes 786440 | tf_op jit(solution)/shard_map/ppermute | solution.py:42
  11.8 1.0 %copy-start.2 = (s32[2,4]{1,0:T(2,128)S(1)}, s32[2,4]{1,0:T(2,128)}, u32[]{:S(2)}) copy-start(s32[2,4]{1,0:T(2,128)} %param.7) | copy-start | bytes 100
  14.6 7.5 %collective-permute-start.6 = (f32[2,32,128]{2,1,0:T(8,128)S(1)}, f32[2,32,128]{2,1,0:T(8,128)S(1)}, u32[]{:S(2)}, u32[]{:S(2)}) collective-permute-start(f32[2,32,128]{2,1,0:T(8,128)S(1)} %get-tuple-element.31), channel_id=1, source_target_pairs={{0,2},{2,0},{4,6},{6,4},{1,3},{3,1},{5,7},{7,5},{8,10},{10,8},{12,... | collective-permute-start | bytes 98312 | tf_op jit(solution)/shard_map/ppermute | solution.py:45
  16.3 5.9 %collective-permute-start.7 = (f32[2,32,128]{2,1,0:T(8,128)S(1)}, f32[2,32,128]{2,1,0:T(8,128)S(1)}, u32[]{:S(2)}, u32[]{:S(2)}) collective-permute-start(f32[2,32,128]{2,1,0:T(8,128)S(1)} %get-tuple-element.30), channel_id=1, source_target_pairs={{0,4},{2,6},{4,0},{6,2},{1,5},{3,7},{5,1},{7,3},{8,12},{10,14},{12... | collective-permute-start | bytes 98312 | tf_op jit(solution)/shard_map/ppermute | solution.py:45
  18.3 6.1 %collective-permute-start.8 = (f32[2,32,128]{2,1,0:T(8,128)S(1)}, f32[2,32,128]{2,1,0:T(8,128)S(1)}, u32[]{:S(2)}, u32[]{:S(2)}) collective-permute-start(f32[2,32,128]{2,1,0:T(8,128)S(1)} %get-tuple-element.29), channel_id=1, source_target_pairs={{0,6},{2,4},{4,2},{6,0},{1,7},{3,5},{5,3},{7,1},{8,14},{10,12},{12... | collective-permute-start | bytes 98312 | tf_op jit(solution)/shard_map/ppermute | solution.py:45
  19.1 13.2 %collective-permute-start.2 = (f32[2,256,128]{2,1,0:T(8,128)S(1)}, f32[2,256,128]{2,1,0:T(8,128)S(1)}, u32[]{:S(2)}, u32[]{:S(2)}) collective-permute-start(f32[2,256,128]{2,1,0:T(8,128)S(1)} %collective-permute-done.1.refs_3_), channel_id=1, source_target_pairs={{0,6},{2,0},{4,2},{6,4},{1,7},{3,1},{5,3},{7,5},{8,14},{10,8},{12,... | collective-permute-start | bytes 786440 | tf_op jit(solution)/shard_map/ppermute | solution.py:42
  24.4 5.0 %collective-permute-start.10 = (f32[4,2,32,128]{3,2,1,0:T(8,128)S(1)}, f32[4,2,32,128]{3,2,1,0:T(8,128)S(1)}, u32[]{:S(2)}, u32[]{:S(2)}) collective-permute-start(f32[4,2,32,128]{3,2,1,0:T(8,128)S(1)} %pad_maximum_fusion.2.refs_4_), channel_id=1, source_target_pairs={{0,16},{8,24},{16,0},{24,8},{1,17},{9,25},{17,1},{25,9},{2,18},{10... | collective-permute-start | bytes 393224 | tf_op jit(solution)/shard_map/ppermute | solution.py:45
  25.7 5.9 %collective-permute-start.11 = (f32[4,2,32,128]{3,2,1,0:T(8,128)S(1)}, f32[4,2,32,128]{3,2,1,0:T(8,128)S(1)}, u32[]{:S(2)}, u32[]{:S(2)}) collective-permute-start(f32[4,2,32,128]{3,2,1,0:T(8,128)S(1)} %pad_maximum_fusion.2.refs_4_), channel_id=1, source_target_pairs={{0,24},{8,16},{16,8},{24,0},{1,25},{9,17},{17,9},{25,1},{2,26},{10... | collective-permute-start | bytes 393224 | tf_op jit(solution)/shard_map/ppermute | solution.py:45
  27.2 5.2 %collective-permute-start.9 = (f32[4,2,32,128]{3,2,1,0:T(8,128)S(1)}, f32[4,2,32,128]{3,2,1,0:T(8,128)S(1)}, u32[]{:S(2)}, u32[]{:S(2)}) collective-permute-start(f32[4,2,32,128]{3,2,1,0:T(8,128)S(1)} %pad_maximum_fusion.2.refs_4_), channel_id=1, source_target_pairs={{0,8},{8,0},{16,24},{24,16},{1,9},{9,1},{17,25},{25,17},{2,10},{10... | collective-permute-start | bytes 393224 | tf_op jit(solution)/shard_map/ppermute | solution.py:45
  33.5 1.8 %collective-permute-start.12 = (f32[2,384,128]{2,1,0:T(8,128)S(1)}, f32[2,384,128]{2,1,0:T(8,128)S(1)}, u32[]{:S(2)}, u32[]{:S(2)}) collective-permute-start(f32[2,384,128]{2,1,0:T(8,128)S(1)} %shard_map.59), channel_id=1, source_target_pairs={{0,1},{1,0},{2,3},{3,2},{4,5},{5,4},{6,7},{7,6},{8,9},{9,8},{10,11... | collective-permute-start | bytes 1179656 | tf_op jit(solution)/shard_map/ppermute | solution.py:42
  35.6 5.9 %collective-permute-start.13 = (f32[72,128]{1,0:T(8,128)S(1)}, f32[72,128]{1,0:T(8,128)S(1)}, u32[]{:S(2)}, u32[]{:S(2)}) collective-permute-start(f32[72,128]{1,0:T(8,128)S(1)} %get-tuple-element.34), channel_id=1, source_target_pairs={{0,6},{2,4},{4,2},{6,0},{1,7},{3,5},{5,3},{7,1},{8,14},{10,12},{12... | collective-permute-start | bytes 110600 | tf_op jit(solution)/shard_map/ppermute | solution.py:45
  36.4 5.7 %collective-permute-start.14 = (f32[72,128]{1,0:T(8,128)S(1)}, f32[72,128]{1,0:T(8,128)S(1)}, u32[]{:S(2)}, u32[]{:S(2)}) collective-permute-start(f32[72,128]{1,0:T(8,128)S(1)} %get-tuple-element.33), channel_id=1, source_target_pairs={{0,4},{2,6},{4,0},{6,2},{1,5},{3,7},{5,1},{7,3},{8,12},{10,14},{12... | collective-permute-start | bytes 110600 | tf_op jit(solution)/shard_map/ppermute | solution.py:45
  38.2 4.2 %collective-permute-start.15 = (f32[72,128]{1,0:T(8,128)S(1)}, f32[72,128]{1,0:T(8,128)S(1)}, u32[]{:S(2)}, u32[]{:S(2)}) collective-permute-start(f32[72,128]{1,0:T(8,128)S(1)} %get-tuple-element.32), channel_id=1, source_target_pairs={{0,2},{2,0},{4,6},{6,4},{1,3},{3,1},{5,7},{7,5},{8,10},{10,8},{12,... | collective-permute-start | bytes 110600 | tf_op jit(solution)/shard_map/ppermute | solution.py:45
  42.6 4.2 %collective-permute-start.16 = (f32[2,512]{1,0:T(2,128)S(1)}, f32[2,512]{1,0:T(2,128)S(1)}, u32[]{:S(2)}, u32[]{:S(2)}) collective-permute-start(f32[2,512]{1,0:T(2,128)S(1)} %pad_maximum_fusion.7), channel_id=1, source_target_pairs={{0,8},{8,0},{16,24},{24,16},{1,9},{9,1},{17,25},{25,17},{2,10},{10... | collective-permute-start | bytes 12296 | tf_op jit(solution)/shard_map/ppermute | solution.py:45
  43.6 3.6 %collective-permute-start.17 = (f32[2,512]{1,0:T(2,128)S(1)}, f32[2,512]{1,0:T(2,128)S(1)}, u32[]{:S(2)}, u32[]{:S(2)}) collective-permute-start(f32[2,512]{1,0:T(2,128)S(1)} %pad_maximum_fusion.7), channel_id=1, source_target_pairs={{0,16},{8,24},{16,0},{24,8},{1,17},{9,25},{17,1},{25,9},{2,18},{10... | collective-permute-start | bytes 12296 | tf_op jit(solution)/shard_map/ppermute | solution.py:45
  44.5 4.5 %collective-permute-start.18 = (f32[2,512]{1,0:T(2,128)S(1)}, f32[2,512]{1,0:T(2,128)S(1)}, u32[]{:S(2)}, u32[]{:S(2)}) collective-permute-start(f32[2,512]{1,0:T(2,128)S(1)} %pad_maximum_fusion.7), channel_id=1, source_target_pairs={{0,24},{8,16},{16,8},{24,0},{1,25},{9,17},{17,9},{25,1},{2,26},{10... | collective-permute-start | bytes 12296 | tf_op jit(solution)/shard_map/ppermute | solution.py:45

commit v23 on v19

--- a/solution.py
+++ b/solution.py
@@ -88,8 +88,8 @@
         for d in range(1, deep):
             slots.append(traded(columns_of(scaled, z ^ d), "z", deep, d))
         if deep > 1:
-            for d in reversed(late):
-                far[d] = shifted(far[d + 1], "z", deep, deep - 1)
+            for d in late:
+                far[d] = shifted(far[d - 1], "z", deep, 1)
         slots = gathered(jnp.stack(slots), "row", rows)
 
         count = jnp.arange(deep, dtype=jnp.int32)

time: 50.4 us -> 53.4 us (1.060)
  waiting for transfers between devices: 14.4 us -> 19.6 us
  starting transfers between devices: 28.7 us -> 26.4 us
    ppermute x15, waiting for transfers between devices: 12.8 us -> 18 us  [traded(): return lax.ppermute(array, axis, [(i, i ^ other) for i in range(size)])]
    ppermute x4, starting transfers between devices: 9.15 us -> 6.83 us  [shifted(): lax.ppermute(array, axis, [(i, (i + shift) % size) for i in range(size)])]
  transfers between devices with their start and end apart: 19 -> 19, of which waited for: 12 -> 9; matrix products, arithmetic and copies ran while one was open for 7% -> 7% of each run, Pallas kernels for 0% -> 0%
where the time goes in v23:
time: 53.4 us; the launch traced here: 53.2 us
  starting transfers between devices  26.4 us (49%)
  waiting for transfers between devices  19.6 us (37%)
  other arithmetic  2.83 us (5%)
  matrix products  1.62 us (3%)
  Pallas kernels  1.61 us (3%)
  between operations  0.86 us (2%)
    ppermute x15, starting transfers between devices, traded(): return lax.ppermute(array, axis, [(i, i ^ other) for i in range(size)])  19.6 us
    ppermute x15, waiting for transfers between devices, traded(): return lax.ppermute(array, axis, [(i, i ^ other) for i in range(size)])  18 us
    ppermute x4, starting transfers between devices, shifted(): lax.ppermute(array, axis, [(i, (i + shift) % size) for i in range(size)])  6.83 us
    dot_general x1, matrix products, per_device(): partial = jnp.einsum('srw,swv->srv', mine, factor_inv, precision=highest)  1.62 us
    pallas_call x1, Pallas kernels, per_device(): pl.pallas_call(functools.partial(multiply_tiles, deep, rows), out_shape=j...  1.61 us
    ppermute x4, waiting for transfers between devices, shifted(): lax.ppermute(array, axis, [(i, (i + shift) % size) for i in range(size)])  1.59 us
  transfers between devices with their start and end apart: 19, of which 9 were waited for; matrix products, arithmetic and copies ran while one was open for 7% of the time, Pallas kernels for 0%

profile of v23, /device:TPU:0, one launch (start us, length us, event | category | flops | bytes accessed | tf_op | source)
XLA Modules:
  0.0 53.2 jit_solution(16195253553467448258)
XLA Ops:
  0.6 0.0 copy-start
  0.6 3.1 %collective-permute-start = (f32[2,256,128]{2,1,0:T(8,128)}, f32[2,256,128]{2,1,0:T(8,128)S(1)}, u32[]{:S(2)}, u32[]{:S(2)}) collective-permute-start(f32[2,256,128]{2,1,0:T(8,128)} %refs_0_.1), channel_id=1, source_target_pairs={{0,2},{2,4},{4,6},{6,0},{1,3},{3,5},{5,7},{7,1},{8,10},{10,12},{12... | collective-permute-start | bytes 786440 | tf_op jit(solution)/shard_map/ppermute | solution.py:42
  3.7 1.6 %fusion = f32[2,128,512]{2,1,0:T(8,128)S(1)} fusion(f32[2,128,512]{2,1,0:T(8,128)} %param.6, f32[2,128,512]{2,1,0:T(8,128)S(1)} %copy-done, s32[]{:T(128)S(6)} %select_n.153), kind=kOutput, calls=%fused_computation.10 | convolution fusion | flops 201326592 | bytes 1179652 | tf_op jit(solution)/shard_map/srw,swv->srv/dot_general | solution.py:72
  5.4 0.0 copy-start.1
  5.4 1.6 %collective-permute-start.3 = (f32[2,32,512]{2,1,0:T(8,128)S(1)}, f32[2,32,512]{2,1,0:T(8,128)S(1)}, u32[]{:S(2)}, u32[]{:S(2)}) collective-permute-start(f32[2,32,512]{2,1,0:T(8,128)S(1)} %get-tuple-element.20), channel_id=1, source_target_pairs={{0,8},{8,0},{16,24},{24,16},{1,9},{9,1},{17,25},{25,17},{2,10},{10... | collective-permute-start | bytes 393224 | tf_op jit(solution)/shard_map/ppermute | solution.py:45
  7.0 1.5 %collective-permute-start.4 = (f32[2,32,512]{2,1,0:T(8,128)S(1)}, f32[2,32,512]{2,1,0:T(8,128)S(1)}, u32[]{:S(2)}, u32[]{:S(2)}) collective-permute-start(f32[2,32,512]{2,1,0:T(8,128)S(1)} %get-tuple-element.19), channel_id=1, source_target_pairs={{0,16},{8,24},{16,0},{24,8},{1,17},{9,25},{17,1},{25,9},{2,18},{10... | collective-permute-start | bytes 393224 | tf_op jit(solution)/shard_map/ppermute | solution.py:45
  8.5 0.5 collective-permute-start.5
  9.0 3.0 %collective-permute-start.2 = (f32[2,256,128]{2,1,0:T(8,128)S(1)}, f32[2,256,128]{2,1,0:T(8,128)S(1)}, u32[]{:S(2)}, u32[]{:S(2)}) collective-permute-start(f32[2,256,128]{2,1,0:T(8,128)S(1)} %copy-done.1), channel_id=1, source_target_pairs={{0,6},{2,0},{4,2},{6,4},{1,7},{3,1},{5,3},{7,5},{8,14},{10,8},{12,... | collective-permute-start | bytes 786440 | tf_op jit(solution)/shard_map/ppermute | solution.py:42
  12.0 0.9 %multiply_reduce_fusion.1 = f32[2,128]{1,0:T(2,128)S(1)} fusion(f32[2,128,512]{2,1,0:T(8,128)} %param.6, s32[]{:T(128)S(6)} %select_n.158), kind=kLoop, calls=%fused_computation.9 | loop fusion | flops 65280 | bytes 132100 | tf_op jit(solution)/shard_map/reduce_sum | solution.py:80
  12.9 0.1 select_reduce_fusion
  13.0 0.0 collective-permute-done.3
  13.0 1.7 %collective-permute-done.4 = f32[2,32,512]{2,1,0:T(8,128)S(1)} collective-permute-done((f32[2,32,512]{2,1,0:T(8,128)S(1)}, f32[2,32,512]{2,1,0:T(8,128)S(1)}, u32[]{:S(2)}, u32[]{:S(2)}) %collective-permute-start.4) | collective-permute-done | bytes 131104 | tf_op jit(solution)/shard_map/ppermute | solution.py:45
  14.8 1.6 %collective-permute-start.6 = (f32[2,32,128]{2,1,0:T(8,128)S(1)}, f32[2,32,128]{2,1,0:T(8,128)S(1)}, u32[]{:S(2)}, u32[]{:S(2)}) collective-permute-start(f32[2,32,128]{2,1,0:T(8,128)S(1)} %get-tuple-element.31), channel_id=1, source_target_pairs={{0,2},{2,0},{4,6},{6,4},{1,3},{3,1},{5,7},{7,5},{8,10},{10,8},{12,... | collective-permute-start | bytes 98312 | tf_op jit(solution)/shard_map/ppermute | solution.py:45
  16.5 2.0 %collective-permute-start.7 = (f32[2,32,128]{2,1,0:T(8,128)S(1)}, f32[2,32,128]{2,1,0:T(8,128)S(1)}, u32[]{:S(2)}, u32[]{:S(2)}) collective-permute-start(f32[2,32,128]{2,1,0:T(8,128)S(1)} %get-tuple-element.30), channel_id=1, source_target_pairs={{0,4},{2,6},{4,0},{6,2},{1,5},{3,7},{5,1},{7,3},{8,12},{10,14},{12... | collective-permute-start | bytes 98312 | tf_op jit(solution)/shard_map/ppermute | solution.py:45
  18.5 0.8 %collective-permute-start.8 = (f32[2,32,128]{2,1,0:T(8,128)S(1)}, f32[2,32,128]{2,1,0:T(8,128)S(1)}, u32[]{:S(2)}, u32[]{:S(2)}) collective-permute-start(f32[2,32,128]{2,1,0:T(8,128)S(1)} %get-tuple-element.29), channel_id=1, source_target_pairs={{0,6},{2,4},{4,2},{6,0},{1,7},{3,5},{5,3},{7,1},{8,14},{10,12},{12... | collective-permute-start | bytes 98312 | tf_op jit(solution)/shard_map/ppermute | solution.py:45
  19.3 0.0 collective-permute-done.refs_1_
  19.3 0.7 %collective-permute-start.1 = (f32[2,256,128]{2,1,0:T(8,128)S(1)}, f32[2,256,128]{2,1,0:T(8,128)S(1)}, u32[]{:S(2)}, u32[]{:S(2)}) collective-permute-start(f32[2,256,128]{2,1,0:T(8,128)S(1)} %collective-permute-done.refs_1_), channel_id=1, source_target_pairs={{0,2},{2,4},{4,6},{6,0},{1,3},{3,5},{5,7},{7,1},{8,10},{10,12},{12... | collective-permute-start | bytes 786440 | tf_op jit(solution)/shard_map/ppermute | solution.py:42
  20.0 0.0 collective-permute-done.6
  20.0 7.9 %collective-permute-done.7 = f32[2,32,128]{2,1,0:T(8,128)S(1)} collective-permute-done((f32[2,32,128]{2,1,0:T(8,128)S(1)}, f32[2,32,128]{2,1,0:T(8,128)S(1)}, u32[]{:S(2)}, u32[]{:S(2)}) %collective-permute-start.7) | collective-permute-done | bytes 32800 | tf_op jit(solution)/shard_map/ppermute | solution.py:45
  27.9 0.1 collective-permute-start.10
  28.0 2.4 %collective-permute-start.11 = (f32[4,2,32,128]{3,2,1,0:T(8,128)S(1)}, f32[4,2,32,128]{3,2,1,0:T(8,128)S(1)}, u32[]{:S(2)}, u32[]{:S(2)}) collective-permute-start(f32[4,2,32,128]{3,2,1,0:T(8,128)S(1)} %pad_maximum_fusion.2.refs_4_), channel_id=1, source_target_pairs={{0,24},{8,16},{16,8},{24,0},{1,25},{9,17},{17,9},{25,1},{2,26},{10... | collective-permute-start | bytes 393224 | tf_op jit(solution)/shard_map/ppermute | solution.py:45
  30.4 1.1 %collective-permute-start.9 = (f32[4,2,32,128]{3,2,1,0:T(8,128)S(1)}, f32[4,2,32,128]{3,2,1,0:T(8,128)S(1)}, u32[]{:S(2)}, u32[]{:S(2)}) collective-permute-start(f32[4,2,32,128]{3,2,1,0:T(8,128)S(1)} %pad_maximum_fusion.2.refs_4_), channel_id=1, source_target_pairs={{0,8},{8,0},{16,24},{24,16},{1,9},{9,1},{17,25},{25,17},{2,10},{10... | collective-permute-start | bytes 393224 | tf_op jit(solution)/shard_map/ppermute | solution.py:45
  31.4 0.1 xor.48
  31.5 0.1 pad_add_fusion.place
  31.6 2.7 %collective-permute-done.10.refs_6_ = f32[4,2,32,128]{3,2,1,0:T(8,128)S(1)} collective-permute-done((f32[4,2,32,128]{3,2,1,0:T(8,128)S(1)}, f32[4,2,32,128]{3,2,1,0:T(8,128)S(1)}, u32[]{:S(2)}, u32[]{:S(2)}) %collective-permute-start.10) | collective-permute-done | bytes 131104 | tf_op jit(solution)/shard_map/ppermute | solution.py:45
  34.3 1.5 %collective-permute-done.9.refs_5_ = f32[4,2,32,128]{3,2,1,0:T(8,128)S(1)} collective-permute-done((f32[4,2,32,128]{3,2,1,0:T(8,128)S(1)}, f32[4,2,32,128]{3,2,1,0:T(8,128)S(1)}, u32[]{:S(2)}, u32[]{:S(2)}) %collective-permute-start.9) | collective-permute-done | bytes 131104 | tf_op jit(solution)/shard_map/ppermute | solution.py:45
  35.8 1.6 %shard_map.59 = f32[2,384,128]{2,1,0:T(8,128)S(1)} custom-call(s32[13]{0:T(128)S(1)} %pad_add_fusion.place, f32[2,256,128]{2,1,0:T(8,128)S(1)} %copy-done.1, f32[2,256,128]{2,1,0:T(8,128)S(1)} %collective-permute-done.refs_1_, f32[2,256,128]{2,1,0:T(8,128)S(1)} %collective-permute-done.1.refs_2_, f32[2,256,128]{2,1,0:T(8,128)S(1)} %collective-permute-done.2.refs_3_, ...), custom_call_target="tpu_custom_call" | custom-call | tf_op jit(solution)/shard_map/pallas_call | solution.py:106
  37.4 0.1 collective-permute-start.12
  37.5 0.1 pad.15.clone
  37.6 1.6 %collective-permute-done.12 = f32[2,384,128]{2,1,0:T(8,128)S(1)} collective-permute-done((f32[2,384,128]{2,1,0:T(8,128)S(1)}, f32[2,384,128]{2,1,0:T(8,128)S(1)}, u32[]{:S(2)}, u32[]{:S(2)}) %collective-permute-start.12) | collective-permute-done | bytes 393248 | tf_op jit(solution)/shard_map/ppermute | solution.py:42
  39.3 0.1 multiply_reduce_fusion
  39.4 0.1 fusion.4
  39.5 0.1 collective-permute-start.13
  39.6 2.4 %collective-permute-start.14 = (f32[72,128]{1,0:T(8,128)S(1)}, f32[72,128]{1,0:T(8,128)S(1)}, u32[]{:S(2)}, u32[]{:S(2)}) collective-permute-start(f32[72,128]{1,0:T(8,128)S(1)} %get-tuple-element.33), channel_id=1, source_target_pairs={{0,4},{2,6},{4,0},{6,2},{1,5},{3,7},{5,1},{7,3},{8,12},{10,14},{12... | collective-permute-start | bytes 110600 | tf_op jit(solution)/shard_map/ppermute | solution.py:45
  41.9 2.0 %collective-permute-start.15 = (f32[72,128]{1,0:T(8,128)S(1)}, f32[72,128]{1,0:T(8,128)S(1)}, u32[]{:S(2)}, u32[]{:S(2)}) collective-permute-start(f32[72,128]{1,0:T(8,128)S(1)} %get-tuple-element.32), channel_id=1, source_target_pairs={{0,2},{2,0},{4,6},{6,4},{1,3},{3,1},{5,7},{7,5},{8,10},{10,8},{12,... | collective-permute-start | bytes 110600 | tf_op jit(solution)/shard_map/ppermute | solution.py:45
  43.9 1.7 %collective-permute-done.13 = f32[72,128]{1,0:T(8,128)S(1)} collective-permute-done((f32[72,128]{1,0:T(8,128)S(1)}, f32[72,128]{1,0:T(8,128)S(1)}, u32[]{:S(2)}, u32[]{:S(2)}) %collective-permute-start.13) | collective-permute-done | bytes 36896 | tf_op jit(solution)/shard_map/ppermute | solution.py:45
  45.7 0.0 collective-permute-done.14
  45.7 0.4 collective-permute-done.15
  46.0 0.1 select_select_fusion.2
  46.1 0.1 select_select_fusion.3
  46.2 1.0 %collective-permute-start.16 = (f32[2,512]{1,0:T(2,128)S(1)}, f32[2,512]{1,0:T(2,128)S(1)}, u32[]{:S(2)}, u32[]{:S(2)}) collective-permute-start(f32[2,512]{1,0:T(2,128)S(1)} %pad_maximum_fusion.7), channel_id=1, source_target_pairs={{0,8},{8,0},{16,24},{24,16},{1,9},{9,1},{17,25},{25,17},{2,10},{10... | collective-permute-start | bytes 12296 | tf_op jit(solution)/shard_map/ppermute | solution.py:45
  47.2 0.8 %collective-permute-start.17 = (f32[2,512]{1,0:T(2,128)S(1)}, f32[2,512]{1,0:T(2,128)S(1)}, u32[]{:S(2)}, u32[]{:S(2)}) collective-permute-start(f32[2,512]{1,0:T(2,128)S(1)} %pad_maximum_fusion.7), channel_id=1, source_target_pairs={{0,16},{8,24},{16,0},{24,8},{1,17},{9,25},{17,1},{25,9},{2,18},{10... | collective-permute-start | bytes 12296 | tf_op jit(solution)/shard_map/ppermute | solution.py:45
  48.1 1.7 %collective-permute-start.18 = (f32[2,512]{1,0:T(2,128)S(1)}, f32[2,512]{1,0:T(2,128)S(1)}, u32[]{:S(2)}, u32[]{:S(2)}) collective-permute-start(f32[2,512]{1,0:T(2,128)S(1)} %pad_maximum_fusion.7), channel_id=1, source_target_pairs={{0,24},{8,16},{16,8},{24,0},{1,25},{9,17},{17,9},{25,1},{2,26},{10... | collective-permute-start | bytes 12296 | tf_op jit(solution)/shard_map/ppermute | solution.py:45
  49.8 0.7 %slice_negate_fusion = f32[64,512]{1,0:T(8,128)} fusion(f32[72,512]{1,0:T(8,128)S(1)} %pad_maximum_fusion.1), kind=kLoop, calls=%fused_computation.4 | loop fusion | flops 32768 | bytes 262144 | tf_op jit(solution)/shard_map/neg | solution.py:133
  50.5 0.0 collective-permute-done.16
  50.5 0.4 collective-permute-done.17
  50.9 1.7 %collective-permute-done.18 = f32[2,512]{1,0:T(2,128)S(1)} collective-permute-done((f32[2,512]{1,0:T(2,128)S(1)}, f32[2,512]{1,0:T(2,128)S(1)}, u32[]{:S(2)}, u32[]{:S(2)}) %collective-permute-start.18) | collective-permute-done | bytes 4128 | tf_op jit(solution)/shard_map/ppermute | solution.py:45
  52.6 0.6 %add_add_fusion.1 = f32[2,512]{1,0:T(2,128)} fusion(f32[2,512]{1,0:T(2,128)S(1)} %collective-permute-done.18, f32[2,512]{1,0:T(2,128)S(1)} %collective-permute-done.17, f32[2,512]{1,0:T(2,128)S(1)} %pad_maximum_fusion.7, f32[2,512]{1,0:T(2,128)S(1)} %collective-permute-done.16), kind=kLoop, calls=%fused_computation.26 | loop fusion | flops 3072 | bytes 20480 | tf_op jit(solution)/shard_map/add | solution.py:137
  (24 shorter events, 0.3 us)
Async XLA Ops:
  0.6 3.1 %copy-start = (f32[2,128,512]{2,1,0:T(8,128)S(1)}, f32[2,128,512]{2,1,0:T(8,128)}, u32[]{:S(2)}) copy-start(f32[2,128,512]{2,1,0:T(8,128)} %param.5) | copy-start | bytes 1572868
  0.6 18.7 %collective-permute-start = (f32[2,256,128]{2,1,0:T(8,128)}, f32[2,256,128]{2,1,0:T(8,128)S(1)}, u32[]{:S(2)}, u32[]{:S(2)}) collective-permute-start(f32[2,256,128]{2,1,0:T(8,128)} %refs_0_.1), channel_id=1, source_target_pairs={{0,2},{2,4},{4,6},{6,0},{1,3},{3,5},{5,7},{7,1},{8,10},{10,12},{12... | collective-permute-start | bytes 786440 | tf_op jit(solution)/shard_map/ppermute | solution.py:42
  5.4 3.6 %copy-start.1 = (f32[2,256,128]{2,1,0:T(8,128)S(1)}, f32[2,256,128]{2,1,0:T(8,128)}, u32[]{:S(2)}) copy-start(f32[2,256,128]{2,1,0:T(8,128)} %refs_0_.1) | copy-start | bytes 786436
  5.4 7.6 %collective-permute-start.3 = (f32[2,32,512]{2,1,0:T(8,128)S(1)}, f32[2,32,512]{2,1,0:T(8,128)S(1)}, u32[]{:S(2)}, u32[]{:S(2)}) collective-permute-start(f32[2,32,512]{2,1,0:T(8,128)S(1)} %get-tuple-element.20), channel_id=1, source_target_pairs={{0,8},{8,0},{16,24},{24,16},{1,9},{9,1},{17,25},{25,17},{2,10},{10... | collective-permute-start | bytes 393224 | tf_op jit(solution)/shard_map/ppermute | solution.py:45
  7.0 7.8 %collective-permute-start.4 = (f32[2,32,512]{2,1,0:T(8,128)S(1)}, f32[2,32,512]{2,1,0:T(8,128)S(1)}, u32[]{:S(2)}, u32[]{:S(2)}) collective-permute-start(f32[2,32,512]{2,1,0:T(8,128)S(1)} %get-tuple-element.19), channel_id=1, source_target_pairs={{0,16},{8,24},{16,0},{24,8},{1,17},{9,25},{17,1},{25,9},{2,18},{10... | collective-permute-start | bytes 393224 | tf_op jit(solution)/shard_map/ppermute | solution.py:45
  8.5 6.3 %collective-permute-start.5 = (f32[2,32,512]{2,1,0:T(8,128)S(1)}, f32[2,32,512]{2,1,0:T(8,128)S(1)}, u32[]{:S(2)}, u32[]{:S(2)}) collective-permute-start(f32[2,32,512]{2,1,0:T(8,128)S(1)} %get-tuple-element.18), channel_id=1, source_target_pairs={{0,24},{8,16},{16,8},{24,0},{1,25},{9,17},{17,9},{25,1},{2,26},{10... | collective-permute-start | bytes 393224 | tf_op jit(solution)/shard_map/ppermute | solution.py:45
  9.0 22.6 %collective-permute-start.2 = (f32[2,256,128]{2,1,0:T(8,128)S(1)}, f32[2,256,128]{2,1,0:T(8,128)S(1)}, u32[]{:S(2)}, u32[]{:S(2)}) collective-permute-start(f32[2,256,128]{2,1,0:T(8,128)S(1)} %copy-done.1), channel_id=1, source_target_pairs={{0,6},{2,0},{4,2},{6,4},{1,7},{3,1},{5,3},{7,5},{8,14},{10,8},{12,... | collective-permute-start | bytes 786440 | tf_op jit(solution)/shard_map/ppermute | solution.py:42
  12.0 1.0 %copy-start.2 = (s32[2,4]{1,0:T(2,128)S(1)}, s32[2,4]{1,0:T(2,128)}, u32[]{:S(2)}) copy-start(s32[2,4]{1,0:T(2,128)} %param.7) | copy-start | bytes 100
  14.8 5.1 %collective-permute-start.6 = (f32[2,32,128]{2,1,0:T(8,128)S(1)}, f32[2,32,128]{2,1,0:T(8,128)S(1)}, u32[]{:S(2)}, u32[]{:S(2)}) collective-permute-start(f32[2,32,128]{2,1,0:T(8,128)S(1)} %get-tuple-element.31), channel_id=1, source_target_pairs={{0,2},{2,0},{4,6},{6,4},{1,3},{3,1},{5,7},{7,5},{8,10},{10,8},{12,... | collective-permute-start | bytes 98312 | tf_op jit(solution)/shard_map/ppermute | solution.py:45
  16.5 11.4 %collective-permute-start.7 = (f32[2,32,128]{2,1,0:T(8,128)S(1)}, f32[2,32,128]{2,1,0:T(8,128)S(1)}, u32[]{:S(2)}, u32[]{:S(2)}) collective-permute-start(f32[2,32,128]{2,1,0:T(8,128)S(1)} %get-tuple-element.30), channel_id=1, source_target_pairs={{0,4},{2,6},{4,0},{6,2},{1,5},{3,7},{5,1},{7,3},{8,12},{10,14},{12... | collective-permute-start | bytes 98312 | tf_op jit(solution)/shard_map/ppermute | solution.py:45
  18.5 9.4 %collective-permute-start.8 = (f32[2,32,128]{2,1,0:T(8,128)S(1)}, f32[2,32,128]{2,1,0:T(8,128)S(1)}, u32[]{:S(2)}, u32[]{:S(2)}) collective-permute-start(f32[2,32,128]{2,1,0:T(8,128)S(1)} %get-tuple-element.29), channel_id=1, source_target_pairs={{0,6},{2,4},{4,2},{6,0},{1,7},{3,5},{5,3},{7,1},{8,14},{10,12},{12... | collective-permute-start | bytes 98312 | tf_op jit(solution)/shard_map/ppermute | solution.py:45
  19.3 16.5 %collective-permute-start.1 = (f32[2,256,128]{2,1,0:T(8,128)S(1)}, f32[2,256,128]{2,1,0:T(8,128)S(1)}, u32[]{:S(2)}, u32[]{:S(2)}) collective-permute-start(f32[2,256,128]{2,1,0:T(8,128)S(1)} %collective-permute-done.refs_1_), channel_id=1, source_target_pairs={{0,2},{2,4},{4,6},{6,0},{1,3},{3,5},{5,7},{7,1},{8,10},{10,12},{12... | collective-permute-start | bytes 786440 | tf_op jit(solution)/shard_map/ppermute | solution.py:42
  27.9 6.4 %collective-permute-start.10 = (f32[4,2,32,128]{3,2,1,0:T(8,128)S(1)}, f32[4,2,32,128]{3,2,1,0:T(8,128)S(1)}, u32[]{:S(2)}, u32[]{:S(2)}) collective-permute-start(f32[4,2,32,128]{3,2,1,0:T(8,128)S(1)} %pad_maximum_fusion.2.refs_4_), channel_id=1, source_target_pairs={{0,16},{8,24},{16,0},{24,8},{1,17},{9,25},{17,1},{25,9},{2,18},{10... | collective-permute-start | bytes 393224 | tf_op jit(solution)/shard_map/ppermute | solution.py:45
  28.0 6.4 %collective-permute-start.11 = (f32[4,2,32,128]{3,2,1,0:T(8,128)S(1)}, f32[4,2,32,128]{3,2,1,0:T(8,128)S(1)}, u32[]{:S(2)}, u32[]{:S(2)}) collective-permute-start(f32[4,2,32,128]{3,2,1,0:T(8,128)S(1)} %pad_maximum_fusion.2.refs_4_), channel_id=1, source_target_pairs={{0,24},{8,16},{16,8},{24,0},{1,25},{9,17},{17,9},{25,1},{2,26},{10... | collective-permute-start | bytes 393224 | tf_op jit(solution)/shard_map/ppermute | solution.py:45
  30.4 5.4 %collective-permute-start.9 = (f32[4,2,32,128]{3,2,1,0:T(8,128)S(1)}, f32[4,2,32,128]{3,2,1,0:T(8,128)S(1)}, u32[]{:S(2)}, u32[]{:S(2)}) collective-permute-start(f32[4,2,32,128]{3,2,1,0:T(8,128)S(1)} %pad_maximum_fusion.2.refs_4_), channel_id=1, source_target_pairs={{0,8},{8,0},{16,24},{24,16},{1,9},{9,1},{17,25},{25,17},{2,10},{10... | collective-permute-start | bytes 393224 | tf_op jit(solution)/shard_map/ppermute | solution.py:45
  37.4 1.8 %collective-permute-start.12 = (f32[2,384,128]{2,1,0:T(8,128)S(1)}, f32[2,384,128]{2,1,0:T(8,128)S(1)}, u32[]{:S(2)}, u32[]{:S(2)}) collective-permute-start(f32[2,384,128]{2,1,0:T(8,128)S(1)} %shard_map.59), channel_id=1, source_target_pairs={{0,1},{1,0},{2,3},{3,2},{4,5},{5,4},{6,7},{7,6},{8,9},{9,8},{10,11... | collective-permute-start | bytes 1179656 | tf_op jit(solution)/shard_map/ppermute | solution.py:42
  39.5 6.2 %collective-permute-start.13 = (f32[72,128]{1,0:T(8,128)S(1)}, f32[72,128]{1,0:T(8,128)S(1)}, u32[]{:S(2)}, u32[]{:S(2)}) collective-permute-start(f32[72,128]{1,0:T(8,128)S(1)} %get-tuple-element.34), channel_id=1, source_target_pairs={{0,6},{2,4},{4,2},{6,0},{1,7},{3,5},{5,3},{7,1},{8,14},{10,12},{12... | collective-permute-start | bytes 110600 | tf_op jit(solution)/shard_map/ppermute | solution.py:45
  39.6 6.1 %collective-permute-start.14 = (f32[72,128]{1,0:T(8,128)S(1)}, f32[72,128]{1,0:T(8,128)S(1)}, u32[]{:S(2)}, u32[]{:S(2)}) collective-permute-start(f32[72,128]{1,0:T(8,128)S(1)} %get-tuple-element.33), channel_id=1, source_target_pairs={{0,4},{2,6},{4,0},{6,2},{1,5},{3,7},{5,1},{7,3},{8,12},{10,14},{12... | collective-permute-start | bytes 110600 | tf_op jit(solution)/shard_map/ppermute | solution.py:45
  41.9 4.1 %collective-permute-start.15 = (f32[72,128]{1,0:T(8,128)S(1)}, f32[72,128]{1,0:T(8,128)S(1)}, u32[]{:S(2)}, u32[]{:S(2)}) collective-permute-start(f32[72,128]{1,0:T(8,128)S(1)} %get-tuple-element.32), channel_id=1, source_target_pairs={{0,2},{2,0},{4,6},{6,4},{1,3},{3,1},{5,7},{7,5},{8,10},{10,8},{12,... | collective-permute-start | bytes 110600 | tf_op jit(solution)/shard_map/ppermute | solution.py:45
  46.2 4.2 %collective-permute-start.16 = (f32[2,512]{1,0:T(2,128)S(1)}, f32[2,512]{1,0:T(2,128)S(1)}, u32[]{:S(2)}, u32[]{:S(2)}) collective-permute-start(f32[2,512]{1,0:T(2,128)S(1)} %pad_maximum_fusion.7), channel_id=1, source_target_pairs={{0,8},{8,0},{16,24},{24,16},{1,9},{9,1},{17,25},{25,17},{2,10},{10... | collective-permute-start | bytes 12296 | tf_op jit(solution)/shard_map/ppermute | solution.py:45
  47.2 3.6 %collective-permute-start.17 = (f32[2,512]{1,0:T(2,128)S(1)}, f32[2,512]{1,0:T(2,128)S(1)}, u32[]{:S(2)}, u32[]{:S(2)}) collective-permute-start(f32[2,512]{1,0:T(2,128)S(1)} %pad_maximum_fusion.7), channel_id=1, source_target_pairs={{0,16},{8,24},{16,0},{24,8},{1,17},{9,25},{17,1},{25,9},{2,18},{10... | collective-permute-start | bytes 12296 | tf_op jit(solution)/shard_map/ppermute | solution.py:45
  48.1 4.5 %collective-permute-start.18 = (f32[2,512]{1,0:T(2,128)S(1)}, f32[2,512]{1,0:T(2,128)S(1)}, u32[]{:S(2)}, u32[]{:S(2)}) collective-permute-start(f32[2,512]{1,0:T(2,128)S(1)} %pad_maximum_fusion.7), channel_id=1, source_target_pairs={{0,24},{8,16},{16,8},{24,0},{1,25},{9,17},{17,9},{25,1},{2,26},{10... | collective-permute-start | bytes 12296 | tf_op jit(solution)/shard_map/ppermute | solution.py:45
